TPU v7x, 32 devices: a whole 2x2x4 slice. The times are simulated.
32 devices in a mesh: dp: 4 (over y, x), ctx: 8 (over z, core).
Axes of the slice: x: 2, y: 2, z: 4, core: 2. Of those that a mesh axis runs over, the one named last changes fastest.
Arguments:
- hidden_in: bfloat16 [4, 1024, 4096], P('dp', 'ctx'), may hold values from -6 to 6
- write_weight: bfloat16 [4096, 128], P(('dp', 'ctx')), may hold values from -0.09375 to 0.09375
- shard_scale: float32 [32], P(('dp', 'ctx')), may hold values from 0.5 to 2
- inner_acts: bfloat16 [4, 1024, 4096], P('dp', 'ctx'), may hold values from -6 to 6
- read_proj: bfloat16 [4, 1024, 128], P('dp', 'ctx'), may hold values from -0.13183594 to 0.13183594
- step_size: float32 [4, 64, 1024], P('dp', None, 'ctx'), may hold values from 0.1 to 1
- log_decay: float32 [4, 64, 1024], P('dp', None, 'ctx'), may hold values from -2 to 0
- grad_fwd: bfloat16 [4, 1024, 4096], P('dp', 'ctx'), may hold values from -1.5 to 1.5
- grad_rev: bfloat16 [4, 1024, 4096], P('dp', 'ctx'), may hold values from -1.5 to 1.5
Outputs:
- grad_inner: bfloat16 [4, 1024, 4096], P('dp', 'ctx')
- grad_hidden: bfloat16 [4, 1024, 4096], P('dp', 'ctx')
- grad_weight: float32 [4096, 128], P(('dp', 'ctx'))
All inputs are finite; a program needn't handle non-finite values.
Results may differ from a plain program's by a relative error of at most 0.0064.
Values may be sent and summed in bfloat16 or wider, within the bound.
No kernel may reach another device: no remote copies, remote signals or barrier semaphores. Data moves between devices by JAX's collectives and lax.ppermute only.
A program may use at most 256 MiB of HBM per device.

v0:
```python
import jax
import jax.numpy as jnp
from jax import lax
from jax.sharding import PartitionSpec as P

BLOCK = 128


masked_low = -1e30


def carried_in(part, axis, combine, identity, reverse):
    count = lax.axis_size(axis)
    place = lax.axis_index(axis)
    ahead = count - 1 - place if reverse else place
    gathered = jax.tree.map(lambda a: lax.all_gather(a, axis), part)
    state = jax.tree.map(lambda a, e: jnp.zeros_like(a) + jnp.asarray(e, a.dtype), part, identity)

    def one(lap, state):
        source = count - 1 - lap if reverse else lap
        return combine(
            state, jax.tree.map(lambda a: lax.dynamic_index_in_dim(a, source, 0, False), gathered)
        )

    return lax.fori_loop(0, ahead, one, state)


def decay_state(decays, state_mat):
    head_count = decays.shape[0]
    shaped = state_mat.reshape(state_mat.shape[0], head_count, state_mat.shape[1] // head_count)
    return (shaped * decays[None, :, None]).reshape(state_mat.shape)


def combine_states(earlier, following):
    return (earlier[0] * following[0], following[1] + decay_state(following[0], earlier[1]))


def block_cums(decay_rows):
    local_cum = jnp.cumsum(decay_rows, axis=1)
    return (local_cum, local_cum - decay_rows)


def block_summary(read_rows, decay_rows, fwd_rows, back_rows):
    local_cum, local_excl = block_cums(decay_rows)
    block_end = local_cum[:, -1:]
    head_count = decay_rows.shape[0]
    row_count = fwd_rows.shape[0]
    col_count = fwd_rows.shape[1]
    fwd_weight = jnp.exp(local_cum).T
    back_weight = jnp.exp(block_end - local_excl).T
    fwd_scaled = (
        (fwd_rows.reshape(row_count, head_count, col_count // head_count) * fwd_weight[:, :, None])
        .reshape(row_count, col_count)
        .astype(jnp.bfloat16)
    )
    back_scaled = (
        (
            back_rows.reshape(row_count, head_count, col_count // head_count)
            * back_weight[:, :, None]
        )
        .reshape(row_count, col_count)
        .astype(jnp.bfloat16)
    )
    right_part = lax.dot_general(
        read_rows, fwd_scaled, (((0,), (0,)), ((), ())), preferred_element_type=jnp.float32
    )
    left_part = lax.dot_general(
        read_rows, back_scaled, (((0,), (0,)), ((), ())), preferred_element_type=jnp.float32
    )
    return (jnp.exp(block_end[:, 0]), right_part, left_part)


def block_outputs(
    inner_rows, read_rows, write_rows, step_rows, decay_rows, fwd_rows, back_rows, right_in, left_in
):
    local_cum, local_excl = block_cums(decay_rows)
    block_end = local_cum[:, -1:]
    row_count = inner_rows.shape[0]
    head_count = step_rows.shape[0]
    col_count = inner_rows.shape[1]
    head_dim = col_count // head_count
    kernel = lax.dot_general(
        write_rows, read_rows, (((1,), (1,)), ((), ())), preferred_element_type=jnp.float32
    )
    position_indices = jnp.arange(row_count)
    upper_mask = position_indices[None, :] >= position_indices[:, None]
    lower_mask = position_indices[None, :] <= position_indices[:, None]
    fwd_decay = jnp.exp(
        jnp.where(upper_mask[None], local_cum[:, None, :] - local_cum[:, :, None], masked_low)
    )
    rev_decay = jnp.exp(
        jnp.where(lower_mask[None], local_excl[:, :, None] - local_excl[:, None, :], masked_low)
    )
    fwd_mix = (fwd_decay * kernel[None]).astype(jnp.bfloat16)
    rev_mix = (rev_decay * kernel[None]).astype(jnp.bfloat16)
    fwd_heads = fwd_rows.reshape(row_count, head_count, head_dim)
    back_heads = back_rows.reshape(row_count, head_count, head_dim)
    inner_heads = inner_rows.reshape(row_count, head_count, head_dim)
    intra_sum = jnp.einsum(
        "hst,thp->shp", fwd_mix, fwd_heads, preferred_element_type=jnp.float32
    ) + jnp.einsum("hst,thp->shp", rev_mix, back_heads, preferred_element_type=jnp.float32)
    write_float = write_rows.astype(jnp.float32)
    right_term = jnp.dot(write_float, right_in, precision=lax.Precision.HIGHEST).reshape(
        row_count, head_count, head_dim
    )
    left_term = jnp.dot(write_float, left_in, precision=lax.Precision.HIGHEST).reshape(
        row_count, head_count, head_dim
    )
    fwd_edge = jnp.exp(block_end - local_cum).T
    back_edge = jnp.exp(local_excl).T
    step_cols = step_rows.T
    combined = intra_sum + fwd_edge[:, :, None] * right_term + back_edge[:, :, None] * left_term
    grad_block = (
        (step_cols[:, :, None] * combined).reshape(row_count, col_count).astype(jnp.bfloat16)
    )
    fwd_dots = jnp.einsum(
        "thp,shp->hst", fwd_heads, inner_heads, preferred_element_type=jnp.float32
    )
    back_dots = jnp.einsum(
        "thp,shp->hst", back_heads, inner_heads, preferred_element_type=jnp.float32
    )
    mixed_weights = jnp.sum(
        step_rows[:, :, None] * (fwd_decay * fwd_dots + rev_decay * back_dots), axis=0
    ).astype(jnp.bfloat16)
    intra_write = jnp.dot(mixed_weights, read_rows, preferred_element_type=jnp.float32)
    fwd_inner = (inner_heads * (step_cols * fwd_edge)[:, :, None]).reshape(row_count, col_count)
    back_inner = (inner_heads * (step_cols * back_edge)[:, :, None]).reshape(row_count, col_count)
    edge_write = lax.dot_general(
        fwd_inner, right_in, (((1,), (1,)), ((), ())), precision=lax.Precision.HIGHEST
    ) + lax.dot_general(
        back_inner, left_in, (((1,), (1,)), ((), ())), precision=lax.Precision.HIGHEST
    )
    write_block = (intra_write + edge_write).astype(jnp.bfloat16)
    return (grad_block, write_block)


def shards(
    hidden_in,
    write_weight,
    shard_scale,
    inner_acts,
    read_proj,
    step_size,
    log_decay,
    grad_fwd,
    grad_rev,
):
    local_weight = (write_weight.astype(jnp.float32) * shard_scale[0]).astype(jnp.bfloat16)
    weight_eff = lax.all_gather(local_weight, ("dp", "ctx"), axis=0, tiled=True)
    hidden = hidden_in[0]
    inner_seq = inner_acts[0]
    read_seq = read_proj[0]
    step_seq = step_size[0]
    decay_seq = log_decay[0]
    fwd_seq = grad_fwd[0]
    flipped = grad_rev[0]
    ctx_count = lax.axis_size("ctx")
    tokens = inner_seq.shape[0]
    pieces = flipped.reshape(ctx_count, tokens // ctx_count, flipped.shape[1])
    pieces = lax.all_to_all(pieces, "ctx", split_axis=0, concat_axis=0, tiled=True)
    pieces = lax.all_to_all(pieces[::-1], "ctx", split_axis=0, concat_axis=0, tiled=True)
    flipped = pieces.reshape(tokens, flipped.shape[1])
    back_seq = flipped[::-1]
    block_count = tokens // BLOCK
    summaries = [block_summary(read_seq, decay_seq, fwd_seq, back_seq)]
    head_count = decay_seq.shape[0]
    zero_state = jnp.zeros((read_seq.shape[1], inner_seq.shape[1]), jnp.float32)
    device_decay = jnp.ones((head_count,), jnp.float32)
    right_sum = zero_state
    left_sum = zero_state
    position = 0
    device_decay = device_decay * summaries[position][0]
    left_sum = summaries[position][2] + decay_state(summaries[position][0], left_sum)
    for position in reversed(range(block_count)):
        right_sum = summaries[position][1] + decay_state(summaries[position][0], right_sum)
    identity = (jnp.ones((head_count,), jnp.float32), zero_state)
    right_edge = carried_in((device_decay, right_sum), "ctx", combine_states, identity, True)[1]
    left_edge = carried_in((device_decay, left_sum), "ctx", combine_states, identity, False)[1]
    write_seq = jnp.dot(hidden, weight_eff, preferred_element_type=jnp.float32).astype(jnp.bfloat16)
    carried = right_edge
    right_ins = []
    for position in reversed(range(block_count)):
        right_ins.insert(0, carried)
        carried = summaries[position][1] + decay_state(summaries[position][0], carried)
    carried = left_edge
    left_ins = [carried]
    position = 0
    grad_block, write_block = block_outputs(
        inner_seq,
        read_seq,
        write_seq,
        step_seq,
        decay_seq,
        fwd_seq,
        back_seq,
        right_ins[position],
        left_ins[position],
    )
    grad_hid = lax.dot_general(
        write_block, weight_eff, (((1,), (1,)), ((), ())), preferred_element_type=jnp.float32
    ).astype(jnp.bfloat16)
    share_rows = lax.psum_scatter(
        lax.dot_general(
            hidden, write_block, (((0,), (0,)), ((), ())), preferred_element_type=jnp.float32
        ),
        "dp",
        scatter_dimension=0,
        tiled=True,
    )
    summed = lax.psum_scatter(share_rows, "ctx", scatter_dimension=0, tiled=True)
    position_total = lax.axis_size("dp") * ctx_count * tokens
    return (grad_block[None], grad_hid[None], summed / position_total)


def solution(mesh):
    in_specs = (
        P("dp", "ctx", None),
        P(("dp", "ctx"), None),
        P(("dp", "ctx")),
        P("dp", "ctx", None),
        P("dp", "ctx", None),
        P("dp", None, "ctx"),
        P("dp", None, "ctx"),
        P("dp", "ctx", None),
        P("dp", "ctx", None),
    )
    out_specs = (P("dp", "ctx", None), P("dp", "ctx", None), P(("dp", "ctx"), None))
    return jax.shard_map(shards, mesh=mesh, in_specs=in_specs, out_specs=out_specs, check_vma=False)
```

profile of v0, /device:TPU:0, one launch (start us, length us, event | category | flops | bytes accessed | tf_op | source)
XLA Modules:
  0.0 494.3 jit_solution(12675327327999915136)
XLA Ops:
  7.2 1.1 reduce_window_sum.12
  8.3 0.2 exponential_reduce_fusion
  8.7 1.6 copy.23
  10.4 0.3 multiply_convert_fusion.4
  10.7 1.9 fusion.1
  12.7 63.9 %all_to_all.10 = bf16[8,16,4096]{2,1,0:T(8,128)(2,1)S(1)} all-to-all(bf16[8,16,4096]{2,1,0:T(8,128)(2,1)} %bitcast.130), channel_id=1, replica_groups=mesh['dp'=4,'ctx'=8] {'ctx'}, dimensions={0} | all-to-all | bytes 2097152 | tf_op jit(solution)/shard_map/all_to_all | solution.py:160
  76.6 1.0 rev.6
  77.6 3.6 all-to-all-start.1
  81.4 60.3 %all-to-all-done.1 = bf16[8,16,4096]{2,1,0:T(8,128)(2,1)S(1)} async-done(((bf16[8,16,4096]{2,1,0:T(8,128)(2,1)}), bf16[8,16,4096]{2,1,0:T(8,128)(2,1)S(1)}, u32[]{:S(2)}, u32[]{:S(2)}) %all-to-all-start.1) | async-done | bytes 1048608 | tf_op jit(solution)/shard_map/all_to_all | solution.py:161
  141.8 1.3 copy.24
  143.1 13.7 %rev.7 = bf16[128,4096]{0,1:T(8,128)(2,1)S(1)} reverse(bf16[128,4096]{0,1:T(8,128)(2,1)} %copy.24), dimensions={0} | reverse | bytes 2097152 | tf_op jit(solution)/shard_map/rev | solution.py:163
  156.7 0.2 fusion.7
  157.0 1.9 fusion
  159.6 0.6 multiply_convert_fusion.7
  160.4 0.6 dynamic-slice
  161.7 0.2 dynamic-update-slice
  161.9 14.4 %all-reduce = f32[512]{0:T(512)S(1)} all-reduce(f32[512]{0:T(512)S(1)} %dynamic-update-slice), channel_id=3, replica_groups=mesh['dp'=4,'ctx'=8] {'ctx'}, use_global_device_ids=true, to_apply=%add | all-reduce | flops 512 | bytes 4096
  176.4 0.7 reshape.149
  177.0 1.6 copy.29
  178.7 2.8 fusion.39
  181.5 6.4 %multiply_reduce_fusion = bf16[128,128]{1,0:T(8,128)(2,1)S(1)} fusion(f32[64,128,128]{2,1,0:T(8,128)} %fusion.39, bf16[128,64,64]{0,2,1:T(8,128)(2,1)S(1)} %bitcast.118, bf16[128,64,64]{0,2,1:T(8,128)(2,1)} %bitcast.125, f32[64,128]{1,0:T(8,128)S(1)} %bitcast.133, f32[64,128]{1,0:T(8,128)S(1)} %get-tuple-element.186, f32[64,128]{1,0:T(8,128)S(1)} %reduce_window_sum.12, ...), kind=kOutput, calls=%fused_computation.11 | convolution fusion | flops 143638528 | bytes 6455296 | tf_op jit(solution)/shard_map/thp,shp->hst/dot_general | solution.py:119
  187.9 0.1 fusion.28
  188.0 18.1 %all-gather.9.cloned.1.call-done = f32[1024,4096]{0,1:T(8,128)} async-done(((f32[128,4096]{0,1:T(8,128)}), f32[1024,4096]{0,1:T(8,128)}) %all-gather.9.cloned.1.call-update) | async-done | bytes 16777232 | tf_op jit(solution)/shard_map/all_gather | solution.py:16
  206.1 17.9 %copy.35 = f32[1024,4096]{1,0:T(8,128)} copy(f32[1024,4096]{0,1:T(8,128)} %all-gather.9.cloned.1.call-done) | data formatting | bytes 33554432 | tf_op jit(solution)/shard_map/while | solution.py:25
  224.0 0.2 broadcast_in_dim.29.clone.1
  224.2 23.2 %while.26 = (s32[]{:T(128)}, f32[128,4096]{1,0:T(8,128)S(1)}, s32[]{:T(128)}, f32[8,128,4096]{2,1,0:T(8,128)}, f32[8,64]{1,0:T(8,128)}, /*index=5*/s32[]{:T(128)}, s32[]{:T(128)}, s32[]{:T(128)}, s32[]{:T(128)}) while((s32[]{:T(128)}, f32[128,4096]{1,0:T(8,128)S(1)}, s32[]{:T(128)}, f32[8,128,4096]{2,1,0:T(8,128)}, f32[8,64]{1,0:T(8,128)}, ...), condition=%wide.region_2.3_spmd, body=%wide.region_1.2_spmd.sunk | while | flops 1048582 | bytes 6357907 | solution.py:25
  224.2 0.7 dynamic-slice_bitcast_fusion.4
  225.1 2.5 bitcast_add_fusion.5
  227.6 0.7 dynamic-slice_bitcast_fusion.4
  228.4 2.5 bitcast_add_fusion.5
  230.9 0.7 dynamic-slice_bitcast_fusion.4
  231.7 2.4 bitcast_add_fusion.5
  234.2 0.7 dynamic-slice_bitcast_fusion.4
  235.0 2.4 bitcast_add_fusion.5
  237.4 0.7 dynamic-slice_bitcast_fusion.4
  238.3 2.4 bitcast_add_fusion.5
  240.7 0.7 dynamic-slice_bitcast_fusion.4
  241.6 2.4 bitcast_add_fusion.5
  244.0 0.7 dynamic-slice_bitcast_fusion.4
  244.8 2.6 bitcast_add_fusion.5
  247.4 0.1 mul.195
  247.6 1.8 copy-done.4
  249.4 3.5 fusion.3
  252.9 107.6 %all-gather.11.cloned.1.call-done = f32[1024,4096]{0,1:T(8,128)} async-done(((f32[128,4096]{0,1:T(8,128)}), f32[1024,4096]{0,1:T(8,128)}) %all-gather.11.cloned.1.call-update) | async-done | bytes 16777232 | tf_op jit(solution)/shard_map/all_gather | solution.py:16
  360.5 17.5 %copy.36 = f32[1024,4096]{1,0:T(8,128)} copy(f32[1024,4096]{0,1:T(8,128)} %all-gather.11.cloned.1.call-done) | data formatting | bytes 33554432 | tf_op jit(solution)/shard_map/while | solution.py:25
  378.0 0.2 broadcast_in_dim.29.clone
  378.2 0.2 while.27
  378.5 0.1 mul.199
  378.6 1.1 copy-done.5
  379.7 3.5 fusion.23
  383.2 1.8 convolution_bitcast_fusion
  385.1 31.1 %all-gather.7.cloned.1.call-done = bf16[4096,128]{1,0:T(8,128)(2,1)} async-done(((bf16[128,128]{1,0:T(8,128)(2,1)}), bf16[4096,128]{1,0:T(8,128)(2,1)}) %all-gather.7.cloned.1.call-update) | async-done | bytes 1048592 | tf_op jit(solution)/shard_map/all_gather | solution.py:149
  416.1 1.8 convolution_convert_fusion.1
  417.9 0.2 fusion.32
  418.1 2.8 fusion.5
  420.9 3.2 fusion.37
  424.1 29.0 %reduce-scatter.3.cloned.1.call-done = f32[1024,128]{0,1:T(8,128)} async-done(((f32[4096,128]{0,1:T(8,128)}), f32[1024,128]{0,1:T(8,128)}) %reduce-scatter.3.cloned.1.call-update) | async-done | bytes 524304 | tf_op jit(solution)/shard_map/reduce_scatter | solution.py:202
  453.2 1.8 fusion.38
  455.1 3.9 fusion.10
  459.0 1.3 copy.31
  460.3 1.4 fusion.2
  461.7 24.5 %reduce-scatter.5.cloned.1.call-done = f32[128,128]{0,1:T(8,128)} async-done(((f32[1024,128]{0,1:T(8,128)}), f32[128,128]{0,1:T(8,128)}) %reduce-scatter.5.cloned.1.call-update) | async-done | bytes 65552 | tf_op jit(solution)/shard_map/reduce_scatter | solution.py:210
  486.2 0.8 broadcast_multiply_fusion
  487.1 0.7 copy.32
  (72 shorter events, 1.8 us)
Async XLA Ops:
  7.2 376.1 %copy-start = (bf16[1,128,4096]{2,1,0:T(8,128)(2,1)S(1)}, bf16[1,128,4096]{2,1,0:T(8,128)(2,1)}, u32[]{:S(2)}) copy-start(bf16[1,128,4096]{2,1,0:T(8,128)(2,1)} %param.13) | copy-start | bytes 3145732
  7.2 199.0 %all-gather.9.cloned.1.call-start = ((), (), s32[]{:S(2)}) async-start(), calls=%async_computation.7 | async-start | bytes 18874368 | tf_op jit(solution)/shard_map/all_gather | solution.py:16
  8.7 2.0 copy-start.12
  10.4 168.3 %copy-start.6 = (bf16[1,128,4096]{1,2,0:T(8,128)(2,1)}, bf16[1,128,4096]{1,2,0:T(8,128)(2,1)S(1)}, u32[]{:S(2)}) copy-start(bf16[1,128,4096]{1,2,0:T(8,128)(2,1)S(1)} %copy.23) | copy-start | bytes 3145732
  76.6 4.7 copy-start.13
  76.6 4.7 copy-start.14
  77.6 64.2 %all-to-all-start.1 = ((bf16[8,16,4096]{2,1,0:T(8,128)(2,1)}), bf16[8,16,4096]{2,1,0:T(8,128)(2,1)S(1)}, u32[]{:S(2)}, u32[]{:S(2)}) async-start(bf16[8,16,4096]{2,1,0:T(8,128)(2,1)} %rev.6), calls=%async_computation.1 | async-start | bytes 2097152 | tf_op jit(solution)/shard_map/all_to_all | solution.py:161
  81.2 279.4 %all-gather.11.cloned.1.call-start = ((), (), s32[]{:S(2)}) async-start(), calls=%async_computation.8 | async-start | bytes 18874368 | tf_op jit(solution)/shard_map/all_gather | solution.py:16
  156.7 2.2 copy-start.8
  157.0 2.7 copy-start.15
  157.0 3.4 copy-start.20
  158.9 257.2 %all-gather.7.cloned.1.call-start = ((), (), s32[]{:S(2)}) async-start(), calls=%async_computation.4 | async-start | bytes 1081344 | tf_op jit(solution)/shard_map/all_gather | solution.py:149
  160.3 292.8 %reduce-scatter.3.cloned.1.call-start = ((), (), s32[]{:S(2)}) async-start(), calls=%async_computation.5 | async-start | bytes 2621440 | tf_op jit(solution)/shard_map/reduce_scatter | solution.py:202
  160.4 21.1 %copy-start.16 = (pred[128,128]{1,0:T(8,128)(4,1)}, pred[128,128]{1,0:T(8,128)(4,1)S(1)}, u32[]{:S(2)}) copy-start(pred[128,128]{1,0:T(8,128)(4,1)S(1)} %get-tuple-element.189) | copy-start | bytes 49156
  160.4 21.1 %copy-start.18 = (pred[128,128]{1,0:T(8,128)(4,1)}, pred[128,128]{1,0:T(8,128)(4,1)S(1)}, u32[]{:S(2)}) copy-start(pred[128,128]{1,0:T(8,128)(4,1)S(1)} %get-tuple-element.190) | copy-start | bytes 49156
  178.7 2.9 copy-start.3
  247.4 5.5 %copy-start.1 = (f32[128,4096]{1,0:T(8,128)}, f32[128,4096]{1,0:T(8,128)S(1)}, u32[]{:S(2)}) copy-start(f32[128,4096]{1,0:T(8,128)S(1)} %get-tuple-element.131) | copy-start | bytes 6291460
  247.4 2.0 copy-start.4
  378.4 1.2 copy-start.5
  385.0 33.1 %copy-start.19 = (pred[128,128]{1,0:T(8,128)(4,1)S(1)}, pred[128,128]{1,0:T(8,128)(4,1)}, u32[]{:S(2)}) copy-start(pred[128,128]{1,0:T(8,128)(4,1)} %copy-done.18) | copy-start | bytes 49156
  385.0 101.2 %reduce-scatter.5.cloned.1.call-start = ((), (), s32[]{:S(2)}) async-start(), calls=%async_computation.6 | async-start | bytes 589824 | tf_op jit(solution)/shard_map/reduce_scatter | solution.py:210
  416.1 2.0 copy-start.7
  418.1 2.8 copy-start.2
  453.2 1.9 copy-start.9
  453.2 1.9 copy-start.11
  453.2 1.9 copy-start.17
  459.0 1.3 copy-start.10
Sparse Core Ops, SparseCore 0:
  12.8 193.3 all-gather.8
  207.7 152.7 all-gather.10
  364.1 51.9 all-gather.6
  418.9 34.1 reduce-scatter.2
  455.3 30.8 reduce-scatter.4
where the time goes:
time: 497 us; the launch traced here: 494 us
  waiting for transfers between devices  271 us (55%)
  blocking collectives  78.3 us (16%)
  local copies, waits for them, and re-layouts  68.1 us (14%)
  matrix products  37.1 us (7%)
  other arithmetic  20.5 us (4%)
  between operations  15.5 us (3%)
    all_gather x2, waiting for transfers between devices, carried_in(): gathered = jax.tree.map(lambda a: lax.all_gather(a, axis), part)  126 us
    all_to_all x1, blocking collectives, shards(): lax.all_to_all(pieces, 'ctx', split_axis=0, concat_axis=0, tiled=True)  63.9 us
    all_to_all x1, waiting for transfers between devices, shards(): lax.all_to_all(pieces[::-1], 'ctx', split_axis=0, concat_axis=0, tiled=True)  60.3 us
    while x2, local copies, waits for them, and re-layouts, carried_in(): return lax.fori_loop(0, ahead, one, state)  35.4 us
    all_gather x1, waiting for transfers between devices, shards(): weight_eff = lax.all_gather(local_weight, ('dp', 'ctx'), axis=0, tiled=True)  31.1 us
    reduce_scatter x1, waiting for transfers between devices, shards(): lax.psum_scatter(lax.dot_general(hidden, write_block, (((0,), (0,)), ((),...  29 us
    reduce_scatter x1, waiting for transfers between devices, shards(): lax.psum_scatter(share_rows, 'ctx', scatter_dimension=0, tiled=True)  24.5 us
    add x7, other arithmetic, combine_states(): following[1] + decay_state(following[0], earlier[1])  17.2 us
  transfers between devices with their start and end apart: 6, of which 6 were waited for; matrix products, arithmetic and copies ran while one was open for 23% of the time, Pallas kernels for 0%

commit v1 on v0

v1 whole, which is shorter than its diff:
```python
import functools

import jax
import jax.numpy as jnp
from jax import lax
from jax.experimental import pallas as pl
from jax.experimental.pallas import tpu as pltpu
from jax.sharding import PartitionSpec as P

BLOCK = 128
LANES = 128
GROUP = 8
LOG2E = 1.4426950408889634
LOW = -1e30
EXACT = lax.Precision.HIGHEST
VMEM_BYTES = 48 * 1024 * 1024

f32 = jnp.float32
bf16 = jnp.bfloat16

CUM2, EXCLR2, W_FWD, W_BACK, FWD_EDGE, BACK_EDGE, STEP = range(7)
C_MIX_FWD, C_MIX_BACK, C_CUM2, C_EXCL2 = range(4)


def local_call(body, out_shape, scratch=()):
    many = isinstance(out_shape, (list, tuple))
    vmem = pl.BlockSpec(memory_space=pltpu.VMEM)
    return pl.pallas_call(
        body,
        out_shape=out_shape,
        out_specs=[vmem] * len(out_shape) if many else vmem,
        scratch_shapes=list(scratch),
        compiler_params=pltpu.CompilerParams(vmem_limit_bytes=VMEM_BYTES),
    )


def iotas(shape):
    return lax.broadcasted_iota(jnp.int32, shape, 0), lax.broadcasted_iota(jnp.int32, shape, 1)


def dot_nt(a, b):
    return lax.dot_general(a, b, (((1,), (1,)), ((), ())), preferred_element_type=f32)


def dot_tn(a, b):
    return lax.dot_general(a, b, (((0,), (0,)), ((), ())), preferred_element_type=f32)


def spread(rows, width):
    high = rows.astype(bf16).astype(f32)
    both = jnp.concatenate([high, rows - high], axis=0).astype(bf16)
    r, c = iotas((2 * GROUP, GROUP * width))
    pick = (r % GROUP == c // width).astype(f32).astype(bf16)
    return dot_tn(both, pick)


def tables_kernel(read_ref, decay_ref, step_ref, readr_ref, rows_ref, cols_ref):
    decay = decay_ref[...]
    heads, n = decay.shape
    r, c = iotas((n, n))
    upto = (r <= c).astype(f32)
    flip = (r + c == n - 1).astype(f32)
    readr_ref[...] = jnp.dot(
        flip.astype(bf16), read_ref[...], preferred_element_type=f32
    ).astype(bf16)
    cum = jnp.dot(decay, upto, precision=EXACT, preferred_element_type=f32)
    decay_r = jnp.dot(decay, flip, precision=EXACT, preferred_element_type=f32)
    cum_r = jnp.dot(decay_r, upto, precision=EXACT, preferred_element_type=f32)
    end = cum[:, n - 1 :]
    excl = cum - decay
    step = step_ref[...]
    log_step = jnp.log(step) * LOG2E
    cum2 = cum * LOG2E
    excl2 = excl * LOG2E
    rows_ref[CUM2] = cum2
    rows_ref[EXCLR2] = (end - cum_r) * LOG2E
    rows_ref[W_FWD] = jnp.exp(cum)
    rows_ref[W_BACK] = jnp.exp(cum_r)
    rows_ref[FWD_EDGE] = step * jnp.exp(end - cum)
    rows_ref[BACK_EDGE] = step * jnp.exp(excl)
    rows_ref[STEP] = step
    planes = (cum2 - log_step, excl2 + log_step, cum2, excl2)
    rest = jnp.zeros((LANES - GROUP * len(planes), n), f32)
    for g in range(heads // GROUP):
        part = [p[g * GROUP : (g + 1) * GROUP] for p in planes]
        cols_ref[g] = jnp.concatenate(part + [rest], axis=0).T


def part_kernel(g_ref, read_ref, w_ref, out_ref):
    heads, n = w_ref.shape
    width = g_ref.shape[1] // heads
    step = GROUP * width
    read_t = read_ref[...].astype(f32).T.astype(bf16)
    state = read_t.shape[0]

    def one(g, carry):
        at = pl.multiple_of(g * step, step)
        scale = spread(w_ref[pl.ds(pl.multiple_of(g * GROUP, GROUP), GROUP)], width)
        scaled = (g_ref[:, pl.ds(at, step)].astype(f32) * scale).astype(bf16)
        part = jnp.dot(read_t, scaled, preferred_element_type=f32)
        out_ref[0:state, pl.ds(at, step)] = part.astype(bf16)
        last = scale[n - 1 :]
        high = last.astype(bf16).astype(f32)
        r, _ = iotas((16, step))
        tail = jnp.where(r == 0, high, jnp.where(r == 1, last - high, 0.0))
        out_ref[state : state + 16, pl.ds(at, step)] = tail.astype(bf16)
        return carry

    lax.fori_loop(0, heads // GROUP, one, 0)


def mix_kernel(fwd, inner_ref, g_ref, row_ref, cols_ref, out_ref):
    heads, n = row_ref.shape
    width = g_ref.shape[1] // heads
    step = GROUP * width
    s, t = iotas((n, n))
    keep = (t >= s) if fwd else (t + s >= n - 1)
    low_half = t < width

    def one(g, acc):
        at = pl.multiple_of(g * step, step)
        rows = row_ref[pl.ds(pl.multiple_of(g * GROUP, GROUP), GROUP)]
        cols = cols_ref[g]
        for pair in range(GROUP // 2):
            here = pl.ds(at + pair * LANES, LANES)
            inner = inner_ref[:, here].astype(f32)
            halves = jnp.concatenate(
                [jnp.where(low_half, inner, 0.0), jnp.where(low_half, 0.0, inner)], axis=0
            ).astype(bf16)
            dots = dot_nt(halves, g_ref[:, here])
            for j in range(2):
                h = 2 * pair + j
                row = rows[h : h + 1]
                if fwd:
                    k = C_MIX_FWD * GROUP + h
                    power = row - cols[:, k : k + 1]
                else:
                    k = C_MIX_BACK * GROUP + h
                    power = cols[:, k : k + 1] - row
                decay = jnp.exp2(jnp.where(keep, power, LOW))
                acc = acc + decay * dots[j * n : (j + 1) * n]
        return acc

    out_ref[...] = lax.fori_loop(0, heads // GROUP, one, jnp.zeros((n, n), f32))


def write_kernel(
    inner_ref, right_ref, left_ref, rows_ref, mixf_ref, mixb_ref, read_ref, readr_ref, out_ref
):
    _, heads, n = rows_ref.shape
    width = inner_ref.shape[1] // heads
    step = GROUP * width

    def one(g, acc):
        at = pl.multiple_of(g * step, step)
        own = pl.ds(pl.multiple_of(g * GROUP, GROUP), GROUP)
        inner = inner_ref[:, pl.ds(at, step)].astype(f32)
        fwd = (inner * spread(rows_ref[FWD_EDGE, own], width)).astype(bf16)
        back = (inner * spread(rows_ref[BACK_EDGE, own], width)).astype(bf16)
        return (
            acc
            + dot_nt(fwd, right_ref[:, pl.ds(at, step)])
            + dot_nt(back, left_ref[:, pl.ds(at, step)])
        )

    acc = jnp.dot(mixf_ref[...].astype(bf16), read_ref[...], preferred_element_type=f32)
    acc = acc + jnp.dot(mixb_ref[...].astype(bf16), readr_ref[...], preferred_element_type=f32)
    out_ref[...] = lax.fori_loop(0, heads // GROUP, one, acc).astype(bf16)


def inner_kernel(
    gf_ref, gb_ref, right_ref, left_ref, rows_ref, cols_ref, write_ref, read_ref, readr_ref, out_ref
):
    _, heads, n = rows_ref.shape
    width = gf_ref.shape[1] // heads
    step = GROUP * width
    write = write_ref[...]
    kernel_f = dot_nt(write, read_ref[...])
    kernel_b = dot_nt(write, readr_ref[...])
    s, t = iotas((n, n))
    low_half = t < width

    def one(g, carry):
        at = pl.multiple_of(g * step, step)
        own = pl.ds(pl.multiple_of(g * GROUP, GROUP), GROUP)
        cols = cols_ref[g]
        cum2 = rows_ref[CUM2, own]
        exclr2 = rows_ref[EXCLR2, own]
        step_e = spread(rows_ref[STEP, own], width)
        edges = spread(rows_ref[FWD_EDGE, own], width) * jnp.dot(
            write, right_ref[:, pl.ds(at, step)], preferred_element_type=f32
        )
        edges = edges + spread(rows_ref[BACK_EDGE, own], width) * jnp.dot(
            write, left_ref[:, pl.ds(at, step)], preferred_element_type=f32
        )
        for pair in range(GROUP // 2):
            mixes = []
            for j in range(2):
                h = 2 * pair + j
                kf = C_CUM2 * GROUP + h
                kb = C_EXCL2 * GROUP + h
                pf = cum2[h : h + 1] - cols[:, kf : kf + 1]
                pb = cols[:, kb : kb + 1] - exclr2[h : h + 1]
                mf = jnp.exp2(jnp.where(t >= s, pf, LOW)) * kernel_f
                mb = jnp.exp2(jnp.where(t + s >= n - 1, pb, LOW)) * kernel_b
                mixes.append(jnp.concatenate([mf, mb], axis=1))
            here = pl.ds(at + pair * LANES, LANES)
            both = jnp.concatenate([gf_ref[:, here], gb_ref[:, here]], axis=0)
            got = jnp.dot(
                jnp.concatenate(mixes, axis=0).astype(bf16), both, preferred_element_type=f32
            )
            intra = jnp.where(low_half, got[:n], got[n:])
            mine = slice(pair * LANES, (pair + 1) * LANES)
            out_ref[:, here] = (step_e[:, mine] * intra + edges[:, mine]).astype(bf16)
        return carry

    lax.fori_loop(0, heads // GROUP, one, 0)


def xor_pairs(count, k):
    return [(i, i ^ k) for i in range(count)]


def chip_states(part, ctx_count, core, upward):
    state = part.shape[0] - 16
    cols = part.shape[1]
    half = cols // 2
    chips = ctx_count // 2
    other = lax.ppermute(part, "ctx", xor_pairs(ctx_count, 1))
    first = core == (0 if upward else 1)

    def split(array):
        mine = lax.dynamic_slice_in_dim(array, core * half, half, 1).astype(f32)
        return mine[:state], mine[state : state + 1] + mine[state + 1 : state + 2]

    own_term, own_decay = split(part)
    other_term, other_decay = split(other)
    later_decay = jnp.where(first, other_decay, own_decay)
    both = jnp.where(first, other_term, own_term) + later_decay * jnp.where(
        first, own_term, other_term
    )
    both_decay = own_decay * other_decay
    entering = jnp.zeros((state, half), bf16)
    for hop in range(chips - 1):
        if upward:
            source, target = hop, hop + 1
        else:
            source, target = chips - 1 - hop, chips - 2 - hop
        if hop:
            leaving = (both + both_decay * entering.astype(f32)).astype(bf16)
        else:
            leaving = both.astype(bf16)
        pairs = [(2 * source + i, 2 * target + i) for i in range(2)]
        entering = entering + lax.ppermute(leaving, "ctx", pairs)
    swapped = lax.ppermute(entering, "ctx", xor_pairs(ctx_count, 1))
    whole = jnp.where(
        core == 0,
        jnp.concatenate([entering, swapped], axis=1),
        jnp.concatenate([swapped, entering], axis=1),
    )
    decay = other[state : state + 1].astype(f32) + other[state + 1 : state + 2].astype(f32)
    second = other[:state].astype(f32) + decay * whole.astype(f32)
    return jnp.where(first, whole, second.astype(bf16))


def shards(
    hidden_in,
    write_weight,
    shard_scale,
    inner_acts,
    read_proj,
    step_size,
    log_decay,
    grad_fwd,
    grad_rev,
):
    ctx_count = lax.axis_size("ctx")
    dp_count = lax.axis_size("dp")
    ctx = lax.axis_index("ctx")
    dp = lax.axis_index("dp")
    core = ctx % 2
    hidden = hidden_in[0]
    inner = inner_acts[0]
    read = read_proj[0]
    step = step_size[0]
    decay = log_decay[0]
    gf = grad_fwd[0]
    n, width = inner.shape
    heads = decay.shape[0]
    state = read.shape[1]
    rows_all = hidden.shape[1]

    gb = lax.ppermute(grad_rev[0], "ctx", [(i, ctx_count - 1 - i) for i in range(ctx_count)])

    local_weight = (write_weight.astype(f32) * shard_scale[0]).astype(bf16)
    weight = lax.all_gather(local_weight, ("dp", "ctx"), axis=0, tiled=True)

    share = rows_all // dp_count

    def of_dp(array, k):
        return lax.dynamic_slice_in_dim(array, (dp ^ k) * share, share, 1)

    hidden_parts = [of_dp(hidden, 0)] + [
        lax.ppermute(of_dp(hidden, k), "dp", xor_pairs(dp_count, k)) for k in range(1, dp_count)
    ]

    sds = jax.ShapeDtypeStruct
    read_r, rows, cols = local_call(
        tables_kernel,
        [
            sds((n, state), bf16),
            sds((7, heads, n), f32),
            sds((heads // GROUP, n, LANES), f32),
        ],
    )(read, decay, step)

    part_call = local_call(part_kernel, sds((state + 16, width), bf16))
    right_part = part_call(gf, read, rows[W_FWD])
    right_in = chip_states(right_part, ctx_count, core, False)
    mix_f = local_call(functools.partial(mix_kernel, True), sds((n, n), f32))(
        inner, gf, rows[CUM2], cols
    )
    left_part = part_call(gb, read_r, rows[W_BACK])
    left_in = chip_states(left_part, ctx_count, core, True)
    mix_b = local_call(functools.partial(mix_kernel, False), sds((n, n), f32))(
        inner, gb, rows[EXCLR2], cols
    )
    grad_write = local_call(write_kernel, sds((n, state), bf16))(
        inner, right_in, left_in, rows, mix_f, mix_b, read, read_r
    )

    gathered = [grad_write] + [
        lax.ppermute(grad_write, "dp", xor_pairs(dp_count, k)) for k in range(1, dp_count)
    ]
    product = lax.dot_general(
        jnp.concatenate(hidden_parts, axis=0),
        jnp.concatenate(gathered, axis=0),
        (((0,), (0,)), ((), ())),
        preferred_element_type=f32,
    )
    chips = ctx_count // 2
    piece = share // ctx_count
    product = product.reshape(chips, 2, piece, state)
    kept = lax.dynamic_index_in_dim(product, core, 1, False)
    given = lax.dynamic_index_in_dim(product, 1 - core, 1, False)
    kept = kept + lax.ppermute(given, "ctx", xor_pairs(ctx_count, 1))
    chip = ctx // 2
    total = lax.dynamic_index_in_dim(kept, chip, 0, False)
    for k in range(1, chips):
        sent = lax.dynamic_index_in_dim(kept, chip ^ k, 0, False).astype(bf16)
        total = total + lax.ppermute(sent, "ctx", xor_pairs(ctx_count, 2 * k)).astype(f32)
    grad_weight = total / (dp_count * ctx_count * n)

    write = jnp.dot(hidden, weight, preferred_element_type=f32).astype(bf16)
    grad_inner = local_call(inner_kernel, sds((n, width), bf16))(
        gf, gb, right_in, left_in, rows, cols, write, read, read_r
    )
    grad_hidden = dot_nt(grad_write, weight).astype(bf16)
    return grad_inner[None], grad_hidden[None], grad_weight


def solution(mesh):
    in_specs = (
        P("dp", "ctx", None),
        P(("dp", "ctx"), None),
        P(("dp", "ctx")),
        P("dp", "ctx", None),
        P("dp", "ctx", None),
        P("dp", None, "ctx"),
        P("dp", None, "ctx"),
        P("dp", "ctx", None),
        P("dp", "ctx", None),
    )
    out_specs = (P("dp", "ctx", None), P("dp", "ctx", None), P(("dp", "ctx"), None))
    return jax.shard_map(shards, mesh=mesh, in_specs=in_specs, out_specs=out_specs, check_vma=False)
```

time: 497 us -> 169 us (0.34)
  waiting for transfers between devices: 271 us -> 57.1 us
  blocking collectives: 78.3 us -> 0 us
  local copies, waits for them, and re-layouts: 68.1 us -> 9.21 us
  starting transfers between devices: 3.76 us -> 45.7 us
  matrix products: 37.1 us -> 4.91 us
  Pallas kernels: 0 us -> 23.3 us
  other arithmetic: 20.5 us -> 13.1 us
    all_gather x3 -> x1, waiting for transfers between devices: 157 us -> 0.01 us  [shards(): weight = lax.all_gather(local_weight, ('dp', 'ctx'), axis=0, tiled=True)]
    all_to_all x1 -> x0, blocking collectives: 63.9 us -> none  [shards(): lax.all_to_all(pieces, 'ctx', split_axis=0, concat_axis=0, tiled=True)]
    all_to_all x1 -> x0, waiting for transfers between devices: 60.3 us -> none  [shards(): lax.all_to_all(pieces[::-1], 'ctx', split_axis=0, concat_axis=0, tiled=True)]
    ppermute x0 -> x21, waiting for transfers between devices: none -> 57.1 us  [the longest x6 38.3 us: chip_states(): entering = entering + lax.ppermute(leaving, 'ctx', pairs)]
    reduce_scatter x2 -> x0, waiting for transfers between devices: 53.5 us -> none  [the longest x1 29 us: shards(): lax.psum_scatter(lax.dot_general(hidden, write_block, (((0,), (0,)), ((),...]
    ppermute x0 -> x21, starting transfers between devices: none -> 45.6 us  [the longest x6 28.7 us: chip_states(): entering = entering + lax.ppermute(leaving, 'ctx', pairs)]
    while x2 -> x0, local copies, waits for them, and re-layouts: 35.4 us -> none  [carried_in(): return lax.fori_loop(0, ahead, one, state)]
    dot_general x15 -> x3, matrix products: 37.1 us -> 4.91 us  [the longest x1 1.76 us: shards(): write = jnp.dot(hidden, weight, preferred_element_type=f32).astype(bf16)]
  transfers between devices with their start and end apart: 6 -> 22, of which waited for: 6 -> 8; matrix products, arithmetic and copies ran while one was open for 23% -> 12% of each run, Pallas kernels for 0% -> 14%
where the time goes in v1:
time: 169 us; the launch traced here: 168 us
  waiting for transfers between devices  57.1 us (34%)
  starting transfers between devices  45.7 us (27%)
  Pallas kernels  23.3 us (14%)
  between operations  15.1 us (9%)
  other arithmetic  13.1 us (8%)
  local copies, waits for them, and re-layouts  9.21 us (5%)
  matrix products  4.91 us (3%)
    ppermute x6, waiting for transfers between devices, chip_states(): entering = entering + lax.ppermute(leaving, 'ctx', pairs)  38.3 us
    ppermute x6, starting transfers between devices, chip_states(): entering = entering + lax.ppermute(leaving, 'ctx', pairs)  28.7 us
    ppermute x1, waiting for transfers between devices, shards(): lax.ppermute(grad_rev[0], 'ctx', [(i, ctx_count - 1 - i) for i in range(c...  14.3 us
    pallas_call x1, Pallas kernels, shards(): local_call(inner_kernel, sds((n, width), bf16))  6.81 us
    unnamed x36, local copies, waits for them, and re-layouts  6.15 us
    ppermute x1, starting transfers between devices, shards(): lax.ppermute(grad_rev[0], 'ctx', [(i, ctx_count - 1 - i) for i in range(c...  4.55 us
    ppermute x3, starting transfers between devices, shards(): lax.ppermute(sent, 'ctx', xor_pairs(ctx_count, 2 * k)).astype(f32)  4.44 us
    ppermute x3, waiting for transfers between devices, shards(): lax.ppermute(grad_write, 'dp', xor_pairs(dp_count, k))  4.21 us
  transfers between devices with their start and end apart: 22, of which 8 were waited for; matrix products, arithmetic and copies ran while one was open for 12% of the time, Pallas kernels for 14%

profile of v1, /device:TPU:0, one launch (start us, length us, event | category | flops | bytes accessed | tf_op | source)
XLA Modules:
  0.0 168.4 jit_solution(8155554158855785365)
XLA Ops:
  7.2 4.6 %collective-permute-start = (bf16[128,4096]{1,0:T(8,128)(2,1)}, bf16[128,4096]{1,0:T(8,128)(2,1)S(1)}, u32[]{:S(2)}, u32[]{:S(2)}) collective-permute-start(bf16[128,4096]{1,0:T(8,128)(2,1)} %bitcast.83), channel_id=1, source_target_pairs={{0,7},{1,6},{2,5},{3,4},{4,3},{5,2},{6,1},{7,0},{8,15},{9,14},{10,... | collective-permute-start | bytes 3145736 | tf_op jit(solution)/shard_map/ppermute | solution.py:293
  11.8 0.8 copy-done.9
  12.5 0.8 copy-done.11
  13.3 0.8 copy-done.12
  14.0 0.5 shard_map.112
  14.5 0.8 copy-done.6
  15.4 1.2 copy-done.1
  16.6 4.1 %shard_map.113 = bf16[144,4096]{1,0:T(8,128)(2,1)} custom-call(bf16[128,4096]{1,0:T(8,128)(2,1)S(1)} %bitcast.63, bf16[128,128]{1,0:T(8,128)(2,1)S(1)} %bitcast.67, f32[64,128]{1,0:T(8,128)S(1)} %get-tuple-element.31.w_ref), custom_call_target="tpu_custom_call" | custom-call | tf_op jit(solution)/shard_map/pallas_call | solution.py:318
  20.7 0.7 collective-permute-start.1
  21.4 14.3 %collective-permute-done.g_ref.gb_ref = bf16[128,4096]{1,0:T(8,128)(2,1)S(1)} collective-permute-done((bf16[128,4096]{1,0:T(8,128)(2,1)}, bf16[128,4096]{1,0:T(8,128)(2,1)S(1)}, u32[]{:S(2)}, u32[]{:S(2)}) %collective-permute-start) | collective-permute-done | bytes 1048608 | tf_op jit(solution)/shard_map/ppermute | solution.py:293
  35.7 4.1 %shard_map.114 = bf16[144,4096]{1,0:T(8,128)(2,1)} custom-call(bf16[128,4096]{1,0:T(8,128)(2,1)S(1)} %collective-permute-done.g_ref.gb_ref, bf16[128,128]{1,0:T(8,128)(2,1)S(1)} %get-tuple-element.7.read_ref.readr_ref, f32[64,128]{1,0:T(8,128)S(1)} %get-tuple-element.30.w_ref), custom_call_target="tpu_custom_call" | custom-call | tf_op jit(solution)/shard_map/pallas_call | solution.py:323
  39.8 0.1 collective-permute-start.6
  39.9 2.3 %dynamic-slice_bitcast_fusion.4 = (bf16[128,1024]{1,0:T(8,128)(2,1)}, bf16[128,1024]{1,0:T(8,128)(2,1)}, bf16[128,1024]{1,0:T(8,128)(2,1)}, bf16[128,1024]{1,0:T(8,128)(2,1)}) fusion(bf16[1,128,4096]{2,1,0:T(8,128)(2,1)} %param.9, s32[]{:T(128)S(6)} %select_n.125, s32[]{:T(128)S(6)} %select_n.126, s32[]{:T(128)S(6)} %select_n.128, s32[]{:T(128)S(6)} %select_n.127), kind=kLoop, calls=%fused_computation.34 | loop fusion | bytes 2097168 | tf_op jit(solution)/shard_map/dynamic_slice | solution.py:301
  42.2 1.9 %collective-permute-start.11 = (bf16[128,1024]{1,0:T(8,128)(2,1)}, bf16[128,1024]{1,0:T(8,128)(2,1)}, u32[]{:S(2)}, u32[]{:S(2)}) collective-permute-start(bf16[128,1024]{1,0:T(8,128)(2,1)} %get-tuple-element.22), channel_id=1, source_target_pairs={{0,8},{8,0},{16,24},{24,16},{1,9},{9,1},{17,25},{25,17},{2,10},{10... | collective-permute-start | bytes 786440 | tf_op jit(solution)/shard_map/ppermute | solution.py:304
  44.1 1.5 collective-permute-start.12
  45.6 0.1 collective-permute-start.13
  46.4 0.6 multiply_convert_fusion
  47.1 1.0 copy-done.7
  48.1 2.1 %shard_map.116.mixf_ref = f32[128,128]{1,0:T(8,128)S(1)} custom-call(bf16[128,4096]{1,0:T(8,128)(2,1)S(1)} %bitcast.60, bf16[128,4096]{1,0:T(8,128)(2,1)S(1)} %bitcast.64, f32[64,128]{1,0:T(8,128)S(1)} %get-tuple-element.29.row_ref, f32[8,128,128]{2,1,0:T(8,128)S(1)} %copy-done.7), custom_call_target="tpu_custom_call" | custom-call | tf_op jit(solution)/shard_map/pallas_call | solution.py:320
  50.2 1.2 dynamic-slice_convert_fusion.2
  51.4 2.1 %shard_map.117.mixb_ref = f32[128,128]{1,0:T(8,128)S(1)} custom-call(bf16[128,4096]{1,0:T(8,128)(2,1)S(1)} %bitcast.61, bf16[128,4096]{1,0:T(8,128)(2,1)S(1)} %collective-permute-done.g_ref.gb_ref, f32[64,128]{1,0:T(8,128)S(1)} %get-tuple-element.28.row_ref, f32[8,128,128]{2,1,0:T(8,128)S(1)} %copy-done.7), custom_call_target="tpu_custom_call" | custom-call | tf_op jit(solution)/shard_map/pallas_call | solution.py:325
  53.4 1.2 dynamic-slice_convert_fusion
  54.7 1.5 dynamic-slice_convert_fusion.1
  56.2 0.2 fusion.31
  56.4 24.6 %collective-permute-start.7 = (bf16[128,2048]{1,0:T(8,128)(2,1)S(1)}, bf16[128,2048]{1,0:T(8,128)(2,1)S(1)}, u32[]{:S(2)}, u32[]{:S(2)}) collective-permute-start(bf16[128,2048]{1,0:T(8,128)(2,1)S(1)} %get-tuple-element.11), channel_id=1, source_target_pairs={{0,2},{1,3},{8,10},{9,11},{16,18},{17,19},{24,26},{25,27}} | collective-permute-start | bytes 1572872 | tf_op jit(solution)/shard_map/ppermute | solution.py:254
  81.1 0.2 fusion.32
  81.3 0.7 collective-permute-start.2
  82.0 10.4 %collective-permute-done.7 = bf16[128,2048]{1,0:T(8,128)(2,1)S(1)} collective-permute-done((bf16[128,2048]{1,0:T(8,128)(2,1)S(1)}, bf16[128,2048]{1,0:T(8,128)(2,1)S(1)}, u32[]{:S(2)}, u32[]{:S(2)}) %collective-permute-start.7) | collective-permute-done | bytes 524320 | tf_op jit(solution)/shard_map/ppermute | solution.py:254
  92.4 0.1 add_convert_fusion.3
  92.5 0.7 collective-permute-start.8
  93.2 0.9 fusion.27
  94.2 0.1 add_convert_fusion.5
  94.3 0.7 collective-permute-start.3
  95.0 0.3 add_convert_fusion.2
  95.3 0.7 collective-permute-start.9
  96.0 0.3 add_convert_fusion.4
  96.3 1.3 collective-permute-start.4
  97.6 0.1 add.127
  97.7 0.1 collective-permute-start.10
  97.8 0.9 fusion.26
  98.7 27.9 %collective-permute-done.4 = bf16[128,2048]{1,0:T(8,128)(2,1)S(1)} collective-permute-done((bf16[128,2048]{1,0:T(8,128)(2,1)S(1)}, bf16[128,2048]{1,0:T(8,128)(2,1)S(1)}, u32[]{:S(2)}, u32[]{:S(2)}) %collective-permute-start.4) | collective-permute-done | bytes 524320 | tf_op jit(solution)/shard_map/ppermute | solution.py:254
  126.6 0.1 add.118
  126.8 0.1 collective-permute-start.5
  126.9 1.8 %fusion.2.left_ref = bf16[128,4096]{1,0:T(8,128)(2,1)S(1)} fusion(bf16[144,4096]{1,0:T(8,128)(2,1)} %collective-permute-done.6, bf16[128,2048]{1,0:T(8,128)(2,1)S(1)} %collective-permute-done.10, bf16[128,2048]{1,0:T(8,128)(2,1)S(1)} %add.127, f32[4096]{0:T(1024)S(1)} %bitcast.80, pred[]{:T(512)S(6)} %eq.11), kind=kLoop, calls=%fused_computation.5 | loop fusion | flops 7864320 | bytes 3162113 | tf_op jit(solution)/shard_map/jit(_where)/select_n | solution.py:263
  128.6 0.1 collective-permute-done.5
  128.8 1.8 %fusion.1.right_ref = bf16[128,4096]{1,0:T(8,128)(2,1)S(1)} fusion(bf16[144,4096]{1,0:T(8,128)(2,1)} %collective-permute-done.1, bf16[128,2048]{1,0:T(8,128)(2,1)S(1)} %collective-permute-done.5, bf16[128,2048]{1,0:T(8,128)(2,1)S(1)} %add.118, f32[4096]{0:T(1024)S(1)} %bitcast.79, pred[]{:T(512)S(6)} %eq.11, pred[]{:T(512)S(6)} %eq.10), kind=kLoop, calls=%fused_computation.4 | loop fusion | flops 7864320 | bytes 3162114 | tf_op jit(solution)/shard_map/jit(_where)/select_n | solution.py:263
  130.5 3.6 %shard_map.118 = bf16[128,128]{1,0:T(8,128)(2,1)S(1)} custom-call(bf16[128,4096]{1,0:T(8,128)(2,1)S(1)} %bitcast.62, bf16[128,4096]{1,0:T(8,128)(2,1)S(1)} %fusion.1.right_ref, bf16[128,4096]{1,0:T(8,128)(2,1)S(1)} %fusion.2.left_ref, f32[7,64,128]{2,1,0:T(8,128)S(1)} %get-tuple-element.6.rows_ref, f32[128,128]{1,0:T(8,128)S(1)} %shard_map.116.mixf_ref, ...), custom_call_target="tpu_custom_call" | custom-call | tf_op jit(solution)/shard_map/pallas_call | solution.py:328
  134.2 1.6 collective-permute-start.14
  135.8 1.3 collective-permute-start.15
  137.0 0.7 collective-permute-start.16
  137.8 0.4 collective-permute-done.14
  138.2 1.5 collective-permute-done.15
  139.7 2.3 %collective-permute-done.16 = bf16[128,128]{1,0:T(8,128)(2,1)} collective-permute-done((bf16[128,128]{1,0:T(8,128)(2,1)S(1)}, bf16[128,128]{1,0:T(8,128)(2,1)}, u32[]{:S(2)}, u32[]{:S(2)}) %collective-permute-start.16) | collective-permute-done | bytes 32800 | tf_op jit(solution)/shard_map/ppermute | solution.py:333
  142.0 1.7 %fusion.4 = f32[1024,128]{1,0:T(8,128)S(1)} fusion(bf16[128,1024]{1,0:T(8,128)(2,1)} %collective-permute-done.13, bf16[128,1024]{1,0:T(8,128)(2,1)} %collective-permute-done.12, bf16[128,1024]{1,0:T(8,128)(2,1)} %collective-permute-done.11, bf16[128,1024]{1,0:T(8,128)(2,1)} %get-tuple-element.21, bf16[128,128]{1,0:T(8,128)(2,1)} %collective-permute-done.16, ...), kind=kOutput, calls=%fused_computation.10 | convolution fusion | flops 138936320 | bytes 1703936 | tf_op jit(solution)/shard_map/dot_general | solution.py:335
  143.7 0.8 copy-done.15
  144.5 0.7 dynamic-slice_bitcast_fusion
  145.3 1.8 %fusion.3.write_ref = bf16[128,128]{1,0:T(8,128)(2,1)S(1)} fusion(bf16[4096,128]{1,0:T(8,128)(2,1)} %all-gather.2.cloned.1.call-done, bf16[1,128,4096]{2,1,0:T(8,128)(2,1)S(1)} %copy-done.13), kind=kOutput, calls=%fused_computation.7 | convolution fusion | flops 134234112 | bytes 2129920 | tf_op jit(solution)/shard_map/dot_general | solution.py:354
  147.0 0.1 collective-permute-done.17
  147.1 1.0 bitcast_add_fusion
  148.3 1.8 %collective-permute-start.19 = (bf16[128,128]{1,0:T(8,128)(2,1)S(1)}, bf16[128,128]{1,0:T(8,128)(2,1)S(1)}, u32[]{:S(2)}, u32[]{:S(2)}) collective-permute-start(bf16[128,128]{1,0:T(8,128)(2,1)S(1)} %get-tuple-element.27), channel_id=1, source_target_pairs={{0,4},{1,5},{2,6},{3,7},{4,0},{5,1},{6,2},{7,3},{8,12},{9,13},{10,... | collective-permute-start | bytes 98312 | tf_op jit(solution)/shard_map/ppermute | solution.py:351
  150.1 2.6 %collective-permute-start.20 = (bf16[128,128]{1,0:T(8,128)(2,1)S(1)}, bf16[128,128]{1,0:T(8,128)(2,1)S(1)}, u32[]{:S(2)}, u32[]{:S(2)}) collective-permute-start(bf16[128,128]{1,0:T(8,128)(2,1)S(1)} %get-tuple-element.26), channel_id=1, source_target_pairs={{0,6},{1,7},{2,4},{3,5},{4,2},{5,3},{6,0},{7,1},{8,14},{9,15},{10,... | collective-permute-start | bytes 98312 | tf_op jit(solution)/shard_map/ppermute | solution.py:351
  152.7 1.4 fusion
  154.1 6.8 %shard_map.115 = bf16[128,4096]{1,0:T(8,128)(2,1)} custom-call(bf16[128,4096]{1,0:T(8,128)(2,1)S(1)} %bitcast.65, bf16[128,4096]{1,0:T(8,128)(2,1)S(1)} %copy-done.5, bf16[128,4096]{1,0:T(8,128)(2,1)S(1)} %fusion.1.right_ref, bf16[128,4096]{1,0:T(8,128)(2,1)S(1)} %fusion.2.left_ref, f32[7,64,128]{2,1,0:T(8,128)S(1)} %get-tuple-element.6.rows_ref, ...), custom_call_target="tpu_custom_call" | custom-call | tf_op jit(solution)/shard_map/pallas_call | solution.py:355
  160.9 0.7 fusion.22
  (51 shorter events, 0.3 us)
Async XLA Ops:
  7.2 138.1 %all-gather.2.cloned.1.call-start = ((), (), s32[]{:S(2)}) async-start(), calls=%async_computation | async-start | bytes 1081344 | tf_op jit(solution)/shard_map/all_gather | solution.py:296
  7.2 28.5 %collective-permute-start = (bf16[128,4096]{1,0:T(8,128)(2,1)}, bf16[128,4096]{1,0:T(8,128)(2,1)S(1)}, u32[]{:S(2)}, u32[]{:S(2)}) collective-permute-start(bf16[128,4096]{1,0:T(8,128)(2,1)} %bitcast.83), channel_id=1, source_target_pairs={{0,7},{1,6},{2,5},{3,4},{4,3},{5,2},{6,1},{7,0},{8,15},{9,14},{10,... | collective-permute-start | bytes 3145736 | tf_op jit(solution)/shard_map/ppermute | solution.py:293
  11.8 0.8 copy-start.9
  12.5 0.8 copy-start.11
  13.3 0.8 copy-start.12
  14.5 0.8 copy-start.6
  15.3 1.2 copy-start.1
  20.7 33.9 %collective-permute-start.1 = (bf16[144,4096]{1,0:T(8,128)(2,1)}, bf16[144,4096]{1,0:T(8,128)(2,1)}, u32[]{:S(2)}, u32[]{:S(2)}) collective-permute-start(bf16[144,4096]{1,0:T(8,128)(2,1)} %shard_map.113), channel_id=1, source_target_pairs={{0,1},{1,0},{2,3},{3,2},{4,5},{5,4},{6,7},{7,6},{8,9},{9,8},{10,11... | collective-permute-start | bytes 3538952 | tf_op jit(solution)/shard_map/ppermute | solution.py:229
  35.7 15.7 %copy-start.4 = (bf16[128,4096]{1,0:T(8,128)(2,1)}, bf16[128,4096]{1,0:T(8,128)(2,1)S(1)}, u32[]{:S(2)}) copy-start(bf16[128,4096]{1,0:T(8,128)(2,1)S(1)} %collective-permute-done.g_ref.gb_ref) | copy-start | bytes 3145732
  39.8 6.6 %copy-start.17 = (bf16[128,128]{1,0:T(8,128)(2,1)S(1)}, bf16[128,128]{1,0:T(8,128)(2,1)}, u32[]{:S(2)}) copy-start(bf16[128,128]{1,0:T(8,128)(2,1)} %param.10) | copy-start | bytes 98308
  39.8 7.2 %copy-start = (bf16[1,128,4096]{2,1,0:T(8,128)(2,1)S(1)}, bf16[1,128,4096]{2,1,0:T(8,128)(2,1)}, u32[]{:S(2)}) copy-start(bf16[1,128,4096]{2,1,0:T(8,128)(2,1)} %param.12) | copy-start | bytes 3145732
  39.8 7.2 %copy-start.2 = (bf16[1,128,4096]{2,1,0:T(8,128)(2,1)S(1)}, bf16[1,128,4096]{2,1,0:T(8,128)(2,1)}, u32[]{:S(2)}) copy-start(bf16[1,128,4096]{2,1,0:T(8,128)(2,1)} %param.16) | copy-start | bytes 3145732
  39.8 14.8 %collective-permute-start.6 = (bf16[144,4096]{1,0:T(8,128)(2,1)}, bf16[144,4096]{1,0:T(8,128)(2,1)}, u32[]{:S(2)}, u32[]{:S(2)}) collective-permute-start(bf16[144,4096]{1,0:T(8,128)(2,1)} %shard_map.114), channel_id=1, source_target_pairs={{0,1},{1,0},{2,3},{3,2},{4,5},{5,4},{6,7},{7,6},{8,9},{9,8},{10,11... | collective-permute-start | bytes 3538952 | tf_op jit(solution)/shard_map/ppermute | solution.py:229
  42.2 94.8 %collective-permute-start.11 = (bf16[128,1024]{1,0:T(8,128)(2,1)}, bf16[128,1024]{1,0:T(8,128)(2,1)}, u32[]{:S(2)}, u32[]{:S(2)}) collective-permute-start(bf16[128,1024]{1,0:T(8,128)(2,1)} %get-tuple-element.22), channel_id=1, source_target_pairs={{0,8},{8,0},{16,24},{24,16},{1,9},{9,1},{17,25},{25,17},{2,10},{10... | collective-permute-start | bytes 786440 | tf_op jit(solution)/shard_map/ppermute | solution.py:304
  44.1 93.7 %collective-permute-start.12 = (bf16[128,1024]{1,0:T(8,128)(2,1)}, bf16[128,1024]{1,0:T(8,128)(2,1)}, u32[]{:S(2)}, u32[]{:S(2)}) collective-permute-start(bf16[128,1024]{1,0:T(8,128)(2,1)} %get-tuple-element.24), channel_id=1, source_target_pairs={{0,16},{8,24},{16,0},{24,8},{1,17},{9,25},{17,1},{25,9},{2,18},{10... | collective-permute-start | bytes 786440 | tf_op jit(solution)/shard_map/ppermute | solution.py:304
  45.6 92.2 %collective-permute-start.13 = (bf16[128,1024]{1,0:T(8,128)(2,1)}, bf16[128,1024]{1,0:T(8,128)(2,1)}, u32[]{:S(2)}, u32[]{:S(2)}) collective-permute-start(bf16[128,1024]{1,0:T(8,128)(2,1)} %get-tuple-element.23), channel_id=1, source_target_pairs={{0,24},{8,16},{16,8},{24,0},{1,25},{9,17},{17,9},{25,1},{2,26},{10... | collective-permute-start | bytes 786440 | tf_op jit(solution)/shard_map/ppermute | solution.py:304
  47.0 1.0 copy-start.7
  56.4 36.0 %collective-permute-start.7 = (bf16[128,2048]{1,0:T(8,128)(2,1)S(1)}, bf16[128,2048]{1,0:T(8,128)(2,1)S(1)}, u32[]{:S(2)}, u32[]{:S(2)}) collective-permute-start(bf16[128,2048]{1,0:T(8,128)(2,1)S(1)} %get-tuple-element.11), channel_id=1, source_target_pairs={{0,2},{1,3},{8,10},{9,11},{16,18},{17,19},{24,26},{25,27}} | collective-permute-start | bytes 1572872 | tf_op jit(solution)/shard_map/ppermute | solution.py:254
  81.3 12.9 %collective-permute-start.2 = (bf16[128,2048]{1,0:T(8,128)(2,1)S(1)}, bf16[128,2048]{1,0:T(8,128)(2,1)S(1)}, u32[]{:S(2)}, u32[]{:S(2)}) collective-permute-start(bf16[128,2048]{1,0:T(8,128)(2,1)S(1)} %get-tuple-element.15), channel_id=1, source_target_pairs={{6,4},{7,5},{14,12},{15,13},{22,20},{23,21},{30,28},{31,29}} | collective-permute-start | bytes 1572872 | tf_op jit(solution)/shard_map/ppermute | solution.py:254
  92.5 2.5 %collective-permute-start.8 = (bf16[128,2048]{1,0:T(8,128)(2,1)S(1)}, bf16[128,2048]{1,0:T(8,128)(2,1)S(1)}, u32[]{:S(2)}, u32[]{:S(2)}) collective-permute-start(bf16[128,2048]{1,0:T(8,128)(2,1)S(1)} %add_convert_fusion.3), channel_id=1, source_target_pairs={{2,4},{3,5},{10,12},{11,13},{18,20},{19,21},{26,28},{27,29}} | collective-permute-start | bytes 1572872 | tf_op jit(solution)/shard_map/ppermute | solution.py:254
  94.3 1.7 collective-permute-start.3
  95.3 2.3 %collective-permute-start.9 = (bf16[128,2048]{1,0:T(8,128)(2,1)S(1)}, bf16[128,2048]{1,0:T(8,128)(2,1)S(1)}, u32[]{:S(2)}, u32[]{:S(2)}) collective-permute-start(bf16[128,2048]{1,0:T(8,128)(2,1)S(1)} %get-tuple-element.9), channel_id=1, source_target_pairs={{4,6},{5,7},{12,14},{13,15},{20,22},{21,23},{28,30},{29,31}} | collective-permute-start | bytes 1572872 | tf_op jit(solution)/shard_map/ppermute | solution.py:254
  96.3 30.4 %collective-permute-start.4 = (bf16[128,2048]{1,0:T(8,128)(2,1)S(1)}, bf16[128,2048]{1,0:T(8,128)(2,1)S(1)}, u32[]{:S(2)}, u32[]{:S(2)}) collective-permute-start(bf16[128,2048]{1,0:T(8,128)(2,1)S(1)} %get-tuple-element.13), channel_id=1, source_target_pairs={{2,0},{3,1},{10,8},{11,9},{18,16},{19,17},{26,24},{27,25}} | collective-permute-start | bytes 1572872 | tf_op jit(solution)/shard_map/ppermute | solution.py:254
  97.7 29.1 %collective-permute-start.10 = (bf16[128,2048]{1,0:T(8,128)(2,1)S(1)}, bf16[128,2048]{1,0:T(8,128)(2,1)S(1)}, u32[]{:S(2)}, u32[]{:S(2)}) collective-permute-start(bf16[128,2048]{1,0:T(8,128)(2,1)S(1)} %add.127), channel_id=1, source_target_pairs={{0,1},{1,0},{2,3},{3,2},{4,5},{5,4},{6,7},{7,6},{8,9},{9,8},{10,11... | collective-permute-start | bytes 1572872 | tf_op jit(solution)/shard_map/ppermute | solution.py:255
  126.8 2.0 %collective-permute-start.5 = (bf16[128,2048]{1,0:T(8,128)(2,1)S(1)}, bf16[128,2048]{1,0:T(8,128)(2,1)S(1)}, u32[]{:S(2)}, u32[]{:S(2)}) collective-permute-start(bf16[128,2048]{1,0:T(8,128)(2,1)S(1)} %add.118), channel_id=1, source_target_pairs={{0,1},{1,0},{2,3},{3,2},{4,5},{5,4},{6,7},{7,6},{8,9},{9,8},{10,11... | collective-permute-start | bytes 1572872 | tf_op jit(solution)/shard_map/ppermute | solution.py:255
  128.8 1.8 %copy-start.10 = (bf16[1,128,128]{2,1,0:T(8,128)(2,1)S(1)}, bf16[1,128,128]{2,1,0:T(8,128)(2,1)}, u32[]{:S(2)}) copy-start(bf16[1,128,128]{2,1,0:T(8,128)(2,1)} %param.13) | copy-start | bytes 98308
  134.2 4.0 %collective-permute-start.14 = (bf16[128,128]{1,0:T(8,128)(2,1)S(1)}, bf16[128,128]{1,0:T(8,128)(2,1)S(1)}, u32[]{:S(2)}, u32[]{:S(2)}) collective-permute-start(bf16[128,128]{1,0:T(8,128)(2,1)S(1)} %shard_map.118), channel_id=1, source_target_pairs={{0,8},{8,0},{16,24},{24,16},{1,9},{9,1},{17,25},{25,17},{2,10},{10... | collective-permute-start | bytes 98312 | tf_op jit(solution)/shard_map/ppermute | solution.py:333
  135.8 3.9 %collective-permute-start.15 = (bf16[128,128]{1,0:T(8,128)(2,1)S(1)}, bf16[128,128]{1,0:T(8,128)(2,1)S(1)}, u32[]{:S(2)}, u32[]{:S(2)}) collective-permute-start(bf16[128,128]{1,0:T(8,128)(2,1)S(1)} %shard_map.118), channel_id=1, source_target_pairs={{0,16},{8,24},{16,0},{24,8},{1,17},{9,25},{17,1},{25,9},{2,18},{10... | collective-permute-start | bytes 98312 | tf_op jit(solution)/shard_map/ppermute | solution.py:333
  137.0 4.9 %collective-permute-start.16 = (bf16[128,128]{1,0:T(8,128)(2,1)S(1)}, bf16[128,128]{1,0:T(8,128)(2,1)}, u32[]{:S(2)}, u32[]{:S(2)}) collective-permute-start(bf16[128,128]{1,0:T(8,128)(2,1)S(1)} %shard_map.118), channel_id=1, source_target_pairs={{0,24},{8,16},{16,8},{24,0},{1,25},{9,17},{17,9},{25,1},{2,26},{10... | collective-permute-start | bytes 98312 | tf_op jit(solution)/shard_map/ppermute | solution.py:333
  142.0 3.3 %copy-start.13 = (bf16[1,128,4096]{2,1,0:T(8,128)(2,1)S(1)}, bf16[1,128,4096]{2,1,0:T(8,128)(2,1)}, u32[]{:S(2)}) copy-start(bf16[1,128,4096]{2,1,0:T(8,128)(2,1)} %param.9) | copy-start | bytes 3145732
  143.7 0.8 copy-start.15
  145.2 1.9 %collective-permute-start.17 = (f32[4,128,128]{2,1,0:T(8,128)}, f32[4,128,128]{2,1,0:T(8,128)}, u32[]{:S(2)}, u32[]{:S(2)}) collective-permute-start(f32[4,128,128]{2,1,0:T(8,128)} %dynamic-slice_bitcast_fusion), channel_id=1, source_target_pairs={{0,1},{1,0},{2,3},{3,2},{4,5},{5,4},{6,7},{7,6},{8,9},{9,8},{10,11... | collective-permute-start | bytes 786440 | tf_op jit(solution)/shard_map/ppermute | solution.py:346
  145.2 1.9 %copy-start.16 = (f32[1024,128]{1,0:T(8,128)S(1)}, f32[1024,128]{1,0:T(8,128)}, u32[]{:S(2)}) copy-start(f32[1024,128]{1,0:T(8,128)} %copy-done.15) | copy-start | bytes 1572868
  145.2 7.4 %copy-start.14 = (bf16[4096,128]{1,0:T(8,128)(2,1)S(1)}, bf16[4096,128]{1,0:T(8,128)(2,1)}, u32[]{:S(2)}) copy-start(bf16[4096,128]{1,0:T(8,128)(2,1)} %all-gather.2.cloned.1.call-done) | copy-start | bytes 3145732
  147.1 7.0 %copy-start.8 = (f32[8,128,128]{2,1,0:T(8,128)S(1)}, f32[8,128,128]{2,1,0:T(8,128)}, u32[]{:S(2)}) copy-start(f32[8,128,128]{2,1,0:T(8,128)} %copy-done.6) | copy-start | bytes 1572868
  148.2 5.9 %copy-start.3 = (bf16[1,128,4096]{2,1,0:T(8,128)(2,1)S(1)}, bf16[1,128,4096]{2,1,0:T(8,128)(2,1)}, u32[]{:S(2)}) copy-start(bf16[1,128,4096]{2,1,0:T(8,128)(2,1)} %param.16) | copy-start | bytes 3145732
  148.2 5.9 %copy-start.5 = (bf16[128,4096]{1,0:T(8,128)(2,1)S(1)}, bf16[128,4096]{1,0:T(8,128)(2,1)}, u32[]{:S(2)}) copy-start(bf16[128,4096]{1,0:T(8,128)(2,1)} %copy-done.4) | copy-start | bytes 3145732
  148.2 12.7 %collective-permute-start.18 = (bf16[128,128]{1,0:T(8,128)(2,1)S(1)}, bf16[128,128]{1,0:T(8,128)(2,1)S(1)}, u32[]{:S(2)}, u32[]{:S(2)}) collective-permute-start(bf16[128,128]{1,0:T(8,128)(2,1)S(1)} %get-tuple-element.25), channel_id=1, source_target_pairs={{0,2},{1,3},{2,0},{3,1},{4,6},{5,7},{6,4},{7,5},{8,10},{9,11},{10,... | collective-permute-start | bytes 98312 | tf_op jit(solution)/shard_map/ppermute | solution.py:351
  148.3 12.6 %collective-permute-start.19 = (bf16[128,128]{1,0:T(8,128)(2,1)S(1)}, bf16[128,128]{1,0:T(8,128)(2,1)S(1)}, u32[]{:S(2)}, u32[]{:S(2)}) collective-permute-start(bf16[128,128]{1,0:T(8,128)(2,1)S(1)} %get-tuple-element.27), channel_id=1, source_target_pairs={{0,4},{1,5},{2,6},{3,7},{4,0},{5,1},{6,2},{7,3},{8,12},{9,13},{10,... | collective-permute-start | bytes 98312 | tf_op jit(solution)/shard_map/ppermute | solution.py:351
  150.1 10.8 %collective-permute-start.20 = (bf16[128,128]{1,0:T(8,128)(2,1)S(1)}, bf16[128,128]{1,0:T(8,128)(2,1)S(1)}, u32[]{:S(2)}, u32[]{:S(2)}) collective-permute-start(bf16[128,128]{1,0:T(8,128)(2,1)S(1)} %get-tuple-element.26), channel_id=1, source_target_pairs={{0,6},{1,7},{2,4},{3,5},{4,2},{5,3},{6,0},{7,1},{8,14},{9,15},{10,... | collective-permute-start | bytes 98312 | tf_op jit(solution)/shard_map/ppermute | solution.py:351
Sparse Core Ops, SparseCore 0:
  47.1 75.7 all-gather.1

commit v2 on v1

v2 whole, which is shorter than its diff:
```python
import functools
import itertools

import jax
import jax.numpy as jnp
from jax import lax
from jax.experimental import pallas as pl
from jax.experimental.pallas import tpu as pltpu
from jax.sharding import PartitionSpec as P

BLOCK = 128
LANES = 128
GROUP = 8
LOG2E = 1.4426950408889634
LOW = -1e30
EXACT = lax.Precision.HIGHEST
VMEM_BYTES = 14 * 1024 * 1024
BEHIND = 5 * 10**9

f32 = jnp.float32
bf16 = jnp.bfloat16

CUM2, EXCLR2, FWD_EDGE, BACK_EDGE, STEP = range(5)
C_MIX_FWD, C_MIX_BACK, C_CUM2, C_EXCL2 = range(4)


def sds(shape, dtype):
    return jax.ShapeDtypeStruct(shape, dtype)


def job(body, outs, *arrays, scalars=()):
    return body, outs, arrays, [jnp.reshape(s, (1,)).astype(jnp.int32) for s in scalars]


def run(*jobs, after=(), flops=0):
    vmem = pl.BlockSpec(memory_space=pltpu.VMEM)
    smem = pl.BlockSpec(memory_space=pltpu.SMEM)
    anywhere = pl.BlockSpec(memory_space=pl.ANY)
    ins, specs, outs, calls = [], [], [], []
    for body, job_outs, arrays, scalars in jobs:
        calls.append((body, len(ins), len(scalars) + len(arrays), len(outs), len(job_outs)))
        ins += [*scalars, *arrays]
        specs += [smem] * len(scalars) + [vmem] * len(arrays)
        outs += job_outs
    lead = len(ins) + len(after)

    def kernel(*refs):
        for body, i, ni, o, no in calls:
            body(*refs[i : i + ni], *refs[lead + o : lead + o + no])

    got = pl.pallas_call(
        kernel,
        out_shape=outs,
        in_specs=specs + [anywhere] * len(after),
        out_specs=[vmem] * len(outs),
        compiler_params=pltpu.CompilerParams(vmem_limit_bytes=VMEM_BYTES),
        cost_estimate=pl.CostEstimate(flops=flops, transcendentals=0, bytes_accessed=0),
    )(*ins, *after)
    return [list(got[o : o + no]) for _, _, _, o, no in calls]


def iotas(shape):
    return lax.broadcasted_iota(jnp.int32, shape, 0), lax.broadcasted_iota(jnp.int32, shape, 1)


def dot_nt(a, b):
    return lax.dot_general(a, b, (((1,), (1,)), ((), ())), preferred_element_type=f32)


def dot_tn(a, b):
    return lax.dot_general(a, b, (((0,), (0,)), ((), ())), preferred_element_type=f32)


def spread(rows, width):
    high = rows.astype(bf16).astype(f32)
    both = jnp.concatenate([high, rows - high], axis=0).astype(bf16)
    r, c = iotas((2 * GROUP, GROUP * width))
    pick = (r % GROUP == c // width).astype(f32).astype(bf16)
    return dot_tn(both, pick)


def tables_kernel(read_ref, decay_ref, step_ref, readr_ref, rows_ref, cols_ref):
    decay = decay_ref[...]
    heads, n = decay.shape
    r, c = iotas((n, n))
    upto = (r <= c).astype(f32)
    flip = (r + c == n - 1).astype(f32)
    readr_ref[...] = jnp.dot(
        flip.astype(bf16), read_ref[...], preferred_element_type=f32
    ).astype(bf16)
    cum = jnp.dot(decay, upto, precision=EXACT, preferred_element_type=f32)
    decay_r = jnp.dot(decay, flip, precision=EXACT, preferred_element_type=f32)
    cum_r = jnp.dot(decay_r, upto, precision=EXACT, preferred_element_type=f32)
    end = cum[:, n - 1 :]
    excl = cum - decay
    step = step_ref[...]
    log_step = jnp.log(step) * LOG2E
    cum2 = cum * LOG2E
    excl2 = excl * LOG2E
    rows_ref[CUM2] = cum2
    rows_ref[EXCLR2] = (end - cum_r) * LOG2E
    rows_ref[FWD_EDGE] = step * jnp.exp(end - cum)
    rows_ref[BACK_EDGE] = step * jnp.exp(excl)
    rows_ref[STEP] = step
    planes = (cum2 - log_step, excl2 + log_step, cum2, excl2)
    rest = jnp.zeros((LANES - GROUP * len(planes), n), f32)
    for g in range(heads // GROUP):
        part = [p[g * GROUP : (g + 1) * GROUP] for p in planes]
        cols_ref[g] = jnp.concatenate(part + [rest], axis=0).T


def part_kernel(backward, core_ref, g_ref, read_ref, decay_ref, own_ref, send_ref):
    heads, n = decay_ref.shape
    width = g_ref.shape[1] // heads
    step = GROUP * width
    r, c = iotas((n, n))
    order = ((r + c == n - 1) if backward else (r == c)).astype(f32)
    upto = (r <= c).astype(f32)
    read_t = dot_tn(read_ref[...].astype(bf16), order.astype(bf16)).astype(bf16)
    decay = decay_ref[...]
    if backward:
        decay = jnp.dot(decay, order, precision=EXACT, preferred_element_type=f32)
    weight = jnp.exp(jnp.dot(decay, upto, precision=EXACT, preferred_element_type=f32))
    state = read_t.shape[0]
    groups = heads // GROUP
    tail_row, _ = iotas((16, step))
    low = core_ref[0] == 0

    def term_of(g):
        scale = spread(weight[g * GROUP : (g + 1) * GROUP], width)
        scaled = (g_ref[:, g * step : (g + 1) * step].astype(f32) * scale).astype(bf16)
        term = jnp.dot(read_t, scaled, preferred_element_type=f32)
        last = scale[n - 1 :]
        high = last.astype(bf16).astype(f32)
        tail = jnp.where(tail_row == 0, high, jnp.where(tail_row == 1, last - high, 0.0))
        return jnp.concatenate([term, tail], axis=0)

    for g in range(groups // 2):
        here = slice(g * step, (g + 1) * step)
        lower, upper = term_of(g), term_of(g + groups // 2)
        own_ref[:, here] = jnp.where(low, lower, upper).astype(bf16)
        send_ref[:, here] = jnp.where(low, upper, lower).astype(bf16)


WIDE = 512


def chip_terms(upward, core, own_ref, near_ref):
    state = own_ref.shape[0] - 16
    first = core == (0 if upward else 1)
    for c in range(own_ref.shape[1] // WIDE):
        here = slice(c * WIDE, (c + 1) * WIDE)
        own = own_ref[:, here].astype(f32)
        other = near_ref[:, here].astype(f32)
        own_term, other_term = own[:state], other[:state]
        own_decay = own[state : state + 1] + own[state + 1 : state + 2]
        other_decay = other[state : state + 1] + other[state + 1 : state + 2]
        later = jnp.where(first, other_decay, own_decay)
        term = jnp.where(first, other_term, own_term) + later * jnp.where(
            first, own_term, other_term
        )
        yield here, term, own_decay * other_decay


def chip_kernel(upward, core_ref, own_ref, near_ref, term_ref, decay_ref):
    for here, term, decay in chip_terms(upward, core_ref[0], own_ref, near_ref):
        term_ref[:, here] = term.astype(bf16)
        decay_ref[:, here] = decay


def entered(refs, here):
    state = refs[0][:, here].astype(f32)
    for ref in refs[1:]:
        state = state + ref[:, here].astype(f32)
    return state


def onward_kernel(term_ref, decay_ref, *refs):
    *entering, out_ref = refs
    for c in range(out_ref.shape[1] // WIDE):
        here = slice(c * WIDE, (c + 1) * WIDE)
        out_ref[:, here] = (
            term_ref[:, here].astype(f32) + decay_ref[:, here] * entered(entering, here)
        ).astype(bf16)


def middle_kernel(flag_ref, term_ref, decay_ref, *refs):
    *entering, out_ref = refs
    for c in range(out_ref.shape[1] // WIDE):
        here = slice(c * WIDE, (c + 1) * WIDE)
        leaving = term_ref[:, here].astype(f32)
        if entering:
            leaving = leaving + decay_ref[:, here] * entered(entering, here)
        out_ref[:, here] = jnp.where(flag_ref[0] == 1, leaving, 0.0).astype(bf16)


def left_kernel(core_ref, own_ref, near_ref, *refs):
    *entering, out_ref = refs
    for here, term, decay in chip_terms(True, core_ref[0], own_ref, near_ref):
        out_ref[:, here] = (term + decay * entered(entering, here)).astype(bf16)


def halves_kernel(count, *refs):
    rights, lefts, out_ref = refs[:count], refs[count:-1], refs[-1]
    half = out_ref.shape[1] // 2
    for c in range(half // WIDE):
        here = slice(c * WIDE, (c + 1) * WIDE)
        there = slice(half + c * WIDE, half + (c + 1) * WIDE)
        out_ref[:, here] = entered(rights, here).astype(bf16)
        out_ref[:, there] = entered(lefts, here).astype(bf16)


def mix_kernel(fwd, inner_ref, g_ref, row_ref, cols_ref, out_ref):
    heads, n = row_ref.shape
    width = g_ref.shape[1] // heads
    step = GROUP * width
    s, t = iotas((n, n))
    keep = (t >= s) if fwd else (t + s >= n - 1)
    low_half = t < width

    def one(g, acc):
        at = pl.multiple_of(g * step, step)
        rows = row_ref[pl.ds(pl.multiple_of(g * GROUP, GROUP), GROUP)]
        cols = cols_ref[g]
        for pair in range(GROUP // 2):
            here = pl.ds(at + pair * LANES, LANES)
            inner = inner_ref[:, here].astype(f32)
            halves = jnp.concatenate(
                [jnp.where(low_half, inner, 0.0), jnp.where(low_half, 0.0, inner)], axis=0
            ).astype(bf16)
            dots = dot_nt(halves, g_ref[:, here])
            for j in range(2):
                h = 2 * pair + j
                row = rows[h : h + 1]
                if fwd:
                    k = C_MIX_FWD * GROUP + h
                    power = row - cols[:, k : k + 1]
                else:
                    k = C_MIX_BACK * GROUP + h
                    power = cols[:, k : k + 1] - row
                decay = jnp.exp2(jnp.where(keep, power, LOW))
                acc = acc + decay * dots[j * n : (j + 1) * n]
        return acc

    out_ref[...] = lax.fori_loop(0, heads // GROUP, one, jnp.zeros((n, n), f32))


def edge_terms(
    upward, core, inner_ref, halves_ref, swapped_ref, near_ref, far_ref, edge, state_ref
):
    heads, n = edge.shape
    width = inner_ref.shape[1] // heads
    step = GROUP * width
    groups = heads // GROUP
    first = core == (0 if upward else 1)
    rows = state_ref.shape[0]
    base = halves_ref.shape[1] // 2 if upward else 0
    acc = 0.0
    for g in range(groups):
        here = slice(g * step, (g + 1) * step)
        at = base + g % (groups // 2) * step
        there = slice(at, at + step)
        near = slice(at - base, at - base + step)
        mine = core == g // (groups // 2)
        whole = jnp.where(mine, halves_ref[:, there].astype(f32), swapped_ref[:, there].astype(f32))
        other = jnp.where(mine, near_ref[:, near].astype(f32), far_ref[:, near].astype(f32))
        decay = other[rows : rows + 1] + other[rows + 1 : rows + 2]
        entering = jnp.where(first, whole, other[:rows] + decay * whole).astype(bf16)
        state_ref[:, here] = entering
        scaled = inner_ref[:, here].astype(f32) * spread(edge[g * GROUP : (g + 1) * GROUP], width)
        acc = acc + dot_nt(scaled.astype(bf16), entering)
    return acc


def write_kernel(
    core_ref,
    inner_ref,
    halves_ref,
    swapped_ref,
    right_near_ref,
    right_far_ref,
    left_near_ref,
    left_far_ref,
    rows_ref,
    mixf_ref,
    mixb_ref,
    read_ref,
    readr_ref,
    right_ref,
    left_ref,
    out_ref,
):
    core = core_ref[0]
    shared = (inner_ref, halves_ref, swapped_ref)
    acc = jnp.dot(mixf_ref[...].astype(bf16), read_ref[...], preferred_element_type=f32)
    acc = acc + jnp.dot(mixb_ref[...].astype(bf16), readr_ref[...], preferred_element_type=f32)
    acc = acc + edge_terms(False, core, *shared, right_near_ref, right_far_ref, rows_ref[FWD_EDGE], right_ref)
    acc = acc + edge_terms(True, core, *shared, left_near_ref, left_far_ref, rows_ref[BACK_EDGE], left_ref)
    out_ref[...] = acc.astype(bf16)


def share_kernel(dp_ref, hidden_ref, weight_ref, *out_refs):
    share = weight_ref.shape[0]
    for k, out_ref in enumerate(out_refs):
        for c in range(share // LANES):
            at = pl.multiple_of((dp_ref[0] ^ k) * share + c * LANES, LANES)
            out_ref[c * LANES : (c + 1) * LANES] = (
                hidden_ref[:, pl.ds(at, LANES)].astype(f32).T.astype(bf16)
            )
        out_ref[share:] = weight_ref[...]


def product_kernel(core_ref, *refs):
    count = (len(refs) - 2) // 2
    hidden_refs, write_refs = refs[:count], refs[count : 2 * count]
    keep_ref, give_ref = refs[2 * count :]
    chips, piece, _ = keep_ref.shape
    writes = [w[...] for w in write_refs]
    for which, out_ref in ((core_ref[0], keep_ref), (1 - core_ref[0], give_ref)):
        for chip in range(chips):
            rows = pl.ds(pl.multiple_of((2 * chip + which) * piece, piece), piece)
            total = jnp.dot(hidden_refs[0][rows], writes[0], preferred_element_type=f32)
            for k in range(1, count):
                total = total + jnp.dot(hidden_refs[k][rows], writes[k], preferred_element_type=f32)
            out_ref[chip] = total.astype(out_ref.dtype)


def deal_kernel(chip_ref, keep_ref, got_ref, own_ref, *out_refs):
    chip = chip_ref[0]
    own_ref[...] = keep_ref[chip] + got_ref[chip].astype(f32)
    for k, out_ref in enumerate(out_refs, 1):
        out_ref[...] = (keep_ref[chip ^ k] + got_ref[chip ^ k].astype(f32)).astype(bf16)


def cut_kernel(start, array_ref, out_ref):
    out_ref[...] = array_ref[:, start : start + out_ref.shape[1]]


def stack_kernel(*refs):
    *arrays, out_ref = refs
    for k, ref in enumerate(arrays):
        out_ref[k] = ref[...].astype(bf16)


def pair_kernel(chip_ref, core_ref, held_ref, got_ref, out_ref):
    chip, core = chip_ref[0], core_ref[0]
    chips = held_ref.shape[0]
    for k in range(chips):
        held_core = core if k < chips - 1 else 1 - core
        out_ref[chip ^ k, held_core] = held_ref[k]
        out_ref[chip ^ k, 1 - held_core] = got_ref[k]


def gather_kernel(index_ref, *refs):
    *arrays, out_ref = refs
    rows = out_ref.shape[1]
    for k, ref in enumerate(arrays):
        out_ref[index_ref[0] ^ k] = ref[ref.shape[0] - rows :]


def inner_kernel(
    gf_ref, gb_ref, right_ref, left_ref, rows_ref, cols_ref, write_ref, read_ref, readr_ref, out_ref
):
    _, heads, n = rows_ref.shape
    width = gf_ref.shape[1] // heads
    step = GROUP * width
    write = write_ref[...]
    kernel_f = dot_nt(write, read_ref[...])
    kernel_b = dot_nt(write, readr_ref[...])
    s, t = iotas((n, n))
    low_half = t < width

    def one(g, carry):
        at = pl.multiple_of(g * step, step)
        own = pl.ds(pl.multiple_of(g * GROUP, GROUP), GROUP)
        cols = cols_ref[g]
        cum2 = rows_ref[CUM2, own]
        exclr2 = rows_ref[EXCLR2, own]
        step_e = spread(rows_ref[STEP, own], width)
        edges = spread(rows_ref[FWD_EDGE, own], width) * jnp.dot(
            write, right_ref[:, pl.ds(at, step)], preferred_element_type=f32
        )
        edges = edges + spread(rows_ref[BACK_EDGE, own], width) * jnp.dot(
            write, left_ref[:, pl.ds(at, step)], preferred_element_type=f32
        )
        for pair in range(GROUP // 2):
            mixes = []
            for j in range(2):
                h = 2 * pair + j
                kf = C_CUM2 * GROUP + h
                kb = C_EXCL2 * GROUP + h
                pf = cum2[h : h + 1] - cols[:, kf : kf + 1]
                pb = cols[:, kb : kb + 1] - exclr2[h : h + 1]
                mf = jnp.exp2(jnp.where(t >= s, pf, LOW)) * kernel_f
                mb = jnp.exp2(jnp.where(t + s >= n - 1, pb, LOW)) * kernel_b
                mixes.append(jnp.concatenate([mf, mb], axis=1))
            here = pl.ds(at + pair * LANES, LANES)
            both = jnp.concatenate([gf_ref[:, here], gb_ref[:, here]], axis=0)
            got = jnp.dot(
                jnp.concatenate(mixes, axis=0).astype(bf16), both, preferred_element_type=f32
            )
            intra = jnp.where(low_half, got[:n], got[n:])
            mine = slice(pair * LANES, (pair + 1) * LANES)
            out_ref[:, here] = (step_e[:, mine] * intra + edges[:, mine]).astype(bf16)
        return carry

    lax.fori_loop(0, heads // GROUP, one, 0)


def xor_pairs(count, k):
    return [(i, i ^ k) for i in range(count)]


def chip_pairs(moves):
    return [(2 * a + i, 2 * b + i) for a, b in moves for i in range(2)]


def shards(
    hidden_in,
    write_weight,
    shard_scale,
    inner_acts,
    read_proj,
    step_size,
    log_decay,
    grad_fwd,
    grad_rev,
):
    ctx_count = lax.axis_size("ctx")
    dp_count = lax.axis_size("dp")
    ctx = lax.axis_index("ctx")
    dp = lax.axis_index("dp")
    core, chip = ctx % 2, ctx // 2
    chips = ctx_count // 2
    span = chips // 2
    hidden = hidden_in[0]
    inner = inner_acts[0]
    read = read_proj[0]
    step = step_size[0]
    decay = log_decay[0]
    gf = grad_fwd[0]
    gr = grad_rev[0]
    n, width = inner.shape
    heads = decay.shape[0]
    state = read.shape[1]
    half = width // 2
    share = hidden.shape[1] // dp_count
    part = functools.partial
    part_shapes = [sds((state + 16, half), bf16)] * 2
    half_shape = sds((state, half), bf16)
    chip_shapes = [half_shape, sds((1, half), f32)]

    def over_cores(array):
        return lax.ppermute(array, "ctx", xor_pairs(ctx_count, 1))

    def over_chips(array, *moves):
        return lax.ppermute(array, "ctx", chip_pairs(moves))

    def over_dp(array, k):
        return lax.ppermute(array, "dp", xor_pairs(dp_count, k))

    def flip(piece):
        return lax.ppermute(piece, "ctx", [(i, ctx_count - 1 - i) for i in range(ctx_count)])

    local = (write_weight.astype(f32) * shard_scale[0]).astype(bf16)
    mirrored = flip(jnp.concatenate([read.astype(f32), decay, local.astype(f32)], axis=0))
    weights = [local] + [
        lax.ppermute(local, "ctx", xor_pairs(ctx_count, 2 * k)) for k in range(1, chips - 1)
    ]
    gr_again, *_ = lax.optimization_barrier((gr, mirrored, *weights))
    flipped = flip(gr_again)

    def part_job(backward, *arrays):
        return job(part(part_kernel, backward), part_shapes, *arrays, scalars=(core,))

    def chip_job(upward, own, near):
        return job(part(chip_kernel, upward), chip_shapes, own, near, scalars=(core,))

    (early_own, send), (held,) = run(
        part_job(True, gr, mirrored[:n], mirrored[n : n + heads]),
        job(stack_kernel, [sds((chips, *local.shape), bf16)], *weights, mirrored[n + heads :]),
    )
    early_near = over_cores(send)
    ((right_own, send),) = run(part_job(False, gf, read, decay))
    right_near = over_cores(send)
    (early_term, early_decay), (read_r, rows, cols) = run(
        chip_job(False, early_own, early_near),
        job(
            tables_kernel,
            [
                sds((n, state), bf16),
                sds((5, heads, n), f32),
                sds((heads // GROUP, n, LANES), f32),
            ],
            read,
            decay,
            step,
        ),
        after=(right_own,),
    )
    earlies = []
    for i in range(span - 1):
        leaving = early_term
        if i:
            ((leaving,),) = run(
                job(onward_kernel, [half_shape], early_term, early_decay, *earlies)
            )
        earlies.append(over_chips(leaving, (chips - 1 - i, chips - 2 - i)))
    ((right_term, right_decay),) = run(
        chip_job(False, right_own, right_near), after=(early_term,)
    )
    rights = [over_chips(right_term, (chips - 1, chips - 2))]
    got = over_cores(held)
    ((held,),) = run(
        job(
            pair_kernel,
            [sds((chips, 2, *local.shape), bf16)],
            held,
            got,
            scalars=(chip, core),
        ),
        after=(right_term,),
    )
    held = held.reshape(-1, state)
    (shares,) = run(
        job(share_kernel, [sds((2 * share, n), bf16)] * dp_count, hidden, held, scalars=(dp,))
    )
    shared = [shares[0]] + [over_dp(shares[k], k) for k in range(1, dp_count)]
    ((mix_f,),) = run(
        job(part(mix_kernel, True), [sds((n, n), f32)], inner, gf, rows[CUM2], cols),
        after=(right_term,),
    )
    right_far = over_cores(right_own)
    ((leaving,),) = run(
        job(onward_kernel, [half_shape], right_term, right_decay, *rights),
        after=(mix_f, right_far, *earlies, *shared[1:3]),
    )
    rights.append(over_chips(leaving, (chips - 2, chips - 3)))

    ((left_own, send),) = run(part_job(True, flipped, read, decay), after=(leaving,))
    left_near = over_cores(send)
    ((middle,),) = run(
        job(
            middle_kernel, [half_shape], early_term, early_decay, *earlies, scalars=(chip == span,)
        ),
        after=(left_own,),
    )
    lefts = [middle]
    for i in range(span - 1):
        ((leaving,),) = run(
            job(left_kernel, [half_shape], left_own, left_near, *lefts, scalars=(core,))
        )
        lefts.append(over_chips(leaving, (i, i + 1), (span + i, span + i + 1)))
    ((mix_b,),) = run(
        job(part(mix_kernel, False), [sds((n, n), f32)], inner, flipped, rows[EXCLR2], cols),
        after=(leaving,),
    )
    left_far = over_cores(left_own)
    for i in range(2, chips - 1):
        ((leaving,),) = run(
            job(onward_kernel, [half_shape], right_term, right_decay, *rights),
            after=(mix_b, *shared[3:]) if i == 2 else (),
            flops=BEHIND,
        )
        rights.append(over_chips(leaving, (chips - 1 - i, chips - 2 - i)))
    ((halves,),) = run(
        job(part(halves_kernel, len(rights)), [sds((state, width), bf16)], *rights, *lefts),
        after=(left_far,),
    )
    swapped = over_cores(halves)

    ((right_in, left_in, grad_write),) = run(
        job(
            write_kernel,
            [sds((state, width), bf16), sds((state, width), bf16), sds((n, state), bf16)],
            inner,
            halves,
            swapped,
            right_near,
            right_far,
            left_near,
            left_far,
            rows,
            mix_f,
            mix_b,
            read,
            read_r,
            scalars=(core,),
        )
    )
    gb = flipped

    writes = [grad_write] + [over_dp(grad_write, k) for k in range(1, dp_count)]
    ((weight,),) = run(
        job(gather_kernel, [sds((dp_count, share, state), bf16)], *shared, scalars=(dp,)),
        after=(grad_write,),
    )
    weight = weight.reshape(-1, state)
    write = jnp.dot(hidden, weight, preferred_element_type=f32).astype(bf16)
    ((grad_inner,),) = run(
        job(
            inner_kernel,
            [sds((n, width), bf16)],
            gf,
            gb,
            right_in,
            left_in,
            rows,
            cols,
            write,
            read,
            read_r,
        )
    )
    piece = share // ctx_count
    ((keep, give),) = run(
        job(
            product_kernel,
            [sds((chips, piece, state), f32), sds((chips, piece, state), bf16)],
            *shared,
            *writes,
            scalars=(core,),
        ),
        after=(grad_inner,),
    )
    ((total, *dealt),) = run(
        job(
            deal_kernel,
            [sds((piece, state), f32)] + [sds((piece, state), bf16)] * (chips - 1),
            keep,
            over_cores(give),
            scalars=(chip,),
        )
    )
    for k in range(1, chips):
        total = total + lax.ppermute(dealt[k - 1], "ctx", xor_pairs(ctx_count, 2 * k)).astype(f32)
    grad_weight = total / (dp_count * ctx_count * n)

    grad_hidden = dot_nt(grad_write, weight).astype(bf16)
    return grad_inner[None], grad_hidden[None], grad_weight


def solution(mesh):
    in_specs = (
        P("dp", "ctx", None),
        P(("dp", "ctx"), None),
        P(("dp", "ctx")),
        P("dp", "ctx", None),
        P("dp", "ctx", None),
        P("dp", None, "ctx"),
        P("dp", None, "ctx"),
        P("dp", "ctx", None),
        P("dp", "ctx", None),
    )
    out_specs = (P("dp", "ctx", None), P("dp", "ctx", None), P(("dp", "ctx"), None))
    return jax.shard_map(shards, mesh=mesh, in_specs=in_specs, out_specs=out_specs, check_vma=False)
```

time: 169 us -> 148 us (0.88)
  waiting for transfers between devices: 57.1 us -> 39.9 us
  Pallas kernels: 23.3 us -> 37.3 us
  between operations: 15.1 us -> 1.7 us
  other arithmetic: 13.1 us -> 3.04 us
  starting transfers between devices: 45.7 us -> 53.1 us
  matrix products: 4.91 us -> 1.82 us
    ppermute x21 -> x26, waiting for transfers between devices: 57.1 us -> 39.9 us  [the longest x6 15 us: over_dp(): return lax.ppermute(array, 'dp', xor_pairs(dp_count, k))]
    pallas_call x7 -> x19, Pallas kernels: 23.3 us -> 37.3 us  [run(): pl.pallas_call(kernel, out_shape=outs, in_specs=specs + [anywhere] * len(...]
    ppermute x21 -> x26, starting transfers between devices: 45.6 us -> 53.1 us  [the longest x5 30.7 us: over_chips(): return lax.ppermute(array, 'ctx', chip_pairs(moves))]
    unnamed x36 -> x70, local copies, waits for them, and re-layouts: 6.15 us -> 10.5 us
    convert_element_type x10 -> x2, other arithmetic: 5.73 us -> 1.62 us  [the longest x1 0.86 us: shards(): local.astype(f32)]
    select_n x2 -> x0, other arithmetic: 3.52 us -> none  [chip_states(): return jnp.where(first, whole, second.astype(bf16))]
    add x5 -> x0, other arithmetic: 3.17 us -> none  [the longest x2 1.88 us: chip_states(): other[state:state + 1].astype(f32) + other[state + 1:state + 2].astype(f32)]
    dynamic_slice x1 -> x0, local copies, waits for them, and re-layouts: 2.31 us -> none  [of_dp(): return lax.dynamic_slice_in_dim(array, (dp ^ k) * share, share, 1)]
  transfers between devices with their start and end apart: 22 -> 26, of which waited for: 8 -> 11; matrix products, arithmetic and copies ran while one was open for 12% -> 1% of each run, Pallas kernels for 14% -> 16%
where the time goes in v2:
time: 148 us; the launch traced here: 147 us
  starting transfers between devices  53.1 us (36%)
  waiting for transfers between devices  39.9 us (27%)
  Pallas kernels  37.3 us (25%)
  local copies, waits for them, and re-layouts  10.6 us (7%)
  other arithmetic  3.04 us (2%)
  matrix products  1.82 us (1%)
  between operations  1.7 us (1%)
    pallas_call x19, Pallas kernels, run(): pl.pallas_call(kernel, out_shape=outs, in_specs=specs + [anywhere] * len(...  37.3 us
    ppermute x5, starting transfers between devices, over_chips(): return lax.ppermute(array, 'ctx', chip_pairs(moves))  30.7 us
    ppermute x6, waiting for transfers between devices, over_dp(): return lax.ppermute(array, 'dp', xor_pairs(dp_count, k))  15 us
    ppermute x5, waiting for transfers between devices, over_chips(): return lax.ppermute(array, 'ctx', chip_pairs(moves))  10.8 us
    unnamed x70, local copies, waits for them, and re-layouts  10.5 us
    ppermute x6, starting transfers between devices, over_dp(): return lax.ppermute(array, 'dp', xor_pairs(dp_count, k))  8.06 us
    ppermute x2, starting transfers between devices, flip(): lax.ppermute(piece, 'ctx', [(i, ctx_count - 1 - i) for i in range(ctx_cou...  7.15 us
    ppermute x3, starting transfers between devices, shards(): lax.ppermute(dealt[k - 1], 'ctx', xor_pairs(ctx_count, 2 * k)).astype(f32)  4.99 us
  transfers between devices with their start and end apart: 26, of which 11 were waited for; matrix products, arithmetic and copies ran while one was open for 1% of the time, Pallas kernels for 16%

profile of v2, /device:TPU:0, one launch (start us, length us, event | category | flops | bytes accessed | tf_op | source)
XLA Modules:
  0.0 147.5 jit_solution(10563715916010109031)
XLA Ops:
  1.3 0.8 bitcast_convert_fusion
  2.1 0.9 fusion.3
  2.9 0.8 pad_maximum_fusion
  3.7 4.6 %collective-permute-start = (f32[320,128]{1,0:T(8,128)S(1)}, f32[320,128]{1,0:T(8,128)S(1)}, u32[]{:S(2)}, u32[]{:S(2)}) collective-permute-start(f32[320,128]{1,0:T(8,128)S(1)} %pad_maximum_fusion), channel_id=1, source_target_pairs={{0,7},{1,6},{2,5},{3,4},{4,3},{5,2},{6,1},{7,0},{8,15},{9,14},{10,... | collective-permute-start | bytes 491528 | tf_op jit(solution)/shard_map/ppermute | solution.py:463
  8.3 1.2 collective-permute-start.1
  9.5 3.5 %collective-permute-done = f32[320,128]{1,0:T(8,128)S(1)} collective-permute-done((f32[320,128]{1,0:T(8,128)S(1)}, f32[320,128]{1,0:T(8,128)S(1)}, u32[]{:S(2)}, u32[]{:S(2)}) %collective-permute-start) | collective-permute-done | bytes 163872 | tf_op jit(solution)/shard_map/ppermute | solution.py:463
  13.0 4.7 %collective-permute-done.2.refs_6_ = bf16[128,128]{1,0:T(8,128)(2,1)S(1)} collective-permute-done((bf16[128,128]{1,0:T(8,128)(2,1)S(1)}, bf16[128,128]{1,0:T(8,128)(2,1)S(1)}, u32[]{:S(2)}, u32[]{:S(2)}) %collective-permute-start.2) | collective-permute-done | bytes 32800 | tf_op jit(solution)/shard_map/ppermute | solution.py:468
  17.6 4.2 %shard_map.113 = (bf16[144,2048]{1,0:T(8,128)(2,1)S(1)}, bf16[144,2048]{1,0:T(8,128)(2,1)}, bf16[4,128,128]{2,1,0:T(8,128)(2,1)S(1)}) custom-call(s32[1]{0:T(128)} %bitcast.5.refs_0_.refs_1_, bf16[128,4096]{1,0:T(8,128)(2,1)} %bitcast.1.refs_1_, f32[128,128]{1,0:T(8,128)S(1)} %get-tuple-element.64.refs_2_, f32[64,128]{1,0:T(8,128)S(1)} %slice.21.refs_3_, ...), custom_call_target="tpu_custom_call" | custom-call | tf_op jit(solution)/shard_map/pallas_call | solution.py:51
  21.9 0.8 copy-done.27
  22.7 3.0 %shard_map.112 = (bf16[144,2048]{1,0:T(8,128)(2,1)}, bf16[144,2048]{1,0:T(8,128)(2,1)}) custom-call(s32[1]{0:T(128)} %bitcast.5.refs_0_.refs_1_, bf16[128,4096]{1,0:T(8,128)(2,1)S(1)} %bitcast.33, bf16[128,128]{1,0:T(8,128)(2,1)S(1)} %bitcast.40, f32[64,128]{1,0:T(8,128)S(1)} %bitcast.47), custom_call_target="tpu_custom_call" | custom-call | tf_op jit(solution)/shard_map/pallas_call | solution.py:51
  25.7 0.5 collective-permute-start.4
  26.2 2.6 %collective-permute-start.3 = (bf16[128,4096]{1,0:T(8,128)(2,1)}, bf16[128,4096]{1,0:T(8,128)(2,1)S(1)}, u32[]{:S(2)}, u32[]{:S(2)}) collective-permute-start(bf16[128,4096]{1,0:T(8,128)(2,1)} %bitcast.1.refs_1_), channel_id=1, source_target_pairs={{0,7},{1,6},{2,5},{3,4},{4,3},{5,2},{6,1},{7,0},{8,15},{9,14},{10,... | collective-permute-start | bytes 3145736 | tf_op jit(solution)/shard_map/ppermute | solution.py:463
  28.9 1.1 copy-done.28
  29.9 2.0 %shard_map.114 = (bf16[128,2048]{1,0:T(8,128)(2,1)S(1)}, f32[1,2048]{1,0:T(1,128)S(1)}, bf16[128,128]{1,0:T(8,128)(2,1)S(1)}, f32[5,64,128]{2,1,0:T(8,128)S(1)}, f32[8,128,128]{2,1,0:T(8,128)S(1)}) custom-call(s32[1]{0:T(128)} %bitcast.5.refs_0_.refs_1_, bf16[144,2048]{1,0:T(8,128)(2,1)S(1)} %copy-done.28, bf16[144,2048]{1,0:T(8,128)(2,1)} %collective-permute-done.5.refs_2_, ...), custom_call_target="tpu_custom_call" | custom-call | tf_op jit(solution)/shard_map/pallas_call | solution.py:51
  32.0 0.8 collective-permute-start.8
  32.9 1.5 %shard_map.115 = (bf16[128,2048]{1,0:T(8,128)(2,1)S(1)}, f32[1,2048]{1,0:T(1,128)S(1)}) custom-call(s32[1]{0:T(128)} %bitcast.5.refs_0_.refs_1_, bf16[144,2048]{1,0:T(8,128)(2,1)} %get-tuple-element.32.refs_6_.refs_1_, bf16[144,2048]{1,0:T(8,128)(2,1)S(1)} %collective-permute-done.4.refs_2_.refs_4_, bf16[128,2048]{1,0:T(8,128)(2,1)S(1)} %get-tuple-element.36.refs_3_.refs_1_), custom_call_target="tpu_custom_call" | custom-call | tf_op jit(solution)/shard_map/pallas_call | solution.py:51
  34.4 0.7 collective-permute-start.6
  35.1 0.6 copy-done.32
  35.8 0.9 copy-done.33
  36.7 1.2 shard_map.118
  38.0 0.8 copy-done.20
  38.8 1.5 %collective-permute-start.10 = (bf16[2048,128]{1,0:T(8,128)(2,1)S(1)}, bf16[2048,128]{1,0:T(8,128)(2,1)S(1)}, u32[]{:S(2)}, u32[]{:S(2)}) collective-permute-start(bf16[2048,128]{1,0:T(8,128)(2,1)S(1)} %get-tuple-element.42), channel_id=1, source_target_pairs={{0,8},{8,0},{16,24},{24,16},{1,9},{9,1},{17,25},{25,17},{2,10},{10... | collective-permute-start | bytes 1572872 | tf_op jit(solution)/shard_map/ppermute | solution.py:460
  40.3 1.5 %collective-permute-start.11 = (bf16[2048,128]{1,0:T(8,128)(2,1)S(1)}, bf16[2048,128]{1,0:T(8,128)(2,1)S(1)}, u32[]{:S(2)}, u32[]{:S(2)}) collective-permute-start(bf16[2048,128]{1,0:T(8,128)(2,1)S(1)} %get-tuple-element.43), channel_id=1, source_target_pairs={{0,16},{8,24},{16,0},{24,8},{1,17},{9,25},{17,1},{25,9},{2,18},{10... | collective-permute-start | bytes 1572872 | tf_op jit(solution)/shard_map/ppermute | solution.py:460
  41.8 2.1 %shard_map.116.refs_3_.refs_9_ = f32[128,128]{1,0:T(8,128)S(1)} custom-call(bf16[128,4096]{1,0:T(8,128)(2,1)S(1)} %bitcast.30, bf16[128,4096]{1,0:T(8,128)(2,1)S(1)} %bitcast.34, f32[64,128]{1,0:T(8,128)S(1)} %get-tuple-element.62.refs_2_, f32[8,128,128]{2,1,0:T(8,128)S(1)} %get-tuple-element.40.refs_3_.refs_5_, ...), custom_call_target="tpu_custom_call" | custom-call | tf_op jit(solution)/shard_map/pallas_call | solution.py:51
  43.9 9.1 %collective-permute-done.10.refs_6_.refs_2_ = bf16[2048,128]{1,0:T(8,128)(2,1)S(1)} collective-permute-done((bf16[2048,128]{1,0:T(8,128)(2,1)S(1)}, bf16[2048,128]{1,0:T(8,128)(2,1)S(1)}, u32[]{:S(2)}, u32[]{:S(2)}) %collective-permute-start.10) | collective-permute-done | bytes 524320 | tf_op jit(solution)/shard_map/ppermute | solution.py:460
  53.0 1.2 collective-permute-done.11.refs_7_.refs_3_
  54.2 1.0 shard_map.119.refs_4_
  55.3 3.0 %shard_map.120 = (bf16[144,2048]{1,0:T(8,128)(2,1)S(1)}, bf16[144,2048]{1,0:T(8,128)(2,1)}) custom-call(s32[1]{0:T(128)} %bitcast.5.refs_0_.refs_1_, bf16[128,4096]{1,0:T(8,128)(2,1)S(1)} %collective-permute-done.3.refs_1_, bf16[128,128]{1,0:T(8,128)(2,1)S(1)} %bitcast.42, f32[64,128]{1,0:T(8,128)S(1)} %bitcast.49, bf16[128,2048]{1,0:T(8,128)(2,1)} %shard_map.119.refs_4_), custom_call_target="tpu_custom_call" | custom-call | tf_op jit(solution)/shard_map/pallas_call | solution.py:51
  58.2 0.8 copy-done.15
  59.1 1.5 %collective-permute-start.14 = (bf16[2048,128]{1,0:T(8,128)(2,1)}, bf16[2048,128]{1,0:T(8,128)(2,1)}, u32[]{:S(2)}, u32[]{:S(2)}) collective-permute-start(bf16[2048,128]{1,0:T(8,128)(2,1)} %get-tuple-element.47), channel_id=1, source_target_pairs={{0,24},{8,16},{16,8},{24,0},{1,25},{9,17},{17,9},{25,1},{2,26},{10... | collective-permute-start | bytes 1572872 | tf_op jit(solution)/shard_map/ppermute | solution.py:460
  60.5 1.5 %collective-permute-start.12 = (bf16[128,2048]{1,0:T(8,128)(2,1)}, bf16[128,2048]{1,0:T(8,128)(2,1)}, u32[]{:S(2)}, u32[]{:S(2)}) collective-permute-start(bf16[128,2048]{1,0:T(8,128)(2,1)} %shard_map.119.refs_4_), channel_id=1, source_target_pairs={{4,2},{5,3},{12,10},{13,11},{20,18},{21,19},{28,26},{29,27}} | collective-permute-start | bytes 1572872 | tf_op jit(solution)/shard_map/ppermute | solution.py:457
  62.0 0.2 collective-permute-start.17
  62.3 1.1 copy-done.16
  63.3 1.0 copy-done.19
  64.4 1.0 copy-done.23
  65.4 0.2 shard_map.121.refs_3_
  65.6 0.8 copy-done.17
  66.5 1.4 shard_map.122.refs_4_
  67.9 2.1 %shard_map.123.refs_4_.refs_10_ = f32[128,128]{1,0:T(8,128)S(1)} custom-call(bf16[128,4096]{1,0:T(8,128)(2,1)S(1)} %bitcast.31, bf16[128,4096]{1,0:T(8,128)(2,1)S(1)} %collective-permute-done.3.refs_1_, f32[64,128]{1,0:T(8,128)S(1)} %get-tuple-element.61.refs_2_, f32[8,128,128]{2,1,0:T(8,128)S(1)} %copy-done.3, bf16[128,2048]{1,0:T(8,128)(2,1)S(1)} %shard_map.122.refs_4_), custom_call_target="tpu_custom_call" | custom-call | tf_op jit(solution)/shard_map/pallas_call | solution.py:51
  70.0 4.6 %collective-permute-done.14.refs_5_.refs_4_ = bf16[2048,128]{1,0:T(8,128)(2,1)} collective-permute-done((bf16[2048,128]{1,0:T(8,128)(2,1)}, bf16[2048,128]{1,0:T(8,128)(2,1)}, u32[]{:S(2)}, u32[]{:S(2)}) %collective-permute-start.14) | collective-permute-done | bytes 524320 | tf_op jit(solution)/shard_map/ppermute | solution.py:460
  74.6 1.3 shard_map.124
  75.9 1.4 collective-permute-start.15
  77.3 26.3 %collective-permute-start.16 = (bf16[128,2048]{1,0:T(8,128)(2,1)S(1)}, bf16[128,2048]{1,0:T(8,128)(2,1)S(1)}, u32[]{:S(2)}, u32[]{:S(2)}) collective-permute-start(bf16[128,2048]{1,0:T(8,128)(2,1)S(1)} %shard_map.122.refs_4_), channel_id=1, source_target_pairs={{0,2},{1,3},{4,6},{5,7},{8,10},{9,11},{12,14},{13,15},{16,18},{17,... | collective-permute-start | bytes 1572872 | tf_op jit(solution)/shard_map/ppermute | solution.py:457
  103.7 9.6 %collective-permute-done.15.refs_2_ = bf16[128,2048]{1,0:T(8,128)(2,1)S(1)} collective-permute-done((bf16[128,2048]{1,0:T(8,128)(2,1)S(1)}, bf16[128,2048]{1,0:T(8,128)(2,1)S(1)}, u32[]{:S(2)}, u32[]{:S(2)}) %collective-permute-start.15) | collective-permute-done | bytes 524320 | tf_op jit(solution)/shard_map/ppermute | solution.py:457
  113.3 1.2 collective-permute-done.16.refs_4_
  114.5 1.3 shard_map.125.refs_2_
  115.9 2.6 %collective-permute-done.18.refs_3_ = bf16[128,4096]{1,0:T(8,128)(2,1)S(1)} collective-permute-done((bf16[128,4096]{1,0:T(8,128)(2,1)S(1)}, bf16[128,4096]{1,0:T(8,128)(2,1)S(1)}, u32[]{:S(2)}, u32[]{:S(2)}) %collective-permute-start.18) | collective-permute-done | bytes 1048608 | tf_op jit(solution)/shard_map/ppermute | solution.py:454
  118.6 3.5 %shard_map.126 = (bf16[128,4096]{1,0:T(8,128)(2,1)S(1)}, bf16[128,4096]{1,0:T(8,128)(2,1)S(1)}, bf16[128,128]{1,0:T(8,128)(2,1)S(1)}) custom-call(s32[1]{0:T(128)} %bitcast.5.refs_0_.refs_1_, bf16[128,4096]{1,0:T(8,128)(2,1)S(1)} %bitcast.32, bf16[128,4096]{1,0:T(8,128)(2,1)S(1)} %shard_map.125.refs_2_, ...), custom_call_target="tpu_custom_call" | custom-call | tf_op jit(solution)/shard_map/pallas_call | solution.py:51
  122.1 0.5 collective-permute-start.21
  122.6 1.5 %collective-permute-start.20 = (bf16[128,128]{1,0:T(8,128)(2,1)S(1)}, bf16[128,128]{1,0:T(8,128)(2,1)S(1)}, u32[]{:S(2)}, u32[]{:S(2)}) collective-permute-start(bf16[128,128]{1,0:T(8,128)(2,1)S(1)} %get-tuple-element.52.refs_5_), channel_id=1, source_target_pairs={{0,16},{8,24},{16,0},{24,8},{1,17},{9,25},{17,1},{25,9},{2,18},{10... | collective-permute-start | bytes 98312 | tf_op jit(solution)/shard_map/ppermute | solution.py:460
  124.2 1.5 %collective-permute-start.19 = (bf16[128,128]{1,0:T(8,128)(2,1)S(1)}, bf16[128,128]{1,0:T(8,128)(2,1)S(1)}, u32[]{:S(2)}, u32[]{:S(2)}) collective-permute-start(bf16[128,128]{1,0:T(8,128)(2,1)S(1)} %get-tuple-element.52.refs_5_), channel_id=1, source_target_pairs={{0,8},{8,0},{16,24},{24,16},{1,9},{9,1},{17,25},{25,17},{2,10},{10... | collective-permute-start | bytes 98312 | tf_op jit(solution)/shard_map/ppermute | solution.py:460
  125.7 1.2 shard_map.127
  126.9 0.2 copy-done.11
  127.0 0.4 fusion.1.refs_6_
  127.5 6.8 %shard_map.128.refs_9_ = bf16[128,4096]{1,0:T(8,128)(2,1)} custom-call(bf16[128,4096]{1,0:T(8,128)(2,1)S(1)} %bitcast.35, bf16[128,4096]{1,0:T(8,128)(2,1)S(1)} %collective-permute-done.3.refs_1_, bf16[128,4096]{1,0:T(8,128)(2,1)S(1)} %get-tuple-element.49.refs_2_, bf16[128,4096]{1,0:T(8,128)(2,1)S(1)} %get-tuple-element.50.refs_3_, ...), custom_call_target="tpu_custom_call" | custom-call | tf_op jit(solution)/shard_map/pallas_call | solution.py:51
  134.3 1.2 copy-done.12
  135.5 1.5 shard_map.129
  137.1 1.3 collective-permute-done.22.refs_2_
  138.4 2.6 %collective-permute-start.23 = (bf16[128,128]{1,0:T(8,128)(2,1)S(1)}, bf16[128,128]{1,0:T(8,128)(2,1)S(1)}, u32[]{:S(2)}, u32[]{:S(2)}) collective-permute-start(bf16[128,128]{1,0:T(8,128)(2,1)S(1)} %get-tuple-element.56), channel_id=1, source_target_pairs={{0,2},{1,3},{2,0},{3,1},{4,6},{5,7},{6,4},{7,5},{8,10},{9,11},{10,... | collective-permute-start | bytes 98312 | tf_op jit(solution)/shard_map/ppermute | solution.py:636
  141.0 2.4 %collective-permute-start.25 = (bf16[128,128]{1,0:T(8,128)(2,1)S(1)}, bf16[128,128]{1,0:T(8,128)(2,1)S(1)}, u32[]{:S(2)}, u32[]{:S(2)}) collective-permute-start(bf16[128,128]{1,0:T(8,128)(2,1)S(1)} %get-tuple-element.58), channel_id=1, source_target_pairs={{0,6},{1,7},{2,4},{3,5},{4,2},{5,3},{6,0},{7,1},{8,14},{9,15},{10,... | collective-permute-start | bytes 98312 | tf_op jit(solution)/shard_map/ppermute | solution.py:636
  143.4 1.4 fusion
  144.8 1.4 collective-permute-done.24
  146.3 0.6 collective-permute-done.25
  146.8 0.6 add_multiply_fusion
  (86 shorter events, 0.5 us)
Async XLA Ops:
  2.0 20.7 %copy-start.1 = (bf16[1,128,4096]{2,1,0:T(8,128)(2,1)S(1)}, bf16[1,128,4096]{2,1,0:T(8,128)(2,1)}, u32[]{:S(2)}) copy-start(bf16[1,128,4096]{2,1,0:T(8,128)(2,1)} %param.16) | copy-start | bytes 3145732
  2.0 20.7 %copy-start.26 = (bf16[1,128,128]{2,1,0:T(8,128)(2,1)S(1)}, bf16[1,128,128]{2,1,0:T(8,128)(2,1)}, u32[]{:S(2)}) copy-start(bf16[1,128,128]{2,1,0:T(8,128)(2,1)} %param.13) | copy-start | bytes 98308
  2.1 20.7 %copy-start.29 = (f32[1,64,128]{2,1,0:T(8,128)S(1)}, f32[1,64,128]{2,1,0:T(8,128)}, u32[]{:S(2)}) copy-start(f32[1,64,128]{2,1,0:T(8,128)} %param.15) | copy-start | bytes 98308
  3.7 9.2 %collective-permute-start = (f32[320,128]{1,0:T(8,128)S(1)}, f32[320,128]{1,0:T(8,128)S(1)}, u32[]{:S(2)}, u32[]{:S(2)}) collective-permute-start(f32[320,128]{1,0:T(8,128)S(1)} %pad_maximum_fusion), channel_id=1, source_target_pairs={{0,7},{1,6},{2,5},{3,4},{4,3},{5,2},{6,1},{7,0},{8,15},{9,14},{10,... | collective-permute-start | bytes 491528 | tf_op jit(solution)/shard_map/ppermute | solution.py:463
  8.3 9.4 %collective-permute-start.2 = (bf16[128,128]{1,0:T(8,128)(2,1)S(1)}, bf16[128,128]{1,0:T(8,128)(2,1)S(1)}, u32[]{:S(2)}, u32[]{:S(2)}) collective-permute-start(bf16[128,128]{1,0:T(8,128)(2,1)S(1)} %get-tuple-element.60.refs_4_), channel_id=1, source_target_pairs={{0,4},{1,5},{2,6},{3,7},{4,0},{5,1},{6,2},{7,3},{8,12},{9,13},{10,... | collective-permute-start | bytes 98312 | tf_op jit(solution)/shard_map/ppermute | solution.py:468
  8.3 9.4 %collective-permute-start.1 = (bf16[128,128]{1,0:T(8,128)(2,1)S(1)}, bf16[128,128]{1,0:T(8,128)(2,1)S(1)}, u32[]{:S(2)}, u32[]{:S(2)}) collective-permute-start(bf16[128,128]{1,0:T(8,128)(2,1)S(1)} %get-tuple-element.60.refs_4_), channel_id=1, source_target_pairs={{0,2},{1,3},{2,0},{3,1},{4,6},{5,7},{6,4},{7,5},{8,10},{9,11},{10,... | collective-permute-start | bytes 98312 | tf_op jit(solution)/shard_map/ppermute | solution.py:468
  17.6 11.2 %copy-start.34 = (f32[1,64,128]{2,1,0:T(8,128)S(1)}, f32[1,64,128]{2,1,0:T(8,128)}, u32[]{:S(2)}) copy-start(f32[1,64,128]{2,1,0:T(8,128)} %param.14) | copy-start | bytes 98308
  21.9 0.8 copy-start.27
  22.7 9.2 %copy-start.30 = (bf16[4,128,128]{2,1,0:T(8,128)(2,1)}, bf16[4,128,128]{2,1,0:T(8,128)(2,1)S(1)}, u32[]{:S(2)}) copy-start(bf16[4,128,128]{2,1,0:T(8,128)(2,1)S(1)} %get-tuple-element.41.refs_2_) | copy-start | bytes 393220
  22.7 6.2 %collective-permute-start.5 = (bf16[144,2048]{1,0:T(8,128)(2,1)}, bf16[144,2048]{1,0:T(8,128)(2,1)}, u32[]{:S(2)}, u32[]{:S(2)}) collective-permute-start(bf16[144,2048]{1,0:T(8,128)(2,1)} %get-tuple-element.35), channel_id=1, source_target_pairs={{0,1},{1,0},{2,3},{3,2},{4,5},{5,4},{6,7},{7,6},{8,9},{9,8},{10,11... | collective-permute-start | bytes 1769480 | tf_op jit(solution)/shard_map/ppermute | solution.py:454
  25.7 7.1 %collective-permute-start.4 = (bf16[144,2048]{1,0:T(8,128)(2,1)}, bf16[144,2048]{1,0:T(8,128)(2,1)S(1)}, u32[]{:S(2)}, u32[]{:S(2)}) collective-permute-start(bf16[144,2048]{1,0:T(8,128)(2,1)} %get-tuple-element.33), channel_id=1, source_target_pairs={{0,1},{1,0},{2,3},{3,2},{4,5},{5,4},{6,7},{7,6},{8,9},{9,8},{10,11... | collective-permute-start | bytes 1769480 | tf_op jit(solution)/shard_map/ppermute | solution.py:454
  26.2 14.1 %collective-permute-start.7 = (bf16[144,2048]{1,0:T(8,128)(2,1)}, bf16[144,2048]{1,0:T(8,128)(2,1)}, u32[]{:S(2)}, u32[]{:S(2)}) collective-permute-start(bf16[144,2048]{1,0:T(8,128)(2,1)} %get-tuple-element.32.refs_6_.refs_1_), channel_id=1, source_target_pairs={{0,1},{1,0},{2,3},{3,2},{4,5},{5,4},{6,7},{7,6},{8,9},{9,8},{10,11... | collective-permute-start | bytes 1769480 | tf_op jit(solution)/shard_map/ppermute | solution.py:454
  26.2 29.0 %collective-permute-start.3 = (bf16[128,4096]{1,0:T(8,128)(2,1)}, bf16[128,4096]{1,0:T(8,128)(2,1)S(1)}, u32[]{:S(2)}, u32[]{:S(2)}) collective-permute-start(bf16[128,4096]{1,0:T(8,128)(2,1)} %bitcast.1.refs_1_), channel_id=1, source_target_pairs={{0,7},{1,6},{2,5},{3,4},{4,3},{5,2},{6,1},{7,0},{8,15},{9,14},{10,... | collective-permute-start | bytes 3145736 | tf_op jit(solution)/shard_map/ppermute | solution.py:463
  28.8 6.3 %collective-permute-start.9 = (bf16[4,128,128]{2,1,0:T(8,128)(2,1)S(1)}, bf16[4,128,128]{2,1,0:T(8,128)(2,1)S(1)}, u32[]{:S(2)}, u32[]{:S(2)}) collective-permute-start(bf16[4,128,128]{2,1,0:T(8,128)(2,1)S(1)} %get-tuple-element.41.refs_2_), channel_id=1, source_target_pairs={{0,1},{1,0},{2,3},{3,2},{4,5},{5,4},{6,7},{7,6},{8,9},{9,8},{10,11... | collective-permute-start | bytes 393224 | tf_op jit(solution)/shard_map/ppermute | solution.py:454
  28.9 1.1 copy-start.28
  32.0 4.8 %copy-start.18 = (bf16[128,2048]{1,0:T(8,128)(2,1)}, bf16[128,2048]{1,0:T(8,128)(2,1)S(1)}, u32[]{:S(2)}) copy-start(bf16[128,2048]{1,0:T(8,128)(2,1)S(1)} %get-tuple-element.36.refs_3_.refs_1_) | copy-start | bytes 1572868
  32.0 9.8 %copy-start.2 = (f32[8,128,128]{2,1,0:T(8,128)}, f32[8,128,128]{2,1,0:T(8,128)S(1)}, u32[]{:S(2)}) copy-start(f32[8,128,128]{2,1,0:T(8,128)S(1)} %get-tuple-element.40.refs_3_.refs_5_) | copy-start | bytes 1572868
  32.0 3.8 %copy-start.31 = (bf16[4,128,128]{2,1,0:T(8,128)(2,1)S(1)}, bf16[4,128,128]{2,1,0:T(8,128)(2,1)}, u32[]{:S(2)}) copy-start(bf16[4,128,128]{2,1,0:T(8,128)(2,1)} %copy-done.30) | copy-start | bytes 393220
  32.0 4.7 %copy-start.10 = (bf16[1,128,4096]{2,1,0:T(8,128)(2,1)S(1)}, bf16[1,128,4096]{2,1,0:T(8,128)(2,1)}, u32[]{:S(2)}) copy-start(bf16[1,128,4096]{2,1,0:T(8,128)(2,1)} %param.9) | copy-start | bytes 3145732
  32.0 11.9 %collective-permute-start.8 = (bf16[128,2048]{1,0:T(8,128)(2,1)S(1)}, bf16[128,2048]{1,0:T(8,128)(2,1)S(1)}, u32[]{:S(2)}, u32[]{:S(2)}) collective-permute-start(bf16[128,2048]{1,0:T(8,128)(2,1)S(1)} %get-tuple-element.36.refs_3_.refs_1_), channel_id=1, source_target_pairs={{6,4},{7,5},{14,12},{15,13},{22,20},{23,21},{30,28},{31,29}} | collective-permute-start | bytes 1572872 | tf_op jit(solution)/shard_map/ppermute | solution.py:457
  32.8 2.3 %copy-start.13 = (bf16[144,2048]{1,0:T(8,128)(2,1)}, bf16[144,2048]{1,0:T(8,128)(2,1)S(1)}, u32[]{:S(2)}) copy-start(bf16[144,2048]{1,0:T(8,128)(2,1)S(1)} %collective-permute-done.4.refs_2_.refs_4_) | copy-start | bytes 1769476
  34.4 19.9 %copy-start.4 = (bf16[128,2048]{1,0:T(8,128)(2,1)}, bf16[128,2048]{1,0:T(8,128)(2,1)S(1)}, u32[]{:S(2)}) copy-start(bf16[128,2048]{1,0:T(8,128)(2,1)S(1)} %get-tuple-element.37.refs_4_.refs_0_) | copy-start | bytes 1572868
  34.4 9.5 %collective-permute-start.6 = (bf16[128,2048]{1,0:T(8,128)(2,1)S(1)}, bf16[128,2048]{1,0:T(8,128)(2,1)S(1)}, u32[]{:S(2)}, u32[]{:S(2)}) collective-permute-start(bf16[128,2048]{1,0:T(8,128)(2,1)S(1)} %get-tuple-element.37.refs_4_.refs_0_), channel_id=1, source_target_pairs={{6,4},{7,5},{14,12},{15,13},{22,20},{23,21},{30,28},{31,29}} | collective-permute-start | bytes 1572872 | tf_op jit(solution)/shard_map/ppermute | solution.py:457
  35.1 0.7 copy-start.32
  35.8 0.9 copy-start.33
  36.7 5.1 %copy-start = (bf16[1,128,4096]{2,1,0:T(8,128)(2,1)S(1)}, bf16[1,128,4096]{2,1,0:T(8,128)(2,1)}, u32[]{:S(2)}) copy-start(bf16[1,128,4096]{2,1,0:T(8,128)(2,1)} %param.12) | copy-start | bytes 3145732
  38.0 0.8 copy-start.20
  38.8 14.3 %collective-permute-start.10 = (bf16[2048,128]{1,0:T(8,128)(2,1)S(1)}, bf16[2048,128]{1,0:T(8,128)(2,1)S(1)}, u32[]{:S(2)}, u32[]{:S(2)}) collective-permute-start(bf16[2048,128]{1,0:T(8,128)(2,1)S(1)} %get-tuple-element.42), channel_id=1, source_target_pairs={{0,8},{8,0},{16,24},{24,16},{1,9},{9,1},{17,25},{25,17},{2,10},{10... | collective-permute-start | bytes 1572872 | tf_op jit(solution)/shard_map/ppermute | solution.py:460
  40.3 14.0 %collective-permute-start.11 = (bf16[2048,128]{1,0:T(8,128)(2,1)S(1)}, bf16[2048,128]{1,0:T(8,128)(2,1)S(1)}, u32[]{:S(2)}, u32[]{:S(2)}) collective-permute-start(bf16[2048,128]{1,0:T(8,128)(2,1)S(1)} %get-tuple-element.43), channel_id=1, source_target_pairs={{0,16},{8,24},{16,0},{24,8},{1,17},{9,25},{17,1},{25,9},{2,18},{10... | collective-permute-start | bytes 1572872 | tf_op jit(solution)/shard_map/ppermute | solution.py:460
  43.9 11.3 %copy-start.22 = (bf16[128,2048]{1,0:T(8,128)(2,1)}, bf16[128,2048]{1,0:T(8,128)(2,1)S(1)}, u32[]{:S(2)}) copy-start(bf16[128,2048]{1,0:T(8,128)(2,1)S(1)} %collective-permute-done.8.refs_5_.refs_3_) | copy-start | bytes 1572868
  43.9 11.3 %copy-start.24 = (bf16[128,2048]{1,0:T(8,128)(2,1)}, bf16[128,2048]{1,0:T(8,128)(2,1)S(1)}, u32[]{:S(2)}) copy-start(bf16[128,2048]{1,0:T(8,128)(2,1)S(1)} %collective-permute-done.6.refs_2_.refs_0_) | copy-start | bytes 1572868
  53.0 2.2 %copy-start.6 = (bf16[2048,128]{1,0:T(8,128)(2,1)}, bf16[2048,128]{1,0:T(8,128)(2,1)S(1)}, u32[]{:S(2)}) copy-start(bf16[2048,128]{1,0:T(8,128)(2,1)S(1)} %collective-permute-done.10.refs_6_.refs_2_) | copy-start | bytes 1572868
  54.2 1.0 copy-start.8
  58.2 0.8 copy-start.15
  59.1 6.6 %collective-permute-start.13 = (bf16[144,2048]{1,0:T(8,128)(2,1)}, bf16[144,2048]{1,0:T(8,128)(2,1)}, u32[]{:S(2)}, u32[]{:S(2)}) collective-permute-start(bf16[144,2048]{1,0:T(8,128)(2,1)} %get-tuple-element.45), channel_id=1, source_target_pairs={{0,1},{1,0},{2,3},{3,2},{4,5},{5,4},{6,7},{7,6},{8,9},{9,8},{10,11... | collective-permute-start | bytes 1769480 | tf_op jit(solution)/shard_map/ppermute | solution.py:454
  59.1 15.6 %collective-permute-start.14 = (bf16[2048,128]{1,0:T(8,128)(2,1)}, bf16[2048,128]{1,0:T(8,128)(2,1)}, u32[]{:S(2)}, u32[]{:S(2)}) collective-permute-start(bf16[2048,128]{1,0:T(8,128)(2,1)} %get-tuple-element.47), channel_id=1, source_target_pairs={{0,24},{8,16},{16,8},{24,0},{1,25},{9,17},{17,9},{25,1},{2,26},{10... | collective-permute-start | bytes 1572872 | tf_op jit(solution)/shard_map/ppermute | solution.py:460
  60.5 14.1 %collective-permute-start.12 = (bf16[128,2048]{1,0:T(8,128)(2,1)}, bf16[128,2048]{1,0:T(8,128)(2,1)}, u32[]{:S(2)}, u32[]{:S(2)}) collective-permute-start(bf16[128,2048]{1,0:T(8,128)(2,1)} %shard_map.119.refs_4_), channel_id=1, source_target_pairs={{4,2},{5,3},{12,10},{13,11},{20,18},{21,19},{28,26},{29,27}} | collective-permute-start | bytes 1572872 | tf_op jit(solution)/shard_map/ppermute | solution.py:457
  62.0 41.6 %collective-permute-start.17 = (bf16[144,2048]{1,0:T(8,128)(2,1)}, bf16[144,2048]{1,0:T(8,128)(2,1)S(1)}, u32[]{:S(2)}, u32[]{:S(2)}) collective-permute-start(bf16[144,2048]{1,0:T(8,128)(2,1)} %copy-done.15), channel_id=1, source_target_pairs={{0,1},{1,0},{2,3},{3,2},{4,5},{5,4},{6,7},{7,6},{8,9},{9,8},{10,11... | collective-permute-start | bytes 1769480 | tf_op jit(solution)/shard_map/ppermute | solution.py:454
  62.3 1.1 copy-start.16
  63.3 1.0 copy-start.19
  64.4 1.0 copy-start.23
  65.4 1.1 copy-start.17
  65.6 2.3 %copy-start.3 = (f32[8,128,128]{2,1,0:T(8,128)S(1)}, f32[8,128,128]{2,1,0:T(8,128)}, u32[]{:S(2)}) copy-start(f32[8,128,128]{2,1,0:T(8,128)} %copy-done.2) | copy-start | bytes 1572868
  67.9 6.7 %copy-start.5 = (bf16[128,2048]{1,0:T(8,128)(2,1)S(1)}, bf16[128,2048]{1,0:T(8,128)(2,1)}, u32[]{:S(2)}) copy-start(bf16[128,2048]{1,0:T(8,128)(2,1)} %copy-done.4) | copy-start | bytes 1572868
  67.9 6.7 %copy-start.25 = (bf16[128,2048]{1,0:T(8,128)(2,1)S(1)}, bf16[128,2048]{1,0:T(8,128)(2,1)}, u32[]{:S(2)}) copy-start(bf16[128,2048]{1,0:T(8,128)(2,1)} %copy-done.24) | copy-start | bytes 1572868
  75.9 42.7 %copy-start.14 = (bf16[144,2048]{1,0:T(8,128)(2,1)S(1)}, bf16[144,2048]{1,0:T(8,128)(2,1)}, u32[]{:S(2)}) copy-start(bf16[144,2048]{1,0:T(8,128)(2,1)} %copy-done.13) | copy-start | bytes 1769476
  75.9 37.4 %collective-permute-start.15 = (bf16[128,2048]{1,0:T(8,128)(2,1)S(1)}, bf16[128,2048]{1,0:T(8,128)(2,1)S(1)}, u32[]{:S(2)}, u32[]{:S(2)}) collective-permute-start(bf16[128,2048]{1,0:T(8,128)(2,1)S(1)} %shard_map.124), channel_id=1, source_target_pairs={{2,0},{3,1},{10,8},{11,9},{18,16},{19,17},{26,24},{27,25}} | collective-permute-start | bytes 1572872 | tf_op jit(solution)/shard_map/ppermute | solution.py:457
  77.3 37.2 %collective-permute-start.16 = (bf16[128,2048]{1,0:T(8,128)(2,1)S(1)}, bf16[128,2048]{1,0:T(8,128)(2,1)S(1)}, u32[]{:S(2)}, u32[]{:S(2)}) collective-permute-start(bf16[128,2048]{1,0:T(8,128)(2,1)S(1)} %shard_map.122.refs_4_), channel_id=1, source_target_pairs={{0,2},{1,3},{4,6},{5,7},{8,10},{9,11},{12,14},{13,15},{16,18},{17,... | collective-permute-start | bytes 1572872 | tf_op jit(solution)/shard_map/ppermute | solution.py:457
  115.8 2.7 %collective-permute-start.18 = (bf16[128,4096]{1,0:T(8,128)(2,1)S(1)}, bf16[128,4096]{1,0:T(8,128)(2,1)S(1)}, u32[]{:S(2)}, u32[]{:S(2)}) collective-permute-start(bf16[128,4096]{1,0:T(8,128)(2,1)S(1)} %shard_map.125.refs_2_), channel_id=1, source_target_pairs={{0,1},{1,0},{2,3},{3,2},{4,5},{5,4},{6,7},{7,6},{8,9},{9,8},{10,11... | collective-permute-start | bytes 3145736 | tf_op jit(solution)/shard_map/ppermute | solution.py:454
  118.6 7.1 %copy-start.7 = (bf16[2048,128]{1,0:T(8,128)(2,1)S(1)}, bf16[2048,128]{1,0:T(8,128)(2,1)}, u32[]{:S(2)}) copy-start(bf16[2048,128]{1,0:T(8,128)(2,1)} %copy-done.6) | copy-start | bytes 1572868
  118.6 7.1 %copy-start.9 = (bf16[2048,128]{1,0:T(8,128)(2,1)S(1)}, bf16[2048,128]{1,0:T(8,128)(2,1)}, u32[]{:S(2)}) copy-start(bf16[2048,128]{1,0:T(8,128)(2,1)} %copy-done.8) | copy-start | bytes 1572868
  118.6 7.1 %copy-start.21 = (bf16[2048,128]{1,0:T(8,128)(2,1)S(1)}, bf16[2048,128]{1,0:T(8,128)(2,1)}, u32[]{:S(2)}) copy-start(bf16[2048,128]{1,0:T(8,128)(2,1)} %copy-done.20) | copy-start | bytes 1572868
  122.1 12.2 %collective-permute-start.21 = (bf16[128,128]{1,0:T(8,128)(2,1)S(1)}, bf16[128,128]{1,0:T(8,128)(2,1)S(1)}, u32[]{:S(2)}, u32[]{:S(2)}) collective-permute-start(bf16[128,128]{1,0:T(8,128)(2,1)S(1)} %get-tuple-element.52.refs_5_), channel_id=1, source_target_pairs={{0,24},{8,16},{16,8},{24,0},{1,25},{9,17},{17,9},{25,1},{2,26},{10... | collective-permute-start | bytes 98312 | tf_op jit(solution)/shard_map/ppermute | solution.py:460
  122.6 11.7 %collective-permute-start.20 = (bf16[128,128]{1,0:T(8,128)(2,1)S(1)}, bf16[128,128]{1,0:T(8,128)(2,1)S(1)}, u32[]{:S(2)}, u32[]{:S(2)}) collective-permute-start(bf16[128,128]{1,0:T(8,128)(2,1)S(1)} %get-tuple-element.52.refs_5_), channel_id=1, source_target_pairs={{0,16},{8,24},{16,0},{24,8},{1,17},{9,25},{17,1},{25,9},{2,18},{10... | collective-permute-start | bytes 98312 | tf_op jit(solution)/shard_map/ppermute | solution.py:460
  124.2 10.1 %collective-permute-start.19 = (bf16[128,128]{1,0:T(8,128)(2,1)S(1)}, bf16[128,128]{1,0:T(8,128)(2,1)S(1)}, u32[]{:S(2)}, u32[]{:S(2)}) collective-permute-start(bf16[128,128]{1,0:T(8,128)(2,1)S(1)} %get-tuple-element.52.refs_5_), channel_id=1, source_target_pairs={{0,8},{8,0},{16,24},{24,16},{1,9},{9,1},{17,25},{25,17},{2,10},{10... | collective-permute-start | bytes 98312 | tf_op jit(solution)/shard_map/ppermute | solution.py:460
  125.7 1.4 copy-start.11
  134.3 1.2 copy-start.12
  137.0 1.4 collective-permute-start.22
  138.4 6.4 %collective-permute-start.23 = (bf16[128,128]{1,0:T(8,128)(2,1)S(1)}, bf16[128,128]{1,0:T(8,128)(2,1)S(1)}, u32[]{:S(2)}, u32[]{:S(2)}) collective-permute-start(bf16[128,128]{1,0:T(8,128)(2,1)S(1)} %get-tuple-element.56), channel_id=1, source_target_pairs={{0,2},{1,3},{2,0},{3,1},{4,6},{5,7},{6,4},{7,5},{8,10},{9,11},{10,... | collective-permute-start | bytes 98312 | tf_op jit(solution)/shard_map/ppermute | solution.py:636
  141.0 5.3 %collective-permute-start.24 = (bf16[128,128]{1,0:T(8,128)(2,1)S(1)}, bf16[128,128]{1,0:T(8,128)(2,1)S(1)}, u32[]{:S(2)}, u32[]{:S(2)}) collective-permute-start(bf16[128,128]{1,0:T(8,128)(2,1)S(1)} %get-tuple-element.57), channel_id=1, source_target_pairs={{0,4},{1,5},{2,6},{3,7},{4,0},{5,1},{6,2},{7,3},{8,12},{9,13},{10,... | collective-permute-start | bytes 98312 | tf_op jit(solution)/shard_map/ppermute | solution.py:636
  141.0 5.8 %collective-permute-start.25 = (bf16[128,128]{1,0:T(8,128)(2,1)S(1)}, bf16[128,128]{1,0:T(8,128)(2,1)S(1)}, u32[]{:S(2)}, u32[]{:S(2)}) collective-permute-start(bf16[128,128]{1,0:T(8,128)(2,1)S(1)} %get-tuple-element.58), channel_id=1, source_target_pairs={{0,6},{1,7},{2,4},{3,5},{4,2},{5,3},{6,0},{7,1},{8,14},{9,15},{10,... | collective-permute-start | bytes 98312 | tf_op jit(solution)/shard_map/ppermute | solution.py:636

commit v3 on v2

--- a/solution.py
+++ b/solution.py
@@ -15,7 +15,8 @@
 LOW = -1e30
 EXACT = lax.Precision.HIGHEST
 VMEM_BYTES = 14 * 1024 * 1024
-BEHIND = 5 * 10**9
+CUT = 1024
+PIECES = 2
 
 f32 = jnp.float32
 bf16 = jnp.bfloat16
@@ -54,9 +55,29 @@
         in_specs=specs + [anywhere] * len(after),
         out_specs=[vmem] * len(outs),
         compiler_params=pltpu.CompilerParams(vmem_limit_bytes=VMEM_BYTES),
-        cost_estimate=pl.CostEstimate(flops=flops, transcendentals=0, bytes_accessed=0),
+        cost_estimate=pl.CostEstimate(flops=flops, transcendentals=0, bytes_accessed=flops // 250),
     )(*ins, *after)
     return [list(got[o : o + no]) for _, _, _, o, no in calls]
+
+
+def run_on_half(body, side, shape, arrays, before, after=()):
+    vmem = pl.BlockSpec(memory_space=pltpu.VMEM)
+    anywhere = pl.BlockSpec(memory_space=pl.ANY)
+    rest = [*before, *after]
+
+    def kernel(*refs):
+        body(*refs[: len(arrays)], refs[-1])
+
+    return pl.pallas_call(
+        kernel,
+        grid=(1,),
+        out_shape=shape,
+        in_specs=[vmem] * len(arrays) + [anywhere] * len(rest),
+        out_specs=pl.BlockSpec((shape.shape[0], shape.shape[1] // 2), lambda i: (0, side)),
+        input_output_aliases={len(arrays): 0} if before else {},
+        compiler_params=pltpu.CompilerParams(vmem_limit_bytes=VMEM_BYTES),
+        cost_estimate=pl.CostEstimate(flops=0, transcendentals=0, bytes_accessed=0),
+    )(*arrays, *rest)
 
 
 def iotas(shape):
@@ -109,9 +130,20 @@
         cols_ref[g] = jnp.concatenate(part + [rest], axis=0).T
 
 
-def part_kernel(backward, core_ref, g_ref, read_ref, decay_ref, own_ref, send_ref):
+def columns(refs, at, count, value=None):
+    for ref in refs:
+        if at < ref.shape[1]:
+            if value is None:
+                return ref[:, at : at + count]
+            ref[:, at : at + count] = value
+            return None
+        at -= ref.shape[1]
+
+
+def part_kernel(backward, count, core_ref, *refs):
+    g_refs, (read_ref, decay_ref, own_ref, *send_refs) = refs[:count], refs[count:]
     heads, n = decay_ref.shape
-    width = g_ref.shape[1] // heads
+    width = sum(ref.shape[1] for ref in g_refs) // heads
     step = GROUP * width
     r, c = iotas((n, n))
     order = ((r + c == n - 1) if backward else (r == c)).astype(f32)
@@ -128,7 +160,8 @@
 
     def term_of(g):
         scale = spread(weight[g * GROUP : (g + 1) * GROUP], width)
-        scaled = (g_ref[:, g * step : (g + 1) * step].astype(f32) * scale).astype(bf16)
+        cotangent = columns(g_refs, g * step, step)
+        scaled = (cotangent.astype(f32) * scale).astype(bf16)
         term = jnp.dot(read_t, scaled, preferred_element_type=f32)
         last = scale[n - 1 :]
         high = last.astype(bf16).astype(f32)
@@ -139,19 +172,20 @@
         here = slice(g * step, (g + 1) * step)
         lower, upper = term_of(g), term_of(g + groups // 2)
         own_ref[:, here] = jnp.where(low, lower, upper).astype(bf16)
-        send_ref[:, here] = jnp.where(low, upper, lower).astype(bf16)
+        sent = jnp.where(low, upper, lower).astype(bf16)
+        columns(send_refs, g * step, step, sent)
 
 
 WIDE = 512
 
 
-def chip_terms(upward, core, own_ref, near_ref):
+def chip_terms(upward, core, own_ref, near_refs):
     state = own_ref.shape[0] - 16
     first = core == (0 if upward else 1)
     for c in range(own_ref.shape[1] // WIDE):
         here = slice(c * WIDE, (c + 1) * WIDE)
         own = own_ref[:, here].astype(f32)
-        other = near_ref[:, here].astype(f32)
+        other = columns(near_refs, c * WIDE, WIDE).astype(f32)
         own_term, other_term = own[:state], other[:state]
         own_decay = own[state : state + 1] + own[state + 1 : state + 2]
         other_decay = other[state : state + 1] + other[state + 1 : state + 2]
@@ -162,8 +196,9 @@
         yield here, term, own_decay * other_decay
 
 
-def chip_kernel(upward, core_ref, own_ref, near_ref, term_ref, decay_ref):
-    for here, term, decay in chip_terms(upward, core_ref[0], own_ref, near_ref):
+def chip_kernel(upward, core_ref, own_ref, *refs):
+    *near_refs, term_ref, decay_ref = refs
+    for here, term, decay in chip_terms(upward, core_ref[0], own_ref, near_refs):
         term_ref[:, here] = term.astype(bf16)
         decay_ref[:, here] = decay
 
@@ -194,9 +229,15 @@
         out_ref[:, here] = jnp.where(flag_ref[0] == 1, leaving, 0.0).astype(bf16)
 
 
-def left_kernel(core_ref, own_ref, near_ref, *refs):
-    *entering, out_ref = refs
-    for here, term, decay in chip_terms(True, core_ref[0], own_ref, near_ref):
+def left_kernel(count, core_ref, flag_ref, own_ref, *refs):
+    near_refs, early, refs = refs[:PIECES], refs[PIECES : PIECES + count], refs[PIECES + count :]
+    if early:
+        out_ref, middle_ref = refs
+        middle_kernel(flag_ref, *early, middle_ref)
+        entering = [middle_ref]
+    else:
+        *entering, out_ref = refs
+    for here, term, decay in chip_terms(True, core_ref[0], own_ref, near_refs):
         out_ref[:, here] = (term + decay * entered(entering, here)).astype(bf16)
 
 
@@ -210,43 +251,50 @@
         out_ref[:, there] = entered(lefts, here).astype(bf16)
 
 
-def mix_kernel(fwd, inner_ref, g_ref, row_ref, cols_ref, out_ref):
+def mix_kernel(fwd, count, *refs):
+    g_refs, (inner_ref, row_ref, cols_ref, out_ref) = refs[:count], refs[count:]
     heads, n = row_ref.shape
-    width = g_ref.shape[1] // heads
+    width = inner_ref.shape[1] // heads
     step = GROUP * width
     s, t = iotas((n, n))
     keep = (t >= s) if fwd else (t + s >= n - 1)
     low_half = t < width
-
-    def one(g, acc):
-        at = pl.multiple_of(g * step, step)
-        rows = row_ref[pl.ds(pl.multiple_of(g * GROUP, GROUP), GROUP)]
-        cols = cols_ref[g]
-        for pair in range(GROUP // 2):
-            here = pl.ds(at + pair * LANES, LANES)
-            inner = inner_ref[:, here].astype(f32)
-            halves = jnp.concatenate(
-                [jnp.where(low_half, inner, 0.0), jnp.where(low_half, 0.0, inner)], axis=0
-            ).astype(bf16)
-            dots = dot_nt(halves, g_ref[:, here])
-            for j in range(2):
-                h = 2 * pair + j
-                row = rows[h : h + 1]
-                if fwd:
-                    k = C_MIX_FWD * GROUP + h
-                    power = row - cols[:, k : k + 1]
-                else:
-                    k = C_MIX_BACK * GROUP + h
-                    power = cols[:, k : k + 1] - row
-                decay = jnp.exp2(jnp.where(keep, power, LOW))
-                acc = acc + decay * dots[j * n : (j + 1) * n]
-        return acc
-
-    out_ref[...] = lax.fori_loop(0, heads // GROUP, one, jnp.zeros((n, n), f32))
+    acc = jnp.zeros((n, n), f32)
+    first = 0
+    for g_ref in g_refs:
+        groups = g_ref.shape[1] // step
+
+        def one(g, acc, g_ref=g_ref, first=first):
+            at = pl.multiple_of(g * step, step)
+            base = pl.multiple_of((first + g) * step, step)
+            rows = row_ref[pl.ds(pl.multiple_of((first + g) * GROUP, GROUP), GROUP)]
+            cols = cols_ref[first + g]
+            for pair in range(GROUP // 2):
+                inner = inner_ref[:, pl.ds(base + pair * LANES, LANES)].astype(f32)
+                halves = jnp.concatenate(
+                    [jnp.where(low_half, inner, 0.0), jnp.where(low_half, 0.0, inner)], axis=0
+                ).astype(bf16)
+                dots = dot_nt(halves, g_ref[:, pl.ds(at + pair * LANES, LANES)])
+                for j in range(2):
+                    h = 2 * pair + j
+                    row = rows[h : h + 1]
+                    if fwd:
+                        k = C_MIX_FWD * GROUP + h
+                        power = row - cols[:, k : k + 1]
+                    else:
+                        k = C_MIX_BACK * GROUP + h
+                        power = cols[:, k : k + 1] - row
+                    decay = jnp.exp2(jnp.where(keep, power, LOW))
+                    acc = acc + decay * dots[j * n : (j + 1) * n]
+            return acc
+
+        acc = lax.fori_loop(0, groups, one, acc)
+        first += groups
+    out_ref[...] = acc
 
 
 def edge_terms(
-    upward, core, inner_ref, halves_ref, swapped_ref, near_ref, far_ref, edge, state_ref
+    upward, core, inner_ref, halves_ref, swapped_ref, near_refs, far_ref, edge, state_ref
 ):
     heads, n = edge.shape
     width = inner_ref.shape[1] // heads
@@ -263,7 +311,8 @@
         near = slice(at - base, at - base + step)
         mine = core == g // (groups // 2)
         whole = jnp.where(mine, halves_ref[:, there].astype(f32), swapped_ref[:, there].astype(f32))
-        other = jnp.where(mine, near_ref[:, near].astype(f32), far_ref[:, near].astype(f32))
+        other = columns(near_refs, at - base, step).astype(f32)
+        other = jnp.where(mine, other, far_ref[:, near].astype(f32))
         decay = other[rows : rows + 1] + other[rows + 1 : rows + 2]
         entering = jnp.where(first, whole, other[:rows] + decay * whole).astype(bf16)
         state_ref[:, here] = entering
@@ -277,25 +326,26 @@
     inner_ref,
     halves_ref,
     swapped_ref,
-    right_near_ref,
     right_far_ref,
-    left_near_ref,
     left_far_ref,
     rows_ref,
     mixf_ref,
     mixb_ref,
     read_ref,
     readr_ref,
-    right_ref,
-    left_ref,
-    out_ref,
+    *refs,
 ):
+    right_near_refs, left_near_refs = refs[:PIECES], refs[PIECES : 2 * PIECES]
+    right_ref, left_ref, out_ref = refs[2 * PIECES :]
     core = core_ref[0]
     shared = (inner_ref, halves_ref, swapped_ref)
     acc = jnp.dot(mixf_ref[...].astype(bf16), read_ref[...], preferred_element_type=f32)
     acc = acc + jnp.dot(mixb_ref[...].astype(bf16), readr_ref[...], preferred_element_type=f32)
-    acc = acc + edge_terms(False, core, *shared, right_near_ref, right_far_ref, rows_ref[FWD_EDGE], right_ref)
-    acc = acc + edge_terms(True, core, *shared, left_near_ref, left_far_ref, rows_ref[BACK_EDGE], left_ref)
+    right_edge, left_edge = rows_ref[FWD_EDGE], rows_ref[BACK_EDGE]
+    acc = acc + edge_terms(
+        False, core, *shared, right_near_refs, right_far_ref, right_edge, right_ref
+    )
+    acc = acc + edge_terms(True, core, *shared, left_near_refs, left_far_ref, left_edge, left_ref)
     out_ref[...] = acc.astype(bf16)
 
 
@@ -359,29 +409,32 @@
 
 
 def inner_kernel(
-    gf_ref, gb_ref, right_ref, left_ref, rows_ref, cols_ref, write_ref, read_ref, readr_ref, out_ref
+    side, gf_ref, right_ref, left_ref, rows_ref, cols_ref, write_ref, read_ref, readr_ref, *refs
 ):
+    *gb_refs, out_ref = refs
     _, heads, n = rows_ref.shape
     width = gf_ref.shape[1] // heads
     step = GROUP * width
+    half = heads // GROUP // 2
     write = write_ref[...]
     kernel_f = dot_nt(write, read_ref[...])
     kernel_b = dot_nt(write, readr_ref[...])
     s, t = iotas((n, n))
     low_half = t < width
 
-    def one(g, carry):
-        at = pl.multiple_of(g * step, step)
-        own = pl.ds(pl.multiple_of(g * GROUP, GROUP), GROUP)
+    for g in range(side * half, (side + 1) * half):
+        at = g * step
+        own = slice(g * GROUP, (g + 1) * GROUP)
+        whole = slice(at, at + step)
         cols = cols_ref[g]
         cum2 = rows_ref[CUM2, own]
         exclr2 = rows_ref[EXCLR2, own]
         step_e = spread(rows_ref[STEP, own], width)
         edges = spread(rows_ref[FWD_EDGE, own], width) * jnp.dot(
-            write, right_ref[:, pl.ds(at, step)], preferred_element_type=f32
+            write, right_ref[:, whole], preferred_element_type=f32
         )
         edges = edges + spread(rows_ref[BACK_EDGE, own], width) * jnp.dot(
-            write, left_ref[:, pl.ds(at, step)], preferred_element_type=f32
+            write, left_ref[:, whole], preferred_element_type=f32
         )
         for pair in range(GROUP // 2):
             mixes = []
@@ -394,17 +447,19 @@
                 mf = jnp.exp2(jnp.where(t >= s, pf, LOW)) * kernel_f
                 mb = jnp.exp2(jnp.where(t + s >= n - 1, pb, LOW)) * kernel_b
                 mixes.append(jnp.concatenate([mf, mb], axis=1))
-            here = pl.ds(at + pair * LANES, LANES)
-            both = jnp.concatenate([gf_ref[:, here], gb_ref[:, here]], axis=0)
+            here = at + pair * LANES
+            both = jnp.concatenate(
+                [gf_ref[:, here : here + LANES], columns(gb_refs, here, LANES)], axis=0
+            )
             got = jnp.dot(
                 jnp.concatenate(mixes, axis=0).astype(bf16), both, preferred_element_type=f32
             )
             intra = jnp.where(low_half, got[:n], got[n:])
             mine = slice(pair * LANES, (pair + 1) * LANES)
-            out_ref[:, here] = (step_e[:, mine] * intra + edges[:, mine]).astype(bf16)
-        return carry
-
-    lax.fori_loop(0, heads // GROUP, one, 0)
+            into = (g - side * half) * step + pair * LANES
+            out_ref[:, into : into + LANES] = (step_e[:, mine] * intra + edges[:, mine]).astype(
+                bf16
+            )
 
 
 def xor_pairs(count, k):
@@ -446,7 +501,8 @@
     half = width // 2
     share = hidden.shape[1] // dp_count
     part = functools.partial
-    part_shapes = [sds((state + 16, half), bf16)] * 2
+    part_shapes = [sds((state + 16, half), bf16)]
+    part_shapes += [sds((state + 16, half // PIECES), bf16)] * PIECES
     half_shape = sds((state, half), bf16)
     chip_shapes = [half_shape, sds((1, half), f32)]
 
@@ -467,22 +523,30 @@
     weights = [local] + [
         lax.ppermute(local, "ctx", xor_pairs(ctx_count, 2 * k)) for k in range(1, chips - 1)
     ]
-    gr_again, *_ = lax.optimization_barrier((gr, mirrored, *weights))
-    flipped = flip(gr_again)
-
-    def part_job(backward, *arrays):
-        return job(part(part_kernel, backward), part_shapes, *arrays, scalars=(core,))
+    cuts = [(0, CUT), (CUT, width)]
+    pieces = run(
+        *(job(part(cut_kernel, a), [sds((n, b - a), bf16)], gr) for a, b in cuts),
+        after=(mirrored, *weights),
+    )
+    flips = [flip(pieces[0][0])]
+    flips.append(flip(lax.optimization_barrier((pieces[1][0], flips[0]))[0]))
+
+    def part_job(backward, pieces, *arrays):
+        body = part(part_kernel, backward, len(pieces))
+        return job(body, part_shapes, *pieces, *arrays, scalars=(core,))
 
     def chip_job(upward, own, near):
-        return job(part(chip_kernel, upward), chip_shapes, own, near, scalars=(core,))
-
-    (early_own, send), (held,) = run(
-        part_job(True, gr, mirrored[:n], mirrored[n : n + heads]),
-        job(stack_kernel, [sds((chips, *local.shape), bf16)], *weights, mirrored[n + heads :]),
-    )
-    early_near = over_cores(send)
-    ((right_own, send),) = run(part_job(False, gf, read, decay))
-    right_near = over_cores(send)
+        return job(part(chip_kernel, upward), chip_shapes, own, *near, scalars=(core,))
+
+    ((held,),) = run(
+        job(stack_kernel, [sds((chips, *local.shape), bf16)], *weights, mirrored[n + heads :])
+    )
+    ((early_own, *sends),) = run(
+        part_job(True, [gr], mirrored[:n], mirrored[n : n + heads]), after=(held,)
+    )
+    early_near = [over_cores(send) for send in sends]
+    ((right_own, *sends),) = run(part_job(False, [gf], read, decay))
+    right_near = [over_cores(send) for send in sends]
     (early_term, early_decay), (read_r, rows, cols) = run(
         chip_job(False, early_own, early_near),
         job(
@@ -527,45 +591,55 @@
     )
     shared = [shares[0]] + [over_dp(shares[k], k) for k in range(1, dp_count)]
     ((mix_f,),) = run(
-        job(part(mix_kernel, True), [sds((n, n), f32)], inner, gf, rows[CUM2], cols),
+        job(part(mix_kernel, True, 1), [sds((n, n), f32)], gf, inner, rows[CUM2], cols),
         after=(right_term,),
     )
     right_far = over_cores(right_own)
     ((leaving,),) = run(
         job(onward_kernel, [half_shape], right_term, right_decay, *rights),
-        after=(mix_f, right_far, *earlies, *shared[1:3]),
+        after=(mix_f, right_far, *shared[1:4]),
     )
     rights.append(over_chips(leaving, (chips - 2, chips - 3)))
 
-    ((left_own, send),) = run(part_job(True, flipped, read, decay), after=(leaving,))
-    left_near = over_cores(send)
-    ((middle,),) = run(
-        job(
-            middle_kernel, [half_shape], early_term, early_decay, *earlies, scalars=(chip == span,)
-        ),
-        after=(left_own,),
-    )
-    lefts = [middle]
+    ((left_own, *sends),) = run(part_job(True, flips, read, decay), after=(leaving,))
+    left_near = [over_cores(send) for send in sends]
+    lefts = []
     for i in range(span - 1):
-        ((leaving,),) = run(
-            job(left_kernel, [half_shape], left_own, left_near, *lefts, scalars=(core,))
+        early = [] if i else [early_term, early_decay, *earlies]
+        shapes = [half_shape] * (1 if i else 2)
+        (leaving, *middle), = run(
+            job(
+                part(left_kernel, len(early)),
+                shapes,
+                left_own,
+                *left_near,
+                *early,
+                *lefts,
+                scalars=(core, chip == span),
+            )
         )
+        lefts += middle
         lefts.append(over_chips(leaving, (i, i + 1), (span + i, span + i + 1)))
-    ((mix_b,),) = run(
-        job(part(mix_kernel, False), [sds((n, n), f32)], inner, flipped, rows[EXCLR2], cols),
-        after=(leaving,),
-    )
     left_far = over_cores(left_own)
     for i in range(2, chips - 1):
         ((leaving,),) = run(
             job(onward_kernel, [half_shape], right_term, right_decay, *rights),
-            after=(mix_b, *shared[3:]) if i == 2 else (),
-            flops=BEHIND,
         )
         rights.append(over_chips(leaving, (chips - 1 - i, chips - 2 - i)))
+    ((mix_b,),) = run(
+        job(
+            part(mix_kernel, False, len(flips)),
+            [sds((n, n), f32)],
+            *flips,
+            inner,
+            rows[EXCLR2],
+            cols,
+        ),
+        after=(leaving,),
+    )
     ((halves,),) = run(
         job(part(halves_kernel, len(rights)), [sds((state, width), bf16)], *rights, *lefts),
-        after=(left_far,),
+        after=(left_far, *shared[4:]),
     )
     swapped = over_cores(halves)
 
@@ -576,19 +650,18 @@
             inner,
             halves,
             swapped,
-            right_near,
             right_far,
-            left_near,
             left_far,
             rows,
             mix_f,
             mix_b,
             read,
             read_r,
+            *right_near,
+            *left_near,
             scalars=(core,),
         )
     )
-    gb = flipped
 
     writes = [grad_write] + [over_dp(grad_write, k) for k in range(1, dp_count)]
     ((weight,),) = run(
@@ -597,21 +670,8 @@
     )
     weight = weight.reshape(-1, state)
     write = jnp.dot(hidden, weight, preferred_element_type=f32).astype(bf16)
-    ((grad_inner,),) = run(
-        job(
-            inner_kernel,
-            [sds((n, width), bf16)],
-            gf,
-            gb,
-            right_in,
-            left_in,
-            rows,
-            cols,
-            write,
-            read,
-            read_r,
-        )
-    )
+    inner_arrays = (gf, right_in, left_in, rows, cols, write, read, read_r, *flips)
+    half_inner = run_on_half(part(inner_kernel, 0), 0, sds((n, width), bf16), inner_arrays, ())
     piece = share // ctx_count
     ((keep, give),) = run(
         job(
@@ -621,7 +681,7 @@
             *writes,
             scalars=(core,),
         ),
-        after=(grad_inner,),
+        after=(half_inner,),
     )
     ((total, *dealt),) = run(
         job(
@@ -636,6 +696,9 @@
         total = total + lax.ppermute(dealt[k - 1], "ctx", xor_pairs(ctx_count, 2 * k)).astype(f32)
     grad_weight = total / (dp_count * ctx_count * n)
 
+    grad_inner = run_on_half(
+        part(inner_kernel, 1), 1, sds((n, width), bf16), inner_arrays, (half_inner,), tuple(dealt[:1])
+    )
     grad_hidden = dot_nt(grad_write, weight).astype(bf16)
     return grad_inner[None], grad_hidden[None], grad_weight
 

time: 148 us -> 126 us (0.85)
  starting transfers between devices: 53.1 us -> 32.2 us
  Pallas kernels: 37.3 us -> 32.3 us
  waiting for transfers between devices: 39.9 us -> 44.5 us
    ppermute x5, starting transfers between devices: 30.7 us -> 9.48 us  [over_chips(): return lax.ppermute(array, 'ctx', chip_pairs(moves))]
    pallas_call x19, Pallas kernels: 37.3 us -> 27 us  [run(): pl.pallas_call(kernel, out_shape=outs, in_specs=specs + [anywhere] * len(...]
    pallas_call x0 -> x2, Pallas kernels: none -> 5.36 us  [run_on_half(): pl.pallas_call(kernel, grid=(1,), out_shape=shape, in_specs=[vmem] * len(...]
    ppermute x6, waiting for transfers between devices: 15 us -> 19 us  [over_dp(): return lax.ppermute(array, 'dp', xor_pairs(dp_count, k))]
    ppermute x5, waiting for transfers between devices: 10.8 us -> 14.2 us  [over_chips(): return lax.ppermute(array, 'ctx', chip_pairs(moves))]
    ppermute x2, waiting for transfers between devices: 4.68 us -> 2.58 us  [shards(): lax.ppermute(local, 'ctx', xor_pairs(ctx_count, 2 * k))]
    ppermute x3, waiting for transfers between devices: 1.98 us -> 0.01 us  [shards(): lax.ppermute(dealt[k - 1], 'ctx', xor_pairs(ctx_count, 2 * k)).astype(f32)]
    ppermute x2 -> x3, starting transfers between devices: 7.15 us -> 8.8 us  [flip(): lax.ppermute(piece, 'ctx', [(i, ctx_count - 1 - i) for i in range(ctx_cou...]
  transfers between devices with their start and end apart: 26 -> 30, of which waited for: 11 -> 10; matrix products, arithmetic and copies ran while one was open for 1% -> 2% of each run, Pallas kernels for 16% -> 21%
where the time goes in v3:
time: 126 us; the launch traced here: 125 us
  waiting for transfers between devices  44.5 us (35%)
  Pallas kernels  32.3 us (26%)
  starting transfers between devices  32.2 us (26%)
  local copies, waits for them, and re-layouts  9.63 us (8%)
  other arithmetic  2.96 us (2%)
  matrix products  1.83 us (1%)
  between operations  1.73 us (1%)
    pallas_call x19, Pallas kernels, run(): pl.pallas_call(kernel, out_shape=outs, in_specs=specs + [anywhere] * len(...  27 us
    ppermute x6, waiting for transfers between devices, over_dp(): return lax.ppermute(array, 'dp', xor_pairs(dp_count, k))  19 us
    ppermute x5, waiting for transfers between devices, over_chips(): return lax.ppermute(array, 'ctx', chip_pairs(moves))  14.2 us
    ppermute x5, starting transfers between devices, over_chips(): return lax.ppermute(array, 'ctx', chip_pairs(moves))  9.48 us
    unnamed x80, local copies, waits for them, and re-layouts  9 us
    ppermute x3, starting transfers between devices, flip(): lax.ppermute(piece, 'ctx', [(i, ctx_count - 1 - i) for i in range(ctx_cou...  8.8 us
    ppermute x6, starting transfers between devices, over_dp(): return lax.ppermute(array, 'dp', xor_pairs(dp_count, k))  7.04 us
    pallas_call x2, Pallas kernels, run_on_half(): pl.pallas_call(kernel, grid=(1,), out_shape=shape, in_specs=[vmem] * len(...  5.36 us
  transfers between devices with their start and end apart: 30, of which 10 were waited for; matrix products, arithmetic and copies ran while one was open for 2% of the time, Pallas kernels for 21%

profile of v3, /device:TPU:0, one launch (start us, length us, event | category | flops | bytes accessed | tf_op | source)
XLA Modules:
  0.0 125.2 jit_solution(14083689733208246663)
XLA Ops:
  1.3 0.8 bitcast_convert_fusion
  2.0 0.8 fusion.3
  2.8 0.8 pad_maximum_fusion
  3.6 4.6 %collective-permute-start.2 = (f32[320,128]{1,0:T(8,128)S(1)}, f32[320,128]{1,0:T(8,128)S(1)}, u32[]{:S(2)}, u32[]{:S(2)}) collective-permute-start(f32[320,128]{1,0:T(8,128)S(1)} %pad_maximum_fusion), channel_id=1, source_target_pairs={{0,7},{1,6},{2,5},{3,4},{4,3},{5,2},{6,1},{7,0},{8,15},{9,14},{10,... | collective-permute-start | bytes 491528 | tf_op jit(solution)/shard_map/ppermute | solution.py:519
  8.1 1.2 collective-permute-start.3
  9.4 1.2 copy-done
  10.6 0.8 copy-done.24
  11.3 0.8 copy-done.32
  12.1 2.9 %shard_map.112 = (bf16[144,2048]{1,0:T(8,128)(2,1)}, bf16[144,1024]{1,0:T(8,128)(2,1)}, bf16[144,1024]{1,0:T(8,128)(2,1)}) custom-call(s32[1]{0:T(128)} %bitcast.1.refs_0_.refs_1_, bf16[128,4096]{1,0:T(8,128)(2,1)S(1)} %bitcast.30, bf16[128,128]{1,0:T(8,128)(2,1)S(1)} %bitcast.44, f32[64,128]{1,0:T(8,128)S(1)} %bitcast.52), custom_call_target="tpu_custom_call" | custom-call | tf_op jit(solution)/shard_map/pallas_call | solution.py:52
  15.0 2.6 %collective-permute-done.4.refs_2_.refs_5_ = bf16[128,128]{1,0:T(8,128)(2,1)S(1)} collective-permute-done((bf16[128,128]{1,0:T(8,128)(2,1)S(1)}, bf16[128,128]{1,0:T(8,128)(2,1)S(1)}, u32[]{:S(2)}, u32[]{:S(2)}) %collective-permute-start.4) | collective-permute-done | bytes 32800 | tf_op jit(solution)/shard_map/ppermute | solution.py:524
  17.5 0.9 shard_map.122
  18.5 2.2 %collective-permute-start.15 = (bf16[128,1024]{1,0:T(8,128)(2,1)S(1)}, bf16[128,1024]{1,0:T(8,128)(2,1)S(1)}, u32[]{:S(2)}, u32[]{:S(2)}) collective-permute-start(bf16[128,1024]{1,0:T(8,128)(2,1)S(1)} %get-tuple-element.51), channel_id=1, source_target_pairs={{0,7},{1,6},{2,5},{3,4},{4,3},{5,2},{6,1},{7,0},{8,15},{9,14},{10,... | collective-permute-start | bytes 786440 | tf_op jit(solution)/shard_map/ppermute | solution.py:519
  20.7 2.2 %shard_map.114 = (bf16[144,2048]{1,0:T(8,128)(2,1)S(1)}, bf16[144,1024]{1,0:T(8,128)(2,1)S(1)}, bf16[144,1024]{1,0:T(8,128)(2,1)S(1)}) custom-call(s32[1]{0:T(128)} %bitcast.1.refs_0_.refs_1_, bf16[128,4096]{1,0:T(8,128)(2,1)S(1)} %bitcast.39, f32[128,128]{1,0:T(8,128)S(1)} %get-tuple-element.76.refs_2_, f32[64,128]{1,0:T(8,128)S(1)} %slice.21.refs_3_, ...), custom_call_target="tpu_custom_call" | custom-call | tf_op jit(solution)/shard_map/pallas_call | solution.py:52
  22.9 0.5 collective-permute-start.5
  23.5 0.4 collective-permute-start
  23.9 4.9 %collective-permute-done.15.refs_1_.refs_0_.refs_8_ = bf16[128,1024]{1,0:T(8,128)(2,1)S(1)} collective-permute-done((bf16[128,1024]{1,0:T(8,128)(2,1)S(1)}, bf16[128,1024]{1,0:T(8,128)(2,1)S(1)}, u32[]{:S(2)}, u32[]{:S(2)}) %collective-permute-start.15) | collective-permute-done | bytes 262176 | tf_op jit(solution)/shard_map/ppermute | solution.py:519
  28.8 0.7 copy-done.15
  29.6 0.5 collective-permute-start.9
  30.1 2.1 %collective-permute-start.16 = (bf16[128,3072]{1,0:T(8,128)(2,1)}, bf16[128,3072]{1,0:T(8,128)(2,1)S(1)}, u32[]{:S(2)}, u32[]{:S(2)}) collective-permute-start(bf16[128,3072]{1,0:T(8,128)(2,1)} %get-tuple-element.53), channel_id=1, source_target_pairs={{0,7},{1,6},{2,5},{3,4},{4,3},{5,2},{6,1},{7,0},{8,15},{9,14},{10,... | collective-permute-start | bytes 2359304 | tf_op jit(solution)/shard_map/ppermute | solution.py:519
  32.2 1.2 shard_map.115
  33.4 0.6 copy-done.34
  34.1 1.6 %shard_map.116 = (bf16[128,2048]{1,0:T(8,128)(2,1)S(1)}, f32[1,2048]{1,0:T(1,128)S(1)}) custom-call(s32[1]{0:T(128)} %bitcast.1.refs_0_.refs_1_, bf16[144,2048]{1,0:T(8,128)(2,1)} %get-tuple-element.37.refs_7_.refs_1_, bf16[144,1024]{1,0:T(8,128)(2,1)S(1)} %collective-permute-done.refs_2_.refs_11_, ...), custom_call_target="tpu_custom_call" | custom-call | tf_op jit(solution)/shard_map/pallas_call | solution.py:52
  35.7 0.7 collective-permute-start.7
  36.4 0.6 copy-done.37
  37.1 0.9 copy-done.38
  38.0 0.4 shard_map.119
  38.5 0.8 copy-done.20
  39.3 1.5 %collective-permute-start.10 = (bf16[2048,128]{1,0:T(8,128)(2,1)S(1)}, bf16[2048,128]{1,0:T(8,128)(2,1)S(1)}, u32[]{:S(2)}, u32[]{:S(2)}) collective-permute-start(bf16[2048,128]{1,0:T(8,128)(2,1)S(1)} %get-tuple-element.48), channel_id=1, source_target_pairs={{0,8},{8,0},{16,24},{24,16},{1,9},{9,1},{17,25},{25,17},{2,10},{10... | collective-permute-start | bytes 1572872 | tf_op jit(solution)/shard_map/ppermute | solution.py:516
  40.8 1.5 %collective-permute-start.11 = (bf16[2048,128]{1,0:T(8,128)(2,1)S(1)}, bf16[2048,128]{1,0:T(8,128)(2,1)S(1)}, u32[]{:S(2)}, u32[]{:S(2)}) collective-permute-start(bf16[2048,128]{1,0:T(8,128)(2,1)S(1)} %get-tuple-element.49), channel_id=1, source_target_pairs={{0,16},{8,24},{16,0},{24,8},{1,17},{9,25},{17,1},{25,9},{2,18},{10... | collective-permute-start | bytes 1572872 | tf_op jit(solution)/shard_map/ppermute | solution.py:516
  42.3 0.5 collective-permute-start.12
  42.8 0.6 slice_bitcast_fusion
  43.4 1.5 %collective-permute-start.19 = (bf16[128,2048]{1,0:T(8,128)(2,1)}, bf16[128,2048]{1,0:T(8,128)(2,1)}, u32[]{:S(2)}, u32[]{:S(2)}) collective-permute-start(bf16[128,2048]{1,0:T(8,128)(2,1)} %get-tuple-element.43.refs_4_.refs_5_), channel_id=1, source_target_pairs={{6,4},{7,5},{14,12},{15,13},{22,20},{23,21},{30,28},{31,29}} | collective-permute-start | bytes 1572872 | tf_op jit(solution)/shard_map/ppermute | solution.py:513
  44.8 2.1 %shard_map.117.refs_3_.refs_7_ = f32[128,128]{1,0:T(8,128)S(1)} custom-call(bf16[128,4096]{1,0:T(8,128)(2,1)S(1)} %bitcast.31, bf16[128,4096]{1,0:T(8,128)(2,1)S(1)} %bitcast.34, f32[64,128]{1,0:T(8,128)S(1)} %get-tuple-element.74.refs_2_, f32[8,128,128]{2,1,0:T(8,128)S(1)} %get-tuple-element.47.refs_3_.refs_4_, ...), custom_call_target="tpu_custom_call" | custom-call | tf_op jit(solution)/shard_map/pallas_call | solution.py:52
  46.9 7.1 %collective-permute-done.10.refs_5_.refs_2_ = bf16[2048,128]{1,0:T(8,128)(2,1)S(1)} collective-permute-done((bf16[2048,128]{1,0:T(8,128)(2,1)S(1)}, bf16[2048,128]{1,0:T(8,128)(2,1)S(1)}, u32[]{:S(2)}, u32[]{:S(2)}) %collective-permute-start.10) | collective-permute-done | bytes 524320 | tf_op jit(solution)/shard_map/ppermute | solution.py:516
  54.0 12.0 %collective-permute-done.11.refs_6_.refs_3_ = bf16[2048,128]{1,0:T(8,128)(2,1)S(1)} collective-permute-done((bf16[2048,128]{1,0:T(8,128)(2,1)S(1)}, bf16[2048,128]{1,0:T(8,128)(2,1)S(1)}, u32[]{:S(2)}, u32[]{:S(2)}) %collective-permute-start.11) | collective-permute-done | bytes 524320 | tf_op jit(solution)/shard_map/ppermute | solution.py:516
  66.0 1.0 shard_map.120.refs_5_
  67.1 1.5 %collective-permute-start.13 = (bf16[128,2048]{1,0:T(8,128)(2,1)}, bf16[128,2048]{1,0:T(8,128)(2,1)}, u32[]{:S(2)}, u32[]{:S(2)}) collective-permute-start(bf16[128,2048]{1,0:T(8,128)(2,1)} %shard_map.120.refs_5_), channel_id=1, source_target_pairs={{4,2},{5,3},{12,10},{13,11},{20,18},{21,19},{28,26},{29,27}} | collective-permute-start | bytes 1572872 | tf_op jit(solution)/shard_map/ppermute | solution.py:513
  68.6 3.1 %shard_map.123 = (bf16[144,2048]{1,0:T(8,128)(2,1)}, bf16[144,1024]{1,0:T(8,128)(2,1)}, bf16[144,1024]{1,0:T(8,128)(2,1)}) custom-call(s32[1]{0:T(128)} %bitcast.1.refs_0_.refs_1_, bf16[128,1024]{1,0:T(8,128)(2,1)S(1)} %copy-done.16, bf16[128,3072]{1,0:T(8,128)(2,1)S(1)} %collective-permute-done.16.refs_2_.refs_1_.refs_9_, bf16[128,128]{1,0:T(8,128)(2,1)S(1)} %bitcast.46, ...), custom_call_target="tpu_custom_call" | custom-call | tf_op jit(solution)/shard_map/pallas_call | solution.py:52
  71.7 0.5 collective-permute-start.18
  72.2 1.4 %collective-permute-done.17.refs_3_.refs_13_ = bf16[144,1024]{1,0:T(8,128)(2,1)} collective-permute-done((bf16[144,1024]{1,0:T(8,128)(2,1)}, bf16[144,1024]{1,0:T(8,128)(2,1)}, u32[]{:S(2)}, u32[]{:S(2)}) %collective-permute-start.17) | collective-permute-done | bytes 294944 | tf_op jit(solution)/shard_map/ppermute | solution.py:510
  73.6 0.4 collective-permute-done.18.refs_4_.refs_14_
  74.0 2.5 %shard_map.124 = (bf16[128,2048]{1,0:T(8,128)(2,1)S(1)}, bf16[128,2048]{1,0:T(8,128)(2,1)S(1)}) custom-call(s32[1]{0:T(128)} %bitcast.1.refs_0_.refs_1_, s32[1]{0:T(128)} %bitcast.13.refs_1_, bf16[144,2048]{1,0:T(8,128)(2,1)} %get-tuple-element.54.refs_2_, bf16[144,1024]{1,0:T(8,128)(2,1)} %collective-permute-done.17.refs_3_.refs_13_, ...), custom_call_target="tpu_custom_call" | custom-call | tf_op jit(solution)/shard_map/pallas_call | solution.py:52
  76.5 4.4 %collective-permute-start.20 = (bf16[128,2048]{1,0:T(8,128)(2,1)S(1)}, bf16[128,2048]{1,0:T(8,128)(2,1)S(1)}, u32[]{:S(2)}, u32[]{:S(2)}) collective-permute-start(bf16[128,2048]{1,0:T(8,128)(2,1)S(1)} %get-tuple-element.59), channel_id=1, source_target_pairs={{0,2},{1,3},{4,6},{5,7},{8,10},{9,11},{12,14},{13,15},{16,18},{17,... | collective-permute-start | bytes 1572872 | tf_op jit(solution)/shard_map/ppermute | solution.py:513
  81.0 1.3 %shard_map.121.refs_5_ = bf16[128,2048]{1,0:T(8,128)(2,1)S(1)} custom-call(bf16[128,2048]{1,0:T(8,128)(2,1)S(1)} %copy-done.6, f32[1,2048]{1,0:T(1,128)S(1)} %get-tuple-element.45.refs_1_, bf16[128,2048]{1,0:T(8,128)(2,1)S(1)} %copy-done.14, bf16[128,2048]{1,0:T(8,128)(2,1)} %collective-permute-done.13.refs_3_.refs_1_), custom_call_target="tpu_custom_call" | custom-call | tf_op jit(solution)/shard_map/pallas_call | solution.py:52
  82.2 1.5 %collective-permute-start.14 = (bf16[128,2048]{1,0:T(8,128)(2,1)S(1)}, bf16[128,2048]{1,0:T(8,128)(2,1)S(1)}, u32[]{:S(2)}, u32[]{:S(2)}) collective-permute-start(bf16[128,2048]{1,0:T(8,128)(2,1)S(1)} %shard_map.121.refs_5_), channel_id=1, source_target_pairs={{2,0},{3,1},{10,8},{11,9},{18,16},{19,17},{26,24},{27,25}} | collective-permute-start | bytes 1572872 | tf_op jit(solution)/shard_map/ppermute | solution.py:513
  83.7 8.6 %collective-permute-done.20.refs_4_ = bf16[128,2048]{1,0:T(8,128)(2,1)S(1)} collective-permute-done((bf16[128,2048]{1,0:T(8,128)(2,1)S(1)}, bf16[128,2048]{1,0:T(8,128)(2,1)S(1)}, u32[]{:S(2)}, u32[]{:S(2)}) %collective-permute-start.20) | collective-permute-done | bytes 524320 | tf_op jit(solution)/shard_map/ppermute | solution.py:513
  92.4 5.5 %collective-permute-done.14.refs_2_ = bf16[128,2048]{1,0:T(8,128)(2,1)S(1)} collective-permute-done((bf16[128,2048]{1,0:T(8,128)(2,1)S(1)}, bf16[128,2048]{1,0:T(8,128)(2,1)S(1)}, u32[]{:S(2)}, u32[]{:S(2)}) %collective-permute-start.14) | collective-permute-done | bytes 524320 | tf_op jit(solution)/shard_map/ppermute | solution.py:513
  97.9 1.4 %shard_map.125.refs_2_ = bf16[128,4096]{1,0:T(8,128)(2,1)S(1)} custom-call(bf16[128,2048]{1,0:T(8,128)(2,1)S(1)} %copy-done.14, bf16[128,2048]{1,0:T(8,128)(2,1)} %collective-permute-done.13.refs_3_.refs_1_, bf16[128,2048]{1,0:T(8,128)(2,1)S(1)} %collective-permute-done.14.refs_2_, bf16[128,2048]{1,0:T(8,128)(2,1)S(1)} %get-tuple-element.58.refs_3_, ...), custom_call_target="tpu_custom_call" | custom-call | tf_op jit(solution)/shard_map/pallas_call | solution.py:52
  99.4 2.0 %shard_map.126.refs_8_ = f32[128,128]{1,0:T(8,128)S(1)} custom-call(bf16[128,1024]{1,0:T(8,128)(2,1)S(1)} %copy-done.17, bf16[128,3072]{1,0:T(8,128)(2,1)S(1)} %collective-permute-done.16.refs_2_.refs_1_.refs_9_, bf16[128,4096]{1,0:T(8,128)(2,1)S(1)} %bitcast.35, f32[64,128]{1,0:T(8,128)S(1)} %copy-done.36, ...), custom_call_target="tpu_custom_call" | custom-call | tf_op jit(solution)/shard_map/pallas_call | solution.py:52
  101.5 0.5 collective-permute-done.22.refs_3_
  102.1 3.8 %shard_map.127 = (bf16[128,4096]{1,0:T(8,128)(2,1)S(1)}, bf16[128,4096]{1,0:T(8,128)(2,1)S(1)}, bf16[128,128]{1,0:T(8,128)(2,1)S(1)}) custom-call(s32[1]{0:T(128)} %bitcast.1.refs_0_.refs_1_, bf16[128,4096]{1,0:T(8,128)(2,1)S(1)} %bitcast.36, bf16[128,4096]{1,0:T(8,128)(2,1)S(1)} %shard_map.125.refs_2_, ...), custom_call_target="tpu_custom_call" | custom-call | tf_op jit(solution)/shard_map/pallas_call | solution.py:52
  105.9 1.5 %collective-permute-start.25 = (bf16[128,128]{1,0:T(8,128)(2,1)S(1)}, bf16[128,128]{1,0:T(8,128)(2,1)S(1)}, u32[]{:S(2)}, u32[]{:S(2)}) collective-permute-start(bf16[128,128]{1,0:T(8,128)(2,1)S(1)} %get-tuple-element.64.refs_5_), channel_id=1, source_target_pairs={{0,24},{8,16},{16,8},{24,0},{1,25},{9,17},{17,9},{25,1},{2,26},{10... | collective-permute-start | bytes 98312 | tf_op jit(solution)/shard_map/ppermute | solution.py:516
  107.3 1.9 %collective-permute-start.24 = (bf16[128,128]{1,0:T(8,128)(2,1)S(1)}, bf16[128,128]{1,0:T(8,128)(2,1)S(1)}, u32[]{:S(2)}, u32[]{:S(2)}) collective-permute-start(bf16[128,128]{1,0:T(8,128)(2,1)S(1)} %get-tuple-element.64.refs_5_), channel_id=1, source_target_pairs={{0,16},{8,24},{16,0},{24,8},{1,17},{9,25},{17,1},{25,9},{2,18},{10... | collective-permute-start | bytes 98312 | tf_op jit(solution)/shard_map/ppermute | solution.py:516
  109.5 1.1 copy-done.19
  110.7 0.4 fusion.1.refs_5_
  111.1 2.7 %shard_map.129.refs_9_.refs_10_ = bf16[128,4096]{1,0:T(8,128)(2,1)} custom-call(bf16[128,4096]{1,0:T(8,128)(2,1)S(1)} %bitcast.32, bf16[128,4096]{1,0:T(8,128)(2,1)S(1)} %get-tuple-element.61.refs_1_, bf16[128,4096]{1,0:T(8,128)(2,1)S(1)} %get-tuple-element.62.refs_2_, f32[5,64,128]{2,1,0:T(8,128)S(1)} %copy-done.23, ...), custom_call_target="tpu_custom_call" | custom-call | tf_op jit(solution)/shard_map/pallas_call | solution.py:71
  113.8 1.2 copy-done.4
  115.0 0.4 shard_map.130
  115.5 1.3 %collective-permute-done.26.refs_2_ = bf16[4,128,128]{2,1,0:T(8,128)(2,1)S(1)} collective-permute-done((bf16[4,128,128]{2,1,0:T(8,128)(2,1)S(1)}, bf16[4,128,128]{2,1,0:T(8,128)(2,1)S(1)}, u32[]{:S(2)}, u32[]{:S(2)}) %collective-permute-start.26) | collective-permute-done | bytes 131104 | tf_op jit(solution)/shard_map/ppermute | solution.py:510
  117.0 1.9 %collective-permute-start.29 = (bf16[128,128]{1,0:T(8,128)(2,1)S(1)}, bf16[128,128]{1,0:T(8,128)(2,1)S(1)}, u32[]{:S(2)}, u32[]{:S(2)}) collective-permute-start(bf16[128,128]{1,0:T(8,128)(2,1)S(1)} %get-tuple-element.70), channel_id=1, source_target_pairs={{0,6},{1,7},{2,4},{3,5},{4,2},{5,3},{6,0},{7,1},{8,14},{9,15},{10,... | collective-permute-start | bytes 98312 | tf_op jit(solution)/shard_map/ppermute | solution.py:696
  118.9 1.6 %collective-permute-start.27 = (bf16[128,128]{1,0:T(8,128)(2,1)S(1)}, bf16[128,128]{1,0:T(8,128)(2,1)S(1)}, u32[]{:S(2)}, u32[]{:S(2)}) collective-permute-start(bf16[128,128]{1,0:T(8,128)(2,1)S(1)} %get-tuple-element.67.refs_11_), channel_id=1, source_target_pairs={{0,2},{1,3},{2,0},{3,1},{4,6},{5,7},{6,4},{7,5},{8,10},{9,11},{10,... | collective-permute-start | bytes 98312 | tf_op jit(solution)/shard_map/ppermute | solution.py:696
  120.5 1.4 %fusion = bf16[1,128,4096]{2,1,0:T(8,128)(2,1)} fusion(bf16[128,128]{1,0:T(8,128)(2,1)S(1)} %get-tuple-element.64.refs_5_, bf16[4096,128]{1,0:T(8,128)(2,1)S(1)} %bitcast.42), kind=kOutput, calls=%fused_computation.1 | convolution fusion | flops 134742016 | bytes 2129920 | tf_op jit(solution)/shard_map/dot_general | solution.py:88
  121.9 2.7 %shard_map.132 = bf16[128,4096]{1,0:T(8,128)(2,1)} custom-call(bf16[128,4096]{1,0:T(8,128)(2,1)S(1)} %bitcast.33, bf16[128,4096]{1,0:T(8,128)(2,1)S(1)} %get-tuple-element.61.refs_1_, bf16[128,4096]{1,0:T(8,128)(2,1)S(1)} %get-tuple-element.62.refs_2_, f32[5,64,128]{2,1,0:T(8,128)S(1)} %copy-done.23, ...), custom_call_target="tpu_custom_call", output_to_operand_aliasing={{}: (10, {})} | custom-call | tf_op jit(solution)/shard_map/pallas_call | solution.py:71
  124.5 0.7 add_multiply_fusion
  (106 shorter events, 1.1 us)
Async XLA Ops:
  3.6 13.9 %collective-permute-start.2 = (f32[320,128]{1,0:T(8,128)S(1)}, f32[320,128]{1,0:T(8,128)S(1)}, u32[]{:S(2)}, u32[]{:S(2)}) collective-permute-start(f32[320,128]{1,0:T(8,128)S(1)} %pad_maximum_fusion), channel_id=1, source_target_pairs={{0,7},{1,6},{2,5},{3,4},{4,3},{5,2},{6,1},{7,0},{8,15},{9,14},{10,... | collective-permute-start | bytes 491528 | tf_op jit(solution)/shard_map/ppermute | solution.py:519
  8.1 9.4 %collective-permute-start.4 = (bf16[128,128]{1,0:T(8,128)(2,1)S(1)}, bf16[128,128]{1,0:T(8,128)(2,1)S(1)}, u32[]{:S(2)}, u32[]{:S(2)}) collective-permute-start(bf16[128,128]{1,0:T(8,128)(2,1)S(1)} %get-tuple-element.72.refs_0_.refs_3_), channel_id=1, source_target_pairs={{0,4},{1,5},{2,6},{3,7},{4,0},{5,1},{6,2},{7,3},{8,12},{9,13},{10,... | collective-permute-start | bytes 98312 | tf_op jit(solution)/shard_map/ppermute | solution.py:524
  8.1 9.4 %collective-permute-start.3 = (bf16[128,128]{1,0:T(8,128)(2,1)S(1)}, bf16[128,128]{1,0:T(8,128)(2,1)S(1)}, u32[]{:S(2)}, u32[]{:S(2)}) collective-permute-start(bf16[128,128]{1,0:T(8,128)(2,1)S(1)} %get-tuple-element.72.refs_0_.refs_3_), channel_id=1, source_target_pairs={{0,2},{1,3},{2,0},{3,1},{4,6},{5,7},{6,4},{7,5},{8,10},{9,11},{10,... | collective-permute-start | bytes 98312 | tf_op jit(solution)/shard_map/ppermute | solution.py:524
  9.3 1.2 copy-start
  12.1 5.4 %copy-start.3 = (bf16[1,128,4096]{2,1,0:T(8,128)(2,1)S(1)}, bf16[1,128,4096]{2,1,0:T(8,128)(2,1)}, u32[]{:S(2)}) copy-start(bf16[1,128,4096]{2,1,0:T(8,128)(2,1)} %param.17) | copy-start | bytes 3145732
  15.0 27.3 %collective-permute-start.8 = (bf16[144,2048]{1,0:T(8,128)(2,1)}, bf16[144,2048]{1,0:T(8,128)(2,1)}, u32[]{:S(2)}, u32[]{:S(2)}) collective-permute-start(bf16[144,2048]{1,0:T(8,128)(2,1)} %get-tuple-element.37.refs_7_.refs_1_), channel_id=1, source_target_pairs={{0,1},{1,0},{2,3},{3,2},{4,5},{5,4},{6,7},{7,6},{8,9},{9,8},{10,11... | collective-permute-start | bytes 1769480 | tf_op jit(solution)/shard_map/ppermute | solution.py:510
  18.5 13.7 %copy-start.25 = (bf16[1,128,128]{2,1,0:T(8,128)(2,1)S(1)}, bf16[1,128,128]{2,1,0:T(8,128)(2,1)}, u32[]{:S(2)}) copy-start(bf16[1,128,128]{2,1,0:T(8,128)(2,1)} %param.13) | copy-start | bytes 98308
  18.5 13.7 %copy-start.33 = (f32[1,64,128]{2,1,0:T(8,128)S(1)}, f32[1,64,128]{2,1,0:T(8,128)}, u32[]{:S(2)}) copy-start(f32[1,64,128]{2,1,0:T(8,128)} %param.15) | copy-start | bytes 98308
  18.5 13.7 %copy-start.39 = (f32[1,64,128]{2,1,0:T(8,128)S(1)}, f32[1,64,128]{2,1,0:T(8,128)}, u32[]{:S(2)}) copy-start(f32[1,64,128]{2,1,0:T(8,128)} %param.14) | copy-start | bytes 98308
  18.5 10.3 %collective-permute-start.15 = (bf16[128,1024]{1,0:T(8,128)(2,1)S(1)}, bf16[128,1024]{1,0:T(8,128)(2,1)S(1)}, u32[]{:S(2)}, u32[]{:S(2)}) collective-permute-start(bf16[128,1024]{1,0:T(8,128)(2,1)S(1)} %get-tuple-element.51), channel_id=1, source_target_pairs={{0,7},{1,6},{2,5},{3,4},{4,3},{5,2},{6,1},{7,0},{8,15},{9,14},{10,... | collective-permute-start | bytes 786440 | tf_op jit(solution)/shard_map/ppermute | solution.py:519
  20.7 12.7 %copy-start.30 = (bf16[4,128,128]{2,1,0:T(8,128)(2,1)}, bf16[4,128,128]{2,1,0:T(8,128)(2,1)S(1)}, u32[]{:S(2)}) copy-start(bf16[4,128,128]{2,1,0:T(8,128)(2,1)S(1)} %shard_map.113.refs_4_.refs_2_) | copy-start | bytes 393220
  22.9 6.7 %collective-permute-start.5 = (bf16[144,1024]{1,0:T(8,128)(2,1)S(1)}, bf16[144,1024]{1,0:T(8,128)(2,1)S(1)}, u32[]{:S(2)}, u32[]{:S(2)}) collective-permute-start(bf16[144,1024]{1,0:T(8,128)(2,1)S(1)} %get-tuple-element.41), channel_id=1, source_target_pairs={{0,1},{1,0},{2,3},{3,2},{4,5},{5,4},{6,7},{7,6},{8,9},{9,8},{10,11... | collective-permute-start | bytes 884744 | tf_op jit(solution)/shard_map/ppermute | solution.py:510
  23.4 6.7 %collective-permute-start.6 = (bf16[144,1024]{1,0:T(8,128)(2,1)S(1)}, bf16[144,1024]{1,0:T(8,128)(2,1)S(1)}, u32[]{:S(2)}, u32[]{:S(2)}) collective-permute-start(bf16[144,1024]{1,0:T(8,128)(2,1)S(1)} %get-tuple-element.42), channel_id=1, source_target_pairs={{0,1},{1,0},{2,3},{3,2},{4,5},{5,4},{6,7},{7,6},{8,9},{9,8},{10,11... | collective-permute-start | bytes 884744 | tf_op jit(solution)/shard_map/ppermute | solution.py:510
  23.5 10.6 %collective-permute-start = (bf16[144,1024]{1,0:T(8,128)(2,1)}, bf16[144,1024]{1,0:T(8,128)(2,1)S(1)}, u32[]{:S(2)}, u32[]{:S(2)}) collective-permute-start(bf16[144,1024]{1,0:T(8,128)(2,1)} %get-tuple-element.38), channel_id=1, source_target_pairs={{0,1},{1,0},{2,3},{3,2},{4,5},{5,4},{6,7},{7,6},{8,9},{9,8},{10,11... | collective-permute-start | bytes 884744 | tf_op jit(solution)/shard_map/ppermute | solution.py:510
  29.6 4.5 %collective-permute-start.1 = (bf16[144,1024]{1,0:T(8,128)(2,1)}, bf16[144,1024]{1,0:T(8,128)(2,1)S(1)}, u32[]{:S(2)}, u32[]{:S(2)}) collective-permute-start(bf16[144,1024]{1,0:T(8,128)(2,1)} %get-tuple-element.39), channel_id=1, source_target_pairs={{0,1},{1,0},{2,3},{3,2},{4,5},{5,4},{6,7},{7,6},{8,9},{9,8},{10,11... | collective-permute-start | bytes 884744 | tf_op jit(solution)/shard_map/ppermute | solution.py:510
  29.6 6.8 %collective-permute-start.9 = (bf16[4,128,128]{2,1,0:T(8,128)(2,1)S(1)}, bf16[4,128,128]{2,1,0:T(8,128)(2,1)S(1)}, u32[]{:S(2)}, u32[]{:S(2)}) collective-permute-start(bf16[4,128,128]{2,1,0:T(8,128)(2,1)S(1)} %shard_map.113.refs_4_.refs_2_), channel_id=1, source_target_pairs={{0,1},{1,0},{2,3},{3,2},{4,5},{5,4},{6,7},{7,6},{8,9},{9,8},{10,11... | collective-permute-start | bytes 393224 | tf_op jit(solution)/shard_map/ppermute | solution.py:510
  30.1 38.5 %collective-permute-start.16 = (bf16[128,3072]{1,0:T(8,128)(2,1)}, bf16[128,3072]{1,0:T(8,128)(2,1)S(1)}, u32[]{:S(2)}, u32[]{:S(2)}) collective-permute-start(bf16[128,3072]{1,0:T(8,128)(2,1)} %get-tuple-element.53), channel_id=1, source_target_pairs={{0,7},{1,6},{2,5},{3,4},{4,3},{5,2},{6,1},{7,0},{8,15},{9,14},{10,... | collective-permute-start | bytes 2359304 | tf_op jit(solution)/shard_map/ppermute | solution.py:519
  34.0 8.7 %copy-start.22 = (f32[5,64,128]{2,1,0:T(8,128)}, f32[5,64,128]{2,1,0:T(8,128)S(1)}, u32[]{:S(2)}) copy-start(f32[5,64,128]{2,1,0:T(8,128)S(1)} %get-tuple-element.46.refs_6_.refs_3_) | copy-start | bytes 491524
  34.0 2.4 %copy-start.26 = (bf16[144,1024]{1,0:T(8,128)(2,1)}, bf16[144,1024]{1,0:T(8,128)(2,1)S(1)}, u32[]{:S(2)}) copy-start(bf16[144,1024]{1,0:T(8,128)(2,1)S(1)} %collective-permute-done.refs_2_.refs_11_) | copy-start | bytes 884740
  34.0 3.1 %copy-start.31 = (bf16[4,128,128]{2,1,0:T(8,128)(2,1)S(1)}, bf16[4,128,128]{2,1,0:T(8,128)(2,1)}, u32[]{:S(2)}) copy-start(bf16[4,128,128]{2,1,0:T(8,128)(2,1)} %copy-done.30) | copy-start | bytes 393220
  34.0 2.4 %copy-start.28 = (bf16[144,1024]{1,0:T(8,128)(2,1)}, bf16[144,1024]{1,0:T(8,128)(2,1)S(1)}, u32[]{:S(2)}) copy-start(bf16[144,1024]{1,0:T(8,128)(2,1)S(1)} %collective-permute-done.1.refs_3_.refs_12_) | copy-start | bytes 884740
  34.1 4.0 %copy-start.18 = (bf16[1,128,4096]{2,1,0:T(8,128)(2,1)S(1)}, bf16[1,128,4096]{2,1,0:T(8,128)(2,1)}, u32[]{:S(2)}) copy-start(bf16[1,128,4096]{2,1,0:T(8,128)(2,1)} %param.9) | copy-start | bytes 3145732
  35.7 30.3 %copy-start.5 = (bf16[128,2048]{1,0:T(8,128)(2,1)}, bf16[128,2048]{1,0:T(8,128)(2,1)S(1)}, u32[]{:S(2)}) copy-start(bf16[128,2048]{1,0:T(8,128)(2,1)S(1)} %get-tuple-element.44.refs_4_.refs_0_) | copy-start | bytes 1572868
  35.7 7.7 %collective-permute-start.7 = (bf16[128,2048]{1,0:T(8,128)(2,1)S(1)}, bf16[128,2048]{1,0:T(8,128)(2,1)S(1)}, u32[]{:S(2)}, u32[]{:S(2)}) collective-permute-start(bf16[128,2048]{1,0:T(8,128)(2,1)S(1)} %get-tuple-element.44.refs_4_.refs_0_), channel_id=1, source_target_pairs={{6,4},{7,5},{14,12},{15,13},{22,20},{23,21},{30,28},{31,29}} | collective-permute-start | bytes 1572872 | tf_op jit(solution)/shard_map/ppermute | solution.py:513
  37.1 0.9 copy-start.38
  38.0 6.9 %copy-start.1 = (bf16[1,128,4096]{2,1,0:T(8,128)(2,1)S(1)}, bf16[1,128,4096]{2,1,0:T(8,128)(2,1)}, u32[]{:S(2)}) copy-start(bf16[1,128,4096]{2,1,0:T(8,128)(2,1)} %param.16) | copy-start | bytes 3145732
  38.0 6.9 %copy-start.2 = (bf16[1,128,4096]{2,1,0:T(8,128)(2,1)S(1)}, bf16[1,128,4096]{2,1,0:T(8,128)(2,1)}, u32[]{:S(2)}) copy-start(bf16[1,128,4096]{2,1,0:T(8,128)(2,1)} %param.12) | copy-start | bytes 3145732
  39.3 14.7 %collective-permute-start.10 = (bf16[2048,128]{1,0:T(8,128)(2,1)S(1)}, bf16[2048,128]{1,0:T(8,128)(2,1)S(1)}, u32[]{:S(2)}, u32[]{:S(2)}) collective-permute-start(bf16[2048,128]{1,0:T(8,128)(2,1)S(1)} %get-tuple-element.48), channel_id=1, source_target_pairs={{0,8},{8,0},{16,24},{24,16},{1,9},{9,1},{17,25},{25,17},{2,10},{10... | collective-permute-start | bytes 1572872 | tf_op jit(solution)/shard_map/ppermute | solution.py:516
  40.8 25.2 %collective-permute-start.11 = (bf16[2048,128]{1,0:T(8,128)(2,1)S(1)}, bf16[2048,128]{1,0:T(8,128)(2,1)S(1)}, u32[]{:S(2)}, u32[]{:S(2)}) collective-permute-start(bf16[2048,128]{1,0:T(8,128)(2,1)S(1)} %get-tuple-element.49), channel_id=1, source_target_pairs={{0,16},{8,24},{16,0},{24,8},{1,17},{9,25},{17,1},{25,9},{2,18},{10... | collective-permute-start | bytes 1572872 | tf_op jit(solution)/shard_map/ppermute | solution.py:516
  42.3 23.7 %collective-permute-start.12 = (bf16[2048,128]{1,0:T(8,128)(2,1)S(1)}, bf16[2048,128]{1,0:T(8,128)(2,1)S(1)}, u32[]{:S(2)}, u32[]{:S(2)}) collective-permute-start(bf16[2048,128]{1,0:T(8,128)(2,1)S(1)} %get-tuple-element.50), channel_id=1, source_target_pairs={{0,24},{8,16},{16,8},{24,0},{1,25},{9,17},{17,9},{25,1},{2,26},{10... | collective-permute-start | bytes 1572872 | tf_op jit(solution)/shard_map/ppermute | solution.py:516
  43.4 22.6 %copy-start.13 = (bf16[128,2048]{1,0:T(8,128)(2,1)}, bf16[128,2048]{1,0:T(8,128)(2,1)S(1)}, u32[]{:S(2)}) copy-start(bf16[128,2048]{1,0:T(8,128)(2,1)S(1)} %collective-permute-done.7.refs_2_.refs_0_) | copy-start | bytes 1572868
  43.4 28.8 %collective-permute-start.19 = (bf16[128,2048]{1,0:T(8,128)(2,1)}, bf16[128,2048]{1,0:T(8,128)(2,1)}, u32[]{:S(2)}, u32[]{:S(2)}) collective-permute-start(bf16[128,2048]{1,0:T(8,128)(2,1)} %get-tuple-element.43.refs_4_.refs_5_), channel_id=1, source_target_pairs={{6,4},{7,5},{14,12},{15,13},{22,20},{23,21},{30,28},{31,29}} | collective-permute-start | bytes 1572872 | tf_op jit(solution)/shard_map/ppermute | solution.py:513
  54.0 13.0 %copy-start.7 = (bf16[2048,128]{1,0:T(8,128)(2,1)}, bf16[2048,128]{1,0:T(8,128)(2,1)S(1)}, u32[]{:S(2)}) copy-start(bf16[2048,128]{1,0:T(8,128)(2,1)S(1)} %collective-permute-done.10.refs_5_.refs_2_) | copy-start | bytes 1572868
  66.0 1.0 copy-start.9
  66.0 1.1 copy-start.11
  66.0 2.6 %copy-start.16 = (bf16[128,1024]{1,0:T(8,128)(2,1)S(1)}, bf16[128,1024]{1,0:T(8,128)(2,1)}, u32[]{:S(2)}) copy-start(bf16[128,1024]{1,0:T(8,128)(2,1)} %copy-done.15) | copy-start | bytes 786436
  67.1 13.8 %collective-permute-start.13 = (bf16[128,2048]{1,0:T(8,128)(2,1)}, bf16[128,2048]{1,0:T(8,128)(2,1)}, u32[]{:S(2)}, u32[]{:S(2)}) collective-permute-start(bf16[128,2048]{1,0:T(8,128)(2,1)} %shard_map.120.refs_5_), channel_id=1, source_target_pairs={{4,2},{5,3},{12,10},{13,11},{20,18},{21,19},{28,26},{29,27}} | collective-permute-start | bytes 1572872 | tf_op jit(solution)/shard_map/ppermute | solution.py:513
  71.6 1.9 %collective-permute-start.17 = (bf16[144,1024]{1,0:T(8,128)(2,1)}, bf16[144,1024]{1,0:T(8,128)(2,1)}, u32[]{:S(2)}, u32[]{:S(2)}) collective-permute-start(bf16[144,1024]{1,0:T(8,128)(2,1)} %get-tuple-element.55), channel_id=1, source_target_pairs={{0,1},{1,0},{2,3},{3,2},{4,5},{5,4},{6,7},{7,6},{8,9},{9,8},{10,11... | collective-permute-start | bytes 884744 | tf_op jit(solution)/shard_map/ppermute | solution.py:510
  71.7 2.3 %collective-permute-start.18 = (bf16[144,1024]{1,0:T(8,128)(2,1)}, bf16[144,1024]{1,0:T(8,128)(2,1)}, u32[]{:S(2)}, u32[]{:S(2)}) collective-permute-start(bf16[144,1024]{1,0:T(8,128)(2,1)} %get-tuple-element.56), channel_id=1, source_target_pairs={{0,1},{1,0},{2,3},{3,2},{4,5},{5,4},{6,7},{7,6},{8,9},{9,8},{10,11... | collective-permute-start | bytes 884744 | tf_op jit(solution)/shard_map/ppermute | solution.py:510
  72.2 11.6 %collective-permute-start.21 = (bf16[144,2048]{1,0:T(8,128)(2,1)}, bf16[144,2048]{1,0:T(8,128)(2,1)}, u32[]{:S(2)}, u32[]{:S(2)}) collective-permute-start(bf16[144,2048]{1,0:T(8,128)(2,1)} %get-tuple-element.54.refs_2_), channel_id=1, source_target_pairs={{0,1},{1,0},{2,3},{3,2},{4,5},{5,4},{6,7},{7,6},{8,9},{9,8},{10,11... | collective-permute-start | bytes 1769480 | tf_op jit(solution)/shard_map/ppermute | solution.py:510
  74.0 6.9 %copy-start.6 = (bf16[128,2048]{1,0:T(8,128)(2,1)S(1)}, bf16[128,2048]{1,0:T(8,128)(2,1)}, u32[]{:S(2)}) copy-start(bf16[128,2048]{1,0:T(8,128)(2,1)} %copy-done.5) | copy-start | bytes 1572868
  74.0 7.0 %copy-start.14 = (bf16[128,2048]{1,0:T(8,128)(2,1)S(1)}, bf16[128,2048]{1,0:T(8,128)(2,1)}, u32[]{:S(2)}) copy-start(bf16[128,2048]{1,0:T(8,128)(2,1)} %copy-done.13) | copy-start | bytes 1572868
  76.5 15.8 %collective-permute-start.20 = (bf16[128,2048]{1,0:T(8,128)(2,1)S(1)}, bf16[128,2048]{1,0:T(8,128)(2,1)S(1)}, u32[]{:S(2)}, u32[]{:S(2)}) collective-permute-start(bf16[128,2048]{1,0:T(8,128)(2,1)S(1)} %get-tuple-element.59), channel_id=1, source_target_pairs={{0,2},{1,3},{4,6},{5,7},{8,10},{9,11},{12,14},{13,15},{16,18},{17,... | collective-permute-start | bytes 1572872 | tf_op jit(solution)/shard_map/ppermute | solution.py:513
  82.2 15.7 %collective-permute-start.14 = (bf16[128,2048]{1,0:T(8,128)(2,1)S(1)}, bf16[128,2048]{1,0:T(8,128)(2,1)S(1)}, u32[]{:S(2)}, u32[]{:S(2)}) collective-permute-start(bf16[128,2048]{1,0:T(8,128)(2,1)S(1)} %shard_map.121.refs_5_), channel_id=1, source_target_pairs={{2,0},{3,1},{10,8},{11,9},{18,16},{19,17},{26,24},{27,25}} | collective-permute-start | bytes 1572872 | tf_op jit(solution)/shard_map/ppermute | solution.py:513
  97.9 1.5 %copy-start.17 = (bf16[128,1024]{1,0:T(8,128)(2,1)S(1)}, bf16[128,1024]{1,0:T(8,128)(2,1)}, u32[]{:S(2)}) copy-start(bf16[128,1024]{1,0:T(8,128)(2,1)} %copy-done.15) | copy-start | bytes 786436
  97.9 1.5 %copy-start.36 = (f32[64,128]{1,0:T(8,128)S(1)}, f32[64,128]{1,0:T(8,128)}, u32[]{:S(2)}) copy-start(f32[64,128]{1,0:T(8,128)} %get-tuple-element.73.refs_3_) | copy-start | bytes 98308
  99.3 2.7 %collective-permute-start.22 = (bf16[128,4096]{1,0:T(8,128)(2,1)S(1)}, bf16[128,4096]{1,0:T(8,128)(2,1)S(1)}, u32[]{:S(2)}, u32[]{:S(2)}) collective-permute-start(bf16[128,4096]{1,0:T(8,128)(2,1)S(1)} %shard_map.125.refs_2_), channel_id=1, source_target_pairs={{0,1},{1,0},{2,3},{3,2},{4,5},{5,4},{6,7},{7,6},{8,9},{9,8},{10,11... | collective-permute-start | bytes 3145736 | tf_op jit(solution)/shard_map/ppermute | solution.py:510
  99.4 2.6 %copy-start.23 = (f32[5,64,128]{2,1,0:T(8,128)S(1)}, f32[5,64,128]{2,1,0:T(8,128)}, u32[]{:S(2)}) copy-start(f32[5,64,128]{2,1,0:T(8,128)} %copy-done.22) | copy-start | bytes 491524
  99.4 2.6 %copy-start.27 = (bf16[144,1024]{1,0:T(8,128)(2,1)S(1)}, bf16[144,1024]{1,0:T(8,128)(2,1)}, u32[]{:S(2)}) copy-start(bf16[144,1024]{1,0:T(8,128)(2,1)} %copy-done.26) | copy-start | bytes 884740
  99.4 2.6 %copy-start.29 = (bf16[144,1024]{1,0:T(8,128)(2,1)S(1)}, bf16[144,1024]{1,0:T(8,128)(2,1)}, u32[]{:S(2)}) copy-start(bf16[144,1024]{1,0:T(8,128)(2,1)} %copy-done.28) | copy-start | bytes 884740
  99.4 2.6 %copy-start.35 = (bf16[128,128]{1,0:T(8,128)(2,1)S(1)}, bf16[128,128]{1,0:T(8,128)(2,1)}, u32[]{:S(2)}) copy-start(bf16[128,128]{1,0:T(8,128)(2,1)} %copy-done.34) | copy-start | bytes 98308
  102.0 7.4 %copy-start.8 = (bf16[2048,128]{1,0:T(8,128)(2,1)S(1)}, bf16[2048,128]{1,0:T(8,128)(2,1)}, u32[]{:S(2)}) copy-start(bf16[2048,128]{1,0:T(8,128)(2,1)} %copy-done.7) | copy-start | bytes 1572868
  102.0 7.4 %copy-start.10 = (bf16[2048,128]{1,0:T(8,128)(2,1)S(1)}, bf16[2048,128]{1,0:T(8,128)(2,1)}, u32[]{:S(2)}) copy-start(bf16[2048,128]{1,0:T(8,128)(2,1)} %copy-done.9) | copy-start | bytes 1572868
  102.1 7.4 %copy-start.12 = (bf16[2048,128]{1,0:T(8,128)(2,1)S(1)}, bf16[2048,128]{1,0:T(8,128)(2,1)}, u32[]{:S(2)}) copy-start(bf16[2048,128]{1,0:T(8,128)(2,1)} %copy-done.11) | copy-start | bytes 1572868
  102.1 7.4 %copy-start.21 = (bf16[2048,128]{1,0:T(8,128)(2,1)S(1)}, bf16[2048,128]{1,0:T(8,128)(2,1)}, u32[]{:S(2)}) copy-start(bf16[2048,128]{1,0:T(8,128)(2,1)} %copy-done.20) | copy-start | bytes 1572868
  105.9 7.9 %collective-permute-start.25 = (bf16[128,128]{1,0:T(8,128)(2,1)S(1)}, bf16[128,128]{1,0:T(8,128)(2,1)S(1)}, u32[]{:S(2)}, u32[]{:S(2)}) collective-permute-start(bf16[128,128]{1,0:T(8,128)(2,1)S(1)} %get-tuple-element.64.refs_5_), channel_id=1, source_target_pairs={{0,24},{8,16},{16,8},{24,0},{1,25},{9,17},{17,9},{25,1},{2,26},{10... | collective-permute-start | bytes 98312 | tf_op jit(solution)/shard_map/ppermute | solution.py:516
  107.3 6.4 %collective-permute-start.24 = (bf16[128,128]{1,0:T(8,128)(2,1)S(1)}, bf16[128,128]{1,0:T(8,128)(2,1)S(1)}, u32[]{:S(2)}, u32[]{:S(2)}) collective-permute-start(bf16[128,128]{1,0:T(8,128)(2,1)S(1)} %get-tuple-element.64.refs_5_), channel_id=1, source_target_pairs={{0,16},{8,24},{16,0},{24,8},{1,17},{9,25},{17,1},{25,9},{2,18},{10... | collective-permute-start | bytes 98312 | tf_op jit(solution)/shard_map/ppermute | solution.py:516
  109.2 4.6 %collective-permute-start.23 = (bf16[128,128]{1,0:T(8,128)(2,1)S(1)}, bf16[128,128]{1,0:T(8,128)(2,1)S(1)}, u32[]{:S(2)}, u32[]{:S(2)}) collective-permute-start(bf16[128,128]{1,0:T(8,128)(2,1)S(1)} %get-tuple-element.64.refs_5_), channel_id=1, source_target_pairs={{0,8},{8,0},{16,24},{24,16},{1,9},{9,1},{17,25},{25,17},{2,10},{10... | collective-permute-start | bytes 98312 | tf_op jit(solution)/shard_map/ppermute | solution.py:516
  109.4 1.2 copy-start.19
  113.8 1.2 copy-start.4
  115.5 1.4 %collective-permute-start.26 = (bf16[4,128,128]{2,1,0:T(8,128)(2,1)S(1)}, bf16[4,128,128]{2,1,0:T(8,128)(2,1)S(1)}, u32[]{:S(2)}, u32[]{:S(2)}) collective-permute-start(bf16[4,128,128]{2,1,0:T(8,128)(2,1)S(1)} %get-tuple-element.66), channel_id=1, source_target_pairs={{0,1},{1,0},{2,3},{3,2},{4,5},{5,4},{6,7},{7,6},{8,9},{9,8},{10,11... | collective-permute-start | bytes 393224 | tf_op jit(solution)/shard_map/ppermute | solution.py:510
  116.9 7.6 %collective-permute-start.28 = (bf16[128,128]{1,0:T(8,128)(2,1)S(1)}, bf16[128,128]{1,0:T(8,128)(2,1)S(1)}, u32[]{:S(2)}, u32[]{:S(2)}) collective-permute-start(bf16[128,128]{1,0:T(8,128)(2,1)S(1)} %get-tuple-element.69), channel_id=1, source_target_pairs={{0,4},{1,5},{2,6},{3,7},{4,0},{5,1},{6,2},{7,3},{8,12},{9,13},{10,... | collective-permute-start | bytes 98312 | tf_op jit(solution)/shard_map/ppermute | solution.py:696
  117.0 7.6 %collective-permute-start.29 = (bf16[128,128]{1,0:T(8,128)(2,1)S(1)}, bf16[128,128]{1,0:T(8,128)(2,1)S(1)}, u32[]{:S(2)}, u32[]{:S(2)}) collective-permute-start(bf16[128,128]{1,0:T(8,128)(2,1)S(1)} %get-tuple-element.70), channel_id=1, source_target_pairs={{0,6},{1,7},{2,4},{3,5},{4,2},{5,3},{6,0},{7,1},{8,14},{9,15},{10,... | collective-permute-start | bytes 98312 | tf_op jit(solution)/shard_map/ppermute | solution.py:696
  118.9 5.7 %collective-permute-start.27 = (bf16[128,128]{1,0:T(8,128)(2,1)S(1)}, bf16[128,128]{1,0:T(8,128)(2,1)S(1)}, u32[]{:S(2)}, u32[]{:S(2)}) collective-permute-start(bf16[128,128]{1,0:T(8,128)(2,1)S(1)} %get-tuple-element.67.refs_11_), channel_id=1, source_target_pairs={{0,2},{1,3},{2,0},{3,1},{4,6},{5,7},{6,4},{7,5},{8,10},{9,11},{10,... | collective-permute-start | bytes 98312 | tf_op jit(solution)/shard_map/ppermute | solution.py:696
  (6 other events, 4.3 us)

commit v4 on v3

--- a/solution.py
+++ b/solution.py
@@ -14,7 +14,7 @@
 LOG2E = 1.4426950408889634
 LOW = -1e30
 EXACT = lax.Precision.HIGHEST
-VMEM_BYTES = 14 * 1024 * 1024
+VMEM_BYTES = 9 * 1024 * 1024
 CUT = 1024
 PIECES = 2
 
@@ -36,14 +36,15 @@
 def run(*jobs, after=(), flops=0):
     vmem = pl.BlockSpec(memory_space=pltpu.VMEM)
     smem = pl.BlockSpec(memory_space=pltpu.SMEM)
-    anywhere = pl.BlockSpec(memory_space=pl.ANY)
     ins, specs, outs, calls = [], [], [], []
     for body, job_outs, arrays, scalars in jobs:
         calls.append((body, len(ins), len(scalars) + len(arrays), len(outs), len(job_outs)))
         ins += [*scalars, *arrays]
         specs += [smem] * len(scalars) + [vmem] * len(arrays)
         outs += job_outs
-    lead = len(ins) + len(after)
+    lead = len(ins)
+    if after:
+        ins[-1] = lax.optimization_barrier((ins[-1], *after))[0]
 
     def kernel(*refs):
         for body, i, ni, o, no in calls:
@@ -52,32 +53,35 @@
     got = pl.pallas_call(
         kernel,
         out_shape=outs,
-        in_specs=specs + [anywhere] * len(after),
+        in_specs=specs,
         out_specs=[vmem] * len(outs),
         compiler_params=pltpu.CompilerParams(vmem_limit_bytes=VMEM_BYTES),
         cost_estimate=pl.CostEstimate(flops=flops, transcendentals=0, bytes_accessed=flops // 250),
-    )(*ins, *after)
+    )(*ins)
     return [list(got[o : o + no]) for _, _, _, o, no in calls]
 
 
-def run_on_half(body, side, shape, arrays, before, after=()):
+def run_on_half(body, side, shape, scalar, arrays, before, after=()):
     vmem = pl.BlockSpec(memory_space=pltpu.VMEM)
+    smem = pl.BlockSpec(memory_space=pltpu.SMEM)
     anywhere = pl.BlockSpec(memory_space=pl.ANY)
-    rest = [*before, *after]
+    rest = [*before]
+    if after:
+        arrays = [*arrays[:-1], lax.optimization_barrier((arrays[-1], *after))[0]]
 
     def kernel(*refs):
-        body(*refs[: len(arrays)], refs[-1])
+        body(*refs[: len(arrays) + 1], refs[-1])
 
     return pl.pallas_call(
         kernel,
         grid=(1,),
         out_shape=shape,
-        in_specs=[vmem] * len(arrays) + [anywhere] * len(rest),
+        in_specs=[smem] + [vmem] * len(arrays) + [anywhere] * len(rest),
         out_specs=pl.BlockSpec((shape.shape[0], shape.shape[1] // 2), lambda i: (0, side)),
-        input_output_aliases={len(arrays): 0} if before else {},
+        input_output_aliases={len(arrays) + 1: 0} if before else {},
         compiler_params=pltpu.CompilerParams(vmem_limit_bytes=VMEM_BYTES),
         cost_estimate=pl.CostEstimate(flops=0, transcendentals=0, bytes_accessed=0),
-    )(*arrays, *rest)
+    )(jnp.reshape(scalar, (1,)).astype(jnp.int32), *arrays, *rest)
 
 
 def iotas(shape):
@@ -140,6 +144,21 @@
         at -= ref.shape[1]
 
 
+def summed(lists, at, count):
+    total = columns(lists[0], at, count)
+    for refs in lists[1:]:
+        total = total + columns(refs, at, count)
+    return total
+
+
+def split(refs, counts):
+    lists = []
+    for count in counts:
+        lists.append(refs[:count])
+        refs = refs[count:]
+    return lists, refs
+
+
 def part_kernel(backward, count, core_ref, *refs):
     g_refs, (read_ref, decay_ref, own_ref, *send_refs) = refs[:count], refs[count:]
     heads, n = decay_ref.shape
@@ -251,8 +270,8 @@
         out_ref[:, there] = entered(lefts, here).astype(bf16)
 
 
-def mix_kernel(fwd, count, *refs):
-    g_refs, (inner_ref, row_ref, cols_ref, out_ref) = refs[:count], refs[count:]
+def mix_kernel(fwd, counts, *refs):
+    lists, (inner_ref, row_ref, cols_ref, out_ref) = split(refs, counts)
     heads, n = row_ref.shape
     width = inner_ref.shape[1] // heads
     step = GROUP * width
@@ -260,92 +279,83 @@
     keep = (t >= s) if fwd else (t + s >= n - 1)
     low_half = t < width
     acc = jnp.zeros((n, n), f32)
-    first = 0
-    for g_ref in g_refs:
-        groups = g_ref.shape[1] // step
-
-        def one(g, acc, g_ref=g_ref, first=first):
-            at = pl.multiple_of(g * step, step)
-            base = pl.multiple_of((first + g) * step, step)
-            rows = row_ref[pl.ds(pl.multiple_of((first + g) * GROUP, GROUP), GROUP)]
-            cols = cols_ref[first + g]
-            for pair in range(GROUP // 2):
-                inner = inner_ref[:, pl.ds(base + pair * LANES, LANES)].astype(f32)
-                halves = jnp.concatenate(
-                    [jnp.where(low_half, inner, 0.0), jnp.where(low_half, 0.0, inner)], axis=0
-                ).astype(bf16)
-                dots = dot_nt(halves, g_ref[:, pl.ds(at + pair * LANES, LANES)])
-                for j in range(2):
-                    h = 2 * pair + j
-                    row = rows[h : h + 1]
-                    if fwd:
-                        k = C_MIX_FWD * GROUP + h
-                        power = row - cols[:, k : k + 1]
-                    else:
-                        k = C_MIX_BACK * GROUP + h
-                        power = cols[:, k : k + 1] - row
-                    decay = jnp.exp2(jnp.where(keep, power, LOW))
-                    acc = acc + decay * dots[j * n : (j + 1) * n]
-            return acc
-
-        acc = lax.fori_loop(0, groups, one, acc)
-        first += groups
+    for g in range(heads // GROUP):
+        rows = row_ref[g * GROUP : (g + 1) * GROUP]
+        cols = cols_ref[g]
+        for pair in range(GROUP // 2):
+            at = g * step + pair * LANES
+            inner = inner_ref[:, at : at + LANES].astype(f32)
+            halves = jnp.concatenate(
+                [jnp.where(low_half, inner, 0.0), jnp.where(low_half, 0.0, inner)], axis=0
+            ).astype(bf16)
+            dots = dot_nt(halves, summed(lists, at, LANES))
+            for j in range(2):
+                h = 2 * pair + j
+                row = rows[h : h + 1]
+                if fwd:
+                    k = C_MIX_FWD * GROUP + h
+                    power = row - cols[:, k : k + 1]
+                else:
+                    k = C_MIX_BACK * GROUP + h
+                    power = cols[:, k : k + 1] - row
+                decay = jnp.exp2(jnp.where(keep, power, LOW))
+                acc = acc + decay * dots[j * n : (j + 1) * n]
     out_ref[...] = acc
 
 
-def edge_terms(
-    upward, core, inner_ref, halves_ref, swapped_ref, near_refs, far_ref, edge, state_ref
-):
-    heads, n = edge.shape
+def edge_terms(upward, own, core, inner_ref, half_ref, near_refs, far_ref, edge_ref, state_ref):
+    heads, n = edge_ref.shape
     width = inner_ref.shape[1] // heads
     step = GROUP * width
-    groups = heads // GROUP
+    groups = heads // GROUP // 2
     first = core == (0 if upward else 1)
     rows = state_ref.shape[0]
-    base = halves_ref.shape[1] // 2 if upward else 0
+    base = core if own else 1 - core
+    at = groups * step if upward else 0
     acc = 0.0
     for g in range(groups):
-        here = slice(g * step, (g + 1) * step)
-        at = base + g % (groups // 2) * step
-        there = slice(at, at + step)
-        near = slice(at - base, at - base + step)
-        mine = core == g // (groups // 2)
-        whole = jnp.where(mine, halves_ref[:, there].astype(f32), swapped_ref[:, there].astype(f32))
-        other = columns(near_refs, at - base, step).astype(f32)
-        other = jnp.where(mine, other, far_ref[:, near].astype(f32))
+        here = pl.ds(pl.multiple_of((base * groups + g) * step, step), step)
+        heads_here = pl.ds(pl.multiple_of((base * groups + g) * GROUP, GROUP), GROUP)
+        whole = half_ref[:, at + g * step : at + (g + 1) * step].astype(f32)
+        other = columns(near_refs, g * step, step) if own else far_ref[:, g * step : (g + 1) * step]
+        other = other.astype(f32)
         decay = other[rows : rows + 1] + other[rows + 1 : rows + 2]
         entering = jnp.where(first, whole, other[:rows] + decay * whole).astype(bf16)
-        state_ref[:, here] = entering
-        scaled = inner_ref[:, here].astype(f32) * spread(edge[g * GROUP : (g + 1) * GROUP], width)
+        state_ref[:, g * step : (g + 1) * step] = entering
+        scaled = inner_ref[:, here].astype(f32) * spread(edge_ref[heads_here], width)
         acc = acc + dot_nt(scaled.astype(bf16), entering)
     return acc
 
 
-def write_kernel(
-    core_ref,
-    inner_ref,
-    halves_ref,
-    swapped_ref,
-    right_far_ref,
-    left_far_ref,
-    rows_ref,
-    mixf_ref,
-    mixb_ref,
-    read_ref,
-    readr_ref,
-    *refs,
+def own_kernel(
+    core_ref, inner_ref, halves_ref, rows_ref, mixf_ref, mixb_ref, read_ref, readr_ref, *refs
 ):
-    right_near_refs, left_near_refs = refs[:PIECES], refs[PIECES : 2 * PIECES]
+    right_refs, left_refs = refs[:PIECES], refs[PIECES : 2 * PIECES]
     right_ref, left_ref, out_ref = refs[2 * PIECES :]
-    core = core_ref[0]
-    shared = (inner_ref, halves_ref, swapped_ref)
     acc = jnp.dot(mixf_ref[...].astype(bf16), read_ref[...], preferred_element_type=f32)
     acc = acc + jnp.dot(mixb_ref[...].astype(bf16), readr_ref[...], preferred_element_type=f32)
-    right_edge, left_edge = rows_ref[FWD_EDGE], rows_ref[BACK_EDGE]
-    acc = acc + edge_terms(
-        False, core, *shared, right_near_refs, right_far_ref, right_edge, right_ref
-    )
-    acc = acc + edge_terms(True, core, *shared, left_near_refs, left_far_ref, left_edge, left_ref)
+    for upward, near, plane, state_ref in (
+        (False, right_refs, FWD_EDGE, right_ref),
+        (True, left_refs, BACK_EDGE, left_ref),
+    ):
+        acc = acc + edge_terms(
+            upward, True, core_ref[0], inner_ref, halves_ref, near, None, rows_ref.at[plane], state_ref
+        )
+    out_ref[...] = acc
+
+
+def write_kernel(
+    core_ref, inner_ref, swapped_ref, rows_ref, acc_ref, right_far_ref, left_far_ref, *refs
+):
+    right_ref, left_ref, out_ref = refs
+    acc = acc_ref[...]
+    for upward, far, plane, state_ref in (
+        (False, right_far_ref, FWD_EDGE, right_ref),
+        (True, left_far_ref, BACK_EDGE, left_ref),
+    ):
+        acc = acc + edge_terms(
+            upward, False, core_ref[0], inner_ref, swapped_ref, None, far, rows_ref.at[plane], state_ref
+        )
     out_ref[...] = acc.astype(bf16)
 
 
@@ -409,9 +419,10 @@
 
 
 def inner_kernel(
-    side, gf_ref, right_ref, left_ref, rows_ref, cols_ref, write_ref, read_ref, readr_ref, *refs
+    side, core_ref, gf_ref, right_own_ref, right_rest_ref, left_own_ref, left_rest_ref, *refs
 ):
-    *gb_refs, out_ref = refs
+    rows_ref, cols_ref, write_ref, read_ref, readr_ref, *gb_refs, out_ref = refs
+    own_side = core_ref[0] == side
     _, heads, n = rows_ref.shape
     width = gf_ref.shape[1] // heads
     step = GROUP * width
@@ -425,16 +436,19 @@
     for g in range(side * half, (side + 1) * half):
         at = g * step
         own = slice(g * GROUP, (g + 1) * GROUP)
-        whole = slice(at, at + step)
+        half_at = at - side * half * step
+        there = slice(half_at, half_at + step)
         cols = cols_ref[g]
+        right = jnp.where(own_side, right_own_ref[:, there], right_rest_ref[:, there])
+        left = jnp.where(own_side, left_own_ref[:, there], left_rest_ref[:, there])
         cum2 = rows_ref[CUM2, own]
         exclr2 = rows_ref[EXCLR2, own]
         step_e = spread(rows_ref[STEP, own], width)
         edges = spread(rows_ref[FWD_EDGE, own], width) * jnp.dot(
-            write, right_ref[:, whole], preferred_element_type=f32
+            write, right, preferred_element_type=f32
         )
         edges = edges + spread(rows_ref[BACK_EDGE, own], width) * jnp.dot(
-            write, left_ref[:, whole], preferred_element_type=f32
+            write, left, preferred_element_type=f32
         )
         for pair in range(GROUP // 2):
             mixes = []
@@ -591,7 +605,7 @@
     )
     shared = [shares[0]] + [over_dp(shares[k], k) for k in range(1, dp_count)]
     ((mix_f,),) = run(
-        job(part(mix_kernel, True, 1), [sds((n, n), f32)], gf, inner, rows[CUM2], cols),
+        job(part(mix_kernel, True, [1]), [sds((n, n), f32)], gf, inner, rows[CUM2], cols),
         after=(right_term,),
     )
     right_far = over_cores(right_own)
@@ -628,7 +642,7 @@
         rights.append(over_chips(leaving, (chips - 1 - i, chips - 2 - i)))
     ((mix_b,),) = run(
         job(
-            part(mix_kernel, False, len(flips)),
+            part(mix_kernel, False, [len(flips)]),
             [sds((n, n), f32)],
             *flips,
             inner,
@@ -639,19 +653,16 @@
     )
     ((halves,),) = run(
         job(part(halves_kernel, len(rights)), [sds((state, width), bf16)], *rights, *lefts),
-        after=(left_far, *shared[4:]),
+        after=(left_far, mix_b, *shared[4:]),
     )
     swapped = over_cores(halves)
 
-    ((right_in, left_in, grad_write),) = run(
+    ((right_own_in, left_own_in, own_write),) = run(
         job(
-            write_kernel,
-            [sds((state, width), bf16), sds((state, width), bf16), sds((n, state), bf16)],
+            own_kernel,
+            [half_shape, half_shape, sds((n, state), f32)],
             inner,
             halves,
-            swapped,
-            right_far,
-            left_far,
             rows,
             mix_f,
             mix_b,
@@ -662,6 +673,19 @@
             scalars=(core,),
         )
     )
+    ((right_rest_in, left_rest_in, grad_write),) = run(
+        job(
+            write_kernel,
+            [half_shape, half_shape, sds((n, state), bf16)],
+            inner,
+            swapped,
+            rows,
+            own_write,
+            right_far,
+            left_far,
+            scalars=(core,),
+        )
+    )
 
     writes = [grad_write] + [over_dp(grad_write, k) for k in range(1, dp_count)]
     ((weight,),) = run(
@@ -670,8 +694,9 @@
     )
     weight = weight.reshape(-1, state)
     write = jnp.dot(hidden, weight, preferred_element_type=f32).astype(bf16)
-    inner_arrays = (gf, right_in, left_in, rows, cols, write, read, read_r, *flips)
-    half_inner = run_on_half(part(inner_kernel, 0), 0, sds((n, width), bf16), inner_arrays, ())
+    entering = (right_own_in, right_rest_in, left_own_in, left_rest_in)
+    inner_arrays = (gf, *entering, rows, cols, write, read, read_r, *flips)
+    half_inner = run_on_half(part(inner_kernel, 0), 0, sds((n, width), bf16), core, inner_arrays, ())
     piece = share // ctx_count
     ((keep, give),) = run(
         job(
@@ -697,7 +722,7 @@
     grad_weight = total / (dp_count * ctx_count * n)
 
     grad_inner = run_on_half(
-        part(inner_kernel, 1), 1, sds((n, width), bf16), inner_arrays, (half_inner,), tuple(dealt[:1])
+        part(inner_kernel, 1), 1, sds((n, width), bf16), core, inner_arrays, (half_inner,), tuple(dealt[:1])
     )
     grad_hidden = dot_nt(grad_write, weight).astype(bf16)
     return grad_inner[None], grad_hidden[None], grad_weight

time: 126 us -> 124 us (0.984)
  local copies, waits for them, and re-layouts: 9.63 us -> 7.54 us
  waiting for transfers between devices: 44.5 us -> 42.8 us
    ppermute x5, waiting for transfers between devices: 14.2 us -> 12.7 us  [over_chips(): return lax.ppermute(array, 'ctx', chip_pairs(moves))]
    unnamed x80 -> x68, local copies, waits for them, and re-layouts: 9 us -> 7.52 us
    pallas_call x21 -> x22, Pallas kernels: 32.3 us -> 33.4 us  [the longest x20 28 us: run(): pl.pallas_call(kernel, out_shape=outs, in_specs=specs, out_specs=[vmem] *...]
  transfers between devices with their start and end apart: 30 -> 30, of which waited for: 10 -> 10; matrix products, arithmetic and copies ran while one was open for 2% -> 2% of each run, Pallas kernels for 21% -> 24%
where the time goes in v4:
time: 124 us; the launch traced here: 123 us
  waiting for transfers between devices  42.8 us (35%)
  Pallas kernels  33.4 us (27%)
  starting transfers between devices  32.8 us (26%)
  local copies, waits for them, and re-layouts  7.54 us (6%)
  other arithmetic  2.96 us (2%)
  matrix products  1.85 us (1%)
  between operations  1.65 us (1%)
    pallas_call x20, Pallas kernels, run(): pl.pallas_call(kernel, out_shape=outs, in_specs=specs, out_specs=[vmem] *...  28 us
    ppermute x6, waiting for transfers between devices, over_dp(): return lax.ppermute(array, 'dp', xor_pairs(dp_count, k))  19.5 us
    ppermute x5, waiting for transfers between devices, over_chips(): return lax.ppermute(array, 'ctx', chip_pairs(moves))  12.7 us
    ppermute x5, starting transfers between devices, over_chips(): return lax.ppermute(array, 'ctx', chip_pairs(moves))  9.87 us
    ppermute x3, starting transfers between devices, flip(): lax.ppermute(piece, 'ctx', [(i, ctx_count - 1 - i) for i in range(ctx_cou...  8.8 us
    unnamed x68, local copies, waits for them, and re-layouts  7.52 us
    ppermute x6, starting transfers between devices, over_dp(): return lax.ppermute(array, 'dp', xor_pairs(dp_count, k))  7.04 us
    pallas_call x2, Pallas kernels, run_on_half(): pl.pallas_call(kernel, grid=(1,), out_shape=shape, in_specs=[smem] + [vme...  5.42 us
  transfers between devices with their start and end apart: 30, of which 10 were waited for; matrix products, arithmetic and copies ran while one was open for 2% of the time, Pallas kernels for 24%

profile of v4, /device:TPU:0, one launch (start us, length us, event | category | flops | bytes accessed | tf_op | source)
XLA Modules:
  0.0 122.9 jit_solution(11030389920964805166)
XLA Ops:
  1.3 0.8 bitcast_convert_fusion
  2.0 0.8 fusion.3
  2.8 0.8 pad_maximum_fusion
  3.6 4.6 %collective-permute-start.2 = (f32[320,128]{1,0:T(8,128)S(1)}, f32[320,128]{1,0:T(8,128)S(1)}, u32[]{:S(2)}, u32[]{:S(2)}) collective-permute-start(f32[320,128]{1,0:T(8,128)S(1)} %pad_maximum_fusion), channel_id=1, source_target_pairs={{0,7},{1,6},{2,5},{3,4},{4,3},{5,2},{6,1},{7,0},{8,15},{9,14},{10,... | collective-permute-start | bytes 491528 | tf_op jit(solution)/shard_map/ppermute | solution.py:533
  8.1 1.2 collective-permute-start.3
  9.4 1.2 copy-done
  10.6 0.8 copy-done.23
  11.3 0.8 copy-done.29
  12.1 2.9 %shard_map.112 = (bf16[144,2048]{1,0:T(8,128)(2,1)}, bf16[144,1024]{1,0:T(8,128)(2,1)S(1)}, bf16[144,1024]{1,0:T(8,128)(2,1)}) custom-call(s32[1]{0:T(128)} %bitcast.refs_0_.refs_1_, bf16[128,4096]{1,0:T(8,128)(2,1)S(1)} %bitcast.30, bf16[128,128]{1,0:T(8,128)(2,1)S(1)} %bitcast.44, f32[64,128]{1,0:T(8,128)S(1)} %bitcast.52), custom_call_target="tpu_custom_call" | custom-call | tf_op jit(solution)/shard_map/pallas_call | solution.py:53
  15.0 2.6 %collective-permute-done.4.refs_2_ = bf16[128,128]{1,0:T(8,128)(2,1)S(1)} collective-permute-done((bf16[128,128]{1,0:T(8,128)(2,1)S(1)}, bf16[128,128]{1,0:T(8,128)(2,1)S(1)}, u32[]{:S(2)}, u32[]{:S(2)}) %collective-permute-start.4) | collective-permute-done | bytes 32800 | tf_op jit(solution)/shard_map/ppermute | solution.py:538
  17.5 0.9 shard_map.122
  18.5 2.2 %collective-permute-start.15 = (bf16[128,1024]{1,0:T(8,128)(2,1)S(1)}, bf16[128,1024]{1,0:T(8,128)(2,1)S(1)}, u32[]{:S(2)}, u32[]{:S(2)}) collective-permute-start(bf16[128,1024]{1,0:T(8,128)(2,1)S(1)} %get-tuple-element.74), channel_id=1, source_target_pairs={{0,7},{1,6},{2,5},{3,4},{4,3},{5,2},{6,1},{7,0},{8,15},{9,14},{10,... | collective-permute-start | bytes 786440 | tf_op jit(solution)/shard_map/ppermute | solution.py:533
  20.7 0.7 shard_map.113.refs_2_
  21.4 2.2 %shard_map.114 = (bf16[144,2048]{1,0:T(8,128)(2,1)S(1)}, bf16[144,1024]{1,0:T(8,128)(2,1)S(1)}, bf16[144,1024]{1,0:T(8,128)(2,1)S(1)}) custom-call(s32[1]{0:T(128)} %bitcast.refs_0_.refs_1_, bf16[128,4096]{1,0:T(8,128)(2,1)S(1)} %bitcast.40, f32[128,128]{1,0:T(8,128)S(1)} %get-tuple-element.108.refs_2_, f32[64,128]{1,0:T(8,128)S(1)} %slice.21.refs_3_), custom_call_target="tpu_custom_call" | custom-call | tf_op jit(solution)/shard_map/pallas_call | solution.py:53
  23.5 0.5 collective-permute-start.5
  24.1 0.4 collective-permute-start.1
  24.5 4.3 %collective-permute-done.15.refs_1_.refs_0_.refs_11_ = bf16[128,1024]{1,0:T(8,128)(2,1)S(1)} collective-permute-done((bf16[128,1024]{1,0:T(8,128)(2,1)S(1)}, bf16[128,1024]{1,0:T(8,128)(2,1)S(1)}, u32[]{:S(2)}, u32[]{:S(2)}) %collective-permute-start.15) | collective-permute-done | bytes 262176 | tf_op jit(solution)/shard_map/ppermute | solution.py:533
  28.8 0.7 copy-done.6
  29.6 0.5 collective-permute-start.9
  30.1 2.1 %collective-permute-start.16 = (bf16[128,3072]{1,0:T(8,128)(2,1)}, bf16[128,3072]{1,0:T(8,128)(2,1)S(1)}, u32[]{:S(2)}, u32[]{:S(2)}) collective-permute-start(bf16[128,3072]{1,0:T(8,128)(2,1)} %get-tuple-element.76), channel_id=1, source_target_pairs={{0,7},{1,6},{2,5},{3,4},{4,3},{5,2},{6,1},{7,0},{8,15},{9,14},{10,... | collective-permute-start | bytes 2359304 | tf_op jit(solution)/shard_map/ppermute | solution.py:533
  32.2 1.3 %shard_map.115 = (bf16[128,2048]{1,0:T(8,128)(2,1)}, f32[1,2048]{1,0:T(1,128)S(1)}, bf16[128,128]{1,0:T(8,128)(2,1)S(1)}, f32[5,64,128]{2,1,0:T(8,128)S(1)}, f32[8,128,128]{2,1,0:T(8,128)S(1)}) custom-call(s32[1]{0:T(128)} %bitcast.refs_0_.refs_1_, bf16[144,2048]{1,0:T(8,128)(2,1)S(1)} %get-tuple-element.57.refs_1_, ...), custom_call_target="tpu_custom_call" | custom-call | tf_op jit(solution)/shard_map/pallas_call | solution.py:53
  33.4 1.5 %shard_map.116 = (bf16[128,2048]{1,0:T(8,128)(2,1)S(1)}, f32[1,2048]{1,0:T(1,128)S(1)}) custom-call(s32[1]{0:T(128)} %bitcast.refs_0_.refs_1_, bf16[144,2048]{1,0:T(8,128)(2,1)} %get-tuple-element.53.refs_1_, bf16[144,1024]{1,0:T(8,128)(2,1)S(1)} %collective-permute-done.refs_2_.refs_8_, bf16[144,1024]{1,0:T(8,128)(2,1)S(1)} %collective-permute-done.1.refs_3_.refs_9_), custom_call_target="tpu_custom_call" | custom-call | tf_op jit(solution)/shard_map/pallas_call | solution.py:53
  34.9 0.7 copy-done.25
  35.6 0.7 copy-done.27
  36.3 0.8 collective-permute-start.7
  37.2 1.0 shard_map.118
  38.2 0.4 shard_map.119
  38.6 0.8 copy-done.13
  39.4 1.5 %collective-permute-start.10 = (bf16[2048,128]{1,0:T(8,128)(2,1)S(1)}, bf16[2048,128]{1,0:T(8,128)(2,1)S(1)}, u32[]{:S(2)}, u32[]{:S(2)}) collective-permute-start(bf16[2048,128]{1,0:T(8,128)(2,1)S(1)} %get-tuple-element.69), channel_id=1, source_target_pairs={{0,8},{8,0},{16,24},{24,16},{1,9},{9,1},{17,25},{25,17},{2,10},{10... | collective-permute-start | bytes 1572872 | tf_op jit(solution)/shard_map/ppermute | solution.py:530
  40.9 1.5 %collective-permute-start.11 = (bf16[2048,128]{1,0:T(8,128)(2,1)S(1)}, bf16[2048,128]{1,0:T(8,128)(2,1)S(1)}, u32[]{:S(2)}, u32[]{:S(2)}) collective-permute-start(bf16[2048,128]{1,0:T(8,128)(2,1)S(1)} %get-tuple-element.70), channel_id=1, source_target_pairs={{0,16},{8,24},{16,0},{24,8},{1,17},{9,25},{17,1},{25,9},{2,18},{10... | collective-permute-start | bytes 1572872 | tf_op jit(solution)/shard_map/ppermute | solution.py:530
  42.4 0.5 collective-permute-start.12
  42.9 1.4 %shard_map.117.refs_4_ = f32[128,128]{1,0:T(8,128)S(1)} custom-call(bf16[128,4096]{1,0:T(8,128)(2,1)S(1)} %bitcast.31, bf16[128,4096]{1,0:T(8,128)(2,1)S(1)} %bitcast.34, f32[64,128]{1,0:T(8,128)S(1)} %get-tuple-element.106.refs_2_, f32[8,128,128]{2,1,0:T(8,128)S(1)} %get-tuple-element.84.refs_3_.refs_4_.refs_7_), custom_call_target="tpu_custom_call" | custom-call | tf_op jit(solution)/shard_map/pallas_call | solution.py:53
  44.3 0.6 copy-done.31
  45.0 1.6 %collective-permute-start.19 = (bf16[128,2048]{1,0:T(8,128)(2,1)}, bf16[128,2048]{1,0:T(8,128)(2,1)}, u32[]{:S(2)}, u32[]{:S(2)}) collective-permute-start(bf16[128,2048]{1,0:T(8,128)(2,1)} %get-tuple-element.61.refs_5_), channel_id=1, source_target_pairs={{6,4},{7,5},{14,12},{15,13},{22,20},{23,21},{30,28},{31,29}} | collective-permute-start | bytes 1572872 | tf_op jit(solution)/shard_map/ppermute | solution.py:527
  46.6 7.6 %collective-permute-done.10.refs_2_ = bf16[2048,128]{1,0:T(8,128)(2,1)S(1)} collective-permute-done((bf16[2048,128]{1,0:T(8,128)(2,1)S(1)}, bf16[2048,128]{1,0:T(8,128)(2,1)S(1)}, u32[]{:S(2)}, u32[]{:S(2)}) %collective-permute-start.10) | collective-permute-done | bytes 524320 | tf_op jit(solution)/shard_map/ppermute | solution.py:530
  54.1 12.0 %collective-permute-done.11.refs_3_ = bf16[2048,128]{1,0:T(8,128)(2,1)S(1)} collective-permute-done((bf16[2048,128]{1,0:T(8,128)(2,1)S(1)}, bf16[2048,128]{1,0:T(8,128)(2,1)S(1)}, u32[]{:S(2)}, u32[]{:S(2)}) %collective-permute-start.11) | collective-permute-done | bytes 524320 | tf_op jit(solution)/shard_map/ppermute | solution.py:530
  66.1 1.1 shard_map.120
  67.2 1.5 %collective-permute-start.13 = (bf16[128,2048]{1,0:T(8,128)(2,1)}, bf16[128,2048]{1,0:T(8,128)(2,1)}, u32[]{:S(2)}, u32[]{:S(2)}) collective-permute-start(bf16[128,2048]{1,0:T(8,128)(2,1)} %shard_map.120), channel_id=1, source_target_pairs={{4,2},{5,3},{12,10},{13,11},{20,18},{21,19},{28,26},{29,27}} | collective-permute-start | bytes 1572872 | tf_op jit(solution)/shard_map/ppermute | solution.py:527
  68.7 3.1 %shard_map.123 = (bf16[144,2048]{1,0:T(8,128)(2,1)}, bf16[144,1024]{1,0:T(8,128)(2,1)}, bf16[144,1024]{1,0:T(8,128)(2,1)}) custom-call(s32[1]{0:T(128)} %bitcast.refs_0_.refs_1_, bf16[128,1024]{1,0:T(8,128)(2,1)S(1)} %copy-done.7, bf16[128,3072]{1,0:T(8,128)(2,1)S(1)} %collective-permute-done.16.refs_2_.refs_1_.refs_12_, bf16[128,128]{1,0:T(8,128)(2,1)S(1)} %bitcast.46, ...), custom_call_target="tpu_custom_call" | custom-call | tf_op jit(solution)/shard_map/pallas_call | solution.py:53
  71.9 0.5 collective-permute-start.18
  72.4 1.3 %collective-permute-done.17.refs_3_.refs_10_ = bf16[144,1024]{1,0:T(8,128)(2,1)} collective-permute-done((bf16[144,1024]{1,0:T(8,128)(2,1)}, bf16[144,1024]{1,0:T(8,128)(2,1)}, u32[]{:S(2)}, u32[]{:S(2)}) %collective-permute-start.17) | collective-permute-done | bytes 294944 | tf_op jit(solution)/shard_map/ppermute | solution.py:524
  74.2 2.5 %shard_map.124 = (bf16[128,2048]{1,0:T(8,128)(2,1)S(1)}, bf16[128,2048]{1,0:T(8,128)(2,1)S(1)}) custom-call(s32[1]{0:T(128)} %bitcast.refs_0_.refs_1_, s32[1]{0:T(128)} %bitcast.13.refs_1_, bf16[144,2048]{1,0:T(8,128)(2,1)} %get-tuple-element.78.refs_2_, bf16[144,1024]{1,0:T(8,128)(2,1)} %collective-permute-done.17.refs_3_.refs_10_, ...), custom_call_target="tpu_custom_call" | custom-call | tf_op jit(solution)/shard_map/pallas_call | solution.py:53
  76.7 4.5 %collective-permute-start.20 = (bf16[128,2048]{1,0:T(8,128)(2,1)S(1)}, bf16[128,2048]{1,0:T(8,128)(2,1)S(1)}, u32[]{:S(2)}, u32[]{:S(2)}) collective-permute-start(bf16[128,2048]{1,0:T(8,128)(2,1)S(1)} %get-tuple-element.83), channel_id=1, source_target_pairs={{0,2},{1,3},{4,6},{5,7},{8,10},{9,11},{12,14},{13,15},{16,18},{17,... | collective-permute-start | bytes 1572872 | tf_op jit(solution)/shard_map/ppermute | solution.py:527
  81.3 1.3 %shard_map.121 = bf16[128,2048]{1,0:T(8,128)(2,1)S(1)} custom-call(bf16[128,2048]{1,0:T(8,128)(2,1)S(1)} %copy-done.22, f32[1,2048]{1,0:T(1,128)S(1)} %get-tuple-element.64.refs_1_, bf16[128,2048]{1,0:T(8,128)(2,1)S(1)} %copy-done.5, bf16[128,2048]{1,0:T(8,128)(2,1)} %collective-permute-done.13.refs_3_.refs_1_), custom_call_target="tpu_custom_call" | custom-call | tf_op jit(solution)/shard_map/pallas_call | solution.py:53
  82.6 1.5 %collective-permute-start.14 = (bf16[128,2048]{1,0:T(8,128)(2,1)S(1)}, bf16[128,2048]{1,0:T(8,128)(2,1)S(1)}, u32[]{:S(2)}, u32[]{:S(2)}) collective-permute-start(bf16[128,2048]{1,0:T(8,128)(2,1)S(1)} %shard_map.121), channel_id=1, source_target_pairs={{2,0},{3,1},{10,8},{11,9},{18,16},{19,17},{26,24},{27,25}} | collective-permute-start | bytes 1572872 | tf_op jit(solution)/shard_map/ppermute | solution.py:527
  84.1 1.4 %shard_map.125.refs_5_ = f32[128,128]{1,0:T(8,128)S(1)} custom-call(bf16[128,1024]{1,0:T(8,128)(2,1)S(1)} %copy-done.8, bf16[128,3072]{1,0:T(8,128)(2,1)S(1)} %collective-permute-done.16.refs_2_.refs_1_.refs_12_, bf16[128,4096]{1,0:T(8,128)(2,1)S(1)} %bitcast.35, f32[64,128]{1,0:T(8,128)S(1)} %get-tuple-element.105.refs_3_, ...), custom_call_target="tpu_custom_call" | custom-call | tf_op jit(solution)/shard_map/pallas_call | solution.py:53
  85.5 7.2 %collective-permute-done.20.refs_4_ = bf16[128,2048]{1,0:T(8,128)(2,1)S(1)} collective-permute-done((bf16[128,2048]{1,0:T(8,128)(2,1)S(1)}, bf16[128,2048]{1,0:T(8,128)(2,1)S(1)}, u32[]{:S(2)}, u32[]{:S(2)}) %collective-permute-start.20) | collective-permute-done | bytes 524320 | tf_op jit(solution)/shard_map/ppermute | solution.py:527
  92.7 5.4 %collective-permute-done.14.refs_2_ = bf16[128,2048]{1,0:T(8,128)(2,1)S(1)} collective-permute-done((bf16[128,2048]{1,0:T(8,128)(2,1)S(1)}, bf16[128,2048]{1,0:T(8,128)(2,1)S(1)}, u32[]{:S(2)}, u32[]{:S(2)}) %collective-permute-start.14) | collective-permute-done | bytes 524320 | tf_op jit(solution)/shard_map/ppermute | solution.py:527
  98.2 1.4 %shard_map.126.refs_2_ = bf16[128,4096]{1,0:T(8,128)(2,1)S(1)} custom-call(bf16[128,2048]{1,0:T(8,128)(2,1)S(1)} %copy-done.5, bf16[128,2048]{1,0:T(8,128)(2,1)} %collective-permute-done.13.refs_3_.refs_1_, bf16[128,2048]{1,0:T(8,128)(2,1)S(1)} %collective-permute-done.14.refs_2_, bf16[128,2048]{1,0:T(8,128)(2,1)S(1)} %get-tuple-element.82.refs_3_, ...), custom_call_target="tpu_custom_call" | custom-call | tf_op jit(solution)/shard_map/pallas_call | solution.py:53
  99.7 2.1 %shard_map.127 = (bf16[128,2048]{1,0:T(8,128)(2,1)S(1)}, bf16[128,2048]{1,0:T(8,128)(2,1)S(1)}, f32[128,128]{1,0:T(8,128)S(1)}) custom-call(s32[1]{0:T(128)} %bitcast.refs_0_.refs_1_, bf16[128,4096]{1,0:T(8,128)(2,1)S(1)} %bitcast.36, bf16[128,4096]{1,0:T(8,128)(2,1)S(1)} %shard_map.126.refs_2_, f32[5,64,128]{2,1,0:T(8,128)S(1)} %copy-done.12, ...), custom_call_target="tpu_custom_call" | custom-call | tf_op jit(solution)/shard_map/pallas_call | solution.py:53
  101.8 0.5 collective-permute-done.22.refs_2_
  102.3 2.4 %shard_map.128 = (bf16[128,2048]{1,0:T(8,128)(2,1)S(1)}, bf16[128,2048]{1,0:T(8,128)(2,1)S(1)}, bf16[128,128]{1,0:T(8,128)(2,1)S(1)}) custom-call(s32[1]{0:T(128)} %bitcast.refs_0_.refs_1_, bf16[128,4096]{1,0:T(8,128)(2,1)S(1)} %bitcast.37, bf16[128,4096]{1,0:T(8,128)(2,1)S(1)} %collective-permute-done.22.refs_2_, f32[5,64,128]{2,1,0:T(8,128)S(1)} %copy-done.12, ...), custom_call_target="tpu_custom_call" | custom-call | tf_op jit(solution)/shard_map/pallas_call | solution.py:53
  104.7 1.6 %collective-permute-start.25 = (bf16[128,128]{1,0:T(8,128)(2,1)S(1)}, bf16[128,128]{1,0:T(8,128)(2,1)S(1)}, u32[]{:S(2)}, u32[]{:S(2)}) collective-permute-start(bf16[128,128]{1,0:T(8,128)(2,1)S(1)} %get-tuple-element.93.refs_5_), channel_id=1, source_target_pairs={{0,24},{8,16},{16,8},{24,0},{1,25},{9,17},{17,9},{25,1},{2,26},{10... | collective-permute-start | bytes 98312 | tf_op jit(solution)/shard_map/ppermute | solution.py:530
  106.3 1.6 %collective-permute-start.24 = (bf16[128,128]{1,0:T(8,128)(2,1)S(1)}, bf16[128,128]{1,0:T(8,128)(2,1)S(1)}, u32[]{:S(2)}, u32[]{:S(2)}) collective-permute-start(bf16[128,128]{1,0:T(8,128)(2,1)S(1)} %get-tuple-element.93.refs_5_), channel_id=1, source_target_pairs={{0,16},{8,24},{16,0},{24,8},{1,17},{9,25},{17,1},{25,9},{2,18},{10... | collective-permute-start | bytes 98312 | tf_op jit(solution)/shard_map/ppermute | solution.py:530
  108.4 1.1 copy-done.10
  109.5 0.4 fusion.1.refs_8_
  110.0 2.7 %shard_map.130.refs_13_ = bf16[128,4096]{1,0:T(8,128)(2,1)} custom-call(s32[1]{0:T(128)} %bitcast.refs_0_.refs_1_, bf16[128,4096]{1,0:T(8,128)(2,1)S(1)} %bitcast.32, bf16[128,2048]{1,0:T(8,128)(2,1)S(1)} %get-tuple-element.87.refs_2_, bf16[128,2048]{1,0:T(8,128)(2,1)S(1)} %get-tuple-element.89.refs_3_, bf16[128,2048]{1,0:T(8,128)(2,1)S(1)} %get-tuple-element.90.refs_4_, ...), custom_call_target="tpu_custom_call" | custom-call | tf_op jit(solution)/shard_map/pallas_call | solution.py:75
  112.7 0.4 shard_map.131
  113.2 1.3 %collective-permute-done.26.refs_2_ = bf16[4,128,128]{2,1,0:T(8,128)(2,1)S(1)} collective-permute-done((bf16[4,128,128]{2,1,0:T(8,128)(2,1)S(1)}, bf16[4,128,128]{2,1,0:T(8,128)(2,1)S(1)}, u32[]{:S(2)}, u32[]{:S(2)}) %collective-permute-start.26) | collective-permute-done | bytes 131104 | tf_op jit(solution)/shard_map/ppermute | solution.py:524
  114.7 1.9 %collective-permute-start.29 = (bf16[128,128]{1,0:T(8,128)(2,1)S(1)}, bf16[128,128]{1,0:T(8,128)(2,1)S(1)}, u32[]{:S(2)}, u32[]{:S(2)}) collective-permute-start(bf16[128,128]{1,0:T(8,128)(2,1)S(1)} %get-tuple-element.102), channel_id=1, source_target_pairs={{0,6},{1,7},{2,4},{3,5},{4,2},{5,3},{6,0},{7,1},{8,14},{9,15},{10,... | collective-permute-start | bytes 98312 | tf_op jit(solution)/shard_map/ppermute | solution.py:721
  116.6 1.6 %collective-permute-start.27 = (bf16[128,128]{1,0:T(8,128)(2,1)S(1)}, bf16[128,128]{1,0:T(8,128)(2,1)S(1)}, u32[]{:S(2)}, u32[]{:S(2)}) collective-permute-start(bf16[128,128]{1,0:T(8,128)(2,1)S(1)} %get-tuple-element.98), channel_id=1, source_target_pairs={{0,2},{1,3},{2,0},{3,1},{4,6},{5,7},{6,4},{7,5},{8,10},{9,11},{10,... | collective-permute-start | bytes 98312 | tf_op jit(solution)/shard_map/ppermute | solution.py:721
  118.2 1.4 %fusion = bf16[1,128,4096]{2,1,0:T(8,128)(2,1)} fusion(bf16[128,128]{1,0:T(8,128)(2,1)S(1)} %get-tuple-element.93.refs_5_, bf16[4096,128]{1,0:T(8,128)(2,1)S(1)} %bitcast.42), kind=kOutput, calls=%fused_computation.1 | convolution fusion | flops 134742016 | bytes 2129920 | tf_op jit(solution)/shard_map/dot_general | solution.py:92
  119.6 2.7 %shard_map.133 = bf16[128,4096]{1,0:T(8,128)(2,1)} custom-call(s32[1]{0:T(128)} %bitcast.refs_0_.refs_1_, bf16[128,4096]{1,0:T(8,128)(2,1)S(1)} %bitcast.33, bf16[128,2048]{1,0:T(8,128)(2,1)S(1)} %get-tuple-element.87.refs_2_, bf16[128,2048]{1,0:T(8,128)(2,1)S(1)} %get-tuple-element.89.refs_3_, ...), custom_call_target="tpu_custom_call", output_to_operand_aliasing={{}: (13, {})} | custom-call | tf_op jit(solution)/shard_map/pallas_call | solution.py:75
  122.3 0.7 add_multiply_fusion
  (95 shorter events, 1.6 us)
Async XLA Ops:
  3.6 13.9 %collective-permute-start.2 = (f32[320,128]{1,0:T(8,128)S(1)}, f32[320,128]{1,0:T(8,128)S(1)}, u32[]{:S(2)}, u32[]{:S(2)}) collective-permute-start(f32[320,128]{1,0:T(8,128)S(1)} %pad_maximum_fusion), channel_id=1, source_target_pairs={{0,7},{1,6},{2,5},{3,4},{4,3},{5,2},{6,1},{7,0},{8,15},{9,14},{10,... | collective-permute-start | bytes 491528 | tf_op jit(solution)/shard_map/ppermute | solution.py:533
  8.1 9.4 %collective-permute-start.4 = (bf16[128,128]{1,0:T(8,128)(2,1)S(1)}, bf16[128,128]{1,0:T(8,128)(2,1)S(1)}, u32[]{:S(2)}, u32[]{:S(2)}) collective-permute-start(bf16[128,128]{1,0:T(8,128)(2,1)S(1)} %get-tuple-element.104.refs_0_), channel_id=1, source_target_pairs={{0,4},{1,5},{2,6},{3,7},{4,0},{5,1},{6,2},{7,3},{8,12},{9,13},{10,... | collective-permute-start | bytes 98312 | tf_op jit(solution)/shard_map/ppermute | solution.py:538
  8.1 9.4 %collective-permute-start.3 = (bf16[128,128]{1,0:T(8,128)(2,1)S(1)}, bf16[128,128]{1,0:T(8,128)(2,1)S(1)}, u32[]{:S(2)}, u32[]{:S(2)}) collective-permute-start(bf16[128,128]{1,0:T(8,128)(2,1)S(1)} %get-tuple-element.104.refs_0_), channel_id=1, source_target_pairs={{0,2},{1,3},{2,0},{3,1},{4,6},{5,7},{6,4},{7,5},{8,10},{9,11},{10,... | collective-permute-start | bytes 98312 | tf_op jit(solution)/shard_map/ppermute | solution.py:538
  9.3 1.2 copy-start
  10.6 0.8 copy-start.23
  11.3 0.8 copy-start.29
  12.1 5.4 %copy-start.3 = (bf16[1,128,4096]{2,1,0:T(8,128)(2,1)S(1)}, bf16[1,128,4096]{2,1,0:T(8,128)(2,1)}, u32[]{:S(2)}) copy-start(bf16[1,128,4096]{2,1,0:T(8,128)(2,1)} %param.17) | copy-start | bytes 3145732
  14.9 27.5 %collective-permute-start.8 = (bf16[144,2048]{1,0:T(8,128)(2,1)}, bf16[144,2048]{1,0:T(8,128)(2,1)}, u32[]{:S(2)}, u32[]{:S(2)}) collective-permute-start(bf16[144,2048]{1,0:T(8,128)(2,1)} %get-tuple-element.53.refs_1_), channel_id=1, source_target_pairs={{0,1},{1,0},{2,3},{3,2},{4,5},{5,4},{6,7},{7,6},{8,9},{9,8},{10,11... | collective-permute-start | bytes 1769480 | tf_op jit(solution)/shard_map/ppermute | solution.py:524
  18.5 13.7 %copy-start.24 = (bf16[1,128,128]{2,1,0:T(8,128)(2,1)S(1)}, bf16[1,128,128]{2,1,0:T(8,128)(2,1)}, u32[]{:S(2)}) copy-start(bf16[1,128,128]{2,1,0:T(8,128)(2,1)} %param.13) | copy-start | bytes 98308
  18.5 13.7 %copy-start.30 = (f32[1,64,128]{2,1,0:T(8,128)S(1)}, f32[1,64,128]{2,1,0:T(8,128)}, u32[]{:S(2)}) copy-start(f32[1,64,128]{2,1,0:T(8,128)} %param.15) | copy-start | bytes 98308
  18.5 13.7 %copy-start.33 = (f32[1,64,128]{2,1,0:T(8,128)S(1)}, f32[1,64,128]{2,1,0:T(8,128)}, u32[]{:S(2)}) copy-start(f32[1,64,128]{2,1,0:T(8,128)} %param.14) | copy-start | bytes 98308
  18.5 10.3 %collective-permute-start.15 = (bf16[128,1024]{1,0:T(8,128)(2,1)S(1)}, bf16[128,1024]{1,0:T(8,128)(2,1)S(1)}, u32[]{:S(2)}, u32[]{:S(2)}) collective-permute-start(bf16[128,1024]{1,0:T(8,128)(2,1)S(1)} %get-tuple-element.74), channel_id=1, source_target_pairs={{0,7},{1,6},{2,5},{3,4},{4,3},{5,2},{6,1},{7,0},{8,15},{9,14},{10,... | collective-permute-start | bytes 786440 | tf_op jit(solution)/shard_map/ppermute | solution.py:533
  23.5 6.1 %collective-permute-start.5 = (bf16[144,1024]{1,0:T(8,128)(2,1)S(1)}, bf16[144,1024]{1,0:T(8,128)(2,1)S(1)}, u32[]{:S(2)}, u32[]{:S(2)}) collective-permute-start(bf16[144,1024]{1,0:T(8,128)(2,1)S(1)} %get-tuple-element.58), channel_id=1, source_target_pairs={{0,1},{1,0},{2,3},{3,2},{4,5},{5,4},{6,7},{7,6},{8,9},{9,8},{10,11... | collective-permute-start | bytes 884744 | tf_op jit(solution)/shard_map/ppermute | solution.py:524
  24.0 6.1 %collective-permute-start.6 = (bf16[144,1024]{1,0:T(8,128)(2,1)S(1)}, bf16[144,1024]{1,0:T(8,128)(2,1)S(1)}, u32[]{:S(2)}, u32[]{:S(2)}) collective-permute-start(bf16[144,1024]{1,0:T(8,128)(2,1)S(1)} %get-tuple-element.59), channel_id=1, source_target_pairs={{0,1},{1,0},{2,3},{3,2},{4,5},{5,4},{6,7},{7,6},{8,9},{9,8},{10,11... | collective-permute-start | bytes 884744 | tf_op jit(solution)/shard_map/ppermute | solution.py:524
  24.1 9.3 %collective-permute-start.1 = (bf16[144,1024]{1,0:T(8,128)(2,1)}, bf16[144,1024]{1,0:T(8,128)(2,1)S(1)}, u32[]{:S(2)}, u32[]{:S(2)}) collective-permute-start(bf16[144,1024]{1,0:T(8,128)(2,1)} %get-tuple-element.55), channel_id=1, source_target_pairs={{0,1},{1,0},{2,3},{3,2},{4,5},{5,4},{6,7},{7,6},{8,9},{9,8},{10,11... | collective-permute-start | bytes 884744 | tf_op jit(solution)/shard_map/ppermute | solution.py:524
  28.8 0.7 copy-start.6
  29.6 3.9 %collective-permute-start = (bf16[144,1024]{1,0:T(8,128)(2,1)S(1)}, bf16[144,1024]{1,0:T(8,128)(2,1)S(1)}, u32[]{:S(2)}, u32[]{:S(2)}) collective-permute-start(bf16[144,1024]{1,0:T(8,128)(2,1)S(1)} %get-tuple-element.54), channel_id=1, source_target_pairs={{0,1},{1,0},{2,3},{3,2},{4,5},{5,4},{6,7},{7,6},{8,9},{9,8},{10,11... | collective-permute-start | bytes 884744 | tf_op jit(solution)/shard_map/ppermute | solution.py:524
  29.6 7.5 %collective-permute-start.9 = (bf16[4,128,128]{2,1,0:T(8,128)(2,1)}, bf16[4,128,128]{2,1,0:T(8,128)(2,1)}, u32[]{:S(2)}, u32[]{:S(2)}) collective-permute-start(bf16[4,128,128]{2,1,0:T(8,128)(2,1)} %shard_map.113.refs_2_), channel_id=1, source_target_pairs={{0,1},{1,0},{2,3},{3,2},{4,5},{5,4},{6,7},{7,6},{8,9},{9,8},{10,11... | collective-permute-start | bytes 393224 | tf_op jit(solution)/shard_map/ppermute | solution.py:524
  30.1 38.6 %collective-permute-start.16 = (bf16[128,3072]{1,0:T(8,128)(2,1)}, bf16[128,3072]{1,0:T(8,128)(2,1)S(1)}, u32[]{:S(2)}, u32[]{:S(2)}) collective-permute-start(bf16[128,3072]{1,0:T(8,128)(2,1)} %get-tuple-element.76), channel_id=1, source_target_pairs={{0,7},{1,6},{2,5},{3,4},{4,3},{5,2},{6,1},{7,0},{8,15},{9,14},{10,... | collective-permute-start | bytes 2359304 | tf_op jit(solution)/shard_map/ppermute | solution.py:533
  33.4 9.5 %copy-start.11 = (f32[5,64,128]{2,1,0:T(8,128)}, f32[5,64,128]{2,1,0:T(8,128)S(1)}, u32[]{:S(2)}) copy-start(f32[5,64,128]{2,1,0:T(8,128)S(1)} %get-tuple-element.65.refs_3_.refs_6_) | copy-start | bytes 491524
  33.4 4.8 %copy-start.9 = (bf16[1,128,4096]{2,1,0:T(8,128)(2,1)S(1)}, bf16[1,128,4096]{2,1,0:T(8,128)(2,1)}, u32[]{:S(2)}) copy-start(bf16[1,128,4096]{2,1,0:T(8,128)(2,1)} %param.9) | copy-start | bytes 3145732
  33.4 9.5 %copy-start.2 = (bf16[1,128,4096]{2,1,0:T(8,128)(2,1)S(1)}, bf16[1,128,4096]{2,1,0:T(8,128)(2,1)}, u32[]{:S(2)}) copy-start(bf16[1,128,4096]{2,1,0:T(8,128)(2,1)} %param.12) | copy-start | bytes 3145732
  34.9 0.7 copy-start.25
  35.6 0.7 copy-start.27
  36.3 29.8 %copy-start.21 = (bf16[128,2048]{1,0:T(8,128)(2,1)}, bf16[128,2048]{1,0:T(8,128)(2,1)S(1)}, u32[]{:S(2)}) copy-start(bf16[128,2048]{1,0:T(8,128)(2,1)S(1)} %get-tuple-element.63.refs_0_) | copy-start | bytes 1572868
  36.3 6.6 %copy-start.1 = (bf16[1,128,4096]{2,1,0:T(8,128)(2,1)S(1)}, bf16[1,128,4096]{2,1,0:T(8,128)(2,1)}, u32[]{:S(2)}) copy-start(bf16[1,128,4096]{2,1,0:T(8,128)(2,1)} %param.16) | copy-start | bytes 3145732
  36.3 8.6 %collective-permute-start.7 = (bf16[128,2048]{1,0:T(8,128)(2,1)S(1)}, bf16[128,2048]{1,0:T(8,128)(2,1)S(1)}, u32[]{:S(2)}, u32[]{:S(2)}) collective-permute-start(bf16[128,2048]{1,0:T(8,128)(2,1)S(1)} %get-tuple-element.63.refs_0_), channel_id=1, source_target_pairs={{6,4},{7,5},{14,12},{15,13},{22,20},{23,21},{30,28},{31,29}} | collective-permute-start | bytes 1572872 | tf_op jit(solution)/shard_map/ppermute | solution.py:527
  38.6 0.8 copy-start.13
  39.4 14.7 %collective-permute-start.10 = (bf16[2048,128]{1,0:T(8,128)(2,1)S(1)}, bf16[2048,128]{1,0:T(8,128)(2,1)S(1)}, u32[]{:S(2)}, u32[]{:S(2)}) collective-permute-start(bf16[2048,128]{1,0:T(8,128)(2,1)S(1)} %get-tuple-element.69), channel_id=1, source_target_pairs={{0,8},{8,0},{16,24},{24,16},{1,9},{9,1},{17,25},{25,17},{2,10},{10... | collective-permute-start | bytes 1572872 | tf_op jit(solution)/shard_map/ppermute | solution.py:530
  40.9 25.2 %collective-permute-start.11 = (bf16[2048,128]{1,0:T(8,128)(2,1)S(1)}, bf16[2048,128]{1,0:T(8,128)(2,1)S(1)}, u32[]{:S(2)}, u32[]{:S(2)}) collective-permute-start(bf16[2048,128]{1,0:T(8,128)(2,1)S(1)} %get-tuple-element.70), channel_id=1, source_target_pairs={{0,16},{8,24},{16,0},{24,8},{1,17},{9,25},{17,1},{25,9},{2,18},{10... | collective-permute-start | bytes 1572872 | tf_op jit(solution)/shard_map/ppermute | solution.py:530
  42.4 23.7 %collective-permute-start.12 = (bf16[2048,128]{1,0:T(8,128)(2,1)S(1)}, bf16[2048,128]{1,0:T(8,128)(2,1)S(1)}, u32[]{:S(2)}, u32[]{:S(2)}) collective-permute-start(bf16[2048,128]{1,0:T(8,128)(2,1)S(1)} %get-tuple-element.71), channel_id=1, source_target_pairs={{0,24},{8,16},{16,8},{24,0},{1,25},{9,17},{17,9},{25,1},{2,26},{10... | collective-permute-start | bytes 1572872 | tf_op jit(solution)/shard_map/ppermute | solution.py:530
  44.3 0.6 copy-start.31
  45.0 23.7 %copy-start.7 = (bf16[128,1024]{1,0:T(8,128)(2,1)S(1)}, bf16[128,1024]{1,0:T(8,128)(2,1)}, u32[]{:S(2)}) copy-start(bf16[128,1024]{1,0:T(8,128)(2,1)} %copy-done.6) | copy-start | bytes 786436
  45.0 26.8 %copy-start.4 = (bf16[128,2048]{1,0:T(8,128)(2,1)}, bf16[128,2048]{1,0:T(8,128)(2,1)S(1)}, u32[]{:S(2)}) copy-start(bf16[128,2048]{1,0:T(8,128)(2,1)S(1)} %collective-permute-done.7.refs_2_.refs_0_) | copy-start | bytes 1572868
  45.0 27.5 %collective-permute-start.19 = (bf16[128,2048]{1,0:T(8,128)(2,1)}, bf16[128,2048]{1,0:T(8,128)(2,1)}, u32[]{:S(2)}, u32[]{:S(2)}) collective-permute-start(bf16[128,2048]{1,0:T(8,128)(2,1)} %get-tuple-element.61.refs_5_), channel_id=1, source_target_pairs={{6,4},{7,5},{14,12},{15,13},{22,20},{23,21},{30,28},{31,29}} | collective-permute-start | bytes 1572872 | tf_op jit(solution)/shard_map/ppermute | solution.py:527
  54.1 17.7 %copy-start.15 = (bf16[2048,128]{1,0:T(8,128)(2,1)}, bf16[2048,128]{1,0:T(8,128)(2,1)S(1)}, u32[]{:S(2)}) copy-start(bf16[2048,128]{1,0:T(8,128)(2,1)S(1)} %collective-permute-done.10.refs_2_) | copy-start | bytes 1572868
  66.1 1.1 copy-start.17
  66.1 5.7 %copy-start.19 = (bf16[2048,128]{1,0:T(8,128)(2,1)}, bf16[2048,128]{1,0:T(8,128)(2,1)S(1)}, u32[]{:S(2)}) copy-start(bf16[2048,128]{1,0:T(8,128)(2,1)S(1)} %collective-permute-done.12.refs_4_) | copy-start | bytes 1572868
  67.2 14.0 %collective-permute-start.13 = (bf16[128,2048]{1,0:T(8,128)(2,1)}, bf16[128,2048]{1,0:T(8,128)(2,1)}, u32[]{:S(2)}, u32[]{:S(2)}) collective-permute-start(bf16[128,2048]{1,0:T(8,128)(2,1)} %shard_map.120), channel_id=1, source_target_pairs={{4,2},{5,3},{12,10},{13,11},{20,18},{21,19},{28,26},{29,27}} | collective-permute-start | bytes 1572872 | tf_op jit(solution)/shard_map/ppermute | solution.py:527
  71.8 2.0 %collective-permute-start.17 = (bf16[144,1024]{1,0:T(8,128)(2,1)}, bf16[144,1024]{1,0:T(8,128)(2,1)}, u32[]{:S(2)}, u32[]{:S(2)}) collective-permute-start(bf16[144,1024]{1,0:T(8,128)(2,1)} %get-tuple-element.79), channel_id=1, source_target_pairs={{0,1},{1,0},{2,3},{3,2},{4,5},{5,4},{6,7},{7,6},{8,9},{9,8},{10,11... | collective-permute-start | bytes 884744 | tf_op jit(solution)/shard_map/ppermute | solution.py:524
  71.9 2.3 %collective-permute-start.18 = (bf16[144,1024]{1,0:T(8,128)(2,1)}, bf16[144,1024]{1,0:T(8,128)(2,1)}, u32[]{:S(2)}, u32[]{:S(2)}) collective-permute-start(bf16[144,1024]{1,0:T(8,128)(2,1)} %get-tuple-element.80), channel_id=1, source_target_pairs={{0,1},{1,0},{2,3},{3,2},{4,5},{5,4},{6,7},{7,6},{8,9},{9,8},{10,11... | collective-permute-start | bytes 884744 | tf_op jit(solution)/shard_map/ppermute | solution.py:524
  72.4 13.1 %collective-permute-start.21 = (bf16[144,2048]{1,0:T(8,128)(2,1)}, bf16[144,2048]{1,0:T(8,128)(2,1)}, u32[]{:S(2)}, u32[]{:S(2)}) collective-permute-start(bf16[144,2048]{1,0:T(8,128)(2,1)} %get-tuple-element.78.refs_2_), channel_id=1, source_target_pairs={{0,1},{1,0},{2,3},{3,2},{4,5},{5,4},{6,7},{7,6},{8,9},{9,8},{10,11... | collective-permute-start | bytes 1769480 | tf_op jit(solution)/shard_map/ppermute | solution.py:524
  74.2 7.1 %copy-start.5 = (bf16[128,2048]{1,0:T(8,128)(2,1)S(1)}, bf16[128,2048]{1,0:T(8,128)(2,1)}, u32[]{:S(2)}) copy-start(bf16[128,2048]{1,0:T(8,128)(2,1)} %copy-done.4) | copy-start | bytes 1572868
  74.2 7.1 %copy-start.22 = (bf16[128,2048]{1,0:T(8,128)(2,1)S(1)}, bf16[128,2048]{1,0:T(8,128)(2,1)}, u32[]{:S(2)}) copy-start(bf16[128,2048]{1,0:T(8,128)(2,1)} %copy-done.21) | copy-start | bytes 1572868
  76.7 7.3 %copy-start.8 = (bf16[128,1024]{1,0:T(8,128)(2,1)S(1)}, bf16[128,1024]{1,0:T(8,128)(2,1)}, u32[]{:S(2)}) copy-start(bf16[128,1024]{1,0:T(8,128)(2,1)} %copy-done.6) | copy-start | bytes 786436
  76.7 16.0 %collective-permute-start.20 = (bf16[128,2048]{1,0:T(8,128)(2,1)S(1)}, bf16[128,2048]{1,0:T(8,128)(2,1)S(1)}, u32[]{:S(2)}, u32[]{:S(2)}) collective-permute-start(bf16[128,2048]{1,0:T(8,128)(2,1)S(1)} %get-tuple-element.83), channel_id=1, source_target_pairs={{0,2},{1,3},{4,6},{5,7},{8,10},{9,11},{12,14},{13,15},{16,18},{17,... | collective-permute-start | bytes 1572872 | tf_op jit(solution)/shard_map/ppermute | solution.py:527
  82.6 15.6 %collective-permute-start.14 = (bf16[128,2048]{1,0:T(8,128)(2,1)S(1)}, bf16[128,2048]{1,0:T(8,128)(2,1)S(1)}, u32[]{:S(2)}, u32[]{:S(2)}) collective-permute-start(bf16[128,2048]{1,0:T(8,128)(2,1)S(1)} %shard_map.121), channel_id=1, source_target_pairs={{2,0},{3,1},{10,8},{11,9},{18,16},{19,17},{26,24},{27,25}} | collective-permute-start | bytes 1572872 | tf_op jit(solution)/shard_map/ppermute | solution.py:527
  98.2 1.5 %copy-start.12 = (f32[5,64,128]{2,1,0:T(8,128)S(1)}, f32[5,64,128]{2,1,0:T(8,128)}, u32[]{:S(2)}) copy-start(f32[5,64,128]{2,1,0:T(8,128)} %copy-done.11) | copy-start | bytes 491524
  98.2 1.5 %copy-start.26 = (bf16[144,1024]{1,0:T(8,128)(2,1)S(1)}, bf16[144,1024]{1,0:T(8,128)(2,1)}, u32[]{:S(2)}) copy-start(bf16[144,1024]{1,0:T(8,128)(2,1)} %copy-done.25) | copy-start | bytes 884740
  98.2 1.5 %copy-start.28 = (bf16[144,1024]{1,0:T(8,128)(2,1)S(1)}, bf16[144,1024]{1,0:T(8,128)(2,1)}, u32[]{:S(2)}) copy-start(bf16[144,1024]{1,0:T(8,128)(2,1)} %copy-done.27) | copy-start | bytes 884740
  98.2 1.6 %copy-start.32 = (f32[128,128]{1,0:T(8,128)S(1)}, f32[128,128]{1,0:T(8,128)}, u32[]{:S(2)}) copy-start(f32[128,128]{1,0:T(8,128)} %copy-done.31) | copy-start | bytes 196612
  99.6 2.7 %collective-permute-start.22 = (bf16[128,4096]{1,0:T(8,128)(2,1)S(1)}, bf16[128,4096]{1,0:T(8,128)(2,1)S(1)}, u32[]{:S(2)}, u32[]{:S(2)}) collective-permute-start(bf16[128,4096]{1,0:T(8,128)(2,1)S(1)} %shard_map.126.refs_2_), channel_id=1, source_target_pairs={{0,1},{1,0},{2,3},{3,2},{4,5},{5,4},{6,7},{7,6},{8,9},{9,8},{10,11... | collective-permute-start | bytes 3145736 | tf_op jit(solution)/shard_map/ppermute | solution.py:524
  102.3 6.0 %copy-start.14 = (bf16[2048,128]{1,0:T(8,128)(2,1)S(1)}, bf16[2048,128]{1,0:T(8,128)(2,1)}, u32[]{:S(2)}) copy-start(bf16[2048,128]{1,0:T(8,128)(2,1)} %copy-done.13) | copy-start | bytes 1572868
  102.3 6.0 %copy-start.16 = (bf16[2048,128]{1,0:T(8,128)(2,1)S(1)}, bf16[2048,128]{1,0:T(8,128)(2,1)}, u32[]{:S(2)}) copy-start(bf16[2048,128]{1,0:T(8,128)(2,1)} %copy-done.15) | copy-start | bytes 1572868
  102.3 6.0 %copy-start.18 = (bf16[2048,128]{1,0:T(8,128)(2,1)S(1)}, bf16[2048,128]{1,0:T(8,128)(2,1)}, u32[]{:S(2)}) copy-start(bf16[2048,128]{1,0:T(8,128)(2,1)} %copy-done.17) | copy-start | bytes 1572868
  102.3 6.0 %copy-start.20 = (bf16[2048,128]{1,0:T(8,128)(2,1)S(1)}, bf16[2048,128]{1,0:T(8,128)(2,1)}, u32[]{:S(2)}) copy-start(bf16[2048,128]{1,0:T(8,128)(2,1)} %copy-done.19) | copy-start | bytes 1572868
  104.7 8.0 %collective-permute-start.25 = (bf16[128,128]{1,0:T(8,128)(2,1)S(1)}, bf16[128,128]{1,0:T(8,128)(2,1)S(1)}, u32[]{:S(2)}, u32[]{:S(2)}) collective-permute-start(bf16[128,128]{1,0:T(8,128)(2,1)S(1)} %get-tuple-element.93.refs_5_), channel_id=1, source_target_pairs={{0,24},{8,16},{16,8},{24,0},{1,25},{9,17},{17,9},{25,1},{2,26},{10... | collective-permute-start | bytes 98312 | tf_op jit(solution)/shard_map/ppermute | solution.py:530
  106.3 6.4 %collective-permute-start.24 = (bf16[128,128]{1,0:T(8,128)(2,1)S(1)}, bf16[128,128]{1,0:T(8,128)(2,1)S(1)}, u32[]{:S(2)}, u32[]{:S(2)}) collective-permute-start(bf16[128,128]{1,0:T(8,128)(2,1)S(1)} %get-tuple-element.93.refs_5_), channel_id=1, source_target_pairs={{0,16},{8,24},{16,0},{24,8},{1,17},{9,25},{17,1},{25,9},{2,18},{10... | collective-permute-start | bytes 98312 | tf_op jit(solution)/shard_map/ppermute | solution.py:530
  107.9 4.8 %collective-permute-start.23 = (bf16[128,128]{1,0:T(8,128)(2,1)S(1)}, bf16[128,128]{1,0:T(8,128)(2,1)S(1)}, u32[]{:S(2)}, u32[]{:S(2)}) collective-permute-start(bf16[128,128]{1,0:T(8,128)(2,1)S(1)} %get-tuple-element.93.refs_5_), channel_id=1, source_target_pairs={{0,8},{8,0},{16,24},{24,16},{1,9},{9,1},{17,25},{25,17},{2,10},{10... | collective-permute-start | bytes 98312 | tf_op jit(solution)/shard_map/ppermute | solution.py:530
  108.3 1.2 copy-start.10
  113.2 1.4 %collective-permute-start.26 = (bf16[4,128,128]{2,1,0:T(8,128)(2,1)S(1)}, bf16[4,128,128]{2,1,0:T(8,128)(2,1)S(1)}, u32[]{:S(2)}, u32[]{:S(2)}) collective-permute-start(bf16[4,128,128]{2,1,0:T(8,128)(2,1)S(1)} %get-tuple-element.97), channel_id=1, source_target_pairs={{0,1},{1,0},{2,3},{3,2},{4,5},{5,4},{6,7},{7,6},{8,9},{9,8},{10,11... | collective-permute-start | bytes 393224 | tf_op jit(solution)/shard_map/ppermute | solution.py:524
  114.6 7.7 %collective-permute-start.28 = (bf16[128,128]{1,0:T(8,128)(2,1)S(1)}, bf16[128,128]{1,0:T(8,128)(2,1)S(1)}, u32[]{:S(2)}, u32[]{:S(2)}) collective-permute-start(bf16[128,128]{1,0:T(8,128)(2,1)S(1)} %get-tuple-element.101), channel_id=1, source_target_pairs={{0,4},{1,5},{2,6},{3,7},{4,0},{5,1},{6,2},{7,3},{8,12},{9,13},{10,... | collective-permute-start | bytes 98312 | tf_op jit(solution)/shard_map/ppermute | solution.py:721
  114.7 7.6 %collective-permute-start.29 = (bf16[128,128]{1,0:T(8,128)(2,1)S(1)}, bf16[128,128]{1,0:T(8,128)(2,1)S(1)}, u32[]{:S(2)}, u32[]{:S(2)}) collective-permute-start(bf16[128,128]{1,0:T(8,128)(2,1)S(1)} %get-tuple-element.102), channel_id=1, source_target_pairs={{0,6},{1,7},{2,4},{3,5},{4,2},{5,3},{6,0},{7,1},{8,14},{9,15},{10,... | collective-permute-start | bytes 98312 | tf_op jit(solution)/shard_map/ppermute | solution.py:721
  116.6 5.7 %collective-permute-start.27 = (bf16[128,128]{1,0:T(8,128)(2,1)S(1)}, bf16[128,128]{1,0:T(8,128)(2,1)S(1)}, u32[]{:S(2)}, u32[]{:S(2)}) collective-permute-start(bf16[128,128]{1,0:T(8,128)(2,1)S(1)} %get-tuple-element.98), channel_id=1, source_target_pairs={{0,2},{1,3},{2,0},{3,1},{4,6},{5,7},{6,4},{7,5},{8,10},{9,11},{10,... | collective-permute-start | bytes 98312 | tf_op jit(solution)/shard_map/ppermute | solution.py:721

commit v5 on v4

--- a/solution.py
+++ b/solution.py
@@ -14,14 +14,15 @@
 LOG2E = 1.4426950408889634
 LOW = -1e30
 EXACT = lax.Precision.HIGHEST
-VMEM_BYTES = 9 * 1024 * 1024
+VMEM_BYTES = 8 * 1024 * 1024
+COSTLY = 10**10
 CUT = 1024
 PIECES = 2
 
 f32 = jnp.float32
 bf16 = jnp.bfloat16
 
-CUM2, EXCLR2, FWD_EDGE, BACK_EDGE, STEP = range(5)
+CUM2, EXCLR2, FWD_EDGE, BACK_EDGE, STEP, BACK_WEIGHT = range(6)
 C_MIX_FWD, C_MIX_BACK, C_CUM2, C_EXCL2 = range(4)
 
 
@@ -104,7 +105,7 @@
     return dot_tn(both, pick)
 
 
-def tables_kernel(read_ref, decay_ref, step_ref, readr_ref, rows_ref, cols_ref):
+def tables_kernel(read_ref, decay_ref, step_ref, readr_ref, readt_ref, rows_ref, cols_ref):
     decay = decay_ref[...]
     heads, n = decay.shape
     r, c = iotas((n, n))
@@ -113,6 +114,7 @@
     readr_ref[...] = jnp.dot(
         flip.astype(bf16), read_ref[...], preferred_element_type=f32
     ).astype(bf16)
+    readt_ref[...] = dot_tn(read_ref[...], flip.astype(bf16)).astype(bf16)
     cum = jnp.dot(decay, upto, precision=EXACT, preferred_element_type=f32)
     decay_r = jnp.dot(decay, flip, precision=EXACT, preferred_element_type=f32)
     cum_r = jnp.dot(decay_r, upto, precision=EXACT, preferred_element_type=f32)
@@ -127,6 +129,7 @@
     rows_ref[FWD_EDGE] = step * jnp.exp(end - cum)
     rows_ref[BACK_EDGE] = step * jnp.exp(excl)
     rows_ref[STEP] = step
+    rows_ref[BACK_WEIGHT] = jnp.exp(cum_r)
     planes = (cum2 - log_step, excl2 + log_step, cum2, excl2)
     rest = jnp.zeros((LANES - GROUP * len(planes), n), f32)
     for g in range(heads // GROUP):
@@ -164,14 +167,17 @@
     heads, n = decay_ref.shape
     width = sum(ref.shape[1] for ref in g_refs) // heads
     step = GROUP * width
-    r, c = iotas((n, n))
-    order = ((r + c == n - 1) if backward else (r == c)).astype(f32)
-    upto = (r <= c).astype(f32)
-    read_t = dot_tn(read_ref[...].astype(bf16), order.astype(bf16)).astype(bf16)
-    decay = decay_ref[...]
-    if backward:
-        decay = jnp.dot(decay, order, precision=EXACT, preferred_element_type=f32)
-    weight = jnp.exp(jnp.dot(decay, upto, precision=EXACT, preferred_element_type=f32))
+    if backward is None:
+        read_t, weight = read_ref[...], decay_ref[...]
+    else:
+        r, c = iotas((n, n))
+        order = ((r + c == n - 1) if backward else (r == c)).astype(f32)
+        upto = (r <= c).astype(f32)
+        read_t = dot_tn(read_ref[...].astype(bf16), order.astype(bf16)).astype(bf16)
+        decay = decay_ref[...]
+        if backward:
+            decay = jnp.dot(decay, order, precision=EXACT, preferred_element_type=f32)
+        weight = jnp.exp(jnp.dot(decay, upto, precision=EXACT, preferred_element_type=f32))
     state = read_t.shape[0]
     groups = heads // GROUP
     tail_row, _ = iotas((16, step))
@@ -561,13 +567,14 @@
     early_near = [over_cores(send) for send in sends]
     ((right_own, *sends),) = run(part_job(False, [gf], read, decay))
     right_near = [over_cores(send) for send in sends]
-    (early_term, early_decay), (read_r, rows, cols) = run(
+    (early_term, early_decay), (read_r, read_t, rows, cols) = run(
         chip_job(False, early_own, early_near),
         job(
             tables_kernel,
             [
                 sds((n, state), bf16),
-                sds((5, heads, n), f32),
+                sds((state, n), bf16),
+                sds((6, heads, n), f32),
                 sds((heads // GROUP, n, LANES), f32),
             ],
             read,
@@ -615,7 +622,9 @@
     )
     rights.append(over_chips(leaving, (chips - 2, chips - 3)))
 
-    ((left_own, *sends),) = run(part_job(True, flips, read, decay), after=(leaving,))
+    ((left_own, *sends),) = run(
+        part_job(None, flips, read_t, rows[BACK_WEIGHT]), after=(leaving,), flops=COSTLY
+    )
     left_near = [over_cores(send) for send in sends]
     lefts = []
     for i in range(span - 1):

time: 124 us -> 123 us (level)
    unnamed x68 -> x66, local copies, waits for them, and re-layouts: 7.52 us -> 6.89 us
  transfers between devices with their start and end apart: 30 -> 30, of which waited for: 10 -> 10; matrix products, arithmetic and copies ran while one was open for 2% -> 2% of each run, Pallas kernels for 24% -> 23%
where the time goes in v5:
time: 123 us
  waiting for transfers between devices  42.9 us (35%)
  Pallas kernels  33 us (27%)
  starting transfers between devices  32.7 us (27%)
  local copies, waits for them, and re-layouts  7.53 us (6%)
  other arithmetic  2.96 us (2%)
  matrix products  1.83 us (1%)
  between operations  1.66 us (1%)
    pallas_call x20, Pallas kernels, run(): pl.pallas_call(kernel, out_shape=outs, in_specs=specs, out_specs=[vmem] *...  27.6 us
    ppermute x6, waiting for transfers between devices, over_dp(): return lax.ppermute(array, 'dp', xor_pairs(dp_count, k))  19.5 us
    ppermute x5, waiting for transfers between devices, over_chips(): return lax.ppermute(array, 'ctx', chip_pairs(moves))  12.9 us
    ppermute x5, starting transfers between devices, over_chips(): return lax.ppermute(array, 'ctx', chip_pairs(moves))  9.87 us
    ppermute x3, starting transfers between devices, flip(): lax.ppermute(piece, 'ctx', [(i, ctx_count - 1 - i) for i in range(ctx_cou...  9.17 us
    ppermute x6, starting transfers between devices, over_dp(): return lax.ppermute(array, 'dp', xor_pairs(dp_count, k))  7.04 us
    unnamed x66, local copies, waits for them, and re-layouts  6.89 us
    pallas_call x2, Pallas kernels, run_on_half(): pl.pallas_call(kernel, grid=(1,), out_shape=shape, in_specs=[smem] + [vme...  5.43 us
  transfers between devices with their start and end apart: 30, of which 10 were waited for; matrix products, arithmetic and copies ran while one was open for 2% of the time, Pallas kernels for 23%

profile of v5, /device:TPU:0, one launch (start us, length us, event | category | flops | bytes accessed | tf_op | source)
XLA Modules:
  0.0 122.7 jit_solution(2973306635434856194)
XLA Ops:
  1.3 0.8 bitcast_convert_fusion
  2.0 0.8 fusion.3
  2.8 0.8 pad_maximum_fusion
  3.6 4.6 %collective-permute-start.2 = (f32[320,128]{1,0:T(8,128)S(1)}, f32[320,128]{1,0:T(8,128)S(1)}, u32[]{:S(2)}, u32[]{:S(2)}) collective-permute-start(f32[320,128]{1,0:T(8,128)S(1)} %pad_maximum_fusion), channel_id=1, source_target_pairs={{0,7},{1,6},{2,5},{3,4},{4,3},{5,2},{6,1},{7,0},{8,15},{9,14},{10,... | collective-permute-start | bytes 491528 | tf_op jit(solution)/shard_map/ppermute | solution.py:539
  8.1 1.2 collective-permute-start.3
  9.4 1.2 copy-done
  10.6 0.8 copy-done.23
  11.3 0.8 copy-done.29
  12.1 2.9 %shard_map.112 = (bf16[144,2048]{1,0:T(8,128)(2,1)}, bf16[144,1024]{1,0:T(8,128)(2,1)}, bf16[144,1024]{1,0:T(8,128)(2,1)}) custom-call(s32[1]{0:T(128)} %bitcast.refs_0_.refs_1_, bf16[128,4096]{1,0:T(8,128)(2,1)S(1)} %bitcast.32, bf16[128,128]{1,0:T(8,128)(2,1)S(1)} %bitcast.46, f32[64,128]{1,0:T(8,128)S(1)} %bitcast.53), custom_call_target="tpu_custom_call" | custom-call | tf_op jit(solution)/shard_map/pallas_call | solution.py:54
  15.0 2.6 %collective-permute-done.4.refs_2_ = bf16[128,128]{1,0:T(8,128)(2,1)S(1)} collective-permute-done((bf16[128,128]{1,0:T(8,128)(2,1)S(1)}, bf16[128,128]{1,0:T(8,128)(2,1)S(1)}, u32[]{:S(2)}, u32[]{:S(2)}) %collective-permute-start.4) | collective-permute-done | bytes 32800 | tf_op jit(solution)/shard_map/ppermute | solution.py:544
  17.5 0.9 shard_map.122
  18.5 2.2 %collective-permute-start.15 = (bf16[128,1024]{1,0:T(8,128)(2,1)S(1)}, bf16[128,1024]{1,0:T(8,128)(2,1)S(1)}, u32[]{:S(2)}, u32[]{:S(2)}) collective-permute-start(bf16[128,1024]{1,0:T(8,128)(2,1)S(1)} %get-tuple-element.75), channel_id=1, source_target_pairs={{0,7},{1,6},{2,5},{3,4},{4,3},{5,2},{6,1},{7,0},{8,15},{9,14},{10,... | collective-permute-start | bytes 786440 | tf_op jit(solution)/shard_map/ppermute | solution.py:539
  20.7 0.7 shard_map.113.refs_2_
  21.4 2.2 %shard_map.114 = (bf16[144,2048]{1,0:T(8,128)(2,1)S(1)}, bf16[144,1024]{1,0:T(8,128)(2,1)S(1)}, bf16[144,1024]{1,0:T(8,128)(2,1)S(1)}) custom-call(s32[1]{0:T(128)} %bitcast.refs_0_.refs_1_, bf16[128,4096]{1,0:T(8,128)(2,1)S(1)} %bitcast.42, f32[128,128]{1,0:T(8,128)S(1)} %get-tuple-element.111.refs_2_, f32[64,128]{1,0:T(8,128)S(1)} %slice.25.refs_3_), custom_call_target="tpu_custom_call" | custom-call | tf_op jit(solution)/shard_map/pallas_call | solution.py:54
  23.5 0.5 collective-permute-start.5
  24.1 0.4 collective-permute-start.1
  24.5 4.3 %collective-permute-done.15.refs_1_.refs_0_.refs_11_ = bf16[128,1024]{1,0:T(8,128)(2,1)S(1)} collective-permute-done((bf16[128,1024]{1,0:T(8,128)(2,1)S(1)}, bf16[128,1024]{1,0:T(8,128)(2,1)S(1)}, u32[]{:S(2)}, u32[]{:S(2)}) %collective-permute-start.15) | collective-permute-done | bytes 262176 | tf_op jit(solution)/shard_map/ppermute | solution.py:539
  28.8 0.7 copy-done.10
  29.6 2.4 %collective-permute-start.16 = (bf16[128,3072]{1,0:T(8,128)(2,1)}, bf16[128,3072]{1,0:T(8,128)(2,1)S(1)}, u32[]{:S(2)}, u32[]{:S(2)}) collective-permute-start(bf16[128,3072]{1,0:T(8,128)(2,1)} %get-tuple-element.77), channel_id=1, source_target_pairs={{0,7},{1,6},{2,5},{3,4},{4,3},{5,2},{6,1},{7,0},{8,15},{9,14},{10,... | collective-permute-start | bytes 2359304 | tf_op jit(solution)/shard_map/ppermute | solution.py:539
  32.2 1.2 %shard_map.115 = (bf16[128,2048]{1,0:T(8,128)(2,1)}, f32[1,2048]{1,0:T(1,128)S(1)}, bf16[128,128]{1,0:T(8,128)(2,1)S(1)}, bf16[128,128]{1,0:T(8,128)(2,1)S(1)}, ...) custom-call(s32[1]{0:T(128)} %bitcast.refs_0_.refs_1_, bf16[144,2048]{1,0:T(8,128)(2,1)S(1)} %get-tuple-element.58.refs_1_, ...), custom_call_target="tpu_custom_call" | custom-call | tf_op jit(solution)/shard_map/pallas_call | solution.py:54
  33.4 1.5 %shard_map.116 = (bf16[128,2048]{1,0:T(8,128)(2,1)S(1)}, f32[1,2048]{1,0:T(1,128)S(1)}) custom-call(s32[1]{0:T(128)} %bitcast.refs_0_.refs_1_, bf16[144,2048]{1,0:T(8,128)(2,1)} %get-tuple-element.54.refs_1_, bf16[144,1024]{1,0:T(8,128)(2,1)S(1)} %collective-permute-done.refs_2_.refs_8_, bf16[144,1024]{1,0:T(8,128)(2,1)S(1)} %collective-permute-done.1.refs_3_.refs_9_), custom_call_target="tpu_custom_call" | custom-call | tf_op jit(solution)/shard_map/pallas_call | solution.py:54
  34.9 0.7 copy-done.25
  35.6 0.7 copy-done.27
  36.3 0.8 collective-permute-start.7
  37.2 1.0 shard_map.118
  38.2 0.4 shard_map.119
  38.6 0.8 copy-done.13
  39.4 1.5 %collective-permute-start.10 = (bf16[2048,128]{1,0:T(8,128)(2,1)S(1)}, bf16[2048,128]{1,0:T(8,128)(2,1)S(1)}, u32[]{:S(2)}, u32[]{:S(2)}) collective-permute-start(bf16[2048,128]{1,0:T(8,128)(2,1)S(1)} %get-tuple-element.70), channel_id=1, source_target_pairs={{0,8},{8,0},{16,24},{24,16},{1,9},{9,1},{17,25},{25,17},{2,10},{10... | collective-permute-start | bytes 1572872 | tf_op jit(solution)/shard_map/ppermute | solution.py:536
  40.9 1.5 %collective-permute-start.11 = (bf16[2048,128]{1,0:T(8,128)(2,1)S(1)}, bf16[2048,128]{1,0:T(8,128)(2,1)S(1)}, u32[]{:S(2)}, u32[]{:S(2)}) collective-permute-start(bf16[2048,128]{1,0:T(8,128)(2,1)S(1)} %get-tuple-element.71), channel_id=1, source_target_pairs={{0,16},{8,24},{16,0},{24,8},{1,17},{9,25},{17,1},{25,9},{2,18},{10... | collective-permute-start | bytes 1572872 | tf_op jit(solution)/shard_map/ppermute | solution.py:536
  42.4 0.5 collective-permute-start.12
  42.9 0.6 slice_bitcast_fusion
  43.5 1.4 %shard_map.117.refs_4_ = f32[128,128]{1,0:T(8,128)S(1)} custom-call(bf16[128,4096]{1,0:T(8,128)(2,1)S(1)} %bitcast.33, bf16[128,4096]{1,0:T(8,128)(2,1)S(1)} %bitcast.36, f32[64,128]{1,0:T(8,128)S(1)} %get-tuple-element.109.refs_2_, f32[8,128,128]{2,1,0:T(8,128)S(1)} %get-tuple-element.86.refs_3_.refs_4_.refs_7_), custom_call_target="tpu_custom_call" | custom-call | tf_op jit(solution)/shard_map/pallas_call | solution.py:54
  45.0 1.6 %collective-permute-start.19 = (bf16[128,2048]{1,0:T(8,128)(2,1)}, bf16[128,2048]{1,0:T(8,128)(2,1)}, u32[]{:S(2)}, u32[]{:S(2)}) collective-permute-start(bf16[128,2048]{1,0:T(8,128)(2,1)} %get-tuple-element.62.refs_5_), channel_id=1, source_target_pairs={{6,4},{7,5},{14,12},{15,13},{22,20},{23,21},{30,28},{31,29}} | collective-permute-start | bytes 1572872 | tf_op jit(solution)/shard_map/ppermute | solution.py:533
  46.6 7.5 %collective-permute-done.10.refs_2_ = bf16[2048,128]{1,0:T(8,128)(2,1)S(1)} collective-permute-done((bf16[2048,128]{1,0:T(8,128)(2,1)S(1)}, bf16[2048,128]{1,0:T(8,128)(2,1)S(1)}, u32[]{:S(2)}, u32[]{:S(2)}) %collective-permute-start.10) | collective-permute-done | bytes 524320 | tf_op jit(solution)/shard_map/ppermute | solution.py:536
  54.1 12.0 %collective-permute-done.11.refs_3_ = bf16[2048,128]{1,0:T(8,128)(2,1)S(1)} collective-permute-done((bf16[2048,128]{1,0:T(8,128)(2,1)S(1)}, bf16[2048,128]{1,0:T(8,128)(2,1)S(1)}, u32[]{:S(2)}, u32[]{:S(2)}) %collective-permute-start.11) | collective-permute-done | bytes 524320 | tf_op jit(solution)/shard_map/ppermute | solution.py:536
  66.1 1.1 shard_map.120
  67.2 1.5 %collective-permute-start.13 = (bf16[128,2048]{1,0:T(8,128)(2,1)}, bf16[128,2048]{1,0:T(8,128)(2,1)}, u32[]{:S(2)}, u32[]{:S(2)}) collective-permute-start(bf16[128,2048]{1,0:T(8,128)(2,1)} %shard_map.120), channel_id=1, source_target_pairs={{4,2},{5,3},{12,10},{13,11},{20,18},{21,19},{28,26},{29,27}} | collective-permute-start | bytes 1572872 | tf_op jit(solution)/shard_map/ppermute | solution.py:533
  68.7 2.7 %shard_map.123 = (bf16[144,2048]{1,0:T(8,128)(2,1)}, bf16[144,1024]{1,0:T(8,128)(2,1)}, bf16[144,1024]{1,0:T(8,128)(2,1)}) custom-call(s32[1]{0:T(128)} %bitcast.refs_0_.refs_1_, bf16[128,1024]{1,0:T(8,128)(2,1)S(1)} %copy-done.11, bf16[128,3072]{1,0:T(8,128)(2,1)S(1)} %collective-permute-done.16.refs_2_.refs_1_.refs_12_, ...), custom_call_target="tpu_custom_call" | custom-call | flops 10000000000 | bytes 40000000 | tf_op jit(solution)/shard_map/pallas_call | solution.py:54
  71.5 0.5 collective-permute-start.18
  72.0 1.3 %collective-permute-done.17.refs_3_.refs_10_ = bf16[144,1024]{1,0:T(8,128)(2,1)} collective-permute-done((bf16[144,1024]{1,0:T(8,128)(2,1)}, bf16[144,1024]{1,0:T(8,128)(2,1)}, u32[]{:S(2)}, u32[]{:S(2)}) %collective-permute-start.17) | collective-permute-done | bytes 294944 | tf_op jit(solution)/shard_map/ppermute | solution.py:530
  73.4 0.4 collective-permute-done.18.refs_4_.refs_11_
  73.8 2.5 %shard_map.124 = (bf16[128,2048]{1,0:T(8,128)(2,1)S(1)}, bf16[128,2048]{1,0:T(8,128)(2,1)S(1)}) custom-call(s32[1]{0:T(128)} %bitcast.refs_0_.refs_1_, s32[1]{0:T(128)} %bitcast.13.refs_1_, bf16[144,2048]{1,0:T(8,128)(2,1)} %get-tuple-element.80.refs_2_, bf16[144,1024]{1,0:T(8,128)(2,1)} %collective-permute-done.17.refs_3_.refs_10_, ...), custom_call_target="tpu_custom_call" | custom-call | tf_op jit(solution)/shard_map/pallas_call | solution.py:54
  76.3 4.5 %collective-permute-start.20 = (bf16[128,2048]{1,0:T(8,128)(2,1)S(1)}, bf16[128,2048]{1,0:T(8,128)(2,1)S(1)}, u32[]{:S(2)}, u32[]{:S(2)}) collective-permute-start(bf16[128,2048]{1,0:T(8,128)(2,1)S(1)} %get-tuple-element.85), channel_id=1, source_target_pairs={{0,2},{1,3},{4,6},{5,7},{8,10},{9,11},{12,14},{13,15},{16,18},{17,... | collective-permute-start | bytes 1572872 | tf_op jit(solution)/shard_map/ppermute | solution.py:533
  80.8 1.3 %shard_map.121 = bf16[128,2048]{1,0:T(8,128)(2,1)S(1)} custom-call(bf16[128,2048]{1,0:T(8,128)(2,1)S(1)} %copy-done.22, f32[1,2048]{1,0:T(1,128)S(1)} %get-tuple-element.65.refs_1_, bf16[128,2048]{1,0:T(8,128)(2,1)S(1)} %copy-done.5, bf16[128,2048]{1,0:T(8,128)(2,1)} %collective-permute-done.13.refs_3_.refs_1_), custom_call_target="tpu_custom_call" | custom-call | tf_op jit(solution)/shard_map/pallas_call | solution.py:54
  82.1 1.5 %collective-permute-start.14 = (bf16[128,2048]{1,0:T(8,128)(2,1)S(1)}, bf16[128,2048]{1,0:T(8,128)(2,1)S(1)}, u32[]{:S(2)}, u32[]{:S(2)}) collective-permute-start(bf16[128,2048]{1,0:T(8,128)(2,1)S(1)} %shard_map.121), channel_id=1, source_target_pairs={{2,0},{3,1},{10,8},{11,9},{18,16},{19,17},{26,24},{27,25}} | collective-permute-start | bytes 1572872 | tf_op jit(solution)/shard_map/ppermute | solution.py:533
  83.6 1.4 %shard_map.125.refs_5_ = f32[128,128]{1,0:T(8,128)S(1)} custom-call(bf16[128,1024]{1,0:T(8,128)(2,1)S(1)} %copy-done.12, bf16[128,3072]{1,0:T(8,128)(2,1)S(1)} %collective-permute-done.16.refs_2_.refs_1_.refs_12_, bf16[128,4096]{1,0:T(8,128)(2,1)S(1)} %bitcast.37, f32[64,128]{1,0:T(8,128)S(1)} %copy-done.31, ...), custom_call_target="tpu_custom_call" | custom-call | tf_op jit(solution)/shard_map/pallas_call | solution.py:54
  85.0 7.2 %collective-permute-done.20.refs_4_ = bf16[128,2048]{1,0:T(8,128)(2,1)S(1)} collective-permute-done((bf16[128,2048]{1,0:T(8,128)(2,1)S(1)}, bf16[128,2048]{1,0:T(8,128)(2,1)S(1)}, u32[]{:S(2)}, u32[]{:S(2)}) %collective-permute-start.20) | collective-permute-done | bytes 524320 | tf_op jit(solution)/shard_map/ppermute | solution.py:533
  92.2 5.6 %collective-permute-done.14.refs_2_ = bf16[128,2048]{1,0:T(8,128)(2,1)S(1)} collective-permute-done((bf16[128,2048]{1,0:T(8,128)(2,1)S(1)}, bf16[128,2048]{1,0:T(8,128)(2,1)S(1)}, u32[]{:S(2)}, u32[]{:S(2)}) %collective-permute-start.14) | collective-permute-done | bytes 524320 | tf_op jit(solution)/shard_map/ppermute | solution.py:533
  97.9 1.4 %shard_map.126.refs_2_ = bf16[128,4096]{1,0:T(8,128)(2,1)S(1)} custom-call(bf16[128,2048]{1,0:T(8,128)(2,1)S(1)} %copy-done.5, bf16[128,2048]{1,0:T(8,128)(2,1)} %collective-permute-done.13.refs_3_.refs_1_, bf16[128,2048]{1,0:T(8,128)(2,1)S(1)} %collective-permute-done.14.refs_2_, bf16[128,2048]{1,0:T(8,128)(2,1)S(1)} %get-tuple-element.84.refs_3_, ...), custom_call_target="tpu_custom_call" | custom-call | tf_op jit(solution)/shard_map/pallas_call | solution.py:54
  99.4 2.1 %shard_map.127 = (bf16[128,2048]{1,0:T(8,128)(2,1)S(1)}, bf16[128,2048]{1,0:T(8,128)(2,1)S(1)}, f32[128,128]{1,0:T(8,128)S(1)}) custom-call(s32[1]{0:T(128)} %bitcast.refs_0_.refs_1_, bf16[128,4096]{1,0:T(8,128)(2,1)S(1)} %bitcast.38, bf16[128,4096]{1,0:T(8,128)(2,1)S(1)} %shard_map.126.refs_2_, f32[6,64,128]{2,1,0:T(8,128)S(1)} %copy-done.9, ...), custom_call_target="tpu_custom_call" | custom-call | tf_op jit(solution)/shard_map/pallas_call | solution.py:54
  101.5 0.5 collective-permute-done.22.refs_2_
  102.1 2.4 %shard_map.128 = (bf16[128,2048]{1,0:T(8,128)(2,1)S(1)}, bf16[128,2048]{1,0:T(8,128)(2,1)S(1)}, bf16[128,128]{1,0:T(8,128)(2,1)S(1)}) custom-call(s32[1]{0:T(128)} %bitcast.refs_0_.refs_1_, bf16[128,4096]{1,0:T(8,128)(2,1)S(1)} %bitcast.39, bf16[128,4096]{1,0:T(8,128)(2,1)S(1)} %collective-permute-done.22.refs_2_, f32[6,64,128]{2,1,0:T(8,128)S(1)} %copy-done.9, ...), custom_call_target="tpu_custom_call" | custom-call | tf_op jit(solution)/shard_map/pallas_call | solution.py:54
  104.5 1.4 %collective-permute-start.25 = (bf16[128,128]{1,0:T(8,128)(2,1)S(1)}, bf16[128,128]{1,0:T(8,128)(2,1)S(1)}, u32[]{:S(2)}, u32[]{:S(2)}) collective-permute-start(bf16[128,128]{1,0:T(8,128)(2,1)S(1)} %get-tuple-element.95.refs_5_), channel_id=1, source_target_pairs={{0,24},{8,16},{16,8},{24,0},{1,25},{9,17},{17,9},{25,1},{2,26},{10... | collective-permute-start | bytes 98312 | tf_op jit(solution)/shard_map/ppermute | solution.py:536
  105.9 1.9 %collective-permute-start.24 = (bf16[128,128]{1,0:T(8,128)(2,1)S(1)}, bf16[128,128]{1,0:T(8,128)(2,1)S(1)}, u32[]{:S(2)}, u32[]{:S(2)}) collective-permute-start(bf16[128,128]{1,0:T(8,128)(2,1)S(1)} %get-tuple-element.95.refs_5_), channel_id=1, source_target_pairs={{0,16},{8,24},{16,0},{24,8},{1,17},{9,25},{17,1},{25,9},{2,18},{10... | collective-permute-start | bytes 98312 | tf_op jit(solution)/shard_map/ppermute | solution.py:536
  108.1 1.1 copy-done.7
  109.3 0.4 fusion.1.refs_8_
  109.7 2.7 %shard_map.130.refs_13_ = bf16[128,4096]{1,0:T(8,128)(2,1)} custom-call(s32[1]{0:T(128)} %bitcast.refs_0_.refs_1_, bf16[128,4096]{1,0:T(8,128)(2,1)S(1)} %bitcast.34, bf16[128,2048]{1,0:T(8,128)(2,1)S(1)} %get-tuple-element.89.refs_2_, bf16[128,2048]{1,0:T(8,128)(2,1)S(1)} %get-tuple-element.91.refs_3_, bf16[128,2048]{1,0:T(8,128)(2,1)S(1)} %get-tuple-element.92.refs_4_, ...), custom_call_target="tpu_custom_call" | custom-call | tf_op jit(solution)/shard_map/pallas_call | solution.py:76
  112.4 0.4 shard_map.131
  113.0 1.3 %collective-permute-done.26.refs_2_ = bf16[4,128,128]{2,1,0:T(8,128)(2,1)S(1)} collective-permute-done((bf16[4,128,128]{2,1,0:T(8,128)(2,1)S(1)}, bf16[4,128,128]{2,1,0:T(8,128)(2,1)S(1)}, u32[]{:S(2)}, u32[]{:S(2)}) %collective-permute-start.26) | collective-permute-done | bytes 131104 | tf_op jit(solution)/shard_map/ppermute | solution.py:530
  114.4 1.9 %collective-permute-start.29 = (bf16[128,128]{1,0:T(8,128)(2,1)S(1)}, bf16[128,128]{1,0:T(8,128)(2,1)S(1)}, u32[]{:S(2)}, u32[]{:S(2)}) collective-permute-start(bf16[128,128]{1,0:T(8,128)(2,1)S(1)} %get-tuple-element.104), channel_id=1, source_target_pairs={{0,6},{1,7},{2,4},{3,5},{4,2},{5,3},{6,0},{7,1},{8,14},{9,15},{10,... | collective-permute-start | bytes 98312 | tf_op jit(solution)/shard_map/ppermute | solution.py:730
  116.3 1.6 %collective-permute-start.27 = (bf16[128,128]{1,0:T(8,128)(2,1)S(1)}, bf16[128,128]{1,0:T(8,128)(2,1)S(1)}, u32[]{:S(2)}, u32[]{:S(2)}) collective-permute-start(bf16[128,128]{1,0:T(8,128)(2,1)S(1)} %get-tuple-element.100), channel_id=1, source_target_pairs={{0,2},{1,3},{2,0},{3,1},{4,6},{5,7},{6,4},{7,5},{8,10},{9,11},{10,... | collective-permute-start | bytes 98312 | tf_op jit(solution)/shard_map/ppermute | solution.py:730
  117.9 1.4 %fusion = bf16[1,128,4096]{2,1,0:T(8,128)(2,1)} fusion(bf16[128,128]{1,0:T(8,128)(2,1)S(1)} %get-tuple-element.95.refs_5_, bf16[4096,128]{1,0:T(8,128)(2,1)S(1)} %bitcast.44), kind=kOutput, calls=%fused_computation.1 | convolution fusion | flops 134742016 | bytes 2129920 | tf_op jit(solution)/shard_map/dot_general | solution.py:93
  119.3 2.7 %shard_map.133 = bf16[128,4096]{1,0:T(8,128)(2,1)} custom-call(s32[1]{0:T(128)} %bitcast.refs_0_.refs_1_, bf16[128,4096]{1,0:T(8,128)(2,1)S(1)} %bitcast.35, bf16[128,2048]{1,0:T(8,128)(2,1)S(1)} %get-tuple-element.89.refs_2_, bf16[128,2048]{1,0:T(8,128)(2,1)S(1)} %get-tuple-element.91.refs_3_, ...), custom_call_target="tpu_custom_call", output_to_operand_aliasing={{}: (13, {})} | custom-call | tf_op jit(solution)/shard_map/pallas_call | solution.py:76
  122.0 0.7 add_multiply_fusion
  (93 shorter events, 1.1 us)
Async XLA Ops:
  3.6 13.9 %collective-permute-start.2 = (f32[320,128]{1,0:T(8,128)S(1)}, f32[320,128]{1,0:T(8,128)S(1)}, u32[]{:S(2)}, u32[]{:S(2)}) collective-permute-start(f32[320,128]{1,0:T(8,128)S(1)} %pad_maximum_fusion), channel_id=1, source_target_pairs={{0,7},{1,6},{2,5},{3,4},{4,3},{5,2},{6,1},{7,0},{8,15},{9,14},{10,... | collective-permute-start | bytes 491528 | tf_op jit(solution)/shard_map/ppermute | solution.py:539
  8.1 9.4 %collective-permute-start.4 = (bf16[128,128]{1,0:T(8,128)(2,1)S(1)}, bf16[128,128]{1,0:T(8,128)(2,1)S(1)}, u32[]{:S(2)}, u32[]{:S(2)}) collective-permute-start(bf16[128,128]{1,0:T(8,128)(2,1)S(1)} %get-tuple-element.106.refs_0_), channel_id=1, source_target_pairs={{0,4},{1,5},{2,6},{3,7},{4,0},{5,1},{6,2},{7,3},{8,12},{9,13},{10,... | collective-permute-start | bytes 98312 | tf_op jit(solution)/shard_map/ppermute | solution.py:544
  8.1 9.4 %collective-permute-start.3 = (bf16[128,128]{1,0:T(8,128)(2,1)S(1)}, bf16[128,128]{1,0:T(8,128)(2,1)S(1)}, u32[]{:S(2)}, u32[]{:S(2)}) collective-permute-start(bf16[128,128]{1,0:T(8,128)(2,1)S(1)} %get-tuple-element.106.refs_0_), channel_id=1, source_target_pairs={{0,2},{1,3},{2,0},{3,1},{4,6},{5,7},{6,4},{7,5},{8,10},{9,11},{10,... | collective-permute-start | bytes 98312 | tf_op jit(solution)/shard_map/ppermute | solution.py:544
  9.3 1.2 copy-start
  10.6 0.8 copy-start.23
  11.3 0.8 copy-start.29
  12.1 5.4 %copy-start.3 = (bf16[1,128,4096]{2,1,0:T(8,128)(2,1)S(1)}, bf16[1,128,4096]{2,1,0:T(8,128)(2,1)}, u32[]{:S(2)}) copy-start(bf16[1,128,4096]{2,1,0:T(8,128)(2,1)} %param.17) | copy-start | bytes 3145732
  15.0 27.4 %collective-permute-start.8 = (bf16[144,2048]{1,0:T(8,128)(2,1)}, bf16[144,2048]{1,0:T(8,128)(2,1)}, u32[]{:S(2)}, u32[]{:S(2)}) collective-permute-start(bf16[144,2048]{1,0:T(8,128)(2,1)} %get-tuple-element.54.refs_1_), channel_id=1, source_target_pairs={{0,1},{1,0},{2,3},{3,2},{4,5},{5,4},{6,7},{7,6},{8,9},{9,8},{10,11... | collective-permute-start | bytes 1769480 | tf_op jit(solution)/shard_map/ppermute | solution.py:530
  18.5 13.7 %copy-start.24 = (bf16[1,128,128]{2,1,0:T(8,128)(2,1)S(1)}, bf16[1,128,128]{2,1,0:T(8,128)(2,1)}, u32[]{:S(2)}) copy-start(bf16[1,128,128]{2,1,0:T(8,128)(2,1)} %param.13) | copy-start | bytes 98308
  18.5 13.7 %copy-start.30 = (f32[1,64,128]{2,1,0:T(8,128)S(1)}, f32[1,64,128]{2,1,0:T(8,128)}, u32[]{:S(2)}) copy-start(f32[1,64,128]{2,1,0:T(8,128)} %param.15) | copy-start | bytes 98308
  18.5 13.7 %copy-start.32 = (f32[1,64,128]{2,1,0:T(8,128)S(1)}, f32[1,64,128]{2,1,0:T(8,128)}, u32[]{:S(2)}) copy-start(f32[1,64,128]{2,1,0:T(8,128)} %param.14) | copy-start | bytes 98308
  18.5 10.3 %collective-permute-start.15 = (bf16[128,1024]{1,0:T(8,128)(2,1)S(1)}, bf16[128,1024]{1,0:T(8,128)(2,1)S(1)}, u32[]{:S(2)}, u32[]{:S(2)}) collective-permute-start(bf16[128,1024]{1,0:T(8,128)(2,1)S(1)} %get-tuple-element.75), channel_id=1, source_target_pairs={{0,7},{1,6},{2,5},{3,4},{4,3},{5,2},{6,1},{7,0},{8,15},{9,14},{10,... | collective-permute-start | bytes 786440 | tf_op jit(solution)/shard_map/ppermute | solution.py:539
  23.5 6.1 %collective-permute-start.5 = (bf16[144,1024]{1,0:T(8,128)(2,1)S(1)}, bf16[144,1024]{1,0:T(8,128)(2,1)S(1)}, u32[]{:S(2)}, u32[]{:S(2)}) collective-permute-start(bf16[144,1024]{1,0:T(8,128)(2,1)S(1)} %get-tuple-element.59), channel_id=1, source_target_pairs={{0,1},{1,0},{2,3},{3,2},{4,5},{5,4},{6,7},{7,6},{8,9},{9,8},{10,11... | collective-permute-start | bytes 884744 | tf_op jit(solution)/shard_map/ppermute | solution.py:530
  24.0 8.1 %collective-permute-start.6 = (bf16[144,1024]{1,0:T(8,128)(2,1)S(1)}, bf16[144,1024]{1,0:T(8,128)(2,1)S(1)}, u32[]{:S(2)}, u32[]{:S(2)}) collective-permute-start(bf16[144,1024]{1,0:T(8,128)(2,1)S(1)} %get-tuple-element.60), channel_id=1, source_target_pairs={{0,1},{1,0},{2,3},{3,2},{4,5},{5,4},{6,7},{7,6},{8,9},{9,8},{10,11... | collective-permute-start | bytes 884744 | tf_op jit(solution)/shard_map/ppermute | solution.py:530
  24.1 9.3 %collective-permute-start.1 = (bf16[144,1024]{1,0:T(8,128)(2,1)}, bf16[144,1024]{1,0:T(8,128)(2,1)S(1)}, u32[]{:S(2)}, u32[]{:S(2)}) collective-permute-start(bf16[144,1024]{1,0:T(8,128)(2,1)} %get-tuple-element.56), channel_id=1, source_target_pairs={{0,1},{1,0},{2,3},{3,2},{4,5},{5,4},{6,7},{7,6},{8,9},{9,8},{10,11... | collective-permute-start | bytes 884744 | tf_op jit(solution)/shard_map/ppermute | solution.py:530
  28.8 0.7 copy-start.10
  29.6 3.9 %collective-permute-start = (bf16[144,1024]{1,0:T(8,128)(2,1)}, bf16[144,1024]{1,0:T(8,128)(2,1)S(1)}, u32[]{:S(2)}, u32[]{:S(2)}) collective-permute-start(bf16[144,1024]{1,0:T(8,128)(2,1)} %get-tuple-element.55), channel_id=1, source_target_pairs={{0,1},{1,0},{2,3},{3,2},{4,5},{5,4},{6,7},{7,6},{8,9},{9,8},{10,11... | collective-permute-start | bytes 884744 | tf_op jit(solution)/shard_map/ppermute | solution.py:530
  29.6 39.1 %collective-permute-start.16 = (bf16[128,3072]{1,0:T(8,128)(2,1)}, bf16[128,3072]{1,0:T(8,128)(2,1)S(1)}, u32[]{:S(2)}, u32[]{:S(2)}) collective-permute-start(bf16[128,3072]{1,0:T(8,128)(2,1)} %get-tuple-element.77), channel_id=1, source_target_pairs={{0,7},{1,6},{2,5},{3,4},{4,3},{5,2},{6,1},{7,0},{8,15},{9,14},{10,... | collective-permute-start | bytes 2359304 | tf_op jit(solution)/shard_map/ppermute | solution.py:539
  32.1 5.1 %collective-permute-start.9 = (bf16[4,128,128]{2,1,0:T(8,128)(2,1)}, bf16[4,128,128]{2,1,0:T(8,128)(2,1)}, u32[]{:S(2)}, u32[]{:S(2)}) collective-permute-start(bf16[4,128,128]{2,1,0:T(8,128)(2,1)} %shard_map.113.refs_2_), channel_id=1, source_target_pairs={{0,1},{1,0},{2,3},{3,2},{4,5},{5,4},{6,7},{7,6},{8,9},{9,8},{10,11... | collective-permute-start | bytes 393224 | tf_op jit(solution)/shard_map/ppermute | solution.py:530
  33.4 9.5 %copy-start.8 = (f32[6,64,128]{2,1,0:T(8,128)}, f32[6,64,128]{2,1,0:T(8,128)S(1)}, u32[]{:S(2)}) copy-start(f32[6,64,128]{2,1,0:T(8,128)S(1)} %get-tuple-element.66.refs_3_.refs_6_) | copy-start | bytes 589828
  33.4 4.7 %copy-start.6 = (bf16[1,128,4096]{2,1,0:T(8,128)(2,1)S(1)}, bf16[1,128,4096]{2,1,0:T(8,128)(2,1)}, u32[]{:S(2)}) copy-start(bf16[1,128,4096]{2,1,0:T(8,128)(2,1)} %param.9) | copy-start | bytes 3145732
  33.4 10.1 %copy-start.2 = (bf16[1,128,4096]{2,1,0:T(8,128)(2,1)S(1)}, bf16[1,128,4096]{2,1,0:T(8,128)(2,1)}, u32[]{:S(2)}) copy-start(bf16[1,128,4096]{2,1,0:T(8,128)(2,1)} %param.12) | copy-start | bytes 3145732
  34.9 0.7 copy-start.25
  35.6 0.7 copy-start.27
  36.3 29.8 %copy-start.21 = (bf16[128,2048]{1,0:T(8,128)(2,1)}, bf16[128,2048]{1,0:T(8,128)(2,1)S(1)}, u32[]{:S(2)}) copy-start(bf16[128,2048]{1,0:T(8,128)(2,1)S(1)} %get-tuple-element.64.refs_0_) | copy-start | bytes 1572868
  36.3 7.2 %copy-start.1 = (bf16[1,128,4096]{2,1,0:T(8,128)(2,1)S(1)}, bf16[1,128,4096]{2,1,0:T(8,128)(2,1)}, u32[]{:S(2)}) copy-start(bf16[1,128,4096]{2,1,0:T(8,128)(2,1)} %param.16) | copy-start | bytes 3145732
  36.3 8.6 %collective-permute-start.7 = (bf16[128,2048]{1,0:T(8,128)(2,1)S(1)}, bf16[128,2048]{1,0:T(8,128)(2,1)S(1)}, u32[]{:S(2)}, u32[]{:S(2)}) collective-permute-start(bf16[128,2048]{1,0:T(8,128)(2,1)S(1)} %get-tuple-element.64.refs_0_), channel_id=1, source_target_pairs={{6,4},{7,5},{14,12},{15,13},{22,20},{23,21},{30,28},{31,29}} | collective-permute-start | bytes 1572872 | tf_op jit(solution)/shard_map/ppermute | solution.py:533
  38.6 0.8 copy-start.13
  39.4 14.7 %collective-permute-start.10 = (bf16[2048,128]{1,0:T(8,128)(2,1)S(1)}, bf16[2048,128]{1,0:T(8,128)(2,1)S(1)}, u32[]{:S(2)}, u32[]{:S(2)}) collective-permute-start(bf16[2048,128]{1,0:T(8,128)(2,1)S(1)} %get-tuple-element.70), channel_id=1, source_target_pairs={{0,8},{8,0},{16,24},{24,16},{1,9},{9,1},{17,25},{25,17},{2,10},{10... | collective-permute-start | bytes 1572872 | tf_op jit(solution)/shard_map/ppermute | solution.py:536
  40.9 25.2 %collective-permute-start.11 = (bf16[2048,128]{1,0:T(8,128)(2,1)S(1)}, bf16[2048,128]{1,0:T(8,128)(2,1)S(1)}, u32[]{:S(2)}, u32[]{:S(2)}) collective-permute-start(bf16[2048,128]{1,0:T(8,128)(2,1)S(1)} %get-tuple-element.71), channel_id=1, source_target_pairs={{0,16},{8,24},{16,0},{24,8},{1,17},{9,25},{17,1},{25,9},{2,18},{10... | collective-permute-start | bytes 1572872 | tf_op jit(solution)/shard_map/ppermute | solution.py:536
  42.4 23.7 %collective-permute-start.12 = (bf16[2048,128]{1,0:T(8,128)(2,1)S(1)}, bf16[2048,128]{1,0:T(8,128)(2,1)S(1)}, u32[]{:S(2)}, u32[]{:S(2)}) collective-permute-start(bf16[2048,128]{1,0:T(8,128)(2,1)S(1)} %get-tuple-element.72), channel_id=1, source_target_pairs={{0,24},{8,16},{16,8},{24,0},{1,25},{9,17},{17,9},{25,1},{2,26},{10... | collective-permute-start | bytes 1572872 | tf_op jit(solution)/shard_map/ppermute | solution.py:536
  44.9 23.8 %copy-start.11 = (bf16[128,1024]{1,0:T(8,128)(2,1)S(1)}, bf16[128,1024]{1,0:T(8,128)(2,1)}, u32[]{:S(2)}) copy-start(bf16[128,1024]{1,0:T(8,128)(2,1)} %copy-done.10) | copy-start | bytes 786436
  45.0 26.4 %copy-start.4 = (bf16[128,2048]{1,0:T(8,128)(2,1)}, bf16[128,2048]{1,0:T(8,128)(2,1)S(1)}, u32[]{:S(2)}) copy-start(bf16[128,2048]{1,0:T(8,128)(2,1)S(1)} %collective-permute-done.7.refs_2_.refs_0_) | copy-start | bytes 1572868
  45.0 27.1 %collective-permute-start.19 = (bf16[128,2048]{1,0:T(8,128)(2,1)}, bf16[128,2048]{1,0:T(8,128)(2,1)}, u32[]{:S(2)}, u32[]{:S(2)}) collective-permute-start(bf16[128,2048]{1,0:T(8,128)(2,1)} %get-tuple-element.62.refs_5_), channel_id=1, source_target_pairs={{6,4},{7,5},{14,12},{15,13},{22,20},{23,21},{30,28},{31,29}} | collective-permute-start | bytes 1572872 | tf_op jit(solution)/shard_map/ppermute | solution.py:533
  54.1 17.3 %copy-start.15 = (bf16[2048,128]{1,0:T(8,128)(2,1)}, bf16[2048,128]{1,0:T(8,128)(2,1)S(1)}, u32[]{:S(2)}) copy-start(bf16[2048,128]{1,0:T(8,128)(2,1)S(1)} %collective-permute-done.10.refs_2_) | copy-start | bytes 1572868
  66.1 5.3 %copy-start.17 = (bf16[2048,128]{1,0:T(8,128)(2,1)}, bf16[2048,128]{1,0:T(8,128)(2,1)S(1)}, u32[]{:S(2)}) copy-start(bf16[2048,128]{1,0:T(8,128)(2,1)S(1)} %collective-permute-done.11.refs_3_) | copy-start | bytes 1572868
  66.1 5.3 %copy-start.19 = (bf16[2048,128]{1,0:T(8,128)(2,1)}, bf16[2048,128]{1,0:T(8,128)(2,1)S(1)}, u32[]{:S(2)}) copy-start(bf16[2048,128]{1,0:T(8,128)(2,1)S(1)} %collective-permute-done.12.refs_4_) | copy-start | bytes 1572868
  67.2 13.6 %collective-permute-start.13 = (bf16[128,2048]{1,0:T(8,128)(2,1)}, bf16[128,2048]{1,0:T(8,128)(2,1)}, u32[]{:S(2)}, u32[]{:S(2)}) collective-permute-start(bf16[128,2048]{1,0:T(8,128)(2,1)} %shard_map.120), channel_id=1, source_target_pairs={{4,2},{5,3},{12,10},{13,11},{20,18},{21,19},{28,26},{29,27}} | collective-permute-start | bytes 1572872 | tf_op jit(solution)/shard_map/ppermute | solution.py:533
  71.4 2.0 %collective-permute-start.17 = (bf16[144,1024]{1,0:T(8,128)(2,1)}, bf16[144,1024]{1,0:T(8,128)(2,1)}, u32[]{:S(2)}, u32[]{:S(2)}) collective-permute-start(bf16[144,1024]{1,0:T(8,128)(2,1)} %get-tuple-element.81), channel_id=1, source_target_pairs={{0,1},{1,0},{2,3},{3,2},{4,5},{5,4},{6,7},{7,6},{8,9},{9,8},{10,11... | collective-permute-start | bytes 884744 | tf_op jit(solution)/shard_map/ppermute | solution.py:530
  71.5 2.3 %collective-permute-start.18 = (bf16[144,1024]{1,0:T(8,128)(2,1)}, bf16[144,1024]{1,0:T(8,128)(2,1)}, u32[]{:S(2)}, u32[]{:S(2)}) collective-permute-start(bf16[144,1024]{1,0:T(8,128)(2,1)} %get-tuple-element.82), channel_id=1, source_target_pairs={{0,1},{1,0},{2,3},{3,2},{4,5},{5,4},{6,7},{7,6},{8,9},{9,8},{10,11... | collective-permute-start | bytes 884744 | tf_op jit(solution)/shard_map/ppermute | solution.py:530
  72.0 13.1 %collective-permute-start.21 = (bf16[144,2048]{1,0:T(8,128)(2,1)}, bf16[144,2048]{1,0:T(8,128)(2,1)}, u32[]{:S(2)}, u32[]{:S(2)}) collective-permute-start(bf16[144,2048]{1,0:T(8,128)(2,1)} %get-tuple-element.80.refs_2_), channel_id=1, source_target_pairs={{0,1},{1,0},{2,3},{3,2},{4,5},{5,4},{6,7},{7,6},{8,9},{9,8},{10,11... | collective-permute-start | bytes 1769480 | tf_op jit(solution)/shard_map/ppermute | solution.py:530
  73.8 7.0 %copy-start.5 = (bf16[128,2048]{1,0:T(8,128)(2,1)S(1)}, bf16[128,2048]{1,0:T(8,128)(2,1)}, u32[]{:S(2)}) copy-start(bf16[128,2048]{1,0:T(8,128)(2,1)} %copy-done.4) | copy-start | bytes 1572868
  73.8 7.0 %copy-start.22 = (bf16[128,2048]{1,0:T(8,128)(2,1)S(1)}, bf16[128,2048]{1,0:T(8,128)(2,1)}, u32[]{:S(2)}) copy-start(bf16[128,2048]{1,0:T(8,128)(2,1)} %copy-done.21) | copy-start | bytes 1572868
  76.3 7.3 %copy-start.12 = (bf16[128,1024]{1,0:T(8,128)(2,1)S(1)}, bf16[128,1024]{1,0:T(8,128)(2,1)}, u32[]{:S(2)}) copy-start(bf16[128,1024]{1,0:T(8,128)(2,1)} %copy-done.10) | copy-start | bytes 786436
  76.3 7.3 %copy-start.31 = (f32[64,128]{1,0:T(8,128)S(1)}, f32[64,128]{1,0:T(8,128)}, u32[]{:S(2)}) copy-start(f32[64,128]{1,0:T(8,128)} %get-tuple-element.107.refs_3_) | copy-start | bytes 98308
  76.3 15.9 %collective-permute-start.20 = (bf16[128,2048]{1,0:T(8,128)(2,1)S(1)}, bf16[128,2048]{1,0:T(8,128)(2,1)S(1)}, u32[]{:S(2)}, u32[]{:S(2)}) collective-permute-start(bf16[128,2048]{1,0:T(8,128)(2,1)S(1)} %get-tuple-element.85), channel_id=1, source_target_pairs={{0,2},{1,3},{4,6},{5,7},{8,10},{9,11},{12,14},{13,15},{16,18},{17,... | collective-permute-start | bytes 1572872 | tf_op jit(solution)/shard_map/ppermute | solution.py:533
  82.1 15.8 %collective-permute-start.14 = (bf16[128,2048]{1,0:T(8,128)(2,1)S(1)}, bf16[128,2048]{1,0:T(8,128)(2,1)S(1)}, u32[]{:S(2)}, u32[]{:S(2)}) collective-permute-start(bf16[128,2048]{1,0:T(8,128)(2,1)S(1)} %shard_map.121), channel_id=1, source_target_pairs={{2,0},{3,1},{10,8},{11,9},{18,16},{19,17},{26,24},{27,25}} | collective-permute-start | bytes 1572872 | tf_op jit(solution)/shard_map/ppermute | solution.py:533
  97.9 1.5 %copy-start.9 = (f32[6,64,128]{2,1,0:T(8,128)S(1)}, f32[6,64,128]{2,1,0:T(8,128)}, u32[]{:S(2)}) copy-start(f32[6,64,128]{2,1,0:T(8,128)} %copy-done.8) | copy-start | bytes 589828
  97.9 1.5 %copy-start.26 = (bf16[144,1024]{1,0:T(8,128)(2,1)S(1)}, bf16[144,1024]{1,0:T(8,128)(2,1)}, u32[]{:S(2)}) copy-start(bf16[144,1024]{1,0:T(8,128)(2,1)} %copy-done.25) | copy-start | bytes 884740
  97.9 1.5 %copy-start.28 = (bf16[144,1024]{1,0:T(8,128)(2,1)S(1)}, bf16[144,1024]{1,0:T(8,128)(2,1)}, u32[]{:S(2)}) copy-start(bf16[144,1024]{1,0:T(8,128)(2,1)} %copy-done.27) | copy-start | bytes 884740
  99.3 2.7 %collective-permute-start.22 = (bf16[128,4096]{1,0:T(8,128)(2,1)S(1)}, bf16[128,4096]{1,0:T(8,128)(2,1)S(1)}, u32[]{:S(2)}, u32[]{:S(2)}) collective-permute-start(bf16[128,4096]{1,0:T(8,128)(2,1)S(1)} %shard_map.126.refs_2_), channel_id=1, source_target_pairs={{0,1},{1,0},{2,3},{3,2},{4,5},{5,4},{6,7},{7,6},{8,9},{9,8},{10,11... | collective-permute-start | bytes 3145736 | tf_op jit(solution)/shard_map/ppermute | solution.py:530
  102.1 6.0 %copy-start.14 = (bf16[2048,128]{1,0:T(8,128)(2,1)S(1)}, bf16[2048,128]{1,0:T(8,128)(2,1)}, u32[]{:S(2)}) copy-start(bf16[2048,128]{1,0:T(8,128)(2,1)} %copy-done.13) | copy-start | bytes 1572868
  102.1 6.0 %copy-start.16 = (bf16[2048,128]{1,0:T(8,128)(2,1)S(1)}, bf16[2048,128]{1,0:T(8,128)(2,1)}, u32[]{:S(2)}) copy-start(bf16[2048,128]{1,0:T(8,128)(2,1)} %copy-done.15) | copy-start | bytes 1572868
  102.1 6.0 %copy-start.18 = (bf16[2048,128]{1,0:T(8,128)(2,1)S(1)}, bf16[2048,128]{1,0:T(8,128)(2,1)}, u32[]{:S(2)}) copy-start(bf16[2048,128]{1,0:T(8,128)(2,1)} %copy-done.17) | copy-start | bytes 1572868
  102.1 6.0 %copy-start.20 = (bf16[2048,128]{1,0:T(8,128)(2,1)S(1)}, bf16[2048,128]{1,0:T(8,128)(2,1)}, u32[]{:S(2)}) copy-start(bf16[2048,128]{1,0:T(8,128)(2,1)} %copy-done.19) | copy-start | bytes 1572868
  104.5 7.9 %collective-permute-start.25 = (bf16[128,128]{1,0:T(8,128)(2,1)S(1)}, bf16[128,128]{1,0:T(8,128)(2,1)S(1)}, u32[]{:S(2)}, u32[]{:S(2)}) collective-permute-start(bf16[128,128]{1,0:T(8,128)(2,1)S(1)} %get-tuple-element.95.refs_5_), channel_id=1, source_target_pairs={{0,24},{8,16},{16,8},{24,0},{1,25},{9,17},{17,9},{25,1},{2,26},{10... | collective-permute-start | bytes 98312 | tf_op jit(solution)/shard_map/ppermute | solution.py:536
  105.9 6.5 %collective-permute-start.24 = (bf16[128,128]{1,0:T(8,128)(2,1)S(1)}, bf16[128,128]{1,0:T(8,128)(2,1)S(1)}, u32[]{:S(2)}, u32[]{:S(2)}) collective-permute-start(bf16[128,128]{1,0:T(8,128)(2,1)S(1)} %get-tuple-element.95.refs_5_), channel_id=1, source_target_pairs={{0,16},{8,24},{16,0},{24,8},{1,17},{9,25},{17,1},{25,9},{2,18},{10... | collective-permute-start | bytes 98312 | tf_op jit(solution)/shard_map/ppermute | solution.py:536
  107.8 4.6 %collective-permute-start.23 = (bf16[128,128]{1,0:T(8,128)(2,1)S(1)}, bf16[128,128]{1,0:T(8,128)(2,1)S(1)}, u32[]{:S(2)}, u32[]{:S(2)}) collective-permute-start(bf16[128,128]{1,0:T(8,128)(2,1)S(1)} %get-tuple-element.95.refs_5_), channel_id=1, source_target_pairs={{0,8},{8,0},{16,24},{24,16},{1,9},{9,1},{17,25},{25,17},{2,10},{10... | collective-permute-start | bytes 98312 | tf_op jit(solution)/shard_map/ppermute | solution.py:536
  108.0 1.2 %copy-start.7 = (bf16[1,128,4096]{2,1,0:T(8,128)(2,1)S(1)}, bf16[1,128,4096]{2,1,0:T(8,128)(2,1)}, u32[]{:S(2)}) copy-start(bf16[1,128,4096]{2,1,0:T(8,128)(2,1)} %param.9) | copy-start | bytes 3145732
  112.9 1.4 %collective-permute-start.26 = (bf16[4,128,128]{2,1,0:T(8,128)(2,1)S(1)}, bf16[4,128,128]{2,1,0:T(8,128)(2,1)S(1)}, u32[]{:S(2)}, u32[]{:S(2)}) collective-permute-start(bf16[4,128,128]{2,1,0:T(8,128)(2,1)S(1)} %get-tuple-element.99), channel_id=1, source_target_pairs={{0,1},{1,0},{2,3},{3,2},{4,5},{5,4},{6,7},{7,6},{8,9},{9,8},{10,11... | collective-permute-start | bytes 393224 | tf_op jit(solution)/shard_map/ppermute | solution.py:530
  114.3 7.7 %collective-permute-start.28 = (bf16[128,128]{1,0:T(8,128)(2,1)S(1)}, bf16[128,128]{1,0:T(8,128)(2,1)S(1)}, u32[]{:S(2)}, u32[]{:S(2)}) collective-permute-start(bf16[128,128]{1,0:T(8,128)(2,1)S(1)} %get-tuple-element.103), channel_id=1, source_target_pairs={{0,4},{1,5},{2,6},{3,7},{4,0},{5,1},{6,2},{7,3},{8,12},{9,13},{10,... | collective-permute-start | bytes 98312 | tf_op jit(solution)/shard_map/ppermute | solution.py:730
  114.4 7.6 %collective-permute-start.29 = (bf16[128,128]{1,0:T(8,128)(2,1)S(1)}, bf16[128,128]{1,0:T(8,128)(2,1)S(1)}, u32[]{:S(2)}, u32[]{:S(2)}) collective-permute-start(bf16[128,128]{1,0:T(8,128)(2,1)S(1)} %get-tuple-element.104), channel_id=1, source_target_pairs={{0,6},{1,7},{2,4},{3,5},{4,2},{5,3},{6,0},{7,1},{8,14},{9,15},{10,... | collective-permute-start | bytes 98312 | tf_op jit(solution)/shard_map/ppermute | solution.py:730
  116.3 5.7 %collective-permute-start.27 = (bf16[128,128]{1,0:T(8,128)(2,1)S(1)}, bf16[128,128]{1,0:T(8,128)(2,1)S(1)}, u32[]{:S(2)}, u32[]{:S(2)}) collective-permute-start(bf16[128,128]{1,0:T(8,128)(2,1)S(1)} %get-tuple-element.100), channel_id=1, source_target_pairs={{0,2},{1,3},{2,0},{3,1},{4,6},{5,7},{6,4},{7,5},{8,10},{9,11},{10,... | collective-permute-start | bytes 98312 | tf_op jit(solution)/shard_map/ppermute | solution.py:730

commit v6 on v4

--- a/solution.py
+++ b/solution.py
@@ -708,6 +708,8 @@
         ),
         after=(half_inner,),
     )
+    ready_write = lax.optimization_barrier((grad_write, give))[0]
+    grad_hidden = dot_nt(ready_write, weight).astype(bf16)
     ((total, *dealt),) = run(
         job(
             deal_kernel,
@@ -715,7 +717,8 @@
             keep,
             over_cores(give),
             scalars=(chip,),
-        )
+        ),
+        after=(grad_hidden,),
     )
     for k in range(1, chips):
         total = total + lax.ppermute(dealt[k - 1], "ctx", xor_pairs(ctx_count, 2 * k)).astype(f32)
@@ -724,7 +727,6 @@
     grad_inner = run_on_half(
         part(inner_kernel, 1), 1, sds((n, width), bf16), core, inner_arrays, (half_inner,), tuple(dealt[:1])
     )
-    grad_hidden = dot_nt(grad_write, weight).astype(bf16)
     return grad_inner[None], grad_hidden[None], grad_weight
 
 

time: 124 us -> 122 us (0.984)
  waiting for transfers between devices: 42.8 us -> 41.4 us
    ppermute x11, waiting for transfers between devices: 3.64 us -> 2.31 us  [over_cores(): return lax.ppermute(array, 'ctx', xor_pairs(ctx_count, 1))]
  transfers between devices with their start and end apart: 30 -> 30, of which waited for: 10 -> 9; matrix products, arithmetic and copies ran while one was open for 2% -> 2% of each run, Pallas kernels for 24% -> 24%
where the time goes in v6:
time: 122 us
  waiting for transfers between devices  41.4 us (34%)
  Pallas kernels  33.4 us (27%)
  starting transfers between devices  32.8 us (27%)
  local copies, waits for them, and re-layouts  7.54 us (6%)
  other arithmetic  2.96 us (2%)
  matrix products  1.85 us (2%)
  between operations  1.65 us (1%)
    pallas_call x20, Pallas kernels, run(): pl.pallas_call(kernel, out_shape=outs, in_specs=specs, out_specs=[vmem] *...  28 us
    ppermute x6, waiting for transfers between devices, over_dp(): return lax.ppermute(array, 'dp', xor_pairs(dp_count, k))  19.5 us
    ppermute x5, waiting for transfers between devices, over_chips(): return lax.ppermute(array, 'ctx', chip_pairs(moves))  12.7 us
    ppermute x5, starting transfers between devices, over_chips(): return lax.ppermute(array, 'ctx', chip_pairs(moves))  9.87 us
    ppermute x3, starting transfers between devices, flip(): lax.ppermute(piece, 'ctx', [(i, ctx_count - 1 - i) for i in range(ctx_cou...  8.8 us
    unnamed x68, local copies, waits for them, and re-layouts  7.52 us
    ppermute x6, starting transfers between devices, over_dp(): return lax.ppermute(array, 'dp', xor_pairs(dp_count, k))  7.04 us
    pallas_call x2, Pallas kernels, run_on_half(): pl.pallas_call(kernel, grid=(1,), out_shape=shape, in_specs=[smem] + [vme...  5.42 us
  transfers between devices with their start and end apart: 30, of which 9 were waited for; matrix products, arithmetic and copies ran while one was open for 2% of the time, Pallas kernels for 24%

profile of v6, /device:TPU:0, one launch (start us, length us, event | category | flops | bytes accessed | tf_op | source)
XLA Modules:
  0.0 121.6 jit_solution(1086578112793010030)
XLA Ops:
  1.3 0.8 bitcast_convert_fusion
  2.0 0.8 fusion.2
  2.8 0.8 pad_maximum_fusion
  3.6 4.6 %collective-permute-start.2 = (f32[320,128]{1,0:T(8,128)S(1)}, f32[320,128]{1,0:T(8,128)S(1)}, u32[]{:S(2)}, u32[]{:S(2)}) collective-permute-start(f32[320,128]{1,0:T(8,128)S(1)} %pad_maximum_fusion), channel_id=1, source_target_pairs={{0,7},{1,6},{2,5},{3,4},{4,3},{5,2},{6,1},{7,0},{8,15},{9,14},{10,... | collective-permute-start | bytes 491528 | tf_op jit(solution)/shard_map/ppermute | solution.py:533
  8.1 1.2 collective-permute-start.3
  9.4 1.2 %copy-done = bf16[1,128,4096]{2,1,0:T(8,128)(2,1)S(1)} copy-done((bf16[1,128,4096]{2,1,0:T(8,128)(2,1)S(1)}, bf16[1,128,4096]{2,1,0:T(8,128)(2,1)}, u32[]{:S(2)}) %copy-start) | copy-done | bytes 1048600
  10.6 0.8 copy-done.23
  11.3 0.8 copy-done.29
  12.1 2.9 %shard_map.112 = (bf16[144,2048]{1,0:T(8,128)(2,1)}, bf16[144,1024]{1,0:T(8,128)(2,1)S(1)}, bf16[144,1024]{1,0:T(8,128)(2,1)}) custom-call(s32[1]{0:T(128)} %bitcast.refs_0_.refs_1_, bf16[128,4096]{1,0:T(8,128)(2,1)S(1)} %bitcast.29, bf16[128,128]{1,0:T(8,128)(2,1)S(1)} %bitcast.43, f32[64,128]{1,0:T(8,128)S(1)} %bitcast.51), custom_call_target="tpu_custom_call" | custom-call | tf_op jit(solution)/shard_map/pallas_call | solution.py:53
  15.0 2.6 %collective-permute-done.4.refs_2_ = bf16[128,128]{1,0:T(8,128)(2,1)S(1)} collective-permute-done((bf16[128,128]{1,0:T(8,128)(2,1)S(1)}, bf16[128,128]{1,0:T(8,128)(2,1)S(1)}, u32[]{:S(2)}, u32[]{:S(2)}) %collective-permute-start.4) | collective-permute-done | bytes 32800 | tf_op jit(solution)/shard_map/ppermute | solution.py:538
  17.5 0.9 shard_map.122
  18.5 2.2 %collective-permute-start.15 = (bf16[128,1024]{1,0:T(8,128)(2,1)S(1)}, bf16[128,1024]{1,0:T(8,128)(2,1)S(1)}, u32[]{:S(2)}, u32[]{:S(2)}) collective-permute-start(bf16[128,1024]{1,0:T(8,128)(2,1)S(1)} %get-tuple-element.76), channel_id=1, source_target_pairs={{0,7},{1,6},{2,5},{3,4},{4,3},{5,2},{6,1},{7,0},{8,15},{9,14},{10,... | collective-permute-start | bytes 786440 | tf_op jit(solution)/shard_map/ppermute | solution.py:533
  20.7 0.7 shard_map.113.refs_2_
  21.4 2.2 %shard_map.114 = (bf16[144,2048]{1,0:T(8,128)(2,1)S(1)}, bf16[144,1024]{1,0:T(8,128)(2,1)S(1)}, bf16[144,1024]{1,0:T(8,128)(2,1)S(1)}) custom-call(s32[1]{0:T(128)} %bitcast.refs_0_.refs_1_, bf16[128,4096]{1,0:T(8,128)(2,1)S(1)} %bitcast.39, f32[128,128]{1,0:T(8,128)S(1)} %get-tuple-element.112.refs_2_, f32[64,128]{1,0:T(8,128)S(1)} %slice.21.refs_3_), custom_call_target="tpu_custom_call" | custom-call | tf_op jit(solution)/shard_map/pallas_call | solution.py:53
  23.5 0.5 collective-permute-start.5
  24.1 0.4 collective-permute-start.1
  24.5 4.3 %collective-permute-done.15.refs_1_.refs_0_.refs_11_ = bf16[128,1024]{1,0:T(8,128)(2,1)S(1)} collective-permute-done((bf16[128,1024]{1,0:T(8,128)(2,1)S(1)}, bf16[128,1024]{1,0:T(8,128)(2,1)S(1)}, u32[]{:S(2)}, u32[]{:S(2)}) %collective-permute-start.15) | collective-permute-done | bytes 262176 | tf_op jit(solution)/shard_map/ppermute | solution.py:533
  28.8 0.7 copy-done.6
  29.6 0.5 collective-permute-start.9
  30.1 2.1 %collective-permute-start.16 = (bf16[128,3072]{1,0:T(8,128)(2,1)}, bf16[128,3072]{1,0:T(8,128)(2,1)S(1)}, u32[]{:S(2)}, u32[]{:S(2)}) collective-permute-start(bf16[128,3072]{1,0:T(8,128)(2,1)} %get-tuple-element.78), channel_id=1, source_target_pairs={{0,7},{1,6},{2,5},{3,4},{4,3},{5,2},{6,1},{7,0},{8,15},{9,14},{10,... | collective-permute-start | bytes 2359304 | tf_op jit(solution)/shard_map/ppermute | solution.py:533
  32.2 1.3 %shard_map.115 = (bf16[128,2048]{1,0:T(8,128)(2,1)}, f32[1,2048]{1,0:T(1,128)S(1)}, bf16[128,128]{1,0:T(8,128)(2,1)S(1)}, f32[5,64,128]{2,1,0:T(8,128)S(1)}, f32[8,128,128]{2,1,0:T(8,128)S(1)}) custom-call(s32[1]{0:T(128)} %bitcast.refs_0_.refs_1_, bf16[144,2048]{1,0:T(8,128)(2,1)S(1)} %get-tuple-element.59.refs_1_, ...), custom_call_target="tpu_custom_call" | custom-call | tf_op jit(solution)/shard_map/pallas_call | solution.py:53
  33.4 1.5 %shard_map.116 = (bf16[128,2048]{1,0:T(8,128)(2,1)S(1)}, f32[1,2048]{1,0:T(1,128)S(1)}) custom-call(s32[1]{0:T(128)} %bitcast.refs_0_.refs_1_, bf16[144,2048]{1,0:T(8,128)(2,1)} %get-tuple-element.55.refs_1_, bf16[144,1024]{1,0:T(8,128)(2,1)S(1)} %collective-permute-done.refs_2_.refs_8_, bf16[144,1024]{1,0:T(8,128)(2,1)S(1)} %collective-permute-done.1.refs_3_.refs_9_), custom_call_target="tpu_custom_call" | custom-call | tf_op jit(solution)/shard_map/pallas_call | solution.py:53
  34.9 0.7 copy-done.25
  35.6 0.7 copy-done.27
  36.3 0.8 collective-permute-start.7
  37.2 1.0 shard_map.118
  38.2 0.4 shard_map.119
  38.6 0.8 copy-done.13
  39.4 1.5 %collective-permute-start.10 = (bf16[2048,128]{1,0:T(8,128)(2,1)S(1)}, bf16[2048,128]{1,0:T(8,128)(2,1)S(1)}, u32[]{:S(2)}, u32[]{:S(2)}) collective-permute-start(bf16[2048,128]{1,0:T(8,128)(2,1)S(1)} %get-tuple-element.71), channel_id=1, source_target_pairs={{0,8},{8,0},{16,24},{24,16},{1,9},{9,1},{17,25},{25,17},{2,10},{10... | collective-permute-start | bytes 1572872 | tf_op jit(solution)/shard_map/ppermute | solution.py:530
  40.9 1.5 %collective-permute-start.11 = (bf16[2048,128]{1,0:T(8,128)(2,1)S(1)}, bf16[2048,128]{1,0:T(8,128)(2,1)S(1)}, u32[]{:S(2)}, u32[]{:S(2)}) collective-permute-start(bf16[2048,128]{1,0:T(8,128)(2,1)S(1)} %get-tuple-element.72), channel_id=1, source_target_pairs={{0,16},{8,24},{16,0},{24,8},{1,17},{9,25},{17,1},{25,9},{2,18},{10... | collective-permute-start | bytes 1572872 | tf_op jit(solution)/shard_map/ppermute | solution.py:530
  42.4 0.5 collective-permute-start.12
  42.9 1.4 %shard_map.117.refs_4_ = f32[128,128]{1,0:T(8,128)S(1)} custom-call(bf16[128,4096]{1,0:T(8,128)(2,1)S(1)} %bitcast.30, bf16[128,4096]{1,0:T(8,128)(2,1)S(1)} %bitcast.33, f32[64,128]{1,0:T(8,128)S(1)} %get-tuple-element.110.refs_2_, f32[8,128,128]{2,1,0:T(8,128)S(1)} %get-tuple-element.86.refs_3_.refs_4_.refs_7_), custom_call_target="tpu_custom_call" | custom-call | tf_op jit(solution)/shard_map/pallas_call | solution.py:53
  44.3 0.6 copy-done.31
  45.0 1.6 %collective-permute-start.19 = (bf16[128,2048]{1,0:T(8,128)(2,1)}, bf16[128,2048]{1,0:T(8,128)(2,1)}, u32[]{:S(2)}, u32[]{:S(2)}) collective-permute-start(bf16[128,2048]{1,0:T(8,128)(2,1)} %get-tuple-element.63.refs_5_), channel_id=1, source_target_pairs={{6,4},{7,5},{14,12},{15,13},{22,20},{23,21},{30,28},{31,29}} | collective-permute-start | bytes 1572872 | tf_op jit(solution)/shard_map/ppermute | solution.py:527
  46.6 7.6 %collective-permute-done.10.refs_2_ = bf16[2048,128]{1,0:T(8,128)(2,1)S(1)} collective-permute-done((bf16[2048,128]{1,0:T(8,128)(2,1)S(1)}, bf16[2048,128]{1,0:T(8,128)(2,1)S(1)}, u32[]{:S(2)}, u32[]{:S(2)}) %collective-permute-start.10) | collective-permute-done | bytes 524320 | tf_op jit(solution)/shard_map/ppermute | solution.py:530
  54.1 12.0 %collective-permute-done.11.refs_3_ = bf16[2048,128]{1,0:T(8,128)(2,1)S(1)} collective-permute-done((bf16[2048,128]{1,0:T(8,128)(2,1)S(1)}, bf16[2048,128]{1,0:T(8,128)(2,1)S(1)}, u32[]{:S(2)}, u32[]{:S(2)}) %collective-permute-start.11) | collective-permute-done | bytes 524320 | tf_op jit(solution)/shard_map/ppermute | solution.py:530
  66.1 1.1 shard_map.120
  67.2 1.5 %collective-permute-start.13 = (bf16[128,2048]{1,0:T(8,128)(2,1)}, bf16[128,2048]{1,0:T(8,128)(2,1)}, u32[]{:S(2)}, u32[]{:S(2)}) collective-permute-start(bf16[128,2048]{1,0:T(8,128)(2,1)} %shard_map.120), channel_id=1, source_target_pairs={{4,2},{5,3},{12,10},{13,11},{20,18},{21,19},{28,26},{29,27}} | collective-permute-start | bytes 1572872 | tf_op jit(solution)/shard_map/ppermute | solution.py:527
  68.7 3.1 %shard_map.123 = (bf16[144,2048]{1,0:T(8,128)(2,1)}, bf16[144,1024]{1,0:T(8,128)(2,1)}, bf16[144,1024]{1,0:T(8,128)(2,1)}) custom-call(s32[1]{0:T(128)} %bitcast.refs_0_.refs_1_, bf16[128,1024]{1,0:T(8,128)(2,1)S(1)} %copy-done.7, bf16[128,3072]{1,0:T(8,128)(2,1)S(1)} %collective-permute-done.16.refs_2_.refs_1_.refs_12_, bf16[128,128]{1,0:T(8,128)(2,1)S(1)} %bitcast.45, ...), custom_call_target="tpu_custom_call" | custom-call | tf_op jit(solution)/shard_map/pallas_call | solution.py:53
  71.9 0.5 collective-permute-start.18
  72.4 1.3 %collective-permute-done.17.refs_3_.refs_10_ = bf16[144,1024]{1,0:T(8,128)(2,1)} collective-permute-done((bf16[144,1024]{1,0:T(8,128)(2,1)}, bf16[144,1024]{1,0:T(8,128)(2,1)}, u32[]{:S(2)}, u32[]{:S(2)}) %collective-permute-start.17) | collective-permute-done | bytes 294944 | tf_op jit(solution)/shard_map/ppermute | solution.py:524
  73.8 0.4 collective-permute-done.18.refs_4_.refs_11_
  74.2 2.5 %shard_map.124 = (bf16[128,2048]{1,0:T(8,128)(2,1)S(1)}, bf16[128,2048]{1,0:T(8,128)(2,1)S(1)}) custom-call(s32[1]{0:T(128)} %bitcast.refs_0_.refs_1_, s32[1]{0:T(128)} %bitcast.13.refs_1_, bf16[144,2048]{1,0:T(8,128)(2,1)} %get-tuple-element.80.refs_2_, bf16[144,1024]{1,0:T(8,128)(2,1)} %collective-permute-done.17.refs_3_.refs_10_, ...), custom_call_target="tpu_custom_call" | custom-call | tf_op jit(solution)/shard_map/pallas_call | solution.py:53
  76.7 4.5 %collective-permute-start.20 = (bf16[128,2048]{1,0:T(8,128)(2,1)S(1)}, bf16[128,2048]{1,0:T(8,128)(2,1)S(1)}, u32[]{:S(2)}, u32[]{:S(2)}) collective-permute-start(bf16[128,2048]{1,0:T(8,128)(2,1)S(1)} %get-tuple-element.85), channel_id=1, source_target_pairs={{0,2},{1,3},{4,6},{5,7},{8,10},{9,11},{12,14},{13,15},{16,18},{17,... | collective-permute-start | bytes 1572872 | tf_op jit(solution)/shard_map/ppermute | solution.py:527
  81.3 1.3 %shard_map.121 = bf16[128,2048]{1,0:T(8,128)(2,1)S(1)} custom-call(bf16[128,2048]{1,0:T(8,128)(2,1)S(1)} %copy-done.22, f32[1,2048]{1,0:T(1,128)S(1)} %get-tuple-element.66.refs_1_, bf16[128,2048]{1,0:T(8,128)(2,1)S(1)} %copy-done.5, bf16[128,2048]{1,0:T(8,128)(2,1)} %collective-permute-done.13.refs_3_.refs_1_), custom_call_target="tpu_custom_call" | custom-call | tf_op jit(solution)/shard_map/pallas_call | solution.py:53
  82.6 1.5 %collective-permute-start.14 = (bf16[128,2048]{1,0:T(8,128)(2,1)S(1)}, bf16[128,2048]{1,0:T(8,128)(2,1)S(1)}, u32[]{:S(2)}, u32[]{:S(2)}) collective-permute-start(bf16[128,2048]{1,0:T(8,128)(2,1)S(1)} %shard_map.121), channel_id=1, source_target_pairs={{2,0},{3,1},{10,8},{11,9},{18,16},{19,17},{26,24},{27,25}} | collective-permute-start | bytes 1572872 | tf_op jit(solution)/shard_map/ppermute | solution.py:527
  84.1 1.4 %shard_map.125.refs_5_ = f32[128,128]{1,0:T(8,128)S(1)} custom-call(bf16[128,1024]{1,0:T(8,128)(2,1)S(1)} %copy-done.8, bf16[128,3072]{1,0:T(8,128)(2,1)S(1)} %collective-permute-done.16.refs_2_.refs_1_.refs_12_, bf16[128,4096]{1,0:T(8,128)(2,1)S(1)} %bitcast.34, f32[64,128]{1,0:T(8,128)S(1)} %get-tuple-element.109.refs_3_, ...), custom_call_target="tpu_custom_call" | custom-call | tf_op jit(solution)/shard_map/pallas_call | solution.py:53
  85.5 7.2 %collective-permute-done.20.refs_4_ = bf16[128,2048]{1,0:T(8,128)(2,1)S(1)} collective-permute-done((bf16[128,2048]{1,0:T(8,128)(2,1)S(1)}, bf16[128,2048]{1,0:T(8,128)(2,1)S(1)}, u32[]{:S(2)}, u32[]{:S(2)}) %collective-permute-start.20) | collective-permute-done | bytes 524320 | tf_op jit(solution)/shard_map/ppermute | solution.py:527
  92.7 5.4 %collective-permute-done.14.refs_2_ = bf16[128,2048]{1,0:T(8,128)(2,1)S(1)} collective-permute-done((bf16[128,2048]{1,0:T(8,128)(2,1)S(1)}, bf16[128,2048]{1,0:T(8,128)(2,1)S(1)}, u32[]{:S(2)}, u32[]{:S(2)}) %collective-permute-start.14) | collective-permute-done | bytes 524320 | tf_op jit(solution)/shard_map/ppermute | solution.py:527
  98.2 1.4 %shard_map.126.refs_2_ = bf16[128,4096]{1,0:T(8,128)(2,1)S(1)} custom-call(bf16[128,2048]{1,0:T(8,128)(2,1)S(1)} %copy-done.5, bf16[128,2048]{1,0:T(8,128)(2,1)} %collective-permute-done.13.refs_3_.refs_1_, bf16[128,2048]{1,0:T(8,128)(2,1)S(1)} %collective-permute-done.14.refs_2_, bf16[128,2048]{1,0:T(8,128)(2,1)S(1)} %get-tuple-element.84.refs_3_, ...), custom_call_target="tpu_custom_call" | custom-call | tf_op jit(solution)/shard_map/pallas_call | solution.py:53
  99.7 2.1 %shard_map.127 = (bf16[128,2048]{1,0:T(8,128)(2,1)S(1)}, bf16[128,2048]{1,0:T(8,128)(2,1)S(1)}, f32[128,128]{1,0:T(8,128)S(1)}) custom-call(s32[1]{0:T(128)} %bitcast.refs_0_.refs_1_, bf16[128,4096]{1,0:T(8,128)(2,1)S(1)} %bitcast.35, bf16[128,4096]{1,0:T(8,128)(2,1)S(1)} %shard_map.126.refs_2_, f32[5,64,128]{2,1,0:T(8,128)S(1)} %copy-done.12, ...), custom_call_target="tpu_custom_call" | custom-call | tf_op jit(solution)/shard_map/pallas_call | solution.py:53
  101.8 0.5 collective-permute-done.22.refs_2_
  102.3 2.4 %shard_map.128 = (bf16[128,2048]{1,0:T(8,128)(2,1)S(1)}, bf16[128,2048]{1,0:T(8,128)(2,1)S(1)}, bf16[128,128]{1,0:T(8,128)(2,1)S(1)}) custom-call(s32[1]{0:T(128)} %bitcast.refs_0_.refs_1_, bf16[128,4096]{1,0:T(8,128)(2,1)S(1)} %bitcast.36, bf16[128,4096]{1,0:T(8,128)(2,1)S(1)} %collective-permute-done.22.refs_2_, f32[5,64,128]{2,1,0:T(8,128)S(1)} %copy-done.12, ...), custom_call_target="tpu_custom_call" | custom-call | tf_op jit(solution)/shard_map/pallas_call | solution.py:53
  104.7 1.6 %collective-permute-start.25 = (bf16[128,128]{1,0:T(8,128)(2,1)S(1)}, bf16[128,128]{1,0:T(8,128)(2,1)S(1)}, u32[]{:S(2)}, u32[]{:S(2)}) collective-permute-start(bf16[128,128]{1,0:T(8,128)(2,1)S(1)} %get-tuple-element.100.refs_5_), channel_id=1, source_target_pairs={{0,24},{8,16},{16,8},{24,0},{1,25},{9,17},{17,9},{25,1},{2,26},{10... | collective-permute-start | bytes 98312 | tf_op jit(solution)/shard_map/ppermute | solution.py:530
  106.3 1.6 %collective-permute-start.24 = (bf16[128,128]{1,0:T(8,128)(2,1)S(1)}, bf16[128,128]{1,0:T(8,128)(2,1)S(1)}, u32[]{:S(2)}, u32[]{:S(2)}) collective-permute-start(bf16[128,128]{1,0:T(8,128)(2,1)S(1)} %get-tuple-element.100.refs_5_), channel_id=1, source_target_pairs={{0,16},{8,24},{16,0},{24,8},{1,17},{9,25},{17,1},{25,9},{2,18},{10... | collective-permute-start | bytes 98312 | tf_op jit(solution)/shard_map/ppermute | solution.py:530
  108.4 1.1 copy-done.10
  109.5 0.4 fusion.refs_8_
  110.0 2.7 %shard_map.130.refs_13_ = bf16[128,4096]{1,0:T(8,128)(2,1)} custom-call(s32[1]{0:T(128)} %bitcast.refs_0_.refs_1_, bf16[128,4096]{1,0:T(8,128)(2,1)S(1)} %bitcast.31, bf16[128,2048]{1,0:T(8,128)(2,1)S(1)} %get-tuple-element.89.refs_2_, bf16[128,2048]{1,0:T(8,128)(2,1)S(1)} %get-tuple-element.91.refs_3_, bf16[128,2048]{1,0:T(8,128)(2,1)S(1)} %get-tuple-element.92.refs_4_, ...), custom_call_target="tpu_custom_call" | custom-call | tf_op jit(solution)/shard_map/pallas_call | solution.py:75
  112.7 0.4 shard_map.131
  113.2 1.4 %convolution_convert_fusion = bf16[128,4096]{1,0:T(8,128)(2,1)} fusion(bf16[128,128]{1,0:T(8,128)(2,1)S(1)} %get-tuple-element.100.refs_5_, bf16[4096,128]{1,0:T(8,128)(2,1)S(1)} %bitcast.41), kind=kOutput, calls=%fused_computation | convolution fusion | flops 134742016 | bytes 2129920 | tf_op jit(solution)/shard_map/dot_general | solution.py:92
  114.8 1.9 %collective-permute-start.29 = (bf16[128,128]{1,0:T(8,128)(2,1)S(1)}, bf16[128,128]{1,0:T(8,128)(2,1)S(1)}, u32[]{:S(2)}, u32[]{:S(2)}) collective-permute-start(bf16[128,128]{1,0:T(8,128)(2,1)S(1)} %get-tuple-element.106), channel_id=1, source_target_pairs={{0,6},{1,7},{2,4},{3,5},{4,2},{5,3},{6,0},{7,1},{8,14},{9,15},{10,... | collective-permute-start | bytes 98312 | tf_op jit(solution)/shard_map/ppermute | solution.py:724
  116.6 1.6 %collective-permute-start.27 = (bf16[128,128]{1,0:T(8,128)(2,1)S(1)}, bf16[128,128]{1,0:T(8,128)(2,1)S(1)}, u32[]{:S(2)}, u32[]{:S(2)}) collective-permute-start(bf16[128,128]{1,0:T(8,128)(2,1)S(1)} %get-tuple-element.102), channel_id=1, source_target_pairs={{0,2},{1,3},{2,0},{3,1},{4,6},{5,7},{6,4},{7,5},{8,10},{9,11},{10,... | collective-permute-start | bytes 98312 | tf_op jit(solution)/shard_map/ppermute | solution.py:724
  118.2 2.7 %shard_map.133 = bf16[128,4096]{1,0:T(8,128)(2,1)} custom-call(s32[1]{0:T(128)} %bitcast.refs_0_.refs_1_, bf16[128,4096]{1,0:T(8,128)(2,1)S(1)} %bitcast.32, bf16[128,2048]{1,0:T(8,128)(2,1)S(1)} %get-tuple-element.89.refs_2_, bf16[128,2048]{1,0:T(8,128)(2,1)S(1)} %get-tuple-element.91.refs_3_, ...), custom_call_target="tpu_custom_call", output_to_operand_aliasing={{}: (13, {})} | custom-call | tf_op jit(solution)/shard_map/pallas_call | solution.py:75
  120.9 0.7 add_multiply_fusion
  (95 shorter events, 1.2 us)
Async XLA Ops:
  3.6 13.9 %collective-permute-start.2 = (f32[320,128]{1,0:T(8,128)S(1)}, f32[320,128]{1,0:T(8,128)S(1)}, u32[]{:S(2)}, u32[]{:S(2)}) collective-permute-start(f32[320,128]{1,0:T(8,128)S(1)} %pad_maximum_fusion), channel_id=1, source_target_pairs={{0,7},{1,6},{2,5},{3,4},{4,3},{5,2},{6,1},{7,0},{8,15},{9,14},{10,... | collective-permute-start | bytes 491528 | tf_op jit(solution)/shard_map/ppermute | solution.py:533
  8.1 9.4 %collective-permute-start.4 = (bf16[128,128]{1,0:T(8,128)(2,1)S(1)}, bf16[128,128]{1,0:T(8,128)(2,1)S(1)}, u32[]{:S(2)}, u32[]{:S(2)}) collective-permute-start(bf16[128,128]{1,0:T(8,128)(2,1)S(1)} %get-tuple-element.108.refs_0_), channel_id=1, source_target_pairs={{0,4},{1,5},{2,6},{3,7},{4,0},{5,1},{6,2},{7,3},{8,12},{9,13},{10,... | collective-permute-start | bytes 98312 | tf_op jit(solution)/shard_map/ppermute | solution.py:538
  8.1 9.4 %collective-permute-start.3 = (bf16[128,128]{1,0:T(8,128)(2,1)S(1)}, bf16[128,128]{1,0:T(8,128)(2,1)S(1)}, u32[]{:S(2)}, u32[]{:S(2)}) collective-permute-start(bf16[128,128]{1,0:T(8,128)(2,1)S(1)} %get-tuple-element.108.refs_0_), channel_id=1, source_target_pairs={{0,2},{1,3},{2,0},{3,1},{4,6},{5,7},{6,4},{7,5},{8,10},{9,11},{10,... | collective-permute-start | bytes 98312 | tf_op jit(solution)/shard_map/ppermute | solution.py:538
  9.3 1.2 %copy-start = (bf16[1,128,4096]{2,1,0:T(8,128)(2,1)S(1)}, bf16[1,128,4096]{2,1,0:T(8,128)(2,1)}, u32[]{:S(2)}) copy-start(bf16[1,128,4096]{2,1,0:T(8,128)(2,1)} %param.16) | copy-start | bytes 3145732
  10.6 0.8 copy-start.23
  11.3 0.8 copy-start.29
  12.1 5.4 %copy-start.3 = (bf16[1,128,4096]{2,1,0:T(8,128)(2,1)S(1)}, bf16[1,128,4096]{2,1,0:T(8,128)(2,1)}, u32[]{:S(2)}) copy-start(bf16[1,128,4096]{2,1,0:T(8,128)(2,1)} %param.17) | copy-start | bytes 3145732
  14.9 27.5 %collective-permute-start.8 = (bf16[144,2048]{1,0:T(8,128)(2,1)}, bf16[144,2048]{1,0:T(8,128)(2,1)}, u32[]{:S(2)}, u32[]{:S(2)}) collective-permute-start(bf16[144,2048]{1,0:T(8,128)(2,1)} %get-tuple-element.55.refs_1_), channel_id=1, source_target_pairs={{0,1},{1,0},{2,3},{3,2},{4,5},{5,4},{6,7},{7,6},{8,9},{9,8},{10,11... | collective-permute-start | bytes 1769480 | tf_op jit(solution)/shard_map/ppermute | solution.py:524
  18.5 13.7 %copy-start.24 = (bf16[1,128,128]{2,1,0:T(8,128)(2,1)S(1)}, bf16[1,128,128]{2,1,0:T(8,128)(2,1)}, u32[]{:S(2)}) copy-start(bf16[1,128,128]{2,1,0:T(8,128)(2,1)} %param.13) | copy-start | bytes 98308
  18.5 13.7 %copy-start.30 = (f32[1,64,128]{2,1,0:T(8,128)S(1)}, f32[1,64,128]{2,1,0:T(8,128)}, u32[]{:S(2)}) copy-start(f32[1,64,128]{2,1,0:T(8,128)} %param.15) | copy-start | bytes 98308
  18.5 13.7 %copy-start.33 = (f32[1,64,128]{2,1,0:T(8,128)S(1)}, f32[1,64,128]{2,1,0:T(8,128)}, u32[]{:S(2)}) copy-start(f32[1,64,128]{2,1,0:T(8,128)} %param.14) | copy-start | bytes 98308
  18.5 10.3 %collective-permute-start.15 = (bf16[128,1024]{1,0:T(8,128)(2,1)S(1)}, bf16[128,1024]{1,0:T(8,128)(2,1)S(1)}, u32[]{:S(2)}, u32[]{:S(2)}) collective-permute-start(bf16[128,1024]{1,0:T(8,128)(2,1)S(1)} %get-tuple-element.76), channel_id=1, source_target_pairs={{0,7},{1,6},{2,5},{3,4},{4,3},{5,2},{6,1},{7,0},{8,15},{9,14},{10,... | collective-permute-start | bytes 786440 | tf_op jit(solution)/shard_map/ppermute | solution.py:533
  23.5 6.1 %collective-permute-start.5 = (bf16[144,1024]{1,0:T(8,128)(2,1)S(1)}, bf16[144,1024]{1,0:T(8,128)(2,1)S(1)}, u32[]{:S(2)}, u32[]{:S(2)}) collective-permute-start(bf16[144,1024]{1,0:T(8,128)(2,1)S(1)} %get-tuple-element.60), channel_id=1, source_target_pairs={{0,1},{1,0},{2,3},{3,2},{4,5},{5,4},{6,7},{7,6},{8,9},{9,8},{10,11... | collective-permute-start | bytes 884744 | tf_op jit(solution)/shard_map/ppermute | solution.py:524
  24.0 6.1 %collective-permute-start.6 = (bf16[144,1024]{1,0:T(8,128)(2,1)S(1)}, bf16[144,1024]{1,0:T(8,128)(2,1)S(1)}, u32[]{:S(2)}, u32[]{:S(2)}) collective-permute-start(bf16[144,1024]{1,0:T(8,128)(2,1)S(1)} %get-tuple-element.61), channel_id=1, source_target_pairs={{0,1},{1,0},{2,3},{3,2},{4,5},{5,4},{6,7},{7,6},{8,9},{9,8},{10,11... | collective-permute-start | bytes 884744 | tf_op jit(solution)/shard_map/ppermute | solution.py:524
  24.1 9.3 %collective-permute-start.1 = (bf16[144,1024]{1,0:T(8,128)(2,1)}, bf16[144,1024]{1,0:T(8,128)(2,1)S(1)}, u32[]{:S(2)}, u32[]{:S(2)}) collective-permute-start(bf16[144,1024]{1,0:T(8,128)(2,1)} %get-tuple-element.57), channel_id=1, source_target_pairs={{0,1},{1,0},{2,3},{3,2},{4,5},{5,4},{6,7},{7,6},{8,9},{9,8},{10,11... | collective-permute-start | bytes 884744 | tf_op jit(solution)/shard_map/ppermute | solution.py:524
  28.8 0.7 copy-start.6
  29.6 3.9 %collective-permute-start = (bf16[144,1024]{1,0:T(8,128)(2,1)S(1)}, bf16[144,1024]{1,0:T(8,128)(2,1)S(1)}, u32[]{:S(2)}, u32[]{:S(2)}) collective-permute-start(bf16[144,1024]{1,0:T(8,128)(2,1)S(1)} %get-tuple-element.56), channel_id=1, source_target_pairs={{0,1},{1,0},{2,3},{3,2},{4,5},{5,4},{6,7},{7,6},{8,9},{9,8},{10,11... | collective-permute-start | bytes 884744 | tf_op jit(solution)/shard_map/ppermute | solution.py:524
  29.6 7.5 %collective-permute-start.9 = (bf16[4,128,128]{2,1,0:T(8,128)(2,1)}, bf16[4,128,128]{2,1,0:T(8,128)(2,1)}, u32[]{:S(2)}, u32[]{:S(2)}) collective-permute-start(bf16[4,128,128]{2,1,0:T(8,128)(2,1)} %shard_map.113.refs_2_), channel_id=1, source_target_pairs={{0,1},{1,0},{2,3},{3,2},{4,5},{5,4},{6,7},{7,6},{8,9},{9,8},{10,11... | collective-permute-start | bytes 393224 | tf_op jit(solution)/shard_map/ppermute | solution.py:524
  30.1 38.6 %collective-permute-start.16 = (bf16[128,3072]{1,0:T(8,128)(2,1)}, bf16[128,3072]{1,0:T(8,128)(2,1)S(1)}, u32[]{:S(2)}, u32[]{:S(2)}) collective-permute-start(bf16[128,3072]{1,0:T(8,128)(2,1)} %get-tuple-element.78), channel_id=1, source_target_pairs={{0,7},{1,6},{2,5},{3,4},{4,3},{5,2},{6,1},{7,0},{8,15},{9,14},{10,... | collective-permute-start | bytes 2359304 | tf_op jit(solution)/shard_map/ppermute | solution.py:533
  33.4 9.5 %copy-start.11 = (f32[5,64,128]{2,1,0:T(8,128)}, f32[5,64,128]{2,1,0:T(8,128)S(1)}, u32[]{:S(2)}) copy-start(f32[5,64,128]{2,1,0:T(8,128)S(1)} %get-tuple-element.67.refs_3_.refs_6_) | copy-start | bytes 491524
  33.4 4.8 %copy-start.9 = (bf16[1,128,4096]{2,1,0:T(8,128)(2,1)S(1)}, bf16[1,128,4096]{2,1,0:T(8,128)(2,1)}, u32[]{:S(2)}) copy-start(bf16[1,128,4096]{2,1,0:T(8,128)(2,1)} %param.9) | copy-start | bytes 3145732
  33.4 9.5 %copy-start.2 = (bf16[1,128,4096]{2,1,0:T(8,128)(2,1)S(1)}, bf16[1,128,4096]{2,1,0:T(8,128)(2,1)}, u32[]{:S(2)}) copy-start(bf16[1,128,4096]{2,1,0:T(8,128)(2,1)} %param.12) | copy-start | bytes 3145732
  34.9 0.7 copy-start.25
  35.6 0.7 copy-start.27
  36.3 29.8 %copy-start.21 = (bf16[128,2048]{1,0:T(8,128)(2,1)}, bf16[128,2048]{1,0:T(8,128)(2,1)S(1)}, u32[]{:S(2)}) copy-start(bf16[128,2048]{1,0:T(8,128)(2,1)S(1)} %get-tuple-element.65.refs_0_) | copy-start | bytes 1572868
  36.3 6.6 %copy-start.1 = (bf16[1,128,4096]{2,1,0:T(8,128)(2,1)S(1)}, bf16[1,128,4096]{2,1,0:T(8,128)(2,1)}, u32[]{:S(2)}) copy-start(bf16[1,128,4096]{2,1,0:T(8,128)(2,1)} %param.16) | copy-start | bytes 3145732
  36.3 8.6 %collective-permute-start.7 = (bf16[128,2048]{1,0:T(8,128)(2,1)S(1)}, bf16[128,2048]{1,0:T(8,128)(2,1)S(1)}, u32[]{:S(2)}, u32[]{:S(2)}) collective-permute-start(bf16[128,2048]{1,0:T(8,128)(2,1)S(1)} %get-tuple-element.65.refs_0_), channel_id=1, source_target_pairs={{6,4},{7,5},{14,12},{15,13},{22,20},{23,21},{30,28},{31,29}} | collective-permute-start | bytes 1572872 | tf_op jit(solution)/shard_map/ppermute | solution.py:527
  38.6 0.8 copy-start.13
  39.4 14.7 %collective-permute-start.10 = (bf16[2048,128]{1,0:T(8,128)(2,1)S(1)}, bf16[2048,128]{1,0:T(8,128)(2,1)S(1)}, u32[]{:S(2)}, u32[]{:S(2)}) collective-permute-start(bf16[2048,128]{1,0:T(8,128)(2,1)S(1)} %get-tuple-element.71), channel_id=1, source_target_pairs={{0,8},{8,0},{16,24},{24,16},{1,9},{9,1},{17,25},{25,17},{2,10},{10... | collective-permute-start | bytes 1572872 | tf_op jit(solution)/shard_map/ppermute | solution.py:530
  40.9 25.2 %collective-permute-start.11 = (bf16[2048,128]{1,0:T(8,128)(2,1)S(1)}, bf16[2048,128]{1,0:T(8,128)(2,1)S(1)}, u32[]{:S(2)}, u32[]{:S(2)}) collective-permute-start(bf16[2048,128]{1,0:T(8,128)(2,1)S(1)} %get-tuple-element.72), channel_id=1, source_target_pairs={{0,16},{8,24},{16,0},{24,8},{1,17},{9,25},{17,1},{25,9},{2,18},{10... | collective-permute-start | bytes 1572872 | tf_op jit(solution)/shard_map/ppermute | solution.py:530
  42.4 23.7 %collective-permute-start.12 = (bf16[2048,128]{1,0:T(8,128)(2,1)S(1)}, bf16[2048,128]{1,0:T(8,128)(2,1)S(1)}, u32[]{:S(2)}, u32[]{:S(2)}) collective-permute-start(bf16[2048,128]{1,0:T(8,128)(2,1)S(1)} %get-tuple-element.73), channel_id=1, source_target_pairs={{0,24},{8,16},{16,8},{24,0},{1,25},{9,17},{17,9},{25,1},{2,26},{10... | collective-permute-start | bytes 1572872 | tf_op jit(solution)/shard_map/ppermute | solution.py:530
  44.3 0.6 copy-start.31
  45.0 23.7 %copy-start.7 = (bf16[128,1024]{1,0:T(8,128)(2,1)S(1)}, bf16[128,1024]{1,0:T(8,128)(2,1)}, u32[]{:S(2)}) copy-start(bf16[128,1024]{1,0:T(8,128)(2,1)} %copy-done.6) | copy-start | bytes 786436
  45.0 26.8 %copy-start.4 = (bf16[128,2048]{1,0:T(8,128)(2,1)}, bf16[128,2048]{1,0:T(8,128)(2,1)S(1)}, u32[]{:S(2)}) copy-start(bf16[128,2048]{1,0:T(8,128)(2,1)S(1)} %collective-permute-done.7.refs_2_.refs_0_) | copy-start | bytes 1572868
  45.0 27.5 %collective-permute-start.19 = (bf16[128,2048]{1,0:T(8,128)(2,1)}, bf16[128,2048]{1,0:T(8,128)(2,1)}, u32[]{:S(2)}, u32[]{:S(2)}) collective-permute-start(bf16[128,2048]{1,0:T(8,128)(2,1)} %get-tuple-element.63.refs_5_), channel_id=1, source_target_pairs={{6,4},{7,5},{14,12},{15,13},{22,20},{23,21},{30,28},{31,29}} | collective-permute-start | bytes 1572872 | tf_op jit(solution)/shard_map/ppermute | solution.py:527
  54.1 17.7 %copy-start.15 = (bf16[2048,128]{1,0:T(8,128)(2,1)}, bf16[2048,128]{1,0:T(8,128)(2,1)S(1)}, u32[]{:S(2)}) copy-start(bf16[2048,128]{1,0:T(8,128)(2,1)S(1)} %collective-permute-done.10.refs_2_) | copy-start | bytes 1572868
  66.1 1.1 copy-start.17
  66.1 5.7 %copy-start.19 = (bf16[2048,128]{1,0:T(8,128)(2,1)}, bf16[2048,128]{1,0:T(8,128)(2,1)S(1)}, u32[]{:S(2)}) copy-start(bf16[2048,128]{1,0:T(8,128)(2,1)S(1)} %collective-permute-done.12.refs_4_) | copy-start | bytes 1572868
  67.2 14.0 %collective-permute-start.13 = (bf16[128,2048]{1,0:T(8,128)(2,1)}, bf16[128,2048]{1,0:T(8,128)(2,1)}, u32[]{:S(2)}, u32[]{:S(2)}) collective-permute-start(bf16[128,2048]{1,0:T(8,128)(2,1)} %shard_map.120), channel_id=1, source_target_pairs={{4,2},{5,3},{12,10},{13,11},{20,18},{21,19},{28,26},{29,27}} | collective-permute-start | bytes 1572872 | tf_op jit(solution)/shard_map/ppermute | solution.py:527
  71.8 2.0 %collective-permute-start.17 = (bf16[144,1024]{1,0:T(8,128)(2,1)}, bf16[144,1024]{1,0:T(8,128)(2,1)}, u32[]{:S(2)}, u32[]{:S(2)}) collective-permute-start(bf16[144,1024]{1,0:T(8,128)(2,1)} %get-tuple-element.81), channel_id=1, source_target_pairs={{0,1},{1,0},{2,3},{3,2},{4,5},{5,4},{6,7},{7,6},{8,9},{9,8},{10,11... | collective-permute-start | bytes 884744 | tf_op jit(solution)/shard_map/ppermute | solution.py:524
  71.9 2.3 %collective-permute-start.18 = (bf16[144,1024]{1,0:T(8,128)(2,1)}, bf16[144,1024]{1,0:T(8,128)(2,1)}, u32[]{:S(2)}, u32[]{:S(2)}) collective-permute-start(bf16[144,1024]{1,0:T(8,128)(2,1)} %get-tuple-element.82), channel_id=1, source_target_pairs={{0,1},{1,0},{2,3},{3,2},{4,5},{5,4},{6,7},{7,6},{8,9},{9,8},{10,11... | collective-permute-start | bytes 884744 | tf_op jit(solution)/shard_map/ppermute | solution.py:524
  72.4 13.1 %collective-permute-start.21 = (bf16[144,2048]{1,0:T(8,128)(2,1)}, bf16[144,2048]{1,0:T(8,128)(2,1)}, u32[]{:S(2)}, u32[]{:S(2)}) collective-permute-start(bf16[144,2048]{1,0:T(8,128)(2,1)} %get-tuple-element.80.refs_2_), channel_id=1, source_target_pairs={{0,1},{1,0},{2,3},{3,2},{4,5},{5,4},{6,7},{7,6},{8,9},{9,8},{10,11... | collective-permute-start | bytes 1769480 | tf_op jit(solution)/shard_map/ppermute | solution.py:524
  74.2 7.1 %copy-start.5 = (bf16[128,2048]{1,0:T(8,128)(2,1)S(1)}, bf16[128,2048]{1,0:T(8,128)(2,1)}, u32[]{:S(2)}) copy-start(bf16[128,2048]{1,0:T(8,128)(2,1)} %copy-done.4) | copy-start | bytes 1572868
  74.2 7.1 %copy-start.22 = (bf16[128,2048]{1,0:T(8,128)(2,1)S(1)}, bf16[128,2048]{1,0:T(8,128)(2,1)}, u32[]{:S(2)}) copy-start(bf16[128,2048]{1,0:T(8,128)(2,1)} %copy-done.21) | copy-start | bytes 1572868
  76.7 7.3 %copy-start.8 = (bf16[128,1024]{1,0:T(8,128)(2,1)S(1)}, bf16[128,1024]{1,0:T(8,128)(2,1)}, u32[]{:S(2)}) copy-start(bf16[128,1024]{1,0:T(8,128)(2,1)} %copy-done.6) | copy-start | bytes 786436
  76.7 16.0 %collective-permute-start.20 = (bf16[128,2048]{1,0:T(8,128)(2,1)S(1)}, bf16[128,2048]{1,0:T(8,128)(2,1)S(1)}, u32[]{:S(2)}, u32[]{:S(2)}) collective-permute-start(bf16[128,2048]{1,0:T(8,128)(2,1)S(1)} %get-tuple-element.85), channel_id=1, source_target_pairs={{0,2},{1,3},{4,6},{5,7},{8,10},{9,11},{12,14},{13,15},{16,18},{17,... | collective-permute-start | bytes 1572872 | tf_op jit(solution)/shard_map/ppermute | solution.py:527
  82.6 15.6 %collective-permute-start.14 = (bf16[128,2048]{1,0:T(8,128)(2,1)S(1)}, bf16[128,2048]{1,0:T(8,128)(2,1)S(1)}, u32[]{:S(2)}, u32[]{:S(2)}) collective-permute-start(bf16[128,2048]{1,0:T(8,128)(2,1)S(1)} %shard_map.121), channel_id=1, source_target_pairs={{2,0},{3,1},{10,8},{11,9},{18,16},{19,17},{26,24},{27,25}} | collective-permute-start | bytes 1572872 | tf_op jit(solution)/shard_map/ppermute | solution.py:527
  98.2 1.5 %copy-start.12 = (f32[5,64,128]{2,1,0:T(8,128)S(1)}, f32[5,64,128]{2,1,0:T(8,128)}, u32[]{:S(2)}) copy-start(f32[5,64,128]{2,1,0:T(8,128)} %copy-done.11) | copy-start | bytes 491524
  98.2 1.5 %copy-start.26 = (bf16[144,1024]{1,0:T(8,128)(2,1)S(1)}, bf16[144,1024]{1,0:T(8,128)(2,1)}, u32[]{:S(2)}) copy-start(bf16[144,1024]{1,0:T(8,128)(2,1)} %copy-done.25) | copy-start | bytes 884740
  98.2 1.5 %copy-start.28 = (bf16[144,1024]{1,0:T(8,128)(2,1)S(1)}, bf16[144,1024]{1,0:T(8,128)(2,1)}, u32[]{:S(2)}) copy-start(bf16[144,1024]{1,0:T(8,128)(2,1)} %copy-done.27) | copy-start | bytes 884740
  98.2 1.6 %copy-start.32 = (f32[128,128]{1,0:T(8,128)S(1)}, f32[128,128]{1,0:T(8,128)}, u32[]{:S(2)}) copy-start(f32[128,128]{1,0:T(8,128)} %copy-done.31) | copy-start | bytes 196612
  99.6 2.7 %collective-permute-start.22 = (bf16[128,4096]{1,0:T(8,128)(2,1)S(1)}, bf16[128,4096]{1,0:T(8,128)(2,1)S(1)}, u32[]{:S(2)}, u32[]{:S(2)}) collective-permute-start(bf16[128,4096]{1,0:T(8,128)(2,1)S(1)} %shard_map.126.refs_2_), channel_id=1, source_target_pairs={{0,1},{1,0},{2,3},{3,2},{4,5},{5,4},{6,7},{7,6},{8,9},{9,8},{10,11... | collective-permute-start | bytes 3145736 | tf_op jit(solution)/shard_map/ppermute | solution.py:524
  102.3 6.0 %copy-start.14 = (bf16[2048,128]{1,0:T(8,128)(2,1)S(1)}, bf16[2048,128]{1,0:T(8,128)(2,1)}, u32[]{:S(2)}) copy-start(bf16[2048,128]{1,0:T(8,128)(2,1)} %copy-done.13) | copy-start | bytes 1572868
  102.3 6.0 %copy-start.16 = (bf16[2048,128]{1,0:T(8,128)(2,1)S(1)}, bf16[2048,128]{1,0:T(8,128)(2,1)}, u32[]{:S(2)}) copy-start(bf16[2048,128]{1,0:T(8,128)(2,1)} %copy-done.15) | copy-start | bytes 1572868
  102.3 6.0 %copy-start.18 = (bf16[2048,128]{1,0:T(8,128)(2,1)S(1)}, bf16[2048,128]{1,0:T(8,128)(2,1)}, u32[]{:S(2)}) copy-start(bf16[2048,128]{1,0:T(8,128)(2,1)} %copy-done.17) | copy-start | bytes 1572868
  102.3 6.0 %copy-start.20 = (bf16[2048,128]{1,0:T(8,128)(2,1)S(1)}, bf16[2048,128]{1,0:T(8,128)(2,1)}, u32[]{:S(2)}) copy-start(bf16[2048,128]{1,0:T(8,128)(2,1)} %copy-done.19) | copy-start | bytes 1572868
  104.7 8.0 %collective-permute-start.25 = (bf16[128,128]{1,0:T(8,128)(2,1)S(1)}, bf16[128,128]{1,0:T(8,128)(2,1)S(1)}, u32[]{:S(2)}, u32[]{:S(2)}) collective-permute-start(bf16[128,128]{1,0:T(8,128)(2,1)S(1)} %get-tuple-element.100.refs_5_), channel_id=1, source_target_pairs={{0,24},{8,16},{16,8},{24,0},{1,25},{9,17},{17,9},{25,1},{2,26},{10... | collective-permute-start | bytes 98312 | tf_op jit(solution)/shard_map/ppermute | solution.py:530
  106.3 6.4 %collective-permute-start.24 = (bf16[128,128]{1,0:T(8,128)(2,1)S(1)}, bf16[128,128]{1,0:T(8,128)(2,1)S(1)}, u32[]{:S(2)}, u32[]{:S(2)}) collective-permute-start(bf16[128,128]{1,0:T(8,128)(2,1)S(1)} %get-tuple-element.100.refs_5_), channel_id=1, source_target_pairs={{0,16},{8,24},{16,0},{24,8},{1,17},{9,25},{17,1},{25,9},{2,18},{10... | collective-permute-start | bytes 98312 | tf_op jit(solution)/shard_map/ppermute | solution.py:530
  107.9 4.8 %collective-permute-start.23 = (bf16[128,128]{1,0:T(8,128)(2,1)S(1)}, bf16[128,128]{1,0:T(8,128)(2,1)S(1)}, u32[]{:S(2)}, u32[]{:S(2)}) collective-permute-start(bf16[128,128]{1,0:T(8,128)(2,1)S(1)} %get-tuple-element.100.refs_5_), channel_id=1, source_target_pairs={{0,8},{8,0},{16,24},{24,16},{1,9},{9,1},{17,25},{25,17},{2,10},{10... | collective-permute-start | bytes 98312 | tf_op jit(solution)/shard_map/ppermute | solution.py:530
  108.3 1.2 %copy-start.10 = (bf16[1,128,4096]{2,1,0:T(8,128)(2,1)S(1)}, bf16[1,128,4096]{2,1,0:T(8,128)(2,1)}, u32[]{:S(2)}) copy-start(bf16[1,128,4096]{2,1,0:T(8,128)(2,1)} %param.9) | copy-start | bytes 3145732
  113.2 1.5 %collective-permute-start.26 = (bf16[4,128,128]{2,1,0:T(8,128)(2,1)S(1)}, bf16[4,128,128]{2,1,0:T(8,128)(2,1)S(1)}, u32[]{:S(2)}, u32[]{:S(2)}) collective-permute-start(bf16[4,128,128]{2,1,0:T(8,128)(2,1)S(1)} %get-tuple-element.99), channel_id=1, source_target_pairs={{0,1},{1,0},{2,3},{3,2},{4,5},{5,4},{6,7},{7,6},{8,9},{9,8},{10,11... | collective-permute-start | bytes 393224 | tf_op jit(solution)/shard_map/ppermute | solution.py:524
  114.7 6.3 %collective-permute-start.28 = (bf16[128,128]{1,0:T(8,128)(2,1)S(1)}, bf16[128,128]{1,0:T(8,128)(2,1)S(1)}, u32[]{:S(2)}, u32[]{:S(2)}) collective-permute-start(bf16[128,128]{1,0:T(8,128)(2,1)S(1)} %get-tuple-element.105), channel_id=1, source_target_pairs={{0,4},{1,5},{2,6},{3,7},{4,0},{5,1},{6,2},{7,3},{8,12},{9,13},{10,... | collective-permute-start | bytes 98312 | tf_op jit(solution)/shard_map/ppermute | solution.py:724
  114.8 6.2 %collective-permute-start.29 = (bf16[128,128]{1,0:T(8,128)(2,1)S(1)}, bf16[128,128]{1,0:T(8,128)(2,1)S(1)}, u32[]{:S(2)}, u32[]{:S(2)}) collective-permute-start(bf16[128,128]{1,0:T(8,128)(2,1)S(1)} %get-tuple-element.106), channel_id=1, source_target_pairs={{0,6},{1,7},{2,4},{3,5},{4,2},{5,3},{6,0},{7,1},{8,14},{9,15},{10,... | collective-permute-start | bytes 98312 | tf_op jit(solution)/shard_map/ppermute | solution.py:724
  116.6 4.3 %collective-permute-start.27 = (bf16[128,128]{1,0:T(8,128)(2,1)S(1)}, bf16[128,128]{1,0:T(8,128)(2,1)S(1)}, u32[]{:S(2)}, u32[]{:S(2)}) collective-permute-start(bf16[128,128]{1,0:T(8,128)(2,1)S(1)} %get-tuple-element.102), channel_id=1, source_target_pairs={{0,2},{1,3},{2,0},{3,1},{4,6},{5,7},{6,4},{7,5},{8,10},{9,11},{10,... | collective-permute-start | bytes 98312 | tf_op jit(solution)/shard_map/ppermute | solution.py:724
